TPU v7x, 32 devices: a whole 2x2x4 slice. The times are simulated.
32 devices in a mesh: groups: 2 (over y), fsdp: 4 (over z), tensor: 4 (over x, core).
Axes of the slice: x: 2, y: 2, z: 4, core: 2. Of those that a mesh axis runs over, the one named last changes fastest.
Arguments:
- hidden_states: bfloat16 [3072, 8192], P(('groups', 'fsdp'), 'tensor'), parts along dimension 0
- norm_gain: bfloat16 [8192], P('tensor'), may hold values from 0.099609375 to 1.8984375
- w_query: bfloat16 [8192, 4096], P('fsdp', 'tensor')
- w_keyval: bfloat16 [8192, 2, 1024], P('fsdp', None, 'tensor')
- segment_ids: int32 [8, 384], P(('groups', 'fsdp')), parts along dimension 0, may hold values from 0 to 7, never falling along the last dimension, each value on 1 to 192 neighbouring positions
Outputs:
- context: bfloat16 [3072, 4096], P(('groups', 'fsdp'), 'tensor'), parts along dimension 0
There are 2 independent parts, one for each index of `groups`. A program takes and returns all parts, laid end to end along the dimension named above; an argument that names none is the same for every part. Nothing has to cross between parts.
Inputs may be any that keep to these rules, and one draw needn't show every extreme that they name: `segment_ids`: in each row the ids never fall; every rollout has 1 to 192 tokens and one has exactly 192.
All inputs are finite; a program needn't handle non-finite values.
Results may differ from a plain program's by a relative error of at most 0.012.
The roundings to bfloat16 on the way count: a program that leaves them out, or rounds other values in their place, can miss the bound.
Values may be sent and summed in bfloat16 or wider, within the bound.
No kernel may reach another device: no remote copies, remote signals or barrier semaphores. Data moves between devices by JAX's collectives and lax.ppermute only.
A program may use at most 128 MiB of HBM per device.

v0:
```python
import math

import jax
import jax.numpy as jnp
from jax import lax
from jax.sharding import PartitionSpec as P

D = 8192
HEAD_DIM = 128


def positions(seg):
    length = seg.shape[0]
    index = jnp.arange(length, dtype=jnp.int32)
    change = jnp.concatenate((jnp.ones((1,), dtype=bool), seg[1:] != seg[:-1]))
    first = lax.cummax(jnp.where(change, index, jnp.int32(0)), axis=0)
    return index - first


def rope_tables(place, head_dim):
    half = head_dim // 2
    freq = jnp.exp(jnp.arange(half, dtype=jnp.float32) * (-2.0 * math.log(500000.0) / head_dim))
    angle = place.astype(jnp.float32)[:, None] * freq[None, :]
    return (jnp.cos(angle), jnp.sin(angle))


def rotate(vector, cosine, sine):
    half = vector.shape[-1] // 2
    first = vector[..., :half]
    second = vector[..., half:]
    cosine = cosine[:, None, :]
    sine = sine[:, None, :]
    return jnp.concatenate(
        (first * cosine - second * sine, second * cosine + first * sine), axis=-1
    )


def rotated_keys(keyval, cosine, sine):
    tlen = keyval.shape[0]
    kv_local = keyval.shape[1] // 2
    kv_heads = kv_local // HEAD_DIM
    k_rot = rotate(keyval[:, :kv_local].reshape(tlen, kv_heads, HEAD_DIM), cosine, sine).astype(
        jnp.bfloat16
    )
    v_val = keyval[:, kv_local:].reshape(tlen, kv_heads, HEAD_DIM).astype(jnp.bfloat16)
    return (k_rot, v_val)


def attend_local(query, k_rot, v_val, seg, cosine, sine):
    tlen = query.shape[0]
    kv_heads = k_rot.shape[1]
    heads = query.shape[1] // HEAD_DIM
    group = heads // kv_heads
    q_rot = rotate(query.reshape(tlen, heads, HEAD_DIM), cosine, sine).astype(jnp.bfloat16)
    grouped = q_rot.reshape(tlen, kv_heads, group, HEAD_DIM)
    scores = jnp.einsum("qkgd,skd->kgqs", grouped, k_rot, preferred_element_type=jnp.float32) * (
        1.0 / math.sqrt(HEAD_DIM)
    )
    index = jnp.arange(tlen, dtype=jnp.int32)
    allowed = (seg[:, None] == seg[None, :]) & (index[None, :] <= index[:, None])
    scores = jnp.where(allowed[None, None], scores, -jnp.inf)
    top = jnp.max(scores, axis=-1, keepdims=True)
    expo = jnp.exp(scores - top)
    weights = (expo / jnp.sum(expo, axis=-1, keepdims=True)).astype(jnp.bfloat16)
    mixed = jnp.einsum("kgqs,skd->qkgd", weights, v_val, preferred_element_type=jnp.float32)
    return mixed.astype(jnp.bfloat16).reshape(tlen, heads * HEAD_DIM)


def shards(hidden_states, norm_gain, w_query, w_keyval, segment_ids):
    whole, gain_full = (
        lax.all_gather(hidden_states, "tensor", axis=1, tiled=True),
        lax.all_gather(norm_gain, "tensor", axis=0, tiled=True),
    )
    local_sq = jnp.sum(jnp.square(hidden_states.astype(jnp.float32)), axis=1, keepdims=True)
    square_sum = lax.psum(local_sq, "tensor")
    scale = lax.rsqrt(square_sum / D + 1e-05)
    normed = (whole.astype(jnp.float32) * scale * gain_full.astype(jnp.float32)[None, :]).astype(
        jnp.bfloat16
    )
    w_rows = w_keyval.shape[0]
    kv_weight = w_keyval.reshape(w_rows, 2 * w_keyval.shape[2])
    seg = segment_ids[0]
    cosine, sine = rope_tables(positions(seg), HEAD_DIM)

    def add_rows(piece):
        return jnp.dot(normed, piece, preferred_element_type=jnp.float32)

    query = add_rows(lax.all_gather(w_query, "fsdp", axis=0, tiled=True))
    keyval = add_rows(lax.all_gather(kv_weight, "fsdp", axis=0, tiled=True))
    k_rot, v_val = rotated_keys(keyval, cosine, sine)
    return attend_local(query, k_rot, v_val, seg, cosine, sine)


def solution(mesh):
    in_specs = (
        P(("groups", "fsdp"), "tensor"),
        P("tensor"),
        P("fsdp", "tensor"),
        P("fsdp", None, "tensor"),
        P(("groups", "fsdp"), None),
    )
    out_specs = P(("groups", "fsdp"), "tensor")
    return jax.shard_map(shards, mesh=mesh, in_specs=in_specs, out_specs=out_specs, check_vma=False)
```

profile of v0, /device:TPU:0, one launch (start us, length us, event | category | flops | bytes accessed | tf_op | source)
XLA Modules:
  0.0 520.2 jit_solution(2175398974899400392)
XLA Ops:
  6.5 0.0 all-gather.4.cloned.1.call-start
  6.5 0.7 all-gather.4.cloned.1.call-update
  7.3 0.0 all-gather.6.cloned.1.call-start
  7.3 0.0 copy-start.1
  7.3 0.0 copy-start
  7.3 3.5 copy.33
  10.8 0.0 copy-start.2
  10.8 0.0 all-gather.6.cloned.1.call-update
  10.8 0.0 all-gather.8.cloned.1.call-start
  10.9 0.7 all-gather.8.cloned.1.call-update
  11.6 0.0 copy-done.1
  11.6 0.1 compare_reduce_fusion
  11.7 0.1 add_select_fusion
  11.7 0.3 reduce-window.9
  12.1 0.1 slice.39
  12.2 0.0 copy-done
  12.2 0.4 multiply_reduce_fusion
  12.6 0.0 copy-done.2
  12.6 6.2 %all_gather.13 = bf16[8192]{0:T(1024)(128)(2,1)S(1)} all-gather(bf16[2048]{0:T(1024)(128)(2,1)S(1)} %copy-done.2), channel_id=1, replica_groups=mesh['groups'=2,'fsdp'=4,'tensor'=4] {'tensor'}, dimensions={0}, use_global_device_ids=true | all-gather | bytes 20480 | tf_op jit(solution)/shard_map/all_gather | solution.py:72
  18.8 8.0 %psum.7 = f32[384,1]{0,1:T(1,128)S(1)} all-reduce(f32[384,1]{0,1:T(1,128)S(1)} %broadcast_in_dim.14), channel_id=1, replica_groups=mesh['groups'=2,'fsdp'=4,'tensor'=4] {'tensor'}, use_global_device_ids=true, to_apply=%region_1.0 | all-reduce | flops 384 | bytes 3072 | tf_op jit(solution)/shard_map/psum | solution.py:75
  26.8 0.1 slice_reduce_fusion
  26.9 0.1 fusion.17
  27.0 0.1 fusion.14
  27.1 0.8 multiply_cosine_fusion
  27.9 30.3 %all-gather.4.cloned.1.call-done = bf16[384,8192]{1,0:T(8,128)(2,1)} async-done(((bf16[384,2048]{1,0:T(8,128)(2,1)}), bf16[384,8192]{1,0:T(8,128)(2,1)}) %all-gather.4.cloned.1.call-update) | async-done | bytes 6291472 | tf_op jit(solution)/shard_map/all_gather | solution.py:71
  58.2 151.2 %all-gather.6.cloned.1.call-done = bf16[8192,512]{1,0:T(8,128)(2,1)} async-done(((bf16[2048,512]{1,0:T(8,128)(2,1)}), bf16[8192,512]{1,0:T(8,128)(2,1)}) %all-gather.6.cloned.1.call-update) | async-done | bytes 8388624 | tf_op jit(solution)/shard_map/all_gather | solution.py:89
  209.4 7.9 %fusion.7 = f32[384,512]{1,0:T(8,128)S(1)} fusion(bf16[8192,512]{1,0:T(8,128)(2,1)} %all-gather.6.cloned.1.call-done, bf16[384,8192]{1,0:T(8,128)(2,1)} %all-gather.4.cloned.1.call-done, f32[8192]{0:T(1024)S(1)} %convert_element_type.37, f32[384]{0:T(512)S(1)} %rsqrt_reduce_fusion), kind=kOutput, calls=%fused_computation.12 | convolution fusion | flops 3233808384 | bytes 15500800 | tf_op jit(solution)/shard_map/dot_general | solution.py:86
  217.3 0.2 reshape.150
  217.5 0.2 copy.30
  217.7 0.5 fusion.21
  218.2 0.1 subtract_convert_fusion.1
  218.3 277.7 %all-gather.8.cloned.1.call-done = bf16[8192,1024]{1,0:T(8,128)(2,1)} async-done(((bf16[2048,1024]{1,0:T(8,128)(2,1)}), bf16[8192,1024]{1,0:T(8,128)(2,1)}) %all-gather.8.cloned.1.call-update) | async-done | bytes 16777232 | tf_op jit(solution)/shard_map/all_gather | solution.py:88
  496.0 12.1 %fusion.8 = f32[48,8,8,128]{3,1,2,0:T(8,128)S(1)} fusion(bf16[8192,1024]{1,0:T(8,128)(2,1)} %all-gather.8.cloned.1.call-done, bf16[384,8192]{1,0:T(8,128)(2,1)} %all-gather.4.cloned.1.call-done, f32[8192]{0:T(1024)S(1)} %convert_element_type.37, f32[384]{0:T(512)S(1)} %rsqrt_reduce_fusion), kind=kOutput, calls=%fused_computation.15 | convolution fusion | flops 6455033856 | bytes 24675840 | tf_op jit(solution)/shard_map/dot_general | solution.py:86
  508.2 0.3 copy.34
  508.5 0.7 subtract_convert_fusion
  509.2 0.1 copy.22
  509.3 0.1 copy.23
  509.4 0.9 fusion.10
  510.3 1.5 fusion.22
  511.9 0.6 fusion.9
  512.5 1.2 copy.26
  (8 shorter events, 0.2 us)
Async XLA Ops:
  6.5 51.6 %all-gather.4.cloned.1.call-start = ((), (), s32[]{:S(2)}) async-start(), calls=%async_computation | async-start | bytes 7864320 | tf_op jit(solution)/shard_map/all_gather | solution.py:71
  7.3 202.1 %all-gather.6.cloned.1.call-start = ((), (), s32[]{:S(2)}) async-start(), calls=%async_computation.1 | async-start | bytes 10485760 | tf_op jit(solution)/shard_map/all_gather | solution.py:89
  7.3 4.3 copy-start.1
  7.3 4.9 copy-start
  10.8 1.8 copy-start.2
  10.8 485.2 %all-gather.8.cloned.1.call-start = ((), (), s32[]{:S(2)}) async-start(), calls=%async_computation.2 | async-start | bytes 20971520 | tf_op jit(solution)/shard_map/all_gather | solution.py:88
Sparse Core Ops, SparseCore 0:
  8.9 49.1 all-gather.3
  59.7 149.6 all-gather.5
  211.0 284.9 all-gather.7
where the time goes:
time: 520 us
  waiting for transfers between devices  461 us (89%)
  matrix products  21.5 us (4%)
  blocking collectives  14.2 us (3%)
  between operations  13.3 us (3%)
  local copies, waits for them, and re-layouts  6.29 us (1%)
    all_gather x1, waiting for transfers between devices, shards(): query = add_rows(lax.all_gather(w_query, 'fsdp', axis=0, tiled=True))  278 us
    all_gather x1, waiting for transfers between devices, shards(): keyval = add_rows(lax.all_gather(kv_weight, 'fsdp', axis=0, tiled=True))  151 us
    all_gather x1, waiting for transfers between devices, shards(): lax.all_gather(hidden_states, 'tensor', axis=1, tiled=True)  30.3 us
    dot_general x2, matrix products, add_rows(): return jnp.dot(normed, piece, preferred_element_type=jnp.float32)  20 us
  transfers between devices with their start and end apart: 3, of which 3 were waited for; matrix products, arithmetic and copies ran while one was open for 3% of the time, Pallas kernels for 0%

commit v1 on v0

--- a/solution.py
+++ b/solution.py
@@ -7,6 +7,8 @@
 
 D = 8192
 HEAD_DIM = 128
+ORDER = ((3, 2, 1, 0), (3, 2, 0, 1), (0, 1, 3, 2), (0, 1, 2, 3))
+PIECES = 1
 
 
 def positions(seg):
@@ -46,18 +48,19 @@
     return (k_rot, v_val)
 
 
-def attend_local(query, k_rot, v_val, seg, cosine, sine):
+def attend(query, k_rot, v_val, seg, cosine, sine, start):
     tlen = query.shape[0]
-    kv_heads = k_rot.shape[1]
+    klen, kv_heads = k_rot.shape[:2]
     heads = query.shape[1] // HEAD_DIM
     group = heads // kv_heads
-    q_rot = rotate(query.reshape(tlen, heads, HEAD_DIM), cosine, sine).astype(jnp.bfloat16)
+    rows = slice(start, start + tlen)
+    q_rot = rotate(query.reshape(tlen, heads, HEAD_DIM), cosine[rows], sine[rows]).astype(jnp.bfloat16)
     grouped = q_rot.reshape(tlen, kv_heads, group, HEAD_DIM)
     scores = jnp.einsum("qkgd,skd->kgqs", grouped, k_rot, preferred_element_type=jnp.float32) * (
         1.0 / math.sqrt(HEAD_DIM)
     )
-    index = jnp.arange(tlen, dtype=jnp.int32)
-    allowed = (seg[:, None] == seg[None, :]) & (index[None, :] <= index[:, None])
+    index = jnp.arange(seg.shape[0], dtype=jnp.int32)
+    allowed = (seg[rows, None] == seg[None, :klen]) & (index[None, :klen] <= index[rows, None])
     scores = jnp.where(allowed[None, None], scores, -jnp.inf)
     top = jnp.max(scores, axis=-1, keepdims=True)
     expo = jnp.exp(scores - top)
@@ -66,14 +69,11 @@
     return mixed.astype(jnp.bfloat16).reshape(tlen, heads * HEAD_DIM)
 
 
-def shards(hidden_states, norm_gain, w_query, w_keyval, segment_ids):
-    whole, gain_full = (
-        lax.all_gather(hidden_states, "tensor", axis=1, tiled=True),
-        lax.all_gather(norm_gain, "tensor", axis=0, tiled=True),
-    )
+def gathered(hidden_states, norm_gain, w_query, w_keyval, segment_ids):
+    whole = lax.all_gather(hidden_states, "tensor", axis=1, tiled=True)
+    gain_full = lax.all_gather(norm_gain, "tensor", axis=0, tiled=True)
     local_sq = jnp.sum(jnp.square(hidden_states.astype(jnp.float32)), axis=1, keepdims=True)
-    square_sum = lax.psum(local_sq, "tensor")
-    scale = lax.rsqrt(square_sum / D + 1e-05)
+    scale = lax.rsqrt(lax.psum(local_sq, "tensor") / D + 1e-05)
     normed = (whole.astype(jnp.float32) * scale * gain_full.astype(jnp.float32)[None, :]).astype(
         jnp.bfloat16
     )
@@ -88,7 +88,97 @@
     query = add_rows(lax.all_gather(w_query, "fsdp", axis=0, tiled=True))
     keyval = add_rows(lax.all_gather(kv_weight, "fsdp", axis=0, tiled=True))
     k_rot, v_val = rotated_keys(keyval, cosine, sine)
-    return attend_local(query, k_rot, v_val, seg, cosine, sine)
+    return attend(query, k_rot, v_val, seg, cosine, sine, 0)
+
+
+def partial_sums(hidden_states, norm_gain, w_query, w_keyval, segment_ids):
+    z = lax.axis_index("fsdp")
+    tokens = hidden_states.shape[0]
+    half = tokens // 2
+    size = half // PIECES
+    both = ("fsdp", "tensor")
+    q_cols = w_query.shape[1]
+
+    def at(row, col):
+        return row * 4 + col
+
+    def over_z(stage, flip):
+        return [(at(ORDER[j][stage], j ^ flip), at(j, j ^ flip)) for j in range(4)]
+
+    def over_x(flip):
+        return [(at(j, j ^ flip), at(j, j ^ flip ^ 2)) for j in range(4)]
+
+    over_core = [(at(j, j ^ flip), at(j, j ^ flip ^ 1)) for j in range(4) for flip in (0, 2)]
+
+    swap_x = [(t, t ^ 2) for t in range(4)]
+    crossed = [
+        lax.ppermute(hidden_states[half + n * size : half + (n + 1) * size], "tensor", swap_x)
+        for n in range(PIECES)
+    ]
+    direct = [hidden_states[n * size : (n + 1) * size] for n in range(PIECES)]
+    sources = [(piece, 0) for piece in direct] + [(piece, 2) for piece in crossed]
+
+    local_sq = jnp.sum(jnp.square(hidden_states.astype(jnp.float32)), axis=1)
+    squares = lax.all_gather(local_sq, both, axis=0, tiled=False).reshape(4, 4, tokens)
+    scales = lax.rsqrt(jnp.sum(squares, axis=1) / D + 1e-05)
+    gain = lax.ppermute(norm_gain, both, [(at(i, j), at(j, i)) for i in range(4) for j in range(4)])
+    gain = gain.astype(jnp.float32)[None, :]
+
+    weight = jnp.concatenate((w_query, w_keyval.reshape(w_keyval.shape[0], -1)), axis=1)
+    seg = segment_ids[0]
+    cosine, sine = rope_tables(positions(seg), HEAD_DIM)
+    order = jnp.array(ORDER, dtype=jnp.int32)[z]
+
+    def spread(piece, flip):
+        other = lax.ppermute(piece, both, over_x(flip))
+        mine = piece + other
+        return mine + lax.ppermute(mine, both, over_core)
+
+    def product(piece, stage, n):
+        scale = lax.dynamic_slice(scales, (order[stage], n * size), (1, size))[0]
+        normed = (piece.astype(jnp.float32) * scale[:, None] * gain).astype(jnp.bfloat16)
+        return jnp.dot(normed, weight, preferred_element_type=jnp.float32)
+
+    own_block = jnp.where(lax.axis_index("tensor") == z, hidden_states, jnp.zeros_like(hidden_states))
+    own_block = spread(own_block, 0)
+    outer_in = [(0, 1), (3, 2)]
+    sums = []
+    for n, (piece, flip) in enumerate(sources):
+        first, second, third = (
+            product(spread(lax.ppermute(piece, both, over_z(stage, flip)), flip), stage, n).astype(
+                jnp.bfloat16
+            )
+            for stage in range(3)
+        )
+        from_far = lax.ppermute(first, "fsdp", outer_in) + first
+        from_mid = lax.ppermute(second, "fsdp", outer_in) + second
+        near = lax.ppermute(third, "fsdp", [(0, 1), (1, 0), (2, 3), (3, 2)])
+        far = lax.ppermute(from_far, "fsdp", [(1, 3), (2, 0)])
+        mid = lax.ppermute(from_mid, "fsdp", [(1, 2), (2, 1)])
+        own = product(own_block[n * size : (n + 1) * size], 3, n)
+        sums.append(
+            own + near.astype(jnp.float32) + far.astype(jnp.float32) + mid.astype(jnp.float32)
+        )
+
+    outs = []
+    keys, values = [], []
+    for n, total in enumerate(sums):
+        rows = slice(n * size, (n + 1) * size)
+        k_rot, v_val = rotated_keys(total[:, q_cols:], cosine[rows], sine[rows])
+        keys.append(k_rot)
+        values.append(v_val)
+        outs.append(
+            attend(
+                total[:, :q_cols],
+                jnp.concatenate(keys),
+                jnp.concatenate(values),
+                seg,
+                cosine,
+                sine,
+                n * size,
+            )
+        )
+    return jnp.concatenate(outs)
 
 
 def solution(mesh):
@@ -100,4 +190,6 @@
         P(("groups", "fsdp"), None),
     )
     out_specs = P(("groups", "fsdp"), "tensor")
-    return jax.shard_map(shards, mesh=mesh, in_specs=in_specs, out_specs=out_specs, check_vma=False)
+    square = mesh.shape["fsdp"] == 4 and mesh.shape["tensor"] == 4
+    step = partial_sums if square else gathered
+    return jax.shard_map(step, mesh=mesh, in_specs=in_specs, out_specs=out_specs, check_vma=False)

time: 520 us -> 237 us (0.46)
  waiting for transfers between devices: 461 us -> 59.3 us
  starting transfers between devices: 0.08 us -> 81.3 us
  local copies, waits for them, and re-layouts: 6.29 us -> 23.4 us
  other arithmetic: 4.24 us -> 16.4 us
  blocking collectives: 14.2 us -> 20.1 us
    all_gather x3 -> x0, waiting for transfers between devices: 459 us -> none  [the longest x1 278 us: shards(): query = add_rows(lax.all_gather(w_query, 'fsdp', axis=0, tiled=True))]
    ppermute x0 -> x32, starting transfers between devices: none -> 81.3 us  [the longest x7 24.2 us: spread(): return mine + lax.ppermute(mine, both, over_core)]
    ppermute x0 -> x32, waiting for transfers between devices: none -> 59.3 us  [the longest x7 27.7 us: spread(): other = lax.ppermute(piece, both, over_x(flip))]
    all_gather x1, blocking collectives: 6.19 us -> 20.1 us  [partial_sums(): lax.all_gather(local_sq, both, axis=0, tiled=False).reshape(4, 4, tokens)]
    add x0 -> x12, other arithmetic: none -> 11.1 us  [the longest x7 5.83 us: spread(): mine = piece + other]
    psum x1 -> x0, blocking collectives: 7.99 us -> none  [shards(): square_sum = lax.psum(local_sq, 'tensor')]
    unnamed x8 -> x39, local copies, waits for them, and re-layouts: 3.82 us -> 10.1 us
    dot_general x4 -> x10, matrix products: 21.5 us -> 22.4 us  [the longest x8 17.4 us: product(): return jnp.dot(normed, weight, preferred_element_type=jnp.float32)]
  transfers between devices with their start and end apart: 3 -> 32, of which waited for: 3 -> 8; matrix products, arithmetic and copies ran while one was open for 3% -> 20% of each run, Pallas kernels for 0% -> 0%
where the time goes in v1:
time: 237 us; the launch traced here: 235 us
  starting transfers between devices  81.3 us (34%)
  waiting for transfers between devices  59.3 us (25%)
  matrix products  25.5 us (11%)
  local copies, waits for them, and re-layouts  23.4 us (10%)
  blocking collectives  20.1 us (8%)
  other arithmetic  16.4 us (7%)
  between operations  8.51 us (4%)
    ppermute x7, waiting for transfers between devices, spread(): other = lax.ppermute(piece, both, over_x(flip))  27.7 us
    ppermute x7, starting transfers between devices, spread(): return mine + lax.ppermute(mine, both, over_core)  24.2 us
    ppermute x2, waiting for transfers between devices, partial_sums(): far = lax.ppermute(from_far, 'fsdp', [(1, 3), (2, 0)])  22.5 us
    all_gather x1, blocking collectives, partial_sums(): lax.all_gather(local_sq, both, axis=0, tiled=False).reshape(4, 4, tokens)  20.1 us
    ppermute x7, starting transfers between devices, spread(): other = lax.ppermute(piece, both, over_x(flip))  19 us
    dot_general x8, matrix products, product(): return jnp.dot(normed, weight, preferred_element_type=jnp.float32)  17.4 us
    ppermute x2, starting transfers between devices, partial_sums(): from_mid = lax.ppermute(second, 'fsdp', outer_in) + second  10.8 us
    unnamed x39, local copies, waits for them, and re-layouts  10.1 us
  transfers between devices with their start and end apart: 32, of which 8 were waited for; matrix products, arithmetic and copies ran while one was open for 20% of the time, Pallas kernels for 0%

profile of v1, /device:TPU:0, one launch (start us, length us, event | category | flops | bytes accessed | tf_op | source)
XLA Modules:
  0.0 234.6 jit_solution(1204616692318412958)
XLA Ops:
  0.0 2.8 %fusion.83 = (bf16[192,2048]{1,0:T(8,128)(2,1)}, bf16[192,2048]{1,0:T(8,128)(2,1)}) fusion(bf16[384,2048]{1,0:T(8,128)(2,1)} %param.6), kind=kLoop, calls=%fused_computation.128 | loop fusion | bytes 3145728 | tf_op jit(solution)/shard_map/slice | solution.py:118
  2.8 1.4 collective-permute-start.12
  4.2 1.3 collective-permute-start.7
  5.5 1.3 collective-permute-start.3
  6.8 7.3 %collective-permute-start.17 = (bf16[192,2048]{1,0:T(8,128)(2,1)}, bf16[192,2048]{1,0:T(8,128)(2,1)}, u32[]{:S(2)}, u32[]{:S(2)}) collective-permute-start(bf16[192,2048]{1,0:T(8,128)(2,1)} %get-tuple-element.6), channel_id=1, source_target_pairs={{0,2},{1,3},{2,0},{3,1},{4,6},{5,7},{6,4},{7,5},{8,10},{9,11},{10,... | collective-permute-start | bytes 2359304 | tf_op jit(solution)/shard_map/ppermute | solution.py:115
  21.2 3.4 %copy.59 = bf16[256,8,2,256]{3,1,2,0:T(8,128)(2,1)} copy(bf16[256,8,2,256]{3,2,1,0:T(2,128)(2,1)} %bitcast.107) | data formatting | bytes 4194304
  24.6 20.1 %all-gather.1 = f32[16,1,384]{2,1,0:T(1,128)S(1)} all-gather(f32[1,1,384]{2,1,0:T(1,128)S(1)} %reshape.223), channel_id=2, replica_groups=mesh['groups'=2,'fsdp'=4,'tensor'=4] {'fsdp','tensor'}, dimensions={0}, use_global_device_ids=true | all-gather | bytes 26112 | tf_op jit(solution)/shard_map/all_gather | solution.py:122
  45.0 0.7 compare_and_fusion
  45.7 0.8 fusion.45
  46.6 10.2 %collective-permute-start.13 = (bf16[192,2048]{1,0:T(8,128)(2,1)}, bf16[192,2048]{1,0:T(8,128)(2,1)}, u32[]{:S(2)}, u32[]{:S(2)}) collective-permute-start(bf16[192,2048]{1,0:T(8,128)(2,1)} %collective-permute-done.12), channel_id=1, source_target_pairs={{0,2},{5,7},{10,8},{15,13},{16,18},{21,23},{26,24},{31,29}} | collective-permute-start | bytes 2359304 | tf_op jit(solution)/shard_map/ppermute | solution.py:133
  56.8 4.7 %constant_dynamic-update-slice_fusion.1 = bf16[2048,1536]{1,0:T(8,128)(2,1)} fusion(bf16[2048,1024]{1,0:T(8,128)(2,1)} %param.8), kind=kLoop, calls=%fused_computation.99 | loop fusion | bytes 8388608
  61.5 2.2 collective-permute-start.8
  66.7 3.1 %constant_dynamic-update-slice_fusion = bf16[2048,1536]{1,0:T(8,128)(2,1)} fusion(bf16[2048,1536]{1,0:T(8,128)(2,1)} %constant_dynamic-update-slice_fusion.1, bf16[2048,512]{1,0:T(8,128)(2,1)} %bitcast.104), kind=kLoop, calls=%fused_computation.98 | loop fusion | bytes 4194304 | tf_op jit(solution)/shard_map/concatenate | solution.py:127
  70.5 3.0 %collective-permute-start.22 = (bf16[192,2048]{1,0:T(8,128)(2,1)}, bf16[192,2048]{1,0:T(8,128)(2,1)S(1)}, u32[]{:S(2)}, u32[]{:S(2)}) collective-permute-start(bf16[192,2048]{1,0:T(8,128)(2,1)} %collective-permute-done.17), channel_id=1, source_target_pairs={{14,2},{15,7},{0,8},{1,13},{30,18},{31,23},{16,24},{17,29}} | collective-permute-start | bytes 2359304 | tf_op jit(solution)/shard_map/ppermute | solution.py:148
  73.6 1.3 collective-permute-start.4
  75.8 1.8 add.125
  77.7 15.0 %collective-permute-start.14 = (bf16[192,2048]{1,0:T(8,128)(2,1)S(1)}, bf16[192,2048]{1,0:T(8,128)(2,1)S(1)}, u32[]{:S(2)}, u32[]{:S(2)}) collective-permute-start(bf16[192,2048]{1,0:T(8,128)(2,1)S(1)} %add.125), channel_id=1, source_target_pairs={{0,1},{2,3},{5,4},{7,6},{10,11},{8,9},{15,14},{13,12},{16,17},{18,... | collective-permute-start | bytes 2359304 | tf_op jit(solution)/shard_map/ppermute | solution.py:135
  92.7 1.4 collective-permute-start
  94.1 0.8 multiply_cosine_fusion
  94.9 1.6 add.120
  97.3 1.3 collective-permute-start.9
  98.6 1.3 collective-permute-start.28
  99.9 0.8 fusion.84
  100.7 1.4 add.116
  102.1 1.3 collective-permute-start.23
  103.4 1.4 convolution_convert_fusion.3
  104.9 1.3 collective-permute-start.5
  106.2 18.4 %collective-permute-done.28 = bf16[192,2048]{1,0:T(8,128)(2,1)S(1)} collective-permute-done((bf16[192,2048]{1,0:T(8,128)(2,1)S(1)}, bf16[192,2048]{1,0:T(8,128)(2,1)S(1)}, u32[]{:S(2)}, u32[]{:S(2)}) %collective-permute-start.28) | collective-permute-done | bytes 786464 | tf_op jit(solution)/shard_map/ppermute | solution.py:133
  124.6 1.3 collective-permute-start.19
  126.2 1.3 collective-permute-start.29
  127.5 1.4 convolution_convert_fusion.4
  129.0 1.3 collective-permute-start.15
  130.3 2.7 %collective-permute-done.23 = bf16[192,2048]{1,0:T(8,128)(2,1)S(1)} collective-permute-done((bf16[192,2048]{1,0:T(8,128)(2,1)S(1)}, bf16[192,2048]{1,0:T(8,128)(2,1)S(1)}, u32[]{:S(2)}, u32[]{:S(2)}) %collective-permute-start.23) | collective-permute-done | bytes 786464 | tf_op jit(solution)/shard_map/ppermute | solution.py:133
  133.0 1.3 collective-permute-start.10
  134.8 6.6 %collective-permute-done.19 = bf16[192,2048]{1,0:T(8,128)(2,1)S(1)} collective-permute-done((bf16[192,2048]{1,0:T(8,128)(2,1)S(1)}, bf16[192,2048]{1,0:T(8,128)(2,1)S(1)}, u32[]{:S(2)}, u32[]{:S(2)}) %collective-permute-start.19) | collective-permute-done | bytes 786464 | tf_op jit(solution)/shard_map/ppermute | solution.py:133
  141.5 1.4 collective-permute-start.1
  142.9 1.3 collective-permute-start.24
  144.2 1.4 convolution_convert_fusion.5
  145.9 2.4 %collective-permute-start.20 = (bf16[192,2048]{1,0:T(8,128)(2,1)S(1)}, bf16[192,2048]{1,0:T(8,128)(2,1)S(1)}, u32[]{:S(2)}, u32[]{:S(2)}) collective-permute-start(bf16[192,2048]{1,0:T(8,128)(2,1)S(1)} %add.132), channel_id=1, source_target_pairs={{0,1},{2,3},{5,4},{7,6},{10,11},{8,9},{15,14},{13,12},{16,17},{18,... | collective-permute-start | bytes 2359304 | tf_op jit(solution)/shard_map/ppermute | solution.py:135
  148.5 5.9 %collective-permute-done.10 = bf16[192,1536]{1,0:T(8,128)(2,1)S(1)} collective-permute-done((bf16[192,1536]{1,0:T(8,128)(2,1)S(1)}, bf16[192,1536]{1,0:T(8,128)(2,1)S(1)}, u32[]{:S(2)}, u32[]{:S(2)}) %collective-permute-start.10) | collective-permute-done | bytes 589856 | tf_op jit(solution)/shard_map/ppermute | solution.py:153
  154.5 2.5 %collective-permute-start.6 = (bf16[192,1536]{1,0:T(8,128)(2,1)S(1)}, bf16[192,1536]{1,0:T(8,128)(2,1)S(1)}, u32[]{:S(2)}, u32[]{:S(2)}) collective-permute-start(bf16[192,1536]{1,0:T(8,128)(2,1)S(1)} %convolution_convert_fusion.5), channel_id=1, source_target_pairs={{0,4},{4,0},{8,12},{12,8},{1,5},{5,1},{9,13},{13,9},{2,6},{6,2},{1... | collective-permute-start | bytes 1769480 | tf_op jit(solution)/shard_map/ppermute | solution.py:155
  157.8 2.3 convolution_convert_fusion
  160.1 1.3 collective-permute-start.11
  161.4 2.3 convolution_convert_fusion.1
  163.6 9.4 %collective-permute-start.30 = (bf16[192,1536]{1,0:T(8,128)(2,1)}, bf16[192,1536]{1,0:T(8,128)(2,1)}, u32[]{:S(2)}, u32[]{:S(2)}) collective-permute-start(bf16[192,1536]{1,0:T(8,128)(2,1)} %convolution_convert_fusion), channel_id=1, source_target_pairs={{0,4},{12,8},{1,5},{13,9},{2,6},{14,10},{3,7},{15,11},{16,20},{28,... | collective-permute-start | bytes 1769480 | tf_op jit(solution)/shard_map/ppermute | solution.py:154
  173.7 2.1 collective-permute-start.25
  175.8 2.2 convolution_convert_fusion.2
  178.1 10.3 %collective-permute-done.11 = bf16[192,1536]{1,0:T(8,128)(2,1)S(1)} collective-permute-done((bf16[192,1536]{1,0:T(8,128)(2,1)S(1)}, bf16[192,1536]{1,0:T(8,128)(2,1)S(1)}, u32[]{:S(2)}, u32[]{:S(2)}) %collective-permute-start.11) | collective-permute-done | bytes 589856 | tf_op jit(solution)/shard_map/ppermute | solution.py:156
  188.4 1.6 fusion.3
  190.0 1.0 copy-done.2
  192.4 2.2 add.141
  194.6 1.5 collective-permute-start.31
  196.1 2.9 %collective-permute-done.25 = bf16[192,1536]{1,0:T(8,128)(2,1)} collective-permute-done((bf16[192,1536]{1,0:T(8,128)(2,1)}, bf16[192,1536]{1,0:T(8,128)(2,1)}, u32[]{:S(2)}, u32[]{:S(2)}) %collective-permute-start.25) | collective-permute-done | bytes 589856 | tf_op jit(solution)/shard_map/ppermute | solution.py:153
  199.0 2.2 add.137
  201.1 1.6 collective-permute-start.26
  202.9 1.0 slice.208
  204.1 1.9 fusion.93
  206.0 1.9 fusion.10
  208.7 12.2 %collective-permute-done.26 = bf16[192,1536]{1,0:T(8,128)(2,1)} collective-permute-done((bf16[192,1536]{1,0:T(8,128)(2,1)}, bf16[192,1536]{1,0:T(8,128)(2,1)}, u32[]{:S(2)}, u32[]{:S(2)}) %collective-permute-start.26) | collective-permute-done | bytes 589856 | tf_op jit(solution)/shard_map/ppermute | solution.py:156
  220.9 4.7 %fusion.5 = f32[192,1536]{1,0:T(8,128)S(1)} fusion(bf16[2048,1536]{1,0:T(8,128)(2,1)} %constant_dynamic-update-slice_fusion, bf16[192,1536]{1,0:T(8,128)(2,1)} %collective-permute-done.31, bf16[192,1536]{1,0:T(8,128)(2,1)} %collective-permute-done.26, bf16[192,1536]{1,0:T(8,128)(2,1)} %collective-permute-done.21, bf16[384,2048]{1,0:T(8,128)(2,1)S(1)} %add.111, ...), kind=kOutput, calls=%fused_computation.8 | convolution fusion | flops 1211301888 | bytes 10036224 | tf_op jit(solution)/shard_map/dot_general | solution.py:140
  225.7 1.4 copy_bitcast_fusion
  228.7 1.2 fusion.90
  230.0 3.1 %fusion.9 = bf16[192,2,4,128]{3,0,2,1:T(8,128)(2,1)S(1)} fusion(f32[2,4,192]{2,1,0:T(4,128)S(1)} %fusion.90, bf16[192,2,128]{2,0,1:T(8,128)(2,1)S(1)} %get-tuple-element.43, bf16[192,2,128]{2,0,1:T(8,128)(2,1)S(1)} %get-tuple-element.44, pred[192,384]{1,0:T(8,128)(4,1)S(1)} %copy-done.12, bf16[192,2,4,64]{3,0,2,1:T(8,128)(2,1)S(1)} %bitcast.109, ...), kind=kOutput, calls=%fused_computation.34 | convolution fusion | flops 307103616 | bytes 1259520 | tf_op jit(solution)/shard_map/kgqs,skd->qkgd/dot_general | solution.py:68
  233.6 0.9 pad_maximum_fusion
  (117 shorter events, 12.3 us)
Async XLA Ops:
  0.0 14.1 %copy-start = (bf16[384,2048]{1,0:T(8,128)(2,1)S(1)}, bf16[384,2048]{1,0:T(8,128)(2,1)}, u32[]{:S(2)}) copy-start(bf16[384,2048]{1,0:T(8,128)(2,1)} %param.6) | copy-start | bytes 4718596
  2.8 11.7 %copy-start.14 = (s32[1,384]{1,0:T(1,128)S(1)}, s32[1,384]{1,0:T(1,128)}, u32[]{:S(2)}) copy-start(s32[1,384]{1,0:T(1,128)} %param.10) | copy-start | bytes 4612
  2.8 43.8 %collective-permute-start.12 = (bf16[192,2048]{1,0:T(8,128)(2,1)}, bf16[192,2048]{1,0:T(8,128)(2,1)}, u32[]{:S(2)}, u32[]{:S(2)}) collective-permute-start(bf16[192,2048]{1,0:T(8,128)(2,1)} %get-tuple-element.5), channel_id=1, source_target_pairs={{8,0},{9,5},{6,10},{7,15},{24,16},{25,21},{22,26},{23,31}} | collective-permute-start | bytes 2359304 | tf_op jit(solution)/shard_map/ppermute | solution.py:148
  4.2 57.2 %collective-permute-start.7 = (bf16[192,2048]{1,0:T(8,128)(2,1)}, bf16[192,2048]{1,0:T(8,128)(2,1)}, u32[]{:S(2)}, u32[]{:S(2)}) collective-permute-start(bf16[192,2048]{1,0:T(8,128)(2,1)} %get-tuple-element.5), channel_id=1, source_target_pairs={{12,0},{13,5},{2,10},{3,15},{28,16},{29,21},{18,26},{19,31}} | collective-permute-start | bytes 2359304 | tf_op jit(solution)/shard_map/ppermute | solution.py:148
  5.5 68.1 %collective-permute-start.3 = (bf16[192,2048]{1,0:T(8,128)(2,1)}, bf16[192,2048]{1,0:T(8,128)(2,1)}, u32[]{:S(2)}, u32[]{:S(2)}) collective-permute-start(bf16[192,2048]{1,0:T(8,128)(2,1)} %get-tuple-element.5), channel_id=1, source_target_pairs={{4,0},{1,5},{14,10},{11,15},{20,16},{17,21},{30,26},{27,31}} | collective-permute-start | bytes 2359304 | tf_op jit(solution)/shard_map/ppermute | solution.py:148
  6.8 63.0 %collective-permute-start.17 = (bf16[192,2048]{1,0:T(8,128)(2,1)}, bf16[192,2048]{1,0:T(8,128)(2,1)}, u32[]{:S(2)}, u32[]{:S(2)}) collective-permute-start(bf16[192,2048]{1,0:T(8,128)(2,1)} %get-tuple-element.6), channel_id=1, source_target_pairs={{0,2},{1,3},{2,0},{3,1},{4,6},{5,7},{6,4},{7,5},{8,10},{9,11},{10,... | collective-permute-start | bytes 2359304 | tf_op jit(solution)/shard_map/ppermute | solution.py:115
  46.6 28.4 %collective-permute-start.13 = (bf16[192,2048]{1,0:T(8,128)(2,1)}, bf16[192,2048]{1,0:T(8,128)(2,1)}, u32[]{:S(2)}, u32[]{:S(2)}) collective-permute-start(bf16[192,2048]{1,0:T(8,128)(2,1)} %collective-permute-done.12), channel_id=1, source_target_pairs={{0,2},{5,7},{10,8},{15,13},{16,18},{21,23},{26,24},{31,29}} | collective-permute-start | bytes 2359304 | tf_op jit(solution)/shard_map/ppermute | solution.py:133
  61.5 31.2 %collective-permute-start.8 = (bf16[192,2048]{1,0:T(8,128)(2,1)}, bf16[192,2048]{1,0:T(8,128)(2,1)}, u32[]{:S(2)}, u32[]{:S(2)}) collective-permute-start(bf16[192,2048]{1,0:T(8,128)(2,1)} %collective-permute-done.7), channel_id=1, source_target_pairs={{0,2},{5,7},{10,8},{15,13},{16,18},{21,23},{26,24},{31,29}} | collective-permute-start | bytes 2359304 | tf_op jit(solution)/shard_map/ppermute | solution.py:133
  66.7 8.3 %copy-start.15 = (bf16[2048]{0:T(1024)(128)(2,1)S(1)}, bf16[2048]{0:T(1024)(128)(2,1)}, u32[]{:S(2)}) copy-start(bf16[2048]{0:T(1024)(128)(2,1)} %param.7) | copy-start | bytes 12292
  69.8 26.7 %collective-permute-start.27 = (bf16[192,2048]{1,0:T(8,128)(2,1)}, bf16[192,2048]{1,0:T(8,128)(2,1)S(1)}, u32[]{:S(2)}, u32[]{:S(2)}) collective-permute-start(bf16[192,2048]{1,0:T(8,128)(2,1)} %collective-permute-done.17), channel_id=1, source_target_pairs={{10,2},{11,7},{4,8},{5,13},{26,18},{27,23},{20,24},{21,29}} | collective-permute-start | bytes 2359304 | tf_op jit(solution)/shard_map/ppermute | solution.py:148
  70.5 26.7 %collective-permute-start.22 = (bf16[192,2048]{1,0:T(8,128)(2,1)}, bf16[192,2048]{1,0:T(8,128)(2,1)S(1)}, u32[]{:S(2)}, u32[]{:S(2)}) collective-permute-start(bf16[192,2048]{1,0:T(8,128)(2,1)} %collective-permute-done.17), channel_id=1, source_target_pairs={{14,2},{15,7},{0,8},{1,13},{30,18},{31,23},{16,24},{17,29}} | collective-permute-start | bytes 2359304 | tf_op jit(solution)/shard_map/ppermute | solution.py:148
  73.6 25.0 %collective-permute-start.4 = (bf16[192,2048]{1,0:T(8,128)(2,1)}, bf16[192,2048]{1,0:T(8,128)(2,1)S(1)}, u32[]{:S(2)}, u32[]{:S(2)}) collective-permute-start(bf16[192,2048]{1,0:T(8,128)(2,1)} %collective-permute-done.3), channel_id=1, source_target_pairs={{0,2},{5,7},{10,8},{15,13},{16,18},{21,23},{26,24},{31,29}} | collective-permute-start | bytes 2359304 | tf_op jit(solution)/shard_map/ppermute | solution.py:133
  75.1 2.6 %collective-permute-start.2 = (bf16[2048]{0:T(1024)(128)(2,1)S(1)}, bf16[2048]{0:T(1024)(128)(2,1)S(1)}, u32[]{:S(2)}, u32[]{:S(2)}) collective-permute-start(bf16[2048]{0:T(1024)(128)(2,1)S(1)} %copy-done.15), channel_id=1, source_target_pairs={{0,0},{1,4},{2,8},{3,12},{4,1},{5,5},{6,9},{7,13},{8,2},{9,6},{10,... | collective-permute-start | bytes 12296 | tf_op jit(solution)/shard_map/ppermute | solution.py:124
  75.8 27.6 %copy-start.1 = (bf16[2048,1536]{1,0:T(8,128)(2,1)S(1)}, bf16[2048,1536]{1,0:T(8,128)(2,1)}, u32[]{:S(2)}) copy-start(bf16[2048,1536]{1,0:T(8,128)(2,1)} %constant_dynamic-update-slice_fusion) | copy-start | bytes 18874372
  77.7 24.5 %collective-permute-start.14 = (bf16[192,2048]{1,0:T(8,128)(2,1)S(1)}, bf16[192,2048]{1,0:T(8,128)(2,1)S(1)}, u32[]{:S(2)}, u32[]{:S(2)}) collective-permute-start(bf16[192,2048]{1,0:T(8,128)(2,1)S(1)} %add.125), channel_id=1, source_target_pairs={{0,1},{2,3},{5,4},{7,6},{10,11},{8,9},{15,14},{13,12},{16,17},{18,... | collective-permute-start | bytes 2359304 | tf_op jit(solution)/shard_map/ppermute | solution.py:135
  92.7 36.3 %collective-permute-start = (bf16[384,2048]{1,0:T(8,128)(2,1)S(1)}, bf16[384,2048]{1,0:T(8,128)(2,1)S(1)}, u32[]{:S(2)}, u32[]{:S(2)}) collective-permute-start(bf16[384,2048]{1,0:T(8,128)(2,1)S(1)} %broadcast_select_fusion), channel_id=1, source_target_pairs={{0,2},{5,7},{10,8},{15,13},{16,18},{21,23},{26,24},{31,29}} | collective-permute-start | bytes 4718600 | tf_op jit(solution)/shard_map/ppermute | solution.py:133
  96.5 8.3 %collective-permute-start.18 = (bf16[192,2048]{1,0:T(8,128)(2,1)}, bf16[192,2048]{1,0:T(8,128)(2,1)S(1)}, u32[]{:S(2)}, u32[]{:S(2)}) collective-permute-start(bf16[192,2048]{1,0:T(8,128)(2,1)} %collective-permute-done.17), channel_id=1, source_target_pairs={{6,2},{3,7},{12,8},{9,13},{22,18},{19,23},{28,24},{25,29}} | collective-permute-start | bytes 2359304 | tf_op jit(solution)/shard_map/ppermute | solution.py:148
  97.3 28.9 %collective-permute-start.9 = (bf16[192,2048]{1,0:T(8,128)(2,1)S(1)}, bf16[192,2048]{1,0:T(8,128)(2,1)S(1)}, u32[]{:S(2)}, u32[]{:S(2)}) collective-permute-start(bf16[192,2048]{1,0:T(8,128)(2,1)S(1)} %add.120), channel_id=1, source_target_pairs={{0,1},{2,3},{5,4},{7,6},{10,11},{8,9},{15,14},{13,12},{16,17},{18,... | collective-permute-start | bytes 2359304 | tf_op jit(solution)/shard_map/ppermute | solution.py:135
  98.6 26.0 %collective-permute-start.28 = (bf16[192,2048]{1,0:T(8,128)(2,1)S(1)}, bf16[192,2048]{1,0:T(8,128)(2,1)S(1)}, u32[]{:S(2)}, u32[]{:S(2)}) collective-permute-start(bf16[192,2048]{1,0:T(8,128)(2,1)S(1)} %collective-permute-done.27), channel_id=1, source_target_pairs={{2,0},{7,5},{8,10},{13,15},{18,16},{23,21},{24,26},{29,31}} | collective-permute-start | bytes 2359304 | tf_op jit(solution)/shard_map/ppermute | solution.py:133
  102.1 30.9 %collective-permute-start.23 = (bf16[192,2048]{1,0:T(8,128)(2,1)S(1)}, bf16[192,2048]{1,0:T(8,128)(2,1)S(1)}, u32[]{:S(2)}, u32[]{:S(2)}) collective-permute-start(bf16[192,2048]{1,0:T(8,128)(2,1)S(1)} %collective-permute-done.22), channel_id=1, source_target_pairs={{2,0},{7,5},{8,10},{13,15},{18,16},{23,21},{24,26},{29,31}} | collective-permute-start | bytes 2359304 | tf_op jit(solution)/shard_map/ppermute | solution.py:133
  104.9 38.0 %collective-permute-start.5 = (bf16[192,2048]{1,0:T(8,128)(2,1)S(1)}, bf16[192,2048]{1,0:T(8,128)(2,1)S(1)}, u32[]{:S(2)}, u32[]{:S(2)}) collective-permute-start(bf16[192,2048]{1,0:T(8,128)(2,1)S(1)} %add.116), channel_id=1, source_target_pairs={{0,1},{2,3},{5,4},{7,6},{10,11},{8,9},{15,14},{13,12},{16,17},{18,... | collective-permute-start | bytes 2359304 | tf_op jit(solution)/shard_map/ppermute | solution.py:135
  124.6 16.9 %collective-permute-start.19 = (bf16[192,2048]{1,0:T(8,128)(2,1)S(1)}, bf16[192,2048]{1,0:T(8,128)(2,1)S(1)}, u32[]{:S(2)}, u32[]{:S(2)}) collective-permute-start(bf16[192,2048]{1,0:T(8,128)(2,1)S(1)} %collective-permute-done.18), channel_id=1, source_target_pairs={{2,0},{7,5},{8,10},{13,15},{18,16},{23,21},{24,26},{29,31}} | collective-permute-start | bytes 2359304 | tf_op jit(solution)/shard_map/ppermute | solution.py:133
  126.2 30.9 %collective-permute-start.29 = (bf16[192,2048]{1,0:T(8,128)(2,1)S(1)}, bf16[192,2048]{1,0:T(8,128)(2,1)S(1)}, u32[]{:S(2)}, u32[]{:S(2)}) collective-permute-start(bf16[192,2048]{1,0:T(8,128)(2,1)S(1)} %add.139), channel_id=1, source_target_pairs={{0,1},{2,3},{5,4},{7,6},{10,11},{8,9},{15,14},{13,12},{16,17},{18,... | collective-permute-start | bytes 2359304 | tf_op jit(solution)/shard_map/ppermute | solution.py:135
  129.0 16.9 %collective-permute-start.15 = (bf16[192,1536]{1,0:T(8,128)(2,1)S(1)}, bf16[192,1536]{1,0:T(8,128)(2,1)S(1)}, u32[]{:S(2)}, u32[]{:S(2)}) collective-permute-start(bf16[192,1536]{1,0:T(8,128)(2,1)S(1)} %convolution_convert_fusion.3), channel_id=1, source_target_pairs={{0,4},{12,8},{1,5},{13,9},{2,6},{14,10},{3,7},{15,11},{16,20},{28,... | collective-permute-start | bytes 1769480 | tf_op jit(solution)/shard_map/ppermute | solution.py:154
  133.0 21.4 %collective-permute-start.10 = (bf16[192,1536]{1,0:T(8,128)(2,1)S(1)}, bf16[192,1536]{1,0:T(8,128)(2,1)S(1)}, u32[]{:S(2)}, u32[]{:S(2)}) collective-permute-start(bf16[192,1536]{1,0:T(8,128)(2,1)S(1)} %convolution_convert_fusion.4), channel_id=1, source_target_pairs={{0,4},{12,8},{1,5},{13,9},{2,6},{14,10},{3,7},{15,11},{16,20},{28,... | collective-permute-start | bytes 1769480 | tf_op jit(solution)/shard_map/ppermute | solution.py:153
  141.5 22.2 %collective-permute-start.1 = (bf16[384,2048]{1,0:T(8,128)(2,1)S(1)}, bf16[384,2048]{1,0:T(8,128)(2,1)S(1)}, u32[]{:S(2)}, u32[]{:S(2)}) collective-permute-start(bf16[384,2048]{1,0:T(8,128)(2,1)S(1)} %fusion.104), channel_id=1, source_target_pairs={{0,1},{2,3},{5,4},{7,6},{10,11},{8,9},{15,14},{13,12},{16,17},{18,... | collective-permute-start | bytes 4718600 | tf_op jit(solution)/shard_map/ppermute | solution.py:135
  142.9 17.2 %collective-permute-start.24 = (bf16[192,2048]{1,0:T(8,128)(2,1)S(1)}, bf16[192,2048]{1,0:T(8,128)(2,1)S(1)}, u32[]{:S(2)}, u32[]{:S(2)}) collective-permute-start(bf16[192,2048]{1,0:T(8,128)(2,1)S(1)} %add.135), channel_id=1, source_target_pairs={{0,1},{2,3},{5,4},{7,6},{10,11},{8,9},{15,14},{13,12},{16,17},{18,... | collective-permute-start | bytes 2359304 | tf_op jit(solution)/shard_map/ppermute | solution.py:135
  145.9 27.7 %collective-permute-start.20 = (bf16[192,2048]{1,0:T(8,128)(2,1)S(1)}, bf16[192,2048]{1,0:T(8,128)(2,1)S(1)}, u32[]{:S(2)}, u32[]{:S(2)}) collective-permute-start(bf16[192,2048]{1,0:T(8,128)(2,1)S(1)} %add.132), channel_id=1, source_target_pairs={{0,1},{2,3},{5,4},{7,6},{10,11},{8,9},{15,14},{13,12},{16,17},{18,... | collective-permute-start | bytes 2359304 | tf_op jit(solution)/shard_map/ppermute | solution.py:135
  154.5 23.6 %collective-permute-start.6 = (bf16[192,1536]{1,0:T(8,128)(2,1)S(1)}, bf16[192,1536]{1,0:T(8,128)(2,1)S(1)}, u32[]{:S(2)}, u32[]{:S(2)}) collective-permute-start(bf16[192,1536]{1,0:T(8,128)(2,1)S(1)} %convolution_convert_fusion.5), channel_id=1, source_target_pairs={{0,4},{4,0},{8,12},{12,8},{1,5},{5,1},{9,13},{13,9},{2,6},{6,2},{1... | collective-permute-start | bytes 1769480 | tf_op jit(solution)/shard_map/ppermute | solution.py:155
  157.1 21.0 %collective-permute-start.16 = (bf16[192,1536]{1,0:T(8,128)(2,1)S(1)}, bf16[192,1536]{1,0:T(8,128)(2,1)S(1)}, u32[]{:S(2)}, u32[]{:S(2)}) collective-permute-start(bf16[192,1536]{1,0:T(8,128)(2,1)S(1)} %add.128), channel_id=1, source_target_pairs={{4,8},{8,4},{5,9},{9,5},{6,10},{10,6},{7,11},{11,7},{20,24},{24,20... | collective-permute-start | bytes 1769480 | tf_op jit(solution)/shard_map/ppermute | solution.py:157
  160.1 28.3 %collective-permute-start.11 = (bf16[192,1536]{1,0:T(8,128)(2,1)S(1)}, bf16[192,1536]{1,0:T(8,128)(2,1)S(1)}, u32[]{:S(2)}, u32[]{:S(2)}) collective-permute-start(bf16[192,1536]{1,0:T(8,128)(2,1)S(1)} %add.123), channel_id=1, source_target_pairs={{4,12},{8,0},{5,13},{9,1},{6,14},{10,2},{7,15},{11,3},{20,28},{24,... | collective-permute-start | bytes 1769480 | tf_op jit(solution)/shard_map/ppermute | solution.py:156
  163.6 28.8 %collective-permute-start.30 = (bf16[192,1536]{1,0:T(8,128)(2,1)}, bf16[192,1536]{1,0:T(8,128)(2,1)}, u32[]{:S(2)}, u32[]{:S(2)}) collective-permute-start(bf16[192,1536]{1,0:T(8,128)(2,1)} %convolution_convert_fusion), channel_id=1, source_target_pairs={{0,4},{12,8},{1,5},{13,9},{2,6},{14,10},{3,7},{15,11},{16,20},{28,... | collective-permute-start | bytes 1769480 | tf_op jit(solution)/shard_map/ppermute | solution.py:154
  173.7 25.3 %collective-permute-start.25 = (bf16[192,1536]{1,0:T(8,128)(2,1)}, bf16[192,1536]{1,0:T(8,128)(2,1)}, u32[]{:S(2)}, u32[]{:S(2)}) collective-permute-start(bf16[192,1536]{1,0:T(8,128)(2,1)} %convolution_convert_fusion.1), channel_id=1, source_target_pairs={{0,4},{12,8},{1,5},{13,9},{2,6},{14,10},{3,7},{15,11},{16,20},{28,... | collective-permute-start | bytes 1769480 | tf_op jit(solution)/shard_map/ppermute | solution.py:153
  178.0 30.6 %collective-permute-start.21 = (bf16[192,1536]{1,0:T(8,128)(2,1)}, bf16[192,1536]{1,0:T(8,128)(2,1)}, u32[]{:S(2)}, u32[]{:S(2)}) collective-permute-start(bf16[192,1536]{1,0:T(8,128)(2,1)} %convolution_convert_fusion.2), channel_id=1, source_target_pairs={{0,4},{4,0},{8,12},{12,8},{1,5},{5,1},{9,13},{13,9},{2,6},{6,2},{1... | collective-permute-start | bytes 1769480 | tf_op jit(solution)/shard_map/ppermute | solution.py:155
  190.0 1.1 copy-start.2
  191.1 0.9 copy-start.6
  191.1 0.9 copy-start.7
  194.6 14.1 %collective-permute-start.31 = (bf16[192,1536]{1,0:T(8,128)(2,1)}, bf16[192,1536]{1,0:T(8,128)(2,1)}, u32[]{:S(2)}, u32[]{:S(2)}) collective-permute-start(bf16[192,1536]{1,0:T(8,128)(2,1)} %add.141), channel_id=1, source_target_pairs={{4,8},{8,4},{5,9},{9,5},{6,10},{10,6},{7,11},{11,7},{20,24},{24,20... | collective-permute-start | bytes 1769480 | tf_op jit(solution)/shard_map/ppermute | solution.py:157
  201.1 2.9 %copy-start.13 = (pred[192,192]{0,1:T(8,128)(4,1)S(1)}, pred[192,192]{0,1:T(8,128)(4,1)}, u32[]{:S(2)}) copy-start(pred[192,192]{0,1:T(8,128)(4,1)} %compare_and_fusion) | copy-start | bytes 110596
  201.1 19.7 %collective-permute-start.26 = (bf16[192,1536]{1,0:T(8,128)(2,1)}, bf16[192,1536]{1,0:T(8,128)(2,1)}, u32[]{:S(2)}, u32[]{:S(2)}) collective-permute-start(bf16[192,1536]{1,0:T(8,128)(2,1)} %add.137), channel_id=1, source_target_pairs={{4,12},{8,0},{5,13},{9,1},{6,14},{10,2},{7,15},{11,3},{20,28},{24,... | collective-permute-start | bytes 1769480 | tf_op jit(solution)/shard_map/ppermute | solution.py:156
  202.9 3.1 %copy-start.8 = (bf16[192,2,64]{2,0,1:T(8,128)(2,1)}, bf16[192,2,64]{2,0,1:T(8,128)(2,1)S(1)}, u32[]{:S(2)}) copy-start(bf16[192,2,64]{2,0,1:T(8,128)(2,1)S(1)} %get-tuple-element.11) | copy-start | bytes 147460
  202.9 3.1 %copy-start.10 = (bf16[192,2,64]{2,0,1:T(8,128)(2,1)}, bf16[192,2,64]{2,0,1:T(8,128)(2,1)S(1)}, u32[]{:S(2)}) copy-start(bf16[192,2,64]{2,0,1:T(8,128)(2,1)S(1)} %get-tuple-element.12) | copy-start | bytes 147460
  225.6 1.6 copy-start.3
  225.7 1.6 copy-start.4
  225.7 1.6 copy-start.5
  227.3 0.9 slice-start
  227.7 0.9 copy-start.9
  227.8 1.0 copy-start.11
  227.8 1.0 copy-start.12

commit v2 on v0

--- a/solution.py
+++ b/solution.py
@@ -7,6 +7,9 @@
 
 D = 8192
 HEAD_DIM = 128
+ORDER = ((3, 2, 1, 0), (3, 2, 0, 1), (0, 1, 3, 2), (0, 1, 2, 3))
+SIZES = (48, 48, 48, 48)
+TURNS = "s0 w s1 x0 s2 c0 x1 s3 m0 c1 x2 m1 c2 x3 m2 c3 f0 m3 f1 f2 f3"
 
 
 def positions(seg):
@@ -46,18 +49,19 @@
     return (k_rot, v_val)
 
 
-def attend_local(query, k_rot, v_val, seg, cosine, sine):
+def attend(query, k_rot, v_val, seg, cosine, sine, start):
     tlen = query.shape[0]
-    kv_heads = k_rot.shape[1]
+    klen, kv_heads = k_rot.shape[:2]
     heads = query.shape[1] // HEAD_DIM
     group = heads // kv_heads
-    q_rot = rotate(query.reshape(tlen, heads, HEAD_DIM), cosine, sine).astype(jnp.bfloat16)
+    rows = slice(start, start + tlen)
+    q_rot = rotate(query.reshape(tlen, heads, HEAD_DIM), cosine[rows], sine[rows]).astype(jnp.bfloat16)
     grouped = q_rot.reshape(tlen, kv_heads, group, HEAD_DIM)
     scores = jnp.einsum("qkgd,skd->kgqs", grouped, k_rot, preferred_element_type=jnp.float32) * (
         1.0 / math.sqrt(HEAD_DIM)
     )
-    index = jnp.arange(tlen, dtype=jnp.int32)
-    allowed = (seg[:, None] == seg[None, :]) & (index[None, :] <= index[:, None])
+    index = jnp.arange(seg.shape[0], dtype=jnp.int32)
+    allowed = (seg[rows, None] == seg[None, :klen]) & (index[None, :klen] <= index[rows, None])
     scores = jnp.where(allowed[None, None], scores, -jnp.inf)
     top = jnp.max(scores, axis=-1, keepdims=True)
     expo = jnp.exp(scores - top)
@@ -66,14 +70,11 @@
     return mixed.astype(jnp.bfloat16).reshape(tlen, heads * HEAD_DIM)
 
 
-def shards(hidden_states, norm_gain, w_query, w_keyval, segment_ids):
-    whole, gain_full = (
-        lax.all_gather(hidden_states, "tensor", axis=1, tiled=True),
-        lax.all_gather(norm_gain, "tensor", axis=0, tiled=True),
-    )
+def gathered(hidden_states, norm_gain, w_query, w_keyval, segment_ids):
+    whole = lax.all_gather(hidden_states, "tensor", axis=1, tiled=True)
+    gain_full = lax.all_gather(norm_gain, "tensor", axis=0, tiled=True)
     local_sq = jnp.sum(jnp.square(hidden_states.astype(jnp.float32)), axis=1, keepdims=True)
-    square_sum = lax.psum(local_sq, "tensor")
-    scale = lax.rsqrt(square_sum / D + 1e-05)
+    scale = lax.rsqrt(lax.psum(local_sq, "tensor") / D + 1e-05)
     normed = (whole.astype(jnp.float32) * scale * gain_full.astype(jnp.float32)[None, :]).astype(
         jnp.bfloat16
     )
@@ -88,7 +89,123 @@
     query = add_rows(lax.all_gather(w_query, "fsdp", axis=0, tiled=True))
     keyval = add_rows(lax.all_gather(kv_weight, "fsdp", axis=0, tiled=True))
     k_rot, v_val = rotated_keys(keyval, cosine, sine)
-    return attend_local(query, k_rot, v_val, seg, cosine, sine)
+    return attend(query, k_rot, v_val, seg, cosine, sine, 0)
+
+
+def partial_sums(hidden_states, norm_gain, w_query, w_keyval, segment_ids):
+    z = lax.axis_index("fsdp")
+    t = lax.axis_index("tensor")
+    tokens = hidden_states.shape[0]
+    both = ("fsdp", "tensor")
+    q_cols = w_query.shape[1]
+
+    def toward(far):
+        pairs = []
+        for i in range(4):
+            for col in range(4):
+                j = col if (col // 2 != i // 2) == far else col ^ 2
+                pairs.append((i * 4 + col, j * 4 + col // 2 * 2 + ORDER[j].index(i) % 2))
+        return pairs
+
+    swap_x = [(n, n ^ 2) for n in range(4)]
+    swap_core = [(n, n ^ 1) for n in range(4)]
+    outer_in = [(0, 1), (3, 2)]
+    count = len(SIZES)
+
+    starts = [sum(SIZES[:n]) * 2 for n in range(count)]
+    crossed = [
+        lax.ppermute(hidden_states[start + size : start + 2 * size], "tensor", swap_x)
+        for start, size in zip(starts, SIZES)
+    ]
+    local_sq = jnp.sum(jnp.square(hidden_states.astype(jnp.float32)), axis=1)
+    square_sum = local_sq
+    for flip in (1, 2, 3):
+        square_sum += lax.ppermute(local_sq, "tensor", [(n, n ^ flip) for n in range(4)])
+    scale = lax.rsqrt(square_sum / D + 1e-05)[:, None]
+    gain = norm_gain.astype(jnp.float32)[None, :]
+    crossed_gain = lax.ppermute(norm_gain, "tensor", swap_x).astype(jnp.float32)[None, :]
+
+    here_far = t // 2 != z // 2
+    even_core = t % 2 == 0
+    done = [scale]
+
+    def in_turn(*arrays):
+        arrays, _ = lax.optimization_barrier((arrays, done[0]))
+        return arrays
+
+    state = [{} for _ in SIZES]
+
+    def send(n):
+        start, size = starts[n], SIZES[n]
+        mid = start + size
+        stay, other = in_turn(hidden_states[start:mid], crossed[n])
+        stay = (stay.astype(jnp.float32) * scale[start:mid] * gain).astype(jnp.bfloat16)
+        other = other.astype(jnp.float32) * scale[mid : mid + size] * crossed_gain
+        other = other.astype(jnp.bfloat16)
+        far = jnp.where(here_far, stay, other)
+        near = jnp.where(here_far, other, stay)
+        done[0] = (far, near)
+        state[n]["z"] = lax.ppermute(far, both, toward(True)), lax.ppermute(near, both, toward(False))
+
+    def cross(n):
+        mine = jnp.stack(in_turn(*state[n]["z"]))
+        done[0] = mine
+        state[n]["x"] = mine, lax.ppermute(mine, "tensor", swap_x)
+
+    def share(n):
+        mine, theirs = in_turn(*state[n]["x"])
+        mine = jnp.where(
+            here_far, jnp.concatenate((theirs, mine), 1), jnp.concatenate((mine, theirs), 1)
+        )
+        done[0] = mine
+        state[n]["c"] = mine, lax.ppermute(mine, "tensor", swap_core)
+
+    def multiply(n):
+        mine, theirs = in_turn(*state[n]["c"])
+        rows = jnp.where(
+            even_core, jnp.stack((mine, theirs), 1), jnp.stack((theirs, mine), 1)
+        ).reshape(8 * SIZES[n], -1)
+        part = jnp.dot(rows, weight, preferred_element_type=jnp.float32)
+        part = part.reshape(4, 2 * SIZES[n], -1)
+        outer = part[:2].astype(jnp.bfloat16)
+        inner = part[2].astype(jnp.bfloat16)
+        done[0] = (outer, inner)
+        passed = lax.ppermute(outer, "fsdp", outer_in)
+        near_sum = lax.ppermute(inner, "fsdp", [(0, 1), (1, 0), (2, 3), (3, 2)])
+        state[n]["p"] = part[3], outer, passed, near_sum
+
+    def forward(n):
+        own, outer, passed, near_sum = state[n]["p"]
+        passed, outer = in_turn(passed, outer)
+        passed = passed + outer
+        done[0] = passed
+        far_sum = lax.ppermute(passed[0], "fsdp", [(1, 3), (2, 0)])
+        mid_sum = lax.ppermute(passed[1], "fsdp", [(1, 2), (2, 1)])
+        state[n]["f"] = own, near_sum, far_sum, mid_sum
+
+    def finish(n):
+        own, near_sum, far_sum, mid_sum = state[n]["f"]
+        return (
+            own
+            + near_sum.astype(jnp.float32)
+            + far_sum.astype(jnp.float32)
+            + mid_sum.astype(jnp.float32)
+        )
+
+    steps = {"s": send, "x": cross, "c": share, "m": multiply, "f": forward}
+    for turn in TURNS.split():
+        if turn == "w":
+            w_query, w_keyval = in_turn(w_query, w_keyval)
+            weight = jnp.concatenate((w_query, w_keyval.reshape(w_keyval.shape[0], -1)), axis=1)
+            done[0] = weight
+        else:
+            steps[turn[0]](int(turn[1]))
+
+    seg = segment_ids[0]
+    cosine, sine = rope_tables(positions(seg), HEAD_DIM)
+    total = jnp.concatenate([finish(n) for n in range(count)])
+    k_rot, v_val = rotated_keys(total[:, q_cols:], cosine, sine)
+    return attend(total[:, :q_cols], k_rot, v_val, seg, cosine, sine, 0)
 
 
 def solution(mesh):
@@ -100,4 +217,6 @@
         P(("groups", "fsdp"), None),
     )
     out_specs = P(("groups", "fsdp"), "tensor")
-    return jax.shard_map(shards, mesh=mesh, in_specs=in_specs, out_specs=out_specs, check_vma=False)
+    square = mesh.shape["fsdp"] == 4 and mesh.shape["tensor"] == 4
+    step = partial_sums if square else gathered
+    return jax.shard_map(step, mesh=mesh, in_specs=in_specs, out_specs=out_specs, check_vma=False)

time: 520 us -> 185 us (0.36)
  waiting for transfers between devices: 461 us -> 82.1 us
  starting transfers between devices: 0.08 us -> 61.5 us
  blocking collectives: 14.2 us -> 0 us
  between operations: 13.3 us -> 0.79 us
  other arithmetic: 4.24 us -> 12.2 us
    all_gather x3 -> x0, waiting for transfers between devices: 459 us -> none  [the longest x1 278 us: shards(): query = add_rows(lax.all_gather(w_query, 'fsdp', axis=0, tiled=True))]
    ppermute x0 -> x40, waiting for transfers between devices: none -> 82.1 us  [the longest x4 27.5 us: multiply(): passed = lax.ppermute(outer, 'fsdp', outer_in)]
    ppermute x0 -> x40, starting transfers between devices: none -> 61.5 us  [the longest x4 13.4 us: multiply(): passed = lax.ppermute(outer, 'fsdp', outer_in)]
    psum x1 -> x0, blocking collectives: 7.99 us -> none  [shards(): square_sum = lax.psum(local_sq, 'tensor')]
    all_gather x1 -> x0, blocking collectives: 6.19 us -> none  [shards(): lax.all_gather(norm_gain, 'tensor', axis=0, tiled=True)]
    dot_general x4 -> x6, matrix products: 21.5 us -> 18.4 us  [the longest x4 16.9 us: multiply(): part = jnp.dot(rows, weight, preferred_element_type=jnp.float32)]
  transfers between devices with their start and end apart: 3 -> 40, of which waited for: 3 -> 16; matrix products, arithmetic and copies ran while one was open for 3% -> 16% of each run, Pallas kernels for 0% -> 0%
where the time goes in v2:
time: 185 us; the launch traced here: 182 us
  waiting for transfers between devices  82.1 us (44%)
  starting transfers between devices  61.5 us (33%)
  matrix products  18.4 us (10%)
  other arithmetic  12.2 us (7%)
  local copies, waits for them, and re-layouts  7.21 us (4%)
    ppermute x4, waiting for transfers between devices, multiply(): passed = lax.ppermute(outer, 'fsdp', outer_in)  27.5 us
    ppermute x4, waiting for transfers between devices, cross(): state[n]['x'] = (mine, lax.ppermute(mine, 'tensor', swap_x))  17.1 us
    dot_general x4, matrix products, multiply(): part = jnp.dot(rows, weight, preferred_element_type=jnp.float32)  16.9 us
    ppermute x4, starting transfers between devices, multiply(): passed = lax.ppermute(outer, 'fsdp', outer_in)  13.4 us
    ppermute x4, starting transfers between devices, send(): lax.ppermute(near, both, toward(False))  10.8 us
    ppermute x4, waiting for transfers between devices, send(): lax.ppermute(near, both, toward(False))  10.8 us
    ppermute x4, waiting for transfers between devices, forward(): far_sum = lax.ppermute(passed[0], 'fsdp', [(1, 3), (2, 0)])  9.94 us
    ppermute x4, starting transfers between devices, multiply(): near_sum = lax.ppermute(inner, 'fsdp', [(0, 1), (1, 0), (2, 3), (3, 2)])  9.39 us
  transfers between devices with their start and end apart: 40, of which 16 were waited for; matrix products, arithmetic and copies ran while one was open for 16% of the time, Pallas kernels for 0%

profile of v2, /device:TPU:0, one launch (start us, length us, event | category | flops | bytes accessed | tf_op | source)
XLA Modules:
  0.0 182.3 jit_solution(13362041478359075038)
XLA Ops:
  0.0 1.9 %multiply_reduce_fusion = f32[384]{0:T(512)S(1)} fusion(bf16[384,2048]{1,0:T(8,128)(2,1)} %param.5), kind=kLoop, calls=%fused_computation.5 | loop fusion | flops 2358912 | bytes 1574400 | tf_op jit(solution)/shard_map/reduce_sum | solution.py:120
  1.9 0.5 collective-permute-start.1
  2.4 2.6 %collective-permute-start.2 = (f32[384]{0:T(512)S(1)}, f32[384]{0:T(512)S(1)}, u32[]{:S(2)}, u32[]{:S(2)}) collective-permute-start(f32[384]{0:T(512)S(1)} %multiply_reduce_fusion), channel_id=1, source_target_pairs={{0,2},{1,3},{2,0},{3,1},{4,6},{5,7},{6,4},{7,5},{8,10},{9,11},{10,... | collective-permute-start | bytes 4616 | tf_op jit(solution)/shard_map/ppermute | solution.py:123
  5.2 1.8 collective-permute-start
  7.3 1.7 collective-permute-start.7
  9.4 3.7 %collective-permute-done.4 = bf16[2048]{0:T(1024)(128)(2,1)S(1)} collective-permute-done((bf16[2048]{0:T(1024)(128)(2,1)S(1)}, bf16[2048]{0:T(1024)(128)(2,1)S(1)}, u32[]{:S(2)}, u32[]{:S(2)}) %collective-permute-start.4) | collective-permute-done | bytes 4128 | tf_op jit(solution)/shard_map/ppermute | solution.py:126
  13.3 2.9 %collective-permute-start.5 = (bf16[48,2048]{1,0:T(8,128)(2,1)S(1)}, bf16[48,2048]{1,0:T(8,128)(2,1)S(1)}, u32[]{:S(2)}, u32[]{:S(2)}) collective-permute-start(bf16[48,2048]{1,0:T(8,128)(2,1)S(1)} %get-tuple-element.116), channel_id=1, source_target_pairs={{0,8},{1,12},{2,10},{3,14},{4,9},{5,13},{6,11},{7,15},{8,1},{9,5},... | collective-permute-start | bytes 589832 | tf_op jit(solution)/shard_map/ppermute | solution.py:148
  16.1 3.2 %collective-permute-start.6 = (bf16[48,2048]{1,0:T(8,128)(2,1)S(1)}, bf16[48,2048]{1,0:T(8,128)(2,1)S(1)}, u32[]{:S(2)}, u32[]{:S(2)}) collective-permute-start(bf16[48,2048]{1,0:T(8,128)(2,1)S(1)} %get-tuple-element.115), channel_id=1, source_target_pairs={{0,1},{1,4},{2,3},{3,6},{4,0},{5,5},{6,2},{7,7},{8,9},{9,12},{10,1... | collective-permute-start | bytes 589832 | tf_op jit(solution)/shard_map/ppermute | solution.py:148
  19.3 2.6 %constant_dynamic-update-slice_fusion.1 = bf16[2048,1536]{1,0:T(8,128)(2,1)S(1)} fusion(bf16[2048,1024]{1,0:T(8,128)(2,1)} %param.7), kind=kLoop, calls=%fused_computation.79 | loop fusion | bytes 8388608
  21.9 0.5 copy.30
  22.9 2.4 %collective-permute-start.13 = (bf16[48,2048]{1,0:T(8,128)(2,1)S(1)}, bf16[48,2048]{1,0:T(8,128)(2,1)S(1)}, u32[]{:S(2)}, u32[]{:S(2)}) collective-permute-start(bf16[48,2048]{1,0:T(8,128)(2,1)S(1)} %get-tuple-element.113), channel_id=1, source_target_pairs={{0,1},{1,4},{2,3},{3,6},{4,0},{5,5},{6,2},{7,7},{8,9},{9,12},{10,1... | collective-permute-start | bytes 589832 | tf_op jit(solution)/shard_map/ppermute | solution.py:148
  25.3 0.9 collective-permute-done.6
  26.2 1.6 collective-permute-start.8
  28.0 8.9 %collective-permute-done.8 = bf16[2,48,2048]{2,1,0:T(8,128)(2,1)S(1)} collective-permute-done((bf16[2,48,2048]{2,1,0:T(8,128)(2,1)S(1)}, bf16[2,48,2048]{2,1,0:T(8,128)(2,1)S(1)}, u32[]{:S(2)}, u32[]{:S(2)}) %collective-permute-start.8) | collective-permute-done | bytes 393248 | tf_op jit(solution)/shard_map/ppermute | solution.py:153
  37.2 1.6 collective-permute-start.11
  38.9 0.6 collective-permute-start.20
  39.4 5.6 %collective-permute-done.11 = bf16[48,2048]{1,0:T(8,128)(2,1)S(1)} collective-permute-done((bf16[48,2048]{1,0:T(8,128)(2,1)S(1)}, bf16[48,2048]{1,0:T(8,128)(2,1)S(1)}, u32[]{:S(2)}, u32[]{:S(2)}) %collective-permute-start.11) | collective-permute-done | bytes 196640 | tf_op jit(solution)/shard_map/ppermute | solution.py:117
  45.5 6.9 %fusion.29 = (bf16[384,1536]{1,0:T(8,128)(2,1)S(1)}, f32[384,1536]{1,0:T(8,128)}) fusion(bf16[384,2048]{1,0:T(8,128)(2,1)S(1)} %bitcast.110, bf16[2048,1536]{1,0:T(8,128)(2,1)} %copy-done.1), kind=kOutput, calls=%fused_computation.94 | convolution fusion | flops 2416508928 | bytes 11403264 | tf_op jit(solution)/shard_map/dot_general | solution.py:168
  52.4 0.6 collective-permute-done.20
  53.2 2.1 %collective-permute-start.18 = (bf16[48,2048]{1,0:T(8,128)(2,1)S(1)}, bf16[48,2048]{1,0:T(8,128)(2,1)S(1)}, u32[]{:S(2)}, u32[]{:S(2)}) collective-permute-start(bf16[48,2048]{1,0:T(8,128)(2,1)S(1)} %get-tuple-element.112), channel_id=1, source_target_pairs={{0,8},{1,12},{2,10},{3,14},{4,9},{5,13},{6,11},{7,15},{8,1},{9,5},... | collective-permute-start | bytes 589832 | tf_op jit(solution)/shard_map/ppermute | solution.py:148
  55.4 1.9 %collective-permute-start.19 = (bf16[48,2048]{1,0:T(8,128)(2,1)S(1)}, bf16[48,2048]{1,0:T(8,128)(2,1)}, u32[]{:S(2)}, u32[]{:S(2)}) collective-permute-start(bf16[48,2048]{1,0:T(8,128)(2,1)S(1)} %get-tuple-element.111), channel_id=1, source_target_pairs={{0,1},{1,4},{2,3},{3,6},{4,0},{5,5},{6,2},{7,7},{8,9},{9,12},{10,1... | collective-permute-start | bytes 589832 | tf_op jit(solution)/shard_map/ppermute | solution.py:148
  57.9 2.9 %collective-permute-done.18 = bf16[48,2048]{1,0:T(8,128)(2,1)S(1)} collective-permute-done((bf16[48,2048]{1,0:T(8,128)(2,1)S(1)}, bf16[48,2048]{1,0:T(8,128)(2,1)S(1)}, u32[]{:S(2)}, u32[]{:S(2)}) %collective-permute-start.18) | collective-permute-done | bytes 196640 | tf_op jit(solution)/shard_map/ppermute | solution.py:148
  60.8 4.2 %collective-permute-done.19 = bf16[48,2048]{1,0:T(8,128)(2,1)} collective-permute-done((bf16[48,2048]{1,0:T(8,128)(2,1)S(1)}, bf16[48,2048]{1,0:T(8,128)(2,1)}, u32[]{:S(2)}, u32[]{:S(2)}) %collective-permute-start.19) | collective-permute-done | bytes 196640 | tf_op jit(solution)/shard_map/ppermute | solution.py:148
  65.0 1.0 pad_maximum_fusion.4
  65.9 1.6 collective-permute-start.21
  67.9 4.9 %fusion.30 = (bf16[384,1536]{1,0:T(8,128)(2,1)S(1)}, f32[384,1536]{1,0:T(8,128)S(1)}) fusion(bf16[384,2048]{1,0:T(8,128)(2,1)S(1)} %bitcast.108, bf16[2048,1536]{1,0:T(8,128)(2,1)} %copy-done.1), kind=kOutput, calls=%fused_computation.95 | convolution fusion | flops 2416508928 | bytes 11403264 | tf_op jit(solution)/shard_map/dot_general | solution.py:168
  72.9 3.8 %collective-permute-done.21 = bf16[2,48,2048]{2,1,0:T(8,128)(2,1)S(1)} collective-permute-done((bf16[2,48,2048]{2,1,0:T(8,128)(2,1)S(1)}, bf16[2,48,2048]{2,1,0:T(8,128)(2,1)S(1)}, u32[]{:S(2)}, u32[]{:S(2)}) %collective-permute-start.21) | collective-permute-done | bytes 393248 | tf_op jit(solution)/shard_map/ppermute | solution.py:153
  77.0 0.8 fusion.19
  77.8 0.4 collective-permute-start.16
  78.2 3.4 %collective-permute-start.17 = (bf16[48,2048]{1,0:T(8,128)(2,1)S(1)}, bf16[48,2048]{1,0:T(8,128)(2,1)S(1)}, u32[]{:S(2)}, u32[]{:S(2)}) collective-permute-start(bf16[48,2048]{1,0:T(8,128)(2,1)S(1)} %get-tuple-element.109), channel_id=1, source_target_pairs={{0,1},{1,4},{2,3},{3,6},{4,0},{5,5},{6,2},{7,7},{8,9},{9,12},{10,1... | collective-permute-start | bytes 589832 | tf_op jit(solution)/shard_map/ppermute | solution.py:148
  81.7 2.4 %collective-permute-start.15 = (bf16[2,96,1536]{2,1,0:T(8,128)(2,1)S(1)}, bf16[2,96,1536]{2,1,0:T(8,128)(2,1)S(1)}, u32[]{:S(2)}, u32[]{:S(2)}) collective-permute-start(bf16[2,96,1536]{2,1,0:T(8,128)(2,1)S(1)} %bitcast.100), channel_id=1, source_target_pairs={{0,4},{12,8},{1,5},{13,9},{2,6},{14,10},{3,7},{15,11},{16,20},{28,... | collective-permute-start | bytes 1769480 | tf_op jit(solution)/shard_map/ppermute | solution.py:173
  84.2 1.7 collective-permute-done.16
  85.9 5.7 %collective-permute-done.17 = bf16[48,2048]{1,0:T(8,128)(2,1)S(1)} collective-permute-done((bf16[48,2048]{1,0:T(8,128)(2,1)S(1)}, bf16[48,2048]{1,0:T(8,128)(2,1)S(1)}, u32[]{:S(2)}, u32[]{:S(2)}) %collective-permute-start.17) | collective-permute-done | bytes 196640 | tf_op jit(solution)/shard_map/ppermute | solution.py:148
  91.6 1.6 collective-permute-start.23
  93.6 2.6 %fusion.31 = (bf16[384,1536]{1,0:T(8,128)(2,1)S(1)}, f32[384,1536]{1,0:T(8,128)S(1)}) fusion(bf16[384,2048]{1,0:T(8,128)(2,1)S(1)} %bitcast.109, bf16[2048,1536]{1,0:T(8,128)(2,1)S(1)} %bitcast.97), kind=kOutput, calls=%fused_computation.96 | convolution fusion | flops 2416508928 | bytes 11403264 | tf_op jit(solution)/shard_map/dot_general | solution.py:168
  96.3 3.8 %collective-permute-done.23 = bf16[2,48,2048]{2,1,0:T(8,128)(2,1)S(1)} collective-permute-done((bf16[2,48,2048]{2,1,0:T(8,128)(2,1)S(1)}, bf16[2,48,2048]{2,1,0:T(8,128)(2,1)S(1)}, u32[]{:S(2)}, u32[]{:S(2)}) %collective-permute-start.23) | collective-permute-done | bytes 393248 | tf_op jit(solution)/shard_map/ppermute | solution.py:153
  100.5 1.3 collective-permute-start.25
  101.8 0.9 collective-permute-start.26
  102.7 0.8 multiply_cosine_fusion
  103.5 7.3 %collective-permute-start.28 = (bf16[2,96,1536]{2,1,0:T(8,128)(2,1)S(1)}, bf16[2,96,1536]{2,1,0:T(8,128)(2,1)S(1)}, u32[]{:S(2)}, u32[]{:S(2)}) collective-permute-start(bf16[2,96,1536]{2,1,0:T(8,128)(2,1)S(1)} %bitcast.98), channel_id=1, source_target_pairs={{0,4},{12,8},{1,5},{13,9},{2,6},{14,10},{3,7},{15,11},{16,20},{28,... | collective-permute-start | bytes 1769480 | tf_op jit(solution)/shard_map/ppermute | solution.py:173
  110.9 2.3 %collective-permute-done.25 = bf16[96,1536]{1,0:T(8,128)(2,1)S(1)} collective-permute-done((bf16[96,1536]{1,0:T(8,128)(2,1)S(1)}, bf16[96,1536]{1,0:T(8,128)(2,1)S(1)}, u32[]{:S(2)}, u32[]{:S(2)}) %collective-permute-start.25) | collective-permute-done | bytes 294944 | tf_op jit(solution)/shard_map/ppermute | solution.py:182
  113.1 1.7 collective-permute-start.33
  114.8 4.8 %collective-permute-start.32 = (bf16[96,1536]{1,0:T(8,128)(2,1)S(1)}, bf16[96,1536]{1,0:T(8,128)(2,1)S(1)}, u32[]{:S(2)}, u32[]{:S(2)}) collective-permute-start(bf16[96,1536]{1,0:T(8,128)(2,1)S(1)} %slice.229), channel_id=1, source_target_pairs={{0,4},{4,0},{8,12},{12,8},{1,5},{5,1},{9,13},{13,9},{2,6},{6,2},{1... | collective-permute-start | bytes 884744 | tf_op jit(solution)/shard_map/ppermute | solution.py:174
  119.6 1.2 fusion.18
  121.2 2.6 %fusion.32 = (bf16[384,1536]{1,0:T(8,128)(2,1)S(1)}, f32[384,1536]{1,0:T(8,128)S(1)}) fusion(bf16[384,2048]{1,0:T(8,128)(2,1)S(1)} %bitcast.107, bf16[2048,1536]{1,0:T(8,128)(2,1)S(1)} %bitcast.97), kind=kOutput, calls=%fused_computation.97 | convolution fusion | flops 2416508928 | bytes 11403264 | tf_op jit(solution)/shard_map/dot_general | solution.py:168
  123.9 1.9 %collective-permute-start.37 = (bf16[2,96,1536]{2,1,0:T(8,128)(2,1)S(1)}, bf16[2,96,1536]{2,1,0:T(8,128)(2,1)S(1)}, u32[]{:S(2)}, u32[]{:S(2)}) collective-permute-start(bf16[2,96,1536]{2,1,0:T(8,128)(2,1)S(1)} %bitcast.104), channel_id=1, source_target_pairs={{0,4},{12,8},{1,5},{13,9},{2,6},{14,10},{3,7},{15,11},{16,20},{28,... | collective-permute-start | bytes 1769480 | tf_op jit(solution)/shard_map/ppermute | solution.py:173
  126.1 1.3 collective-permute-start.30
  127.4 16.1 %collective-permute-done.33 = bf16[2,96,1536]{2,1,0:T(8,128)(2,1)S(1)} collective-permute-done((bf16[2,96,1536]{2,1,0:T(8,128)(2,1)S(1)}, bf16[2,96,1536]{2,1,0:T(8,128)(2,1)S(1)}, u32[]{:S(2)}, u32[]{:S(2)}) %collective-permute-start.33) | collective-permute-done | bytes 589856 | tf_op jit(solution)/shard_map/ppermute | solution.py:173
  143.4 0.7 collective-permute-start.31
  144.3 4.5 %collective-permute-start.36 = (bf16[96,1536]{1,0:T(8,128)(2,1)S(1)}, bf16[96,1536]{1,0:T(8,128)(2,1)S(1)}, u32[]{:S(2)}, u32[]{:S(2)}) collective-permute-start(bf16[96,1536]{1,0:T(8,128)(2,1)S(1)} %slice.234), channel_id=1, source_target_pairs={{0,4},{4,0},{8,12},{12,8},{1,5},{5,1},{9,13},{13,9},{2,6},{6,2},{1... | collective-permute-start | bytes 884744 | tf_op jit(solution)/shard_map/ppermute | solution.py:174
  148.8 1.3 collective-permute-start.34
  150.1 0.7 collective-permute-start.35
  150.9 11.5 %collective-permute-done.37 = bf16[2,96,1536]{2,1,0:T(8,128)(2,1)S(1)} collective-permute-done((bf16[2,96,1536]{2,1,0:T(8,128)(2,1)S(1)}, bf16[2,96,1536]{2,1,0:T(8,128)(2,1)S(1)}, u32[]{:S(2)}, u32[]{:S(2)}) %collective-permute-start.37) | collective-permute-done | bytes 589856 | tf_op jit(solution)/shard_map/ppermute | solution.py:173
  162.6 1.3 collective-permute-start.38
  163.9 0.7 collective-permute-start.39
  164.7 2.9 %collective-permute-done.36 = bf16[96,1536]{1,0:T(8,128)(2,1)S(1)} collective-permute-done((bf16[96,1536]{1,0:T(8,128)(2,1)S(1)}, bf16[96,1536]{1,0:T(8,128)(2,1)S(1)}, u32[]{:S(2)}, u32[]{:S(2)}) %collective-permute-start.36) | collective-permute-done | bytes 294944 | tf_op jit(solution)/shard_map/ppermute | solution.py:174
  167.7 7.7 %collective-permute-done.38 = bf16[96,1536]{1,0:T(8,128)(2,1)S(1)} collective-permute-done((bf16[96,1536]{1,0:T(8,128)(2,1)S(1)}, bf16[96,1536]{1,0:T(8,128)(2,1)S(1)}, u32[]{:S(2)}, u32[]{:S(2)}) %collective-permute-start.38) | collective-permute-done | bytes 294944 | tf_op jit(solution)/shard_map/ppermute | solution.py:182
  176.0 0.5 fusion.27
  176.5 0.3 copy.31
  176.8 0.7 subtract_convert_fusion
  178.1 0.9 fusion.7
  179.0 1.5 fusion.33
  180.5 0.6 fusion.6
  181.1 1.2 copy.23
  (112 shorter events, 7.7 us)
Async XLA Ops:
  0.0 5.1 %copy-start = (bf16[384,2048]{1,0:T(8,128)(2,1)S(1)}, bf16[384,2048]{1,0:T(8,128)(2,1)}, u32[]{:S(2)}) copy-start(bf16[384,2048]{1,0:T(8,128)(2,1)} %param.5) | copy-start | bytes 4718596
  1.9 5.1 %copy-start.5 = (bf16[2048]{0:T(1024)(128)(2,1)S(1)}, bf16[2048]{0:T(1024)(128)(2,1)}, u32[]{:S(2)}) copy-start(bf16[2048]{0:T(1024)(128)(2,1)} %param.6) | copy-start | bytes 12292
  1.9 5.4 %collective-permute-start.1 = (f32[384]{0:T(512)S(1)}, f32[384]{0:T(512)S(1)}, u32[]{:S(2)}, u32[]{:S(2)}) collective-permute-start(f32[384]{0:T(512)S(1)} %multiply_reduce_fusion), channel_id=1, source_target_pairs={{0,1},{1,0},{2,3},{3,2},{4,5},{5,4},{6,7},{7,6},{8,9},{9,8},{10,11... | collective-permute-start | bytes 4616 | tf_op jit(solution)/shard_map/ppermute | solution.py:123
  2.4 6.6 %collective-permute-start.2 = (f32[384]{0:T(512)S(1)}, f32[384]{0:T(512)S(1)}, u32[]{:S(2)}, u32[]{:S(2)}) collective-permute-start(f32[384]{0:T(512)S(1)} %multiply_reduce_fusion), channel_id=1, source_target_pairs={{0,2},{1,3},{2,0},{3,1},{4,6},{5,7},{6,4},{7,5},{8,10},{9,11},{10,... | collective-permute-start | bytes 4616 | tf_op jit(solution)/shard_map/ppermute | solution.py:123
  5.0 4.3 %collective-permute-start.3 = (f32[384]{0:T(512)S(1)}, f32[384]{0:T(512)S(1)}, u32[]{:S(2)}, u32[]{:S(2)}) collective-permute-start(f32[384]{0:T(512)S(1)} %multiply_reduce_fusion), channel_id=1, source_target_pairs={{0,3},{1,2},{2,1},{3,0},{4,7},{5,6},{6,5},{7,4},{8,11},{9,10},{10,... | collective-permute-start | bytes 4616 | tf_op jit(solution)/shard_map/ppermute | solution.py:123
  5.2 7.9 %collective-permute-start = (bf16[48,2048]{1,0:T(8,128)(2,1)S(1)}, bf16[48,2048]{1,0:T(8,128)(2,1)S(1)}, u32[]{:S(2)}, u32[]{:S(2)}) collective-permute-start(bf16[48,2048]{1,0:T(8,128)(2,1)S(1)} %get-tuple-element.95), channel_id=1, source_target_pairs={{0,2},{1,3},{2,0},{3,1},{4,6},{5,7},{6,4},{7,5},{8,10},{9,11},{10,... | collective-permute-start | bytes 589832 | tf_op jit(solution)/shard_map/ppermute | solution.py:117
  7.0 6.1 %collective-permute-start.4 = (bf16[2048]{0:T(1024)(128)(2,1)S(1)}, bf16[2048]{0:T(1024)(128)(2,1)S(1)}, u32[]{:S(2)}, u32[]{:S(2)}) collective-permute-start(bf16[2048]{0:T(1024)(128)(2,1)S(1)} %copy-done.5), channel_id=1, source_target_pairs={{0,2},{1,3},{2,0},{3,1},{4,6},{5,7},{6,4},{7,5},{8,10},{9,11},{10,... | collective-permute-start | bytes 12296 | tf_op jit(solution)/shard_map/ppermute | solution.py:126
  7.3 15.3 %collective-permute-start.7 = (bf16[48,2048]{1,0:T(8,128)(2,1)S(1)}, bf16[48,2048]{1,0:T(8,128)(2,1)S(1)}, u32[]{:S(2)}, u32[]{:S(2)}) collective-permute-start(bf16[48,2048]{1,0:T(8,128)(2,1)S(1)} %get-tuple-element.93), channel_id=1, source_target_pairs={{0,2},{1,3},{2,0},{3,1},{4,6},{5,7},{6,4},{7,5},{8,10},{9,11},{10,... | collective-permute-start | bytes 589832 | tf_op jit(solution)/shard_map/ppermute | solution.py:117
  9.0 18.8 %collective-permute-start.9 = (bf16[48,2048]{1,0:T(8,128)(2,1)S(1)}, bf16[48,2048]{1,0:T(8,128)(2,1)S(1)}, u32[]{:S(2)}, u32[]{:S(2)}) collective-permute-start(bf16[48,2048]{1,0:T(8,128)(2,1)S(1)} %get-tuple-element.91), channel_id=1, source_target_pairs={{0,2},{1,3},{2,0},{3,1},{4,6},{5,7},{6,4},{7,5},{8,10},{9,11},{10,... | collective-permute-start | bytes 589832 | tf_op jit(solution)/shard_map/ppermute | solution.py:117
  13.3 12.0 %collective-permute-start.5 = (bf16[48,2048]{1,0:T(8,128)(2,1)S(1)}, bf16[48,2048]{1,0:T(8,128)(2,1)S(1)}, u32[]{:S(2)}, u32[]{:S(2)}) collective-permute-start(bf16[48,2048]{1,0:T(8,128)(2,1)S(1)} %get-tuple-element.116), channel_id=1, source_target_pairs={{0,8},{1,12},{2,10},{3,14},{4,9},{5,13},{6,11},{7,15},{8,1},{9,5},... | collective-permute-start | bytes 589832 | tf_op jit(solution)/shard_map/ppermute | solution.py:148
  16.1 5.8 %copy-start.2 = (bf16[2048,2,256]{2,1,0:T(2,128)(2,1)S(1)}, bf16[2048,2,256]{2,1,0:T(2,128)(2,1)}, u32[]{:S(2)}) copy-start(bf16[2048,2,256]{2,1,0:T(2,128)(2,1)} %param.8) | copy-start | bytes 6291460
  16.1 10.0 %collective-permute-start.6 = (bf16[48,2048]{1,0:T(8,128)(2,1)S(1)}, bf16[48,2048]{1,0:T(8,128)(2,1)S(1)}, u32[]{:S(2)}, u32[]{:S(2)}) collective-permute-start(bf16[48,2048]{1,0:T(8,128)(2,1)S(1)} %get-tuple-element.115), channel_id=1, source_target_pairs={{0,1},{1,4},{2,3},{3,6},{4,0},{5,5},{6,2},{7,7},{8,9},{9,12},{10,1... | collective-permute-start | bytes 589832 | tf_op jit(solution)/shard_map/ppermute | solution.py:148
  22.6 14.4 %copy-start.1 = (bf16[2048,1536]{1,0:T(8,128)(2,1)}, bf16[2048,1536]{1,0:T(8,128)(2,1)S(1)}, u32[]{:S(2)}) copy-start(bf16[2048,1536]{1,0:T(8,128)(2,1)S(1)} %constant_dynamic-update-slice_fusion) | copy-start | bytes 18874372
  22.8 16.0 %collective-permute-start.12 = (bf16[48,2048]{1,0:T(8,128)(2,1)S(1)}, bf16[48,2048]{1,0:T(8,128)(2,1)S(1)}, u32[]{:S(2)}, u32[]{:S(2)}) collective-permute-start(bf16[48,2048]{1,0:T(8,128)(2,1)S(1)} %get-tuple-element.114), channel_id=1, source_target_pairs={{0,8},{1,12},{2,10},{3,14},{4,9},{5,13},{6,11},{7,15},{8,1},{9,5},... | collective-permute-start | bytes 589832 | tf_op jit(solution)/shard_map/ppermute | solution.py:148
  22.9 15.9 %collective-permute-start.13 = (bf16[48,2048]{1,0:T(8,128)(2,1)S(1)}, bf16[48,2048]{1,0:T(8,128)(2,1)S(1)}, u32[]{:S(2)}, u32[]{:S(2)}) collective-permute-start(bf16[48,2048]{1,0:T(8,128)(2,1)S(1)} %get-tuple-element.113), channel_id=1, source_target_pairs={{0,1},{1,4},{2,3},{3,6},{4,0},{5,5},{6,2},{7,7},{8,9},{9,12},{10,1... | collective-permute-start | bytes 589832 | tf_op jit(solution)/shard_map/ppermute | solution.py:148
  26.2 10.8 %collective-permute-start.8 = (bf16[2,48,2048]{2,1,0:T(8,128)(2,1)S(1)}, bf16[2,48,2048]{2,1,0:T(8,128)(2,1)S(1)}, u32[]{:S(2)}, u32[]{:S(2)}) collective-permute-start(bf16[2,48,2048]{2,1,0:T(8,128)(2,1)S(1)} %pad_maximum_fusion.2), channel_id=1, source_target_pairs={{0,2},{1,3},{2,0},{3,1},{4,6},{5,7},{6,4},{7,5},{8,10},{9,11},{10,... | collective-permute-start | bytes 1179656 | tf_op jit(solution)/shard_map/ppermute | solution.py:153
  37.2 8.0 %collective-permute-start.10 = (bf16[2,96,2048]{2,1,0:T(8,128)(2,1)S(1)}, bf16[2,96,2048]{2,1,0:T(8,128)(2,1)S(1)}, u32[]{:S(2)}, u32[]{:S(2)}) collective-permute-start(bf16[2,96,2048]{2,1,0:T(8,128)(2,1)S(1)} %maximum_select_fusion.4), channel_id=1, source_target_pairs={{0,1},{1,0},{2,3},{3,2},{4,5},{5,4},{6,7},{7,6},{8,9},{9,8},{10,11... | collective-permute-start | bytes 2359304 | tf_op jit(solution)/shard_map/ppermute | solution.py:161
  37.2 7.8 %collective-permute-start.11 = (bf16[48,2048]{1,0:T(8,128)(2,1)S(1)}, bf16[48,2048]{1,0:T(8,128)(2,1)S(1)}, u32[]{:S(2)}, u32[]{:S(2)}) collective-permute-start(bf16[48,2048]{1,0:T(8,128)(2,1)S(1)} %get-tuple-element.97), channel_id=1, source_target_pairs={{0,2},{1,3},{2,0},{3,1},{4,6},{5,7},{6,4},{7,5},{8,10},{9,11},{10,... | collective-permute-start | bytes 589832 | tf_op jit(solution)/shard_map/ppermute | solution.py:117
  38.9 14.1 %collective-permute-start.20 = (bf16[2,48,2048]{2,1,0:T(8,128)(2,1)S(1)}, bf16[2,48,2048]{2,1,0:T(8,128)(2,1)S(1)}, u32[]{:S(2)}, u32[]{:S(2)}) collective-permute-start(bf16[2,48,2048]{2,1,0:T(8,128)(2,1)S(1)} %pad_maximum_fusion.3), channel_id=1, source_target_pairs={{0,2},{1,3},{2,0},{3,1},{4,6},{5,7},{6,4},{7,5},{8,10},{9,11},{10,... | collective-permute-start | bytes 1179656 | tf_op jit(solution)/shard_map/ppermute | solution.py:153
  52.3 0.9 copy-start.4
  53.1 14.4 %collective-permute-start.22 = (bf16[2,96,2048]{2,1,0:T(8,128)(2,1)S(1)}, bf16[2,96,2048]{2,1,0:T(8,128)(2,1)S(1)}, u32[]{:S(2)}, u32[]{:S(2)}) collective-permute-start(bf16[2,96,2048]{2,1,0:T(8,128)(2,1)S(1)} %maximum_select_fusion.5), channel_id=1, source_target_pairs={{0,1},{1,0},{2,3},{3,2},{4,5},{5,4},{6,7},{7,6},{8,9},{9,8},{10,11... | collective-permute-start | bytes 2359304 | tf_op jit(solution)/shard_map/ppermute | solution.py:161
  53.2 7.5 %collective-permute-start.18 = (bf16[48,2048]{1,0:T(8,128)(2,1)S(1)}, bf16[48,2048]{1,0:T(8,128)(2,1)S(1)}, u32[]{:S(2)}, u32[]{:S(2)}) collective-permute-start(bf16[48,2048]{1,0:T(8,128)(2,1)S(1)} %get-tuple-element.112), channel_id=1, source_target_pairs={{0,8},{1,12},{2,10},{3,14},{4,9},{5,13},{6,11},{7,15},{8,1},{9,5},... | collective-permute-start | bytes 589832 | tf_op jit(solution)/shard_map/ppermute | solution.py:148
  55.4 9.6 %collective-permute-start.19 = (bf16[48,2048]{1,0:T(8,128)(2,1)S(1)}, bf16[48,2048]{1,0:T(8,128)(2,1)}, u32[]{:S(2)}, u32[]{:S(2)}) collective-permute-start(bf16[48,2048]{1,0:T(8,128)(2,1)S(1)} %get-tuple-element.111), channel_id=1, source_target_pairs={{0,1},{1,4},{2,3},{3,6},{4,0},{5,5},{6,2},{7,7},{8,9},{9,12},{10,1... | collective-permute-start | bytes 589832 | tf_op jit(solution)/shard_map/ppermute | solution.py:148
  65.9 10.7 %collective-permute-start.21 = (bf16[2,48,2048]{2,1,0:T(8,128)(2,1)S(1)}, bf16[2,48,2048]{2,1,0:T(8,128)(2,1)S(1)}, u32[]{:S(2)}, u32[]{:S(2)}) collective-permute-start(bf16[2,48,2048]{2,1,0:T(8,128)(2,1)S(1)} %pad_maximum_fusion.4), channel_id=1, source_target_pairs={{0,2},{1,3},{2,0},{3,1},{4,6},{5,7},{6,4},{7,5},{8,10},{9,11},{10,... | collective-permute-start | bytes 1179656 | tf_op jit(solution)/shard_map/ppermute | solution.py:153
  67.8 25.8 %slice-start = ((s8[6291456]{0:T(1024)(128)(4,1)}), s8[4194304]{0:T(1024)(128)(4,1)S(1)}, s32[]{:S(2)}) async-start(s8[6291456]{0:T(1024)(128)(4,1)} %bitcast.96), calls=%async_computation | async-start | bytes 8388608
  67.9 25.7 %slice-start.1 = ((s8[6291456]{0:T(1024)(128)(4,1)}), s8[2097152]{0:T(1024)(128)(4,1)S(1)}, s32[]{:S(2)}) async-start(s8[6291456]{0:T(1024)(128)(4,1)} %bitcast.96), calls=%async_computation.1 | async-start | bytes 4194304
  76.8 16.3 %collective-permute-start.24 = (bf16[2,96,2048]{2,1,0:T(8,128)(2,1)S(1)}, bf16[2,96,2048]{2,1,0:T(8,128)(2,1)S(1)}, u32[]{:S(2)}, u32[]{:S(2)}) collective-permute-start(bf16[2,96,2048]{2,1,0:T(8,128)(2,1)S(1)} %maximum_select_fusion.6), channel_id=1, source_target_pairs={{0,1},{1,0},{2,3},{3,2},{4,5},{5,4},{6,7},{7,6},{8,9},{9,8},{10,11... | collective-permute-start | bytes 2359304 | tf_op jit(solution)/shard_map/ppermute | solution.py:161
  77.8 8.1 %collective-permute-start.16 = (bf16[48,2048]{1,0:T(8,128)(2,1)S(1)}, bf16[48,2048]{1,0:T(8,128)(2,1)S(1)}, u32[]{:S(2)}, u32[]{:S(2)}) collective-permute-start(bf16[48,2048]{1,0:T(8,128)(2,1)S(1)} %get-tuple-element.110), channel_id=1, source_target_pairs={{0,8},{1,12},{2,10},{3,14},{4,9},{5,13},{6,11},{7,15},{8,1},{9,5},... | collective-permute-start | bytes 589832 | tf_op jit(solution)/shard_map/ppermute | solution.py:148
  78.2 13.4 %collective-permute-start.17 = (bf16[48,2048]{1,0:T(8,128)(2,1)S(1)}, bf16[48,2048]{1,0:T(8,128)(2,1)S(1)}, u32[]{:S(2)}, u32[]{:S(2)}) collective-permute-start(bf16[48,2048]{1,0:T(8,128)(2,1)S(1)} %get-tuple-element.109), channel_id=1, source_target_pairs={{0,1},{1,4},{2,3},{3,6},{4,0},{5,5},{6,2},{7,7},{8,9},{9,12},{10,1... | collective-permute-start | bytes 589832 | tf_op jit(solution)/shard_map/ppermute | solution.py:148
  81.7 18.7 %collective-permute-start.15 = (bf16[2,96,1536]{2,1,0:T(8,128)(2,1)S(1)}, bf16[2,96,1536]{2,1,0:T(8,128)(2,1)S(1)}, u32[]{:S(2)}, u32[]{:S(2)}) collective-permute-start(bf16[2,96,1536]{2,1,0:T(8,128)(2,1)S(1)} %bitcast.100), channel_id=1, source_target_pairs={{0,4},{12,8},{1,5},{13,9},{2,6},{14,10},{3,7},{15,11},{16,20},{28,... | collective-permute-start | bytes 1769480 | tf_op jit(solution)/shard_map/ppermute | solution.py:173
  84.1 26.7 %collective-permute-start.14 = (bf16[96,1536]{1,0:T(8,128)(2,1)S(1)}, bf16[96,1536]{1,0:T(8,128)(2,1)S(1)}, u32[]{:S(2)}, u32[]{:S(2)}) collective-permute-start(bf16[96,1536]{1,0:T(8,128)(2,1)S(1)} %slice.224), channel_id=1, source_target_pairs={{0,4},{4,0},{8,12},{12,8},{1,5},{5,1},{9,13},{13,9},{2,6},{6,2},{1... | collective-permute-start | bytes 884744 | tf_op jit(solution)/shard_map/ppermute | solution.py:174
  91.6 8.5 %collective-permute-start.23 = (bf16[2,48,2048]{2,1,0:T(8,128)(2,1)S(1)}, bf16[2,48,2048]{2,1,0:T(8,128)(2,1)S(1)}, u32[]{:S(2)}, u32[]{:S(2)}) collective-permute-start(bf16[2,48,2048]{2,1,0:T(8,128)(2,1)S(1)} %pad_maximum_fusion.5), channel_id=1, source_target_pairs={{0,2},{1,3},{2,0},{3,1},{4,6},{5,7},{6,4},{7,5},{8,10},{9,11},{10,... | collective-permute-start | bytes 1179656 | tf_op jit(solution)/shard_map/ppermute | solution.py:153
  100.3 20.6 %collective-permute-start.29 = (bf16[2,96,2048]{2,1,0:T(8,128)(2,1)S(1)}, bf16[2,96,2048]{2,1,0:T(8,128)(2,1)S(1)}, u32[]{:S(2)}, u32[]{:S(2)}) collective-permute-start(bf16[2,96,2048]{2,1,0:T(8,128)(2,1)S(1)} %maximum_select_fusion.7), channel_id=1, source_target_pairs={{0,1},{1,0},{2,3},{3,2},{4,5},{5,4},{6,7},{7,6},{8,9},{9,8},{10,11... | collective-permute-start | bytes 2359304 | tf_op jit(solution)/shard_map/ppermute | solution.py:161
  100.5 12.6 %collective-permute-start.25 = (bf16[96,1536]{1,0:T(8,128)(2,1)S(1)}, bf16[96,1536]{1,0:T(8,128)(2,1)S(1)}, u32[]{:S(2)}, u32[]{:S(2)}) collective-permute-start(bf16[96,1536]{1,0:T(8,128)(2,1)S(1)} %get-tuple-element.101), channel_id=1, source_target_pairs={{4,12},{8,0},{5,13},{9,1},{6,14},{10,2},{7,15},{11,3},{20,28},{24,... | collective-permute-start | bytes 884744 | tf_op jit(solution)/shard_map/ppermute | solution.py:182
  101.8 13.0 %collective-permute-start.26 = (bf16[96,1536]{1,0:T(8,128)(2,1)S(1)}, bf16[96,1536]{1,0:T(8,128)(2,1)S(1)}, u32[]{:S(2)}, u32[]{:S(2)}) collective-permute-start(bf16[96,1536]{1,0:T(8,128)(2,1)S(1)} %get-tuple-element.102), channel_id=1, source_target_pairs={{4,8},{8,4},{5,9},{9,5},{6,10},{10,6},{7,11},{11,7},{20,24},{24,20... | collective-permute-start | bytes 884744 | tf_op jit(solution)/shard_map/ppermute | solution.py:183
  103.5 22.4 %collective-permute-start.28 = (bf16[2,96,1536]{2,1,0:T(8,128)(2,1)S(1)}, bf16[2,96,1536]{2,1,0:T(8,128)(2,1)S(1)}, u32[]{:S(2)}, u32[]{:S(2)}) collective-permute-start(bf16[2,96,1536]{2,1,0:T(8,128)(2,1)S(1)} %bitcast.98), channel_id=1, source_target_pairs={{0,4},{12,8},{1,5},{13,9},{2,6},{14,10},{3,7},{15,11},{16,20},{28,... | collective-permute-start | bytes 1769480 | tf_op jit(solution)/shard_map/ppermute | solution.py:173
  110.8 33.5 %collective-permute-start.27 = (bf16[96,1536]{1,0:T(8,128)(2,1)S(1)}, bf16[96,1536]{1,0:T(8,128)(2,1)S(1)}, u32[]{:S(2)}, u32[]{:S(2)}) collective-permute-start(bf16[96,1536]{1,0:T(8,128)(2,1)S(1)} %slice.227), channel_id=1, source_target_pairs={{0,4},{4,0},{8,12},{12,8},{1,5},{5,1},{9,13},{13,9},{2,6},{6,2},{1... | collective-permute-start | bytes 884744 | tf_op jit(solution)/shard_map/ppermute | solution.py:174
  113.1 30.3 %collective-permute-start.33 = (bf16[2,96,1536]{2,1,0:T(8,128)(2,1)S(1)}, bf16[2,96,1536]{2,1,0:T(8,128)(2,1)S(1)}, u32[]{:S(2)}, u32[]{:S(2)}) collective-permute-start(bf16[2,96,1536]{2,1,0:T(8,128)(2,1)S(1)} %bitcast.102), channel_id=1, source_target_pairs={{0,4},{12,8},{1,5},{13,9},{2,6},{14,10},{3,7},{15,11},{16,20},{28,... | collective-permute-start | bytes 1769480 | tf_op jit(solution)/shard_map/ppermute | solution.py:173
  114.8 49.0 %collective-permute-start.32 = (bf16[96,1536]{1,0:T(8,128)(2,1)S(1)}, bf16[96,1536]{1,0:T(8,128)(2,1)S(1)}, u32[]{:S(2)}, u32[]{:S(2)}) collective-permute-start(bf16[96,1536]{1,0:T(8,128)(2,1)S(1)} %slice.229), channel_id=1, source_target_pairs={{0,4},{4,0},{8,12},{12,8},{1,5},{5,1},{9,13},{13,9},{2,6},{6,2},{1... | collective-permute-start | bytes 884744 | tf_op jit(solution)/shard_map/ppermute | solution.py:174
  123.9 38.5 %collective-permute-start.37 = (bf16[2,96,1536]{2,1,0:T(8,128)(2,1)S(1)}, bf16[2,96,1536]{2,1,0:T(8,128)(2,1)S(1)}, u32[]{:S(2)}, u32[]{:S(2)}) collective-permute-start(bf16[2,96,1536]{2,1,0:T(8,128)(2,1)S(1)} %bitcast.104), channel_id=1, source_target_pairs={{0,4},{12,8},{1,5},{13,9},{2,6},{14,10},{3,7},{15,11},{16,20},{28,... | collective-permute-start | bytes 1769480 | tf_op jit(solution)/shard_map/ppermute | solution.py:173
  126.1 22.7 %collective-permute-start.30 = (bf16[96,1536]{1,0:T(8,128)(2,1)S(1)}, bf16[96,1536]{1,0:T(8,128)(2,1)S(1)}, u32[]{:S(2)}, u32[]{:S(2)}) collective-permute-start(bf16[96,1536]{1,0:T(8,128)(2,1)S(1)} %get-tuple-element.103), channel_id=1, source_target_pairs={{4,12},{8,0},{5,13},{9,1},{6,14},{10,2},{7,15},{11,3},{20,28},{24,... | collective-permute-start | bytes 884744 | tf_op jit(solution)/shard_map/ppermute | solution.py:182
  143.4 6.7 %collective-permute-start.31 = (bf16[96,1536]{1,0:T(8,128)(2,1)S(1)}, bf16[96,1536]{1,0:T(8,128)(2,1)S(1)}, u32[]{:S(2)}, u32[]{:S(2)}) collective-permute-start(bf16[96,1536]{1,0:T(8,128)(2,1)S(1)} %get-tuple-element.104), channel_id=1, source_target_pairs={{4,8},{8,4},{5,9},{9,5},{6,10},{10,6},{7,11},{11,7},{20,24},{24,20... | collective-permute-start | bytes 884744 | tf_op jit(solution)/shard_map/ppermute | solution.py:183
  144.3 23.3 %collective-permute-start.36 = (bf16[96,1536]{1,0:T(8,128)(2,1)S(1)}, bf16[96,1536]{1,0:T(8,128)(2,1)S(1)}, u32[]{:S(2)}, u32[]{:S(2)}) collective-permute-start(bf16[96,1536]{1,0:T(8,128)(2,1)S(1)} %slice.234), channel_id=1, source_target_pairs={{0,4},{4,0},{8,12},{12,8},{1,5},{5,1},{9,13},{13,9},{2,6},{6,2},{1... | collective-permute-start | bytes 884744 | tf_op jit(solution)/shard_map/ppermute | solution.py:174
  148.8 15.8 %collective-permute-start.34 = (bf16[96,1536]{1,0:T(8,128)(2,1)S(1)}, bf16[96,1536]{1,0:T(8,128)(2,1)S(1)}, u32[]{:S(2)}, u32[]{:S(2)}) collective-permute-start(bf16[96,1536]{1,0:T(8,128)(2,1)S(1)} %get-tuple-element.105), channel_id=1, source_target_pairs={{4,12},{8,0},{5,13},{9,1},{6,14},{10,2},{7,15},{11,3},{20,28},{24,... | collective-permute-start | bytes 884744 | tf_op jit(solution)/shard_map/ppermute | solution.py:182
  150.1 14.5 %collective-permute-start.35 = (bf16[96,1536]{1,0:T(8,128)(2,1)S(1)}, bf16[96,1536]{1,0:T(8,128)(2,1)S(1)}, u32[]{:S(2)}, u32[]{:S(2)}) collective-permute-start(bf16[96,1536]{1,0:T(8,128)(2,1)S(1)} %get-tuple-element.106), channel_id=1, source_target_pairs={{4,8},{8,4},{5,9},{9,5},{6,10},{10,6},{7,11},{11,7},{20,24},{24,20... | collective-permute-start | bytes 884744 | tf_op jit(solution)/shard_map/ppermute | solution.py:183
  162.6 12.7 %collective-permute-start.38 = (bf16[96,1536]{1,0:T(8,128)(2,1)S(1)}, bf16[96,1536]{1,0:T(8,128)(2,1)S(1)}, u32[]{:S(2)}, u32[]{:S(2)}) collective-permute-start(bf16[96,1536]{1,0:T(8,128)(2,1)S(1)} %get-tuple-element.107), channel_id=1, source_target_pairs={{4,12},{8,0},{5,13},{9,1},{6,14},{10,2},{7,15},{11,3},{20,28},{24,... | collective-permute-start | bytes 884744 | tf_op jit(solution)/shard_map/ppermute | solution.py:182
  163.9 11.4 %collective-permute-start.39 = (bf16[96,1536]{1,0:T(8,128)(2,1)S(1)}, bf16[96,1536]{1,0:T(8,128)(2,1)S(1)}, u32[]{:S(2)}, u32[]{:S(2)}) collective-permute-start(bf16[96,1536]{1,0:T(8,128)(2,1)S(1)} %get-tuple-element.108), channel_id=1, source_target_pairs={{4,8},{8,4},{5,9},{9,5},{6,10},{10,6},{7,11},{11,7},{20,24},{24,20... | collective-permute-start | bytes 884744 | tf_op jit(solution)/shard_map/ppermute | solution.py:183
  178.0 0.9 copy-start.3

commit v3 on v2

--- a/solution.py
+++ b/solution.py
@@ -1,15 +1,50 @@
+import functools
 import math
 
 import jax
 import jax.numpy as jnp
 from jax import lax
+from jax.experimental import pallas as pl
+from jax.experimental.pallas import tpu as pltpu
 from jax.sharding import PartitionSpec as P
 
 D = 8192
 HEAD_DIM = 128
 ORDER = ((3, 2, 1, 0), (3, 2, 0, 1), (0, 1, 3, 2), (0, 1, 2, 3))
 SIZES = (48, 48, 48, 48)
-TURNS = "s0 w s1 x0 s2 c0 x1 s3 m0 c1 x2 m1 c2 x3 m2 c3 f0 m3 f1 f2 f3"
+PIECES = ((0, 0, 96), (1, 0, 96), (2, 0, 96), (3, 0, 96))
+TURNS = (
+    "a0",
+    "a1",
+    "n",
+    "s0",
+    "a2",
+    "s1",
+    "x0",
+    "w",
+    "a3",
+    "s2",
+    "x1",
+    "c0",
+    "s3",
+    "x2",
+    "c1",
+    "m0",
+    "x3",
+    "c2",
+    "m1",
+    "f0",
+    "c3",
+    "m2",
+    "f1",
+    "d0",
+    "m3",
+    "f2",
+    "d1",
+    "f3",
+    "d2",
+    "d3",
+)
 
 
 def positions(seg):
@@ -92,6 +127,84 @@
     return attend(query, k_rot, v_val, seg, cosine, sine, 0)
 
 
+def attend_kernel(start, *refs):
+    own_ref, near_ref, far_ref, mid_ref, cos_ref, sin_ref, column_ref, row_ref, *refs = refs
+    if start:
+        old_ref, _, out_ref, kv_ref, held, sem = refs
+        kv_ref[...] = old_ref[...]
+    else:
+        out_ref, kv_ref, held, sem = refs
+        kv_ref[...] = jnp.zeros_like(kv_ref)
+    size = own_ref.shape[0]
+    q_cols = held.shape[1]
+    kv_cols = kv_ref.shape[2]
+    group = q_cols // kv_cols
+    rows = slice(start, start + size)
+    seen = min(-(-(start + size) // HEAD_DIM) * HEAD_DIM, kv_ref.shape[1])
+    cosine, sine = cos_ref[rows, :], sin_ref[rows, :]
+
+    def total(col):
+        cols = slice(col, col + HEAD_DIM)
+        return (
+            own_ref[:, cols]
+            + near_ref[:, cols].astype(jnp.float32)
+            + far_ref[:, cols].astype(jnp.float32)
+            + mid_ref[:, cols].astype(jnp.float32)
+        )
+
+    def rotated(col):
+        head = total(col)
+        return (head * cosine + pltpu.roll(head, HEAD_DIM // 2, 1) * sine).astype(jnp.bfloat16)
+
+    for col in range(0, kv_cols, HEAD_DIM):
+        kv_ref[0, rows, col : col + HEAD_DIM] = rotated(q_cols + col)
+        kv_ref[1, rows, col : col + HEAD_DIM] = total(q_cols + kv_cols + col).astype(jnp.bfloat16)
+    shape = (size, seen)
+    later = lax.broadcasted_iota(jnp.int32, shape, 1) > lax.broadcasted_iota(jnp.int32, shape, 0) + start
+    allowed = jnp.logical_and(column_ref[rows, :] == row_ref[:, :seen], jnp.logical_not(later))
+    bias = jnp.where(allowed, 0.0, -jnp.inf)
+    bias = jnp.concatenate([bias] * group)
+    for head in range(kv_cols // HEAD_DIM):
+        cols = slice(head * HEAD_DIM, (head + 1) * HEAD_DIM)
+        base = head * group * HEAD_DIM
+        queries = jnp.concatenate([rotated(base + g * HEAD_DIM) for g in range(group)])
+        scores = lax.dot_general(
+            queries,
+            kv_ref[0, :seen, cols],
+            (((1,), (1,)), ((), ())),
+            preferred_element_type=jnp.float32,
+        )
+        scores = scores * (1.0 / math.sqrt(HEAD_DIM)) + bias
+        expo = jnp.exp(scores - jnp.max(scores, axis=1, keepdims=True))
+        weights = (expo * (1.0 / jnp.sum(expo, axis=1, keepdims=True))).astype(jnp.bfloat16)
+        mixed = jnp.dot(weights, kv_ref[1, :seen, cols], preferred_element_type=jnp.float32)
+        for g in range(group):
+            held[:, base + g * HEAD_DIM : base + (g + 1) * HEAD_DIM] = mixed[
+                g * size : (g + 1) * size
+            ].astype(jnp.bfloat16)
+    copy = pltpu.make_async_copy(held, out_ref.at[pl.ds(start, size)], sem)
+    copy.start()
+    copy.wait()
+
+
+def attend_piece(start, sums, tables, before, tokens, q_cols):
+    size, cols = sums[0].shape
+    kv = jax.ShapeDtypeStruct((2, tokens, (cols - q_cols) // 2), jnp.bfloat16)
+    out = jax.ShapeDtypeStruct((tokens, q_cols), jnp.bfloat16)
+    here = pl.BlockSpec(memory_space=pltpu.VMEM)
+    anywhere = pl.BlockSpec(memory_space=pl.ANY)
+    return pl.pallas_call(
+        functools.partial(attend_kernel, start),
+        in_specs=[here] * 8 + ([here, anywhere] if start else []),
+        out_specs=[anywhere, here],
+        out_shape=[out, kv],
+        scratch_shapes=[pltpu.VMEM((size, q_cols), jnp.bfloat16), pltpu.SemaphoreType.DMA],
+        input_output_aliases={9: 0} if start else {},
+        compiler_params=pltpu.CompilerParams(vmem_limit_bytes=24 * 2**20),
+        cost_estimate=pl.CostEstimate(flops=0, bytes_accessed=0, transcendentals=0),
+    )(*sums, *tables, *before)
+
+
 def partial_sums(hidden_states, norm_gain, w_query, w_keyval, segment_ids):
     z = lax.axis_index("fsdp")
     t = lax.axis_index("tensor")
@@ -113,32 +226,39 @@
     count = len(SIZES)
 
     starts = [sum(SIZES[:n]) * 2 for n in range(count)]
-    crossed = [
-        lax.ppermute(hidden_states[start + size : start + 2 * size], "tensor", swap_x)
-        for start, size in zip(starts, SIZES)
+    local_sq = jnp.sum(jnp.square(hidden_states.astype(jnp.float32)), axis=1)
+    gain = norm_gain.astype(jnp.float32)
+    squares = [
+        lax.ppermute(local_sq, "tensor", [(n, n ^ flip) for n in range(4)]) for flip in (1, 3)
     ]
-    local_sq = jnp.sum(jnp.square(hidden_states.astype(jnp.float32)), axis=1)
-    square_sum = local_sq
-    for flip in (1, 2, 3):
-        square_sum += lax.ppermute(local_sq, "tensor", [(n, n ^ flip) for n in range(4)])
-    scale = lax.rsqrt(square_sum / D + 1e-05)[:, None]
-    gain = norm_gain.astype(jnp.float32)[None, :]
-    crossed_gain = lax.ppermute(norm_gain, "tensor", swap_x).astype(jnp.float32)[None, :]
+    partner = lax.ppermute(jnp.concatenate((local_sq, gain)), "tensor", swap_x)
+    crossed_gain = partner[None, tokens:]
+    gain = gain[None, :]
 
     here_far = t // 2 != z // 2
     even_core = t % 2 == 0
-    done = [scale]
+    done = [local_sq]
 
     def in_turn(*arrays):
         arrays, _ = lax.optimization_barrier((arrays, done[0]))
         return arrays
 
     state = [{} for _ in SIZES]
+    sums = [{} for _ in PIECES]
+    before = ()
+
+    def across(n):
+        start, size = starts[n], SIZES[n]
+        piece = hidden_states[start + size : start + 2 * size]
+        if n:
+            (piece,) = in_turn(piece)
+            done[0] = piece
+        state[n]["a"] = lax.ppermute(piece, "tensor", swap_x)
 
     def send(n):
         start, size = starts[n], SIZES[n]
         mid = start + size
-        stay, other = in_turn(hidden_states[start:mid], crossed[n])
+        stay, other = in_turn(hidden_states[start:mid], state[n]["a"])
         stay = (stay.astype(jnp.float32) * scale[start:mid] * gain).astype(jnp.bfloat16)
         other = other.astype(jnp.float32) * scale[mid : mid + size] * crossed_gain
         other = other.astype(jnp.bfloat16)
@@ -161,51 +281,58 @@
         state[n]["c"] = mine, lax.ppermute(mine, "tensor", swap_core)
 
     def multiply(n):
-        mine, theirs = in_turn(*state[n]["c"])
-        rows = jnp.where(
-            even_core, jnp.stack((mine, theirs), 1), jnp.stack((theirs, mine), 1)
-        ).reshape(8 * SIZES[n], -1)
+        batch, begin, end = PIECES[n]
+        mine, theirs = in_turn(*(array[:, begin:end] for array in state[batch]["c"]))
+        rows = jnp.where(even_core, jnp.stack((mine, theirs), 1), jnp.stack((theirs, mine), 1))
+        rows = rows.reshape(4 * (end - begin), -1)
         part = jnp.dot(rows, weight, preferred_element_type=jnp.float32)
-        part = part.reshape(4, 2 * SIZES[n], -1)
+        part = part.reshape(4, end - begin, -1)
         outer = part[:2].astype(jnp.bfloat16)
         inner = part[2].astype(jnp.bfloat16)
         done[0] = (outer, inner)
         passed = lax.ppermute(outer, "fsdp", outer_in)
         near_sum = lax.ppermute(inner, "fsdp", [(0, 1), (1, 0), (2, 3), (3, 2)])
-        state[n]["p"] = part[3], outer, passed, near_sum
+        sums[n]["p"] = part[3], outer, passed, near_sum
 
     def forward(n):
-        own, outer, passed, near_sum = state[n]["p"]
+        own, outer, passed, near_sum = sums[n]["p"]
         passed, outer = in_turn(passed, outer)
         passed = passed + outer
         done[0] = passed
         far_sum = lax.ppermute(passed[0], "fsdp", [(1, 3), (2, 0)])
         mid_sum = lax.ppermute(passed[1], "fsdp", [(1, 2), (2, 1)])
-        state[n]["f"] = own, near_sum, far_sum, mid_sum
+        sums[n]["f"] = own, near_sum, far_sum, mid_sum
 
     def finish(n):
-        own, near_sum, far_sum, mid_sum = state[n]["f"]
-        return (
-            own
-            + near_sum.astype(jnp.float32)
-            + far_sum.astype(jnp.float32)
-            + mid_sum.astype(jnp.float32)
-        )
-
-    steps = {"s": send, "x": cross, "c": share, "m": multiply, "f": forward}
-    for turn in TURNS.split():
-        if turn == "w":
+        batch, begin, _ = PIECES[n]
+        added = in_turn(*sums[n]["f"])
+        out, kv = attend_piece(starts[batch] + begin, added, tables, before, tokens, q_cols)
+        done[0] = kv
+        return kv, out
+
+    seg = segment_ids[0]
+    cosine, sine = rope_tables(positions(seg), HEAD_DIM)
+    tables = (
+        jnp.concatenate((cosine, cosine), 1),
+        jnp.concatenate((-sine, sine), 1),
+        seg[:, None],
+        seg[None, :],
+    )
+    steps = {"a": across, "s": send, "x": cross, "c": share, "m": multiply, "f": forward}
+    for turn in TURNS:
+        if turn == "n":
+            *received, state[0]["a"] = in_turn(partner[:tokens], *squares, state[0]["a"])
+            done[0] = scale = lax.rsqrt((local_sq + sum(received)) / D + 1e-05)[:, None]
+        elif turn == "w":
             w_query, w_keyval = in_turn(w_query, w_keyval)
             weight = jnp.concatenate((w_query, w_keyval.reshape(w_keyval.shape[0], -1)), axis=1)
             done[0] = weight
+        elif turn[0] == "d":
+            before = finish(int(turn[1]))
         else:
             steps[turn[0]](int(turn[1]))
 
-    seg = segment_ids[0]
-    cosine, sine = rope_tables(positions(seg), HEAD_DIM)
-    total = jnp.concatenate([finish(n) for n in range(count)])
-    k_rot, v_val = rotated_keys(total[:, q_cols:], cosine, sine)
-    return attend(total[:, :q_cols], k_rot, v_val, seg, cosine, sine, 0)
+    return before[1]
 
 
 def solution(mesh):

time: 185 us -> 160 us (0.86)
  waiting for transfers between devices: 82.1 us -> 58.4 us
  matrix products: 18.4 us -> 10.5 us
  Pallas kernels: 0 us -> 7.81 us
  starting transfers between devices: 61.5 us -> 66.3 us
  other arithmetic: 12.2 us -> 9.14 us
    ppermute x4, waiting for transfers between devices: 17.1 us -> 1.89 us  [cross(): state[n]['x'] = (mine, lax.ppermute(mine, 'tensor', swap_x))]
    ppermute x4, waiting for transfers between devices: 10.8 us -> 0.01 us  [send(): lax.ppermute(near, both, toward(False))]
    pallas_call x0 -> x4, Pallas kernels: none -> 7.81 us  [attend_piece(): pl.pallas_call(functools.partial(attend_kernel, start), in_specs=[here] *...]
    ppermute x4, starting transfers between devices: 9.39 us -> 2.29 us  [multiply(): near_sum = lax.ppermute(inner, 'fsdp', [(0, 1), (1, 0), (2, 3), (3, 2)])]
    dot_general x4, matrix products: 16.9 us -> 10.5 us  [multiply(): part = jnp.dot(rows, weight, preferred_element_type=jnp.float32)]
    ppermute x4, starting transfers between devices: 13.4 us -> 17.6 us  [multiply(): passed = lax.ppermute(outer, 'fsdp', outer_in)]
    ppermute x4, starting transfers between devices: 10.8 us -> 15 us  [send(): lax.ppermute(near, both, toward(False))]
    ppermute x4, starting transfers between devices: 0.28 us -> 3.68 us  [share(): state[n]['c'] = (mine, lax.ppermute(mine, 'tensor', swap_core))]
  transfers between devices with their start and end apart: 40 -> 39, of which waited for: 16 -> 9; matrix products, arithmetic and copies ran while one was open for 16% -> 13% of each run, Pallas kernels for 0% -> 3%
where the time goes in v3:
time: 160 us; the launch traced here: 159 us
  starting transfers between devices  66.3 us (41%)
  waiting for transfers between devices  58.4 us (36%)
  matrix products  10.5 us (7%)
  other arithmetic  9.14 us (6%)
  Pallas kernels  7.81 us (5%)
  local copies, waits for them, and re-layouts  5.85 us (4%)
    ppermute x4, waiting for transfers between devices, multiply(): passed = lax.ppermute(outer, 'fsdp', outer_in)  29.2 us
    ppermute x4, starting transfers between devices, multiply(): passed = lax.ppermute(outer, 'fsdp', outer_in)  17.6 us
    ppermute x4, starting transfers between devices, send(): lax.ppermute(near, both, toward(False))  15 us
    ppermute x4, waiting for transfers between devices, forward(): far_sum = lax.ppermute(passed[0], 'fsdp', [(1, 3), (2, 0)])  12.1 us
    dot_general x4, matrix products, multiply(): part = jnp.dot(rows, weight, preferred_element_type=jnp.float32)  10.5 us
    pallas_call x4, Pallas kernels, attend_piece(): pl.pallas_call(functools.partial(attend_kernel, start), in_specs=[here] *...  7.81 us
    ppermute x4, waiting for transfers between devices, across(): state[n]['a'] = lax.ppermute(piece, 'tensor', swap_x)  7.46 us
    ppermute x4, starting transfers between devices, send(): lax.ppermute(far, both, toward(True))  6.55 us
  transfers between devices with their start and end apart: 39, of which 9 were waited for; matrix products, arithmetic and copies ran while one was open for 13% of the time, Pallas kernels for 3%

profile of v3, /device:TPU:0, one launch (start us, length us, event | category | flops | bytes accessed | tf_op | source)
XLA Modules:
  0.0 158.9 jit_solution(15238126612431431136)
XLA Ops:
  0.0 1.9 %multiply_reduce_fusion = f32[384]{0:T(512)S(1)} fusion(bf16[384,2048]{1,0:T(8,128)(2,1)} %param.5), kind=kLoop, calls=%fused_computation | loop fusion | flops 2358912 | bytes 1574400 | tf_op jit(solution)/shard_map/reduce_sum | solution.py:229
  1.9 2.4 %collective-permute-start.2 = (f32[384]{0:T(512)S(1)}, f32[384]{0:T(512)S(1)}, u32[]{:S(2)}, u32[]{:S(2)}) collective-permute-start(f32[384]{0:T(512)S(1)} %multiply_reduce_fusion), channel_id=1, source_target_pairs={{0,3},{1,2},{2,1},{3,0},{4,7},{5,6},{6,5},{7,4},{8,11},{9,10},{10,... | collective-permute-start | bytes 4616 | tf_op jit(solution)/shard_map/ppermute | solution.py:232
  4.3 0.7 collective-permute-start.1
  5.0 0.7 convert_element_type.82
  5.8 0.9 fusion.2
  6.8 2.0 %collective-permute-start.6 = (bf16[48,2048]{1,0:T(8,128)(2,1)}, bf16[48,2048]{1,0:T(8,128)(2,1)}, u32[]{:S(2)}, u32[]{:S(2)}) collective-permute-start(bf16[48,2048]{1,0:T(8,128)(2,1)} %get-tuple-element.77), channel_id=1, source_target_pairs={{0,2},{1,3},{2,0},{3,1},{4,6},{5,7},{6,4},{7,5},{8,10},{9,11},{10,... | collective-permute-start | bytes 589832 | tf_op jit(solution)/shard_map/ppermute | solution.py:256
  9.0 0.3 reduce-window.9
  9.6 0.8 fusion
  10.8 7.5 %collective-permute-done.3 = bf16[48,2048]{1,0:T(8,128)(2,1)} collective-permute-done((bf16[48,2048]{1,0:T(8,128)(2,1)}, bf16[48,2048]{1,0:T(8,128)(2,1)}, u32[]{:S(2)}, u32[]{:S(2)}) %collective-permute-start.3) | collective-permute-done | bytes 196640 | tf_op jit(solution)/shard_map/ppermute | solution.py:256
  18.4 1.1 broadcast_select_fusion.6
  19.5 1.9 %collective-permute-start.5 = (bf16[48,2048]{1,0:T(8,128)(2,1)S(1)}, bf16[48,2048]{1,0:T(8,128)(2,1)S(1)}, u32[]{:S(2)}, u32[]{:S(2)}) collective-permute-start(bf16[48,2048]{1,0:T(8,128)(2,1)S(1)} %get-tuple-element.171), channel_id=1, source_target_pairs={{0,1},{1,4},{2,3},{3,6},{4,0},{5,5},{6,2},{7,7},{8,9},{9,12},{10,1... | collective-permute-start | bytes 589832 | tf_op jit(solution)/shard_map/ppermute | solution.py:268
  21.4 2.7 %collective-permute-start.4 = (bf16[48,2048]{1,0:T(8,128)(2,1)S(1)}, bf16[48,2048]{1,0:T(8,128)(2,1)S(1)}, u32[]{:S(2)}, u32[]{:S(2)}) collective-permute-start(bf16[48,2048]{1,0:T(8,128)(2,1)S(1)} %get-tuple-element.172), channel_id=1, source_target_pairs={{0,8},{1,12},{2,10},{3,14},{4,9},{5,13},{6,11},{7,15},{8,1},{9,5},... | collective-permute-start | bytes 589832 | tf_op jit(solution)/shard_map/ppermute | solution.py:268
  24.1 1.5 collective-permute-start.11
  25.6 1.1 broadcast_select_fusion.4
  26.7 3.2 %collective-permute-start.10 = (bf16[48,2048]{1,0:T(8,128)(2,1)S(1)}, bf16[48,2048]{1,0:T(8,128)(2,1)S(1)}, u32[]{:S(2)}, u32[]{:S(2)}) collective-permute-start(bf16[48,2048]{1,0:T(8,128)(2,1)S(1)} %get-tuple-element.169), channel_id=1, source_target_pairs={{0,1},{1,4},{2,3},{3,6},{4,0},{5,5},{6,2},{7,7},{8,9},{9,12},{10,1... | collective-permute-start | bytes 589832 | tf_op jit(solution)/shard_map/ppermute | solution.py:268
  29.9 0.4 collective-permute-start.9
  30.3 2.9 %collective-permute-done.4 = bf16[48,2048]{1,0:T(8,128)(2,1)S(1)} collective-permute-done((bf16[48,2048]{1,0:T(8,128)(2,1)S(1)}, bf16[48,2048]{1,0:T(8,128)(2,1)S(1)}, u32[]{:S(2)}, u32[]{:S(2)}) %collective-permute-start.4) | collective-permute-done | bytes 196640 | tf_op jit(solution)/shard_map/ppermute | solution.py:268
  33.3 1.6 %collective-permute-start.8 = (bf16[2,48,2048]{2,1,0:T(8,128)(2,1)S(1)}, bf16[2,48,2048]{2,1,0:T(8,128)(2,1)S(1)}, u32[]{:S(2)}, u32[]{:S(2)}) collective-permute-start(bf16[2,48,2048]{2,1,0:T(8,128)(2,1)S(1)} %pad_maximum_fusion), channel_id=1, source_target_pairs={{0,2},{1,3},{2,0},{3,1},{4,6},{5,7},{6,4},{7,5},{8,10},{9,11},{10,... | collective-permute-start | bytes 1179656 | tf_op jit(solution)/shard_map/ppermute | solution.py:273
  34.9 0.5 copy.17
  35.4 1.7 %copy-done.2 = bf16[2048,1024]{1,0:T(8,128)(2,1)S(1)} copy-done((bf16[2048,1024]{1,0:T(8,128)(2,1)S(1)}, bf16[2048,1024]{1,0:T(8,128)(2,1)}, u32[]{:S(2)}) %copy-start.2) | copy-done | bytes 4194328
  37.1 0.4 constant_dynamic-update-slice_fusion.1
  37.7 0.8 copy-done.4
  38.5 0.5 collective-permute-start.7
  39.1 7.5 %collective-permute-start.17 = (bf16[48,2048]{1,0:T(8,128)(2,1)S(1)}, bf16[48,2048]{1,0:T(8,128)(2,1)S(1)}, u32[]{:S(2)}, u32[]{:S(2)}) collective-permute-start(bf16[48,2048]{1,0:T(8,128)(2,1)S(1)} %get-tuple-element.167), channel_id=1, source_target_pairs={{0,1},{1,4},{2,3},{3,6},{4,0},{5,5},{6,2},{7,7},{8,9},{9,12},{10,1... | collective-permute-start | bytes 589832 | tf_op jit(solution)/shard_map/ppermute | solution.py:268
  46.7 1.9 %collective-permute-start.16 = (bf16[48,2048]{1,0:T(8,128)(2,1)S(1)}, bf16[48,2048]{1,0:T(8,128)(2,1)S(1)}, u32[]{:S(2)}, u32[]{:S(2)}) collective-permute-start(bf16[48,2048]{1,0:T(8,128)(2,1)S(1)} %get-tuple-element.168), channel_id=1, source_target_pairs={{0,8},{1,12},{2,10},{3,14},{4,9},{5,13},{6,11},{7,15},{8,1},{9,5},... | collective-permute-start | bytes 589832 | tf_op jit(solution)/shard_map/ppermute | solution.py:268
  48.6 1.6 collective-permute-start.15
  50.4 0.2 broadcast_select_fusion
  50.6 2.4 %collective-permute-start.13 = (bf16[48,2048]{1,0:T(8,128)(2,1)S(1)}, bf16[48,2048]{1,0:T(8,128)(2,1)S(1)}, u32[]{:S(2)}, u32[]{:S(2)}) collective-permute-start(bf16[48,2048]{1,0:T(8,128)(2,1)S(1)} %get-tuple-element.165), channel_id=1, source_target_pairs={{0,1},{1,4},{2,3},{3,6},{4,0},{5,5},{6,2},{7,7},{8,9},{9,12},{10,1... | collective-permute-start | bytes 589832 | tf_op jit(solution)/shard_map/ppermute | solution.py:268
  53.0 1.5 collective-permute-start.12
  54.6 2.4 %collective-permute-start.21 = (bf16[2,48,2048]{2,1,0:T(8,128)(2,1)S(1)}, bf16[2,48,2048]{2,1,0:T(8,128)(2,1)S(1)}, u32[]{:S(2)}, u32[]{:S(2)}) collective-permute-start(bf16[2,48,2048]{2,1,0:T(8,128)(2,1)S(1)} %pad_maximum_fusion.2), channel_id=1, source_target_pairs={{0,2},{1,3},{2,0},{3,1},{4,6},{5,7},{6,4},{7,5},{8,10},{9,11},{10,... | collective-permute-start | bytes 1179656 | tf_op jit(solution)/shard_map/ppermute | solution.py:273
  57.0 1.9 %collective-permute-done.15 = bf16[2,48,2048]{2,1,0:T(8,128)(2,1)S(1)} collective-permute-done((bf16[2,48,2048]{2,1,0:T(8,128)(2,1)S(1)}, bf16[2,48,2048]{2,1,0:T(8,128)(2,1)S(1)}, u32[]{:S(2)}, u32[]{:S(2)}) %collective-permute-start.15) | collective-permute-done | bytes 393248 | tf_op jit(solution)/shard_map/ppermute | solution.py:273
  59.0 3.5 %collective-permute-start.20 = (bf16[2,96,2048]{2,1,0:T(8,128)(2,1)S(1)}, bf16[2,96,2048]{2,1,0:T(8,128)(2,1)S(1)}, u32[]{:S(2)}, u32[]{:S(2)}) collective-permute-start(bf16[2,96,2048]{2,1,0:T(8,128)(2,1)S(1)} %maximum_select_fusion.5), channel_id=1, source_target_pairs={{0,1},{1,0},{2,3},{3,2},{4,5},{5,4},{6,7},{7,6},{8,9},{9,8},{10,11... | collective-permute-start | bytes 2359304 | tf_op jit(solution)/shard_map/ppermute | solution.py:281
  62.5 0.3 maximum_select_fusion
  62.8 2.6 %fusion.4 = (bf16[384,1536]{1,0:T(8,128)(2,1)S(1)}, f32[384,1536]{1,0:T(8,128)S(1)}) fusion(bf16[384,2048]{1,0:T(8,128)(2,1)S(1)} %bitcast.77, bf16[2048,1536]{1,0:T(8,128)(2,1)S(1)} %constant_dynamic-update-slice_fusion), kind=kOutput, calls=%fused_computation.55 | convolution fusion | flops 2416508928 | bytes 11403264 | tf_op jit(solution)/shard_map/dot_general | solution.py:288
  65.5 3.9 %collective-permute-start.19 = (bf16[2,96,1536]{2,1,0:T(8,128)(2,1)S(1)}, bf16[2,96,1536]{2,1,0:T(8,128)(2,1)S(1)}, u32[]{:S(2)}, u32[]{:S(2)}) collective-permute-start(bf16[2,96,1536]{2,1,0:T(8,128)(2,1)S(1)} %bitcast.67), channel_id=1, source_target_pairs={{0,4},{12,8},{1,5},{13,9},{2,6},{14,10},{3,7},{15,11},{16,20},{28,... | collective-permute-start | bytes 1769480 | tf_op jit(solution)/shard_map/ppermute | solution.py:293
  69.5 0.4 collective-permute-start.18
  70.2 0.3 maximum_select_fusion.1
  70.6 2.6 %fusion.5 = (bf16[384,1536]{1,0:T(8,128)(2,1)S(1)}, f32[384,1536]{1,0:T(8,128)S(1)}) fusion(bf16[384,2048]{1,0:T(8,128)(2,1)S(1)} %bitcast.75, bf16[2048,1536]{1,0:T(8,128)(2,1)S(1)} %constant_dynamic-update-slice_fusion), kind=kOutput, calls=%fused_computation.56 | convolution fusion | flops 2416508928 | bytes 11403264 | tf_op jit(solution)/shard_map/dot_general | solution.py:288
  73.4 12.1 %collective-permute-done.19 = bf16[2,96,1536]{2,1,0:T(8,128)(2,1)S(1)} collective-permute-done((bf16[2,96,1536]{2,1,0:T(8,128)(2,1)S(1)}, bf16[2,96,1536]{2,1,0:T(8,128)(2,1)S(1)}, u32[]{:S(2)}, u32[]{:S(2)}) %collective-permute-start.19) | collective-permute-done | bytes 589856 | tf_op jit(solution)/shard_map/ppermute | solution.py:293
  85.5 4.4 %collective-permute-start.26 = (bf16[2,96,1536]{2,1,0:T(8,128)(2,1)S(1)}, bf16[2,96,1536]{2,1,0:T(8,128)(2,1)S(1)}, u32[]{:S(2)}, u32[]{:S(2)}) collective-permute-start(bf16[2,96,1536]{2,1,0:T(8,128)(2,1)S(1)} %bitcast.71), channel_id=1, source_target_pairs={{0,4},{12,8},{1,5},{13,9},{2,6},{14,10},{3,7},{15,11},{16,20},{28,... | collective-permute-start | bytes 1769480 | tf_op jit(solution)/shard_map/ppermute | solution.py:293
  90.1 0.9 collective-permute-start.25
  91.3 0.3 maximum_select_fusion.2
  91.6 2.6 %fusion.6 = (bf16[384,1536]{1,0:T(8,128)(2,1)S(1)}, f32[384,1536]{1,0:T(8,128)S(1)}) fusion(bf16[384,2048]{1,0:T(8,128)(2,1)S(1)} %bitcast.76, bf16[2048,1536]{1,0:T(8,128)(2,1)S(1)} %constant_dynamic-update-slice_fusion), kind=kOutput, calls=%fused_computation.57 | convolution fusion | flops 2416508928 | bytes 11403264 | tf_op jit(solution)/shard_map/dot_general | solution.py:288
  94.3 9.5 %collective-permute-done.26 = bf16[2,96,1536]{2,1,0:T(8,128)(2,1)S(1)} collective-permute-done((bf16[2,96,1536]{2,1,0:T(8,128)(2,1)S(1)}, bf16[2,96,1536]{2,1,0:T(8,128)(2,1)S(1)}, u32[]{:S(2)}, u32[]{:S(2)}) %collective-permute-start.26) | collective-permute-done | bytes 589856 | tf_op jit(solution)/shard_map/ppermute | solution.py:293
  103.9 1.3 collective-permute-start.24
  105.4 4.6 %collective-permute-start.33 = (bf16[2,96,1536]{2,1,0:T(8,128)(2,1)S(1)}, bf16[2,96,1536]{2,1,0:T(8,128)(2,1)S(1)}, u32[]{:S(2)}, u32[]{:S(2)}) collective-permute-start(bf16[2,96,1536]{2,1,0:T(8,128)(2,1)S(1)} %bitcast.65), channel_id=1, source_target_pairs={{0,4},{12,8},{1,5},{13,9},{2,6},{14,10},{3,7},{15,11},{16,20},{28,... | collective-permute-start | bytes 1769480 | tf_op jit(solution)/shard_map/ppermute | solution.py:293
  110.0 0.7 collective-permute-start.32
  110.7 5.9 %collective-permute-done.24.refs_2_ = bf16[96,1536]{1,0:T(8,128)(2,1)S(1)} collective-permute-done((bf16[96,1536]{1,0:T(8,128)(2,1)S(1)}, bf16[96,1536]{1,0:T(8,128)(2,1)S(1)}, u32[]{:S(2)}, u32[]{:S(2)}) %collective-permute-start.24) | collective-permute-done | bytes 294944 | tf_op jit(solution)/shard_map/ppermute | solution.py:302
  116.6 1.3 collective-permute-start.31
  117.9 1.6 %shard_map.55 = (bf16[384,1024]{1,0:T(8,128)(2,1)}, bf16[2,384,256]{2,1,0:T(8,128)(2,1)S(1)}) custom-call(f32[96,1536]{1,0:T(8,128)S(1)} %slice.205.refs_0_, bf16[96,1536]{1,0:T(8,128)(2,1)S(1)} %collective-permute-done.23.refs_1_, bf16[96,1536]{1,0:T(8,128)(2,1)S(1)} %collective-permute-done.24.refs_2_, ...), custom_call_target="tpu_custom_call" | custom-call | tf_op jit(solution)/shard_map/pallas_call | solution.py:196
  119.5 0.3 maximum_select_fusion.3
  120.0 2.6 %fusion.7 = (bf16[384,1536]{1,0:T(8,128)(2,1)S(1)}, f32[384,1536]{1,0:T(8,128)S(1)}) fusion(bf16[384,2048]{1,0:T(8,128)(2,1)S(1)} %bitcast.74, bf16[2048,1536]{1,0:T(8,128)(2,1)S(1)} %constant_dynamic-update-slice_fusion), kind=kOutput, calls=%fused_computation.58 | convolution fusion | flops 2416508928 | bytes 11403264 | tf_op jit(solution)/shard_map/dot_general | solution.py:288
  122.6 4.6 %collective-permute-start.29 = (bf16[2,96,1536]{2,1,0:T(8,128)(2,1)S(1)}, bf16[2,96,1536]{2,1,0:T(8,128)(2,1)S(1)}, u32[]{:S(2)}, u32[]{:S(2)}) collective-permute-start(bf16[2,96,1536]{2,1,0:T(8,128)(2,1)S(1)} %bitcast.69), channel_id=1, source_target_pairs={{0,4},{12,8},{1,5},{13,9},{2,6},{14,10},{3,7},{15,11},{16,20},{28,... | collective-permute-start | bytes 1769480 | tf_op jit(solution)/shard_map/ppermute | solution.py:293
  127.6 2.1 %collective-permute-start.28 = (bf16[96,1536]{1,0:T(8,128)(2,1)S(1)}, bf16[96,1536]{1,0:T(8,128)(2,1)S(1)}, u32[]{:S(2)}, u32[]{:S(2)}) collective-permute-start(bf16[96,1536]{1,0:T(8,128)(2,1)S(1)} %slice.211), channel_id=1, source_target_pairs={{0,4},{4,0},{8,12},{12,8},{1,5},{5,1},{9,13},{13,9},{2,6},{6,2},{1... | collective-permute-start | bytes 884744 | tf_op jit(solution)/shard_map/ppermute | solution.py:294
  129.7 0.7 collective-permute-start.38
  130.4 1.3 collective-permute-start.37
  131.7 1.7 %shard_map.56 = (bf16[384,1024]{1,0:T(8,128)(2,1)}, bf16[2,384,256]{2,1,0:T(8,128)(2,1)S(1)}) custom-call(f32[96,1536]{1,0:T(8,128)S(1)} %slice.213.refs_0_, bf16[96,1536]{1,0:T(8,128)(2,1)S(1)} %collective-permute-done.30.refs_1_, bf16[96,1536]{1,0:T(8,128)(2,1)S(1)} %collective-permute-done.31.refs_2_, ...), custom_call_target="tpu_custom_call", output_to_operand_aliasing={{0}: (9, {})} | custom-call | tf_op jit(solution)/shard_map/pallas_call | solution.py:196
  133.4 7.5 %collective-permute-done.29 = bf16[2,96,1536]{2,1,0:T(8,128)(2,1)S(1)} collective-permute-done((bf16[2,96,1536]{2,1,0:T(8,128)(2,1)S(1)}, bf16[2,96,1536]{2,1,0:T(8,128)(2,1)S(1)}, u32[]{:S(2)}, u32[]{:S(2)}) %collective-permute-start.29) | collective-permute-done | bytes 589856 | tf_op jit(solution)/shard_map/ppermute | solution.py:293
  141.2 0.7 collective-permute-start.35
  141.9 4.8 %collective-permute-done.36.refs_1_ = bf16[96,1536]{1,0:T(8,128)(2,1)S(1)} collective-permute-done((bf16[96,1536]{1,0:T(8,128)(2,1)S(1)}, bf16[96,1536]{1,0:T(8,128)(2,1)S(1)}, u32[]{:S(2)}, u32[]{:S(2)}) %collective-permute-start.36) | collective-permute-done | bytes 294944 | tf_op jit(solution)/shard_map/ppermute | solution.py:294
  146.7 1.3 collective-permute-start.34
  148.1 1.9 %shard_map.57 = (bf16[384,1024]{1,0:T(8,128)(2,1)}, bf16[2,384,256]{2,1,0:T(8,128)(2,1)S(1)}) custom-call(f32[96,1536]{1,0:T(8,128)S(1)} %slice.218.refs_0_, bf16[96,1536]{1,0:T(8,128)(2,1)S(1)} %collective-permute-done.36.refs_1_, bf16[96,1536]{1,0:T(8,128)(2,1)S(1)} %collective-permute-done.37.refs_2_, ...), custom_call_target="tpu_custom_call", output_to_operand_aliasing={{0}: (9, {})} | custom-call | tf_op jit(solution)/shard_map/pallas_call | solution.py:196
  150.0 6.2 %collective-permute-done.34.refs_2_ = bf16[96,1536]{1,0:T(8,128)(2,1)S(1)} collective-permute-done((bf16[96,1536]{1,0:T(8,128)(2,1)S(1)}, bf16[96,1536]{1,0:T(8,128)(2,1)S(1)}, u32[]{:S(2)}, u32[]{:S(2)}) %collective-permute-start.34) | collective-permute-done | bytes 294944 | tf_op jit(solution)/shard_map/ppermute | solution.py:302
  156.2 2.6 %shard_map.58 = (bf16[384,1024]{1,0:T(8,128)(2,1)}, bf16[2,384,256]{2,1,0:T(8,128)(2,1)}) custom-call(f32[96,1536]{1,0:T(8,128)S(1)} %slice.210.refs_0_, bf16[96,1536]{1,0:T(8,128)(2,1)S(1)} %collective-permute-done.28.refs_1_, bf16[96,1536]{1,0:T(8,128)(2,1)S(1)} %collective-permute-done.34.refs_2_, ...), custom_call_target="tpu_custom_call", output_to_operand_aliasing={{0}: (9, {})} | custom-call | tf_op jit(solution)/shard_map/pallas_call | solution.py:196
  (93 shorter events, 4.2 us)
Async XLA Ops:
  0.0 5.8 %copy-start.1 = (bf16[384,2048]{1,0:T(8,128)(2,1)S(1)}, bf16[384,2048]{1,0:T(8,128)(2,1)}, u32[]{:S(2)}) copy-start(bf16[384,2048]{1,0:T(8,128)(2,1)} %param.5) | copy-start | bytes 4718596
  1.9 8.9 %collective-permute-start.2 = (f32[384]{0:T(512)S(1)}, f32[384]{0:T(512)S(1)}, u32[]{:S(2)}, u32[]{:S(2)}) collective-permute-start(f32[384]{0:T(512)S(1)} %multiply_reduce_fusion), channel_id=1, source_target_pairs={{0,3},{1,2},{2,1},{3,0},{4,7},{5,6},{6,5},{7,4},{8,11},{9,10},{10,... | collective-permute-start | bytes 4616 | tf_op jit(solution)/shard_map/ppermute | solution.py:232
  4.3 6.5 %collective-permute-start.1 = (f32[384]{0:T(512)S(1)}, f32[384]{0:T(512)S(1)}, u32[]{:S(2)}, u32[]{:S(2)}) collective-permute-start(f32[384]{0:T(512)S(1)} %multiply_reduce_fusion), channel_id=1, source_target_pairs={{0,1},{1,0},{2,3},{3,2},{4,5},{5,4},{6,7},{7,6},{8,9},{9,8},{10,11... | collective-permute-start | bytes 4616 | tf_op jit(solution)/shard_map/ppermute | solution.py:232
  5.7 3.1 %copy-start = (s32[1,384]{1,0:T(1,128)S(1)}, s32[1,384]{1,0:T(1,128)}, u32[]{:S(2)}) copy-start(s32[1,384]{1,0:T(1,128)} %refs_7_.7) | copy-start | bytes 4612
  5.7 5.0 %collective-permute-start = (f32[2432]{0:T(1024)S(1)}, f32[2432]{0:T(1024)S(1)}, u32[]{:S(2)}, u32[]{:S(2)}) collective-permute-start(f32[2432]{0:T(1024)S(1)} %pad_maximum_fusion.6), channel_id=1, source_target_pairs={{0,2},{1,3},{2,0},{3,1},{4,6},{5,7},{6,4},{7,5},{8,10},{9,11},{10,... | collective-permute-start | bytes 29192 | tf_op jit(solution)/shard_map/ppermute | solution.py:234
  6.8 18.8 %collective-permute-start.6 = (bf16[48,2048]{1,0:T(8,128)(2,1)}, bf16[48,2048]{1,0:T(8,128)(2,1)}, u32[]{:S(2)}, u32[]{:S(2)}) collective-permute-start(bf16[48,2048]{1,0:T(8,128)(2,1)} %get-tuple-element.77), channel_id=1, source_target_pairs={{0,2},{1,3},{2,0},{3,1},{4,6},{5,7},{6,4},{7,5},{8,10},{9,11},{10,... | collective-permute-start | bytes 589832 | tf_op jit(solution)/shard_map/ppermute | solution.py:256
  8.8 9.5 %collective-permute-start.3 = (bf16[48,2048]{1,0:T(8,128)(2,1)}, bf16[48,2048]{1,0:T(8,128)(2,1)}, u32[]{:S(2)}, u32[]{:S(2)}) collective-permute-start(bf16[48,2048]{1,0:T(8,128)(2,1)} %get-tuple-element.152), channel_id=1, source_target_pairs={{0,2},{1,3},{2,0},{3,1},{4,6},{5,7},{6,4},{7,5},{8,10},{9,11},{10,... | collective-permute-start | bytes 589832 | tf_op jit(solution)/shard_map/ppermute | solution.py:256
  10.6 24.3 %copy-start.3 = (bf16[2048,2,256]{2,1,0:T(2,128)(2,1)S(1)}, bf16[2048,2,256]{2,1,0:T(2,128)(2,1)}, u32[]{:S(2)}) copy-start(bf16[2048,2,256]{2,1,0:T(2,128)(2,1)} %param.8) | copy-start | bytes 6291460
  19.5 10.8 %collective-permute-start.5 = (bf16[48,2048]{1,0:T(8,128)(2,1)S(1)}, bf16[48,2048]{1,0:T(8,128)(2,1)S(1)}, u32[]{:S(2)}, u32[]{:S(2)}) collective-permute-start(bf16[48,2048]{1,0:T(8,128)(2,1)S(1)} %get-tuple-element.171), channel_id=1, source_target_pairs={{0,1},{1,4},{2,3},{3,6},{4,0},{5,5},{6,2},{7,7},{8,9},{9,12},{10,1... | collective-permute-start | bytes 589832 | tf_op jit(solution)/shard_map/ppermute | solution.py:268
  21.4 11.8 %collective-permute-start.4 = (bf16[48,2048]{1,0:T(8,128)(2,1)S(1)}, bf16[48,2048]{1,0:T(8,128)(2,1)S(1)}, u32[]{:S(2)}, u32[]{:S(2)}) collective-permute-start(bf16[48,2048]{1,0:T(8,128)(2,1)S(1)} %get-tuple-element.172), channel_id=1, source_target_pairs={{0,8},{1,12},{2,10},{3,14},{4,9},{5,13},{6,11},{7,15},{8,1},{9,5},... | collective-permute-start | bytes 589832 | tf_op jit(solution)/shard_map/ppermute | solution.py:268
  24.1 14.8 %collective-permute-start.11 = (bf16[48,2048]{1,0:T(8,128)(2,1)}, bf16[48,2048]{1,0:T(8,128)(2,1)S(1)}, u32[]{:S(2)}, u32[]{:S(2)}) collective-permute-start(bf16[48,2048]{1,0:T(8,128)(2,1)} %get-tuple-element.84), channel_id=1, source_target_pairs={{0,2},{1,3},{2,0},{3,1},{4,6},{5,7},{6,4},{7,5},{8,10},{9,11},{10,... | collective-permute-start | bytes 589832 | tf_op jit(solution)/shard_map/ppermute | solution.py:256
  26.7 19.9 %collective-permute-start.10 = (bf16[48,2048]{1,0:T(8,128)(2,1)S(1)}, bf16[48,2048]{1,0:T(8,128)(2,1)S(1)}, u32[]{:S(2)}, u32[]{:S(2)}) collective-permute-start(bf16[48,2048]{1,0:T(8,128)(2,1)S(1)} %get-tuple-element.169), channel_id=1, source_target_pairs={{0,1},{1,4},{2,3},{3,6},{4,0},{5,5},{6,2},{7,7},{8,9},{9,12},{10,1... | collective-permute-start | bytes 589832 | tf_op jit(solution)/shard_map/ppermute | solution.py:268
  29.9 18.6 %collective-permute-start.9 = (bf16[48,2048]{1,0:T(8,128)(2,1)S(1)}, bf16[48,2048]{1,0:T(8,128)(2,1)S(1)}, u32[]{:S(2)}, u32[]{:S(2)}) collective-permute-start(bf16[48,2048]{1,0:T(8,128)(2,1)S(1)} %get-tuple-element.170), channel_id=1, source_target_pairs={{0,8},{1,12},{2,10},{3,14},{4,9},{5,13},{6,11},{7,15},{8,1},{9,5},... | collective-permute-start | bytes 589832 | tf_op jit(solution)/shard_map/ppermute | solution.py:268
  33.3 16.9 %collective-permute-start.8 = (bf16[2,48,2048]{2,1,0:T(8,128)(2,1)S(1)}, bf16[2,48,2048]{2,1,0:T(8,128)(2,1)S(1)}, u32[]{:S(2)}, u32[]{:S(2)}) collective-permute-start(bf16[2,48,2048]{2,1,0:T(8,128)(2,1)S(1)} %pad_maximum_fusion), channel_id=1, source_target_pairs={{0,2},{1,3},{2,0},{3,1},{4,6},{5,7},{6,4},{7,5},{8,10},{9,11},{10,... | collective-permute-start | bytes 1179656 | tf_op jit(solution)/shard_map/ppermute | solution.py:273
  34.9 2.2 %copy-start.2 = (bf16[2048,1024]{1,0:T(8,128)(2,1)S(1)}, bf16[2048,1024]{1,0:T(8,128)(2,1)}, u32[]{:S(2)}) copy-start(bf16[2048,1024]{1,0:T(8,128)(2,1)} %param.7) | copy-start | bytes 12582916
  37.5 0.9 copy-start.4
  38.5 12.0 %collective-permute-start.7 = (bf16[48,2048]{1,0:T(8,128)(2,1)S(1)}, bf16[48,2048]{1,0:T(8,128)(2,1)S(1)}, u32[]{:S(2)}, u32[]{:S(2)}) collective-permute-start(bf16[48,2048]{1,0:T(8,128)(2,1)S(1)} %copy-done.4), channel_id=1, source_target_pairs={{0,2},{1,3},{2,0},{3,1},{4,6},{5,7},{6,4},{7,5},{8,10},{9,11},{10,... | collective-permute-start | bytes 589832 | tf_op jit(solution)/shard_map/ppermute | solution.py:256
  39.1 13.9 %collective-permute-start.17 = (bf16[48,2048]{1,0:T(8,128)(2,1)S(1)}, bf16[48,2048]{1,0:T(8,128)(2,1)S(1)}, u32[]{:S(2)}, u32[]{:S(2)}) collective-permute-start(bf16[48,2048]{1,0:T(8,128)(2,1)S(1)} %get-tuple-element.167), channel_id=1, source_target_pairs={{0,1},{1,4},{2,3},{3,6},{4,0},{5,5},{6,2},{7,7},{8,9},{9,12},{10,1... | collective-permute-start | bytes 589832 | tf_op jit(solution)/shard_map/ppermute | solution.py:268
  46.7 7.9 %collective-permute-start.16 = (bf16[48,2048]{1,0:T(8,128)(2,1)S(1)}, bf16[48,2048]{1,0:T(8,128)(2,1)S(1)}, u32[]{:S(2)}, u32[]{:S(2)}) collective-permute-start(bf16[48,2048]{1,0:T(8,128)(2,1)S(1)} %get-tuple-element.168), channel_id=1, source_target_pairs={{0,8},{1,12},{2,10},{3,14},{4,9},{5,13},{6,11},{7,15},{8,1},{9,5},... | collective-permute-start | bytes 589832 | tf_op jit(solution)/shard_map/ppermute | solution.py:268
  48.6 10.3 %collective-permute-start.15 = (bf16[2,48,2048]{2,1,0:T(8,128)(2,1)S(1)}, bf16[2,48,2048]{2,1,0:T(8,128)(2,1)S(1)}, u32[]{:S(2)}, u32[]{:S(2)}) collective-permute-start(bf16[2,48,2048]{2,1,0:T(8,128)(2,1)S(1)} %pad_maximum_fusion.1), channel_id=1, source_target_pairs={{0,2},{1,3},{2,0},{3,1},{4,6},{5,7},{6,4},{7,5},{8,10},{9,11},{10,... | collective-permute-start | bytes 1179656 | tf_op jit(solution)/shard_map/ppermute | solution.py:273
  50.3 12.2 %collective-permute-start.14 = (bf16[2,96,2048]{2,1,0:T(8,128)(2,1)S(1)}, bf16[2,96,2048]{2,1,0:T(8,128)(2,1)S(1)}, u32[]{:S(2)}, u32[]{:S(2)}) collective-permute-start(bf16[2,96,2048]{2,1,0:T(8,128)(2,1)S(1)} %maximum_select_fusion.4), channel_id=1, source_target_pairs={{0,1},{1,0},{2,3},{3,2},{4,5},{5,4},{6,7},{7,6},{8,9},{9,8},{10,11... | collective-permute-start | bytes 2359304 | tf_op jit(solution)/shard_map/ppermute | solution.py:281
  50.6 14.9 %collective-permute-start.13 = (bf16[48,2048]{1,0:T(8,128)(2,1)S(1)}, bf16[48,2048]{1,0:T(8,128)(2,1)S(1)}, u32[]{:S(2)}, u32[]{:S(2)}) collective-permute-start(bf16[48,2048]{1,0:T(8,128)(2,1)S(1)} %get-tuple-element.165), channel_id=1, source_target_pairs={{0,1},{1,4},{2,3},{3,6},{4,0},{5,5},{6,2},{7,7},{8,9},{9,12},{10,1... | collective-permute-start | bytes 589832 | tf_op jit(solution)/shard_map/ppermute | solution.py:268
  53.0 16.5 %collective-permute-start.12 = (bf16[48,2048]{1,0:T(8,128)(2,1)S(1)}, bf16[48,2048]{1,0:T(8,128)(2,1)S(1)}, u32[]{:S(2)}, u32[]{:S(2)}) collective-permute-start(bf16[48,2048]{1,0:T(8,128)(2,1)S(1)} %get-tuple-element.166), channel_id=1, source_target_pairs={{0,8},{1,12},{2,10},{3,14},{4,9},{5,13},{6,11},{7,15},{8,1},{9,5},... | collective-permute-start | bytes 589832 | tf_op jit(solution)/shard_map/ppermute | solution.py:268
  54.6 15.3 %collective-permute-start.21 = (bf16[2,48,2048]{2,1,0:T(8,128)(2,1)S(1)}, bf16[2,48,2048]{2,1,0:T(8,128)(2,1)S(1)}, u32[]{:S(2)}, u32[]{:S(2)}) collective-permute-start(bf16[2,48,2048]{2,1,0:T(8,128)(2,1)S(1)} %pad_maximum_fusion.2), channel_id=1, source_target_pairs={{0,2},{1,3},{2,0},{3,1},{4,6},{5,7},{6,4},{7,5},{8,10},{9,11},{10,... | collective-permute-start | bytes 1179656 | tf_op jit(solution)/shard_map/ppermute | solution.py:273
  59.0 11.1 %collective-permute-start.20 = (bf16[2,96,2048]{2,1,0:T(8,128)(2,1)S(1)}, bf16[2,96,2048]{2,1,0:T(8,128)(2,1)S(1)}, u32[]{:S(2)}, u32[]{:S(2)}) collective-permute-start(bf16[2,96,2048]{2,1,0:T(8,128)(2,1)S(1)} %maximum_select_fusion.5), channel_id=1, source_target_pairs={{0,1},{1,0},{2,3},{3,2},{4,5},{5,4},{6,7},{7,6},{8,9},{9,8},{10,11... | collective-permute-start | bytes 2359304 | tf_op jit(solution)/shard_map/ppermute | solution.py:281
  65.5 39.9 %collective-permute-start.23 = (bf16[96,1536]{1,0:T(8,128)(2,1)S(1)}, bf16[96,1536]{1,0:T(8,128)(2,1)S(1)}, u32[]{:S(2)}, u32[]{:S(2)}) collective-permute-start(bf16[96,1536]{1,0:T(8,128)(2,1)S(1)} %slice.202), channel_id=1, source_target_pairs={{0,4},{4,0},{8,12},{12,8},{1,5},{5,1},{9,13},{13,9},{2,6},{6,2},{1... | collective-permute-start | bytes 884744 | tf_op jit(solution)/shard_map/ppermute | solution.py:294
  65.5 20.0 %collective-permute-start.19 = (bf16[2,96,1536]{2,1,0:T(8,128)(2,1)S(1)}, bf16[2,96,1536]{2,1,0:T(8,128)(2,1)S(1)}, u32[]{:S(2)}, u32[]{:S(2)}) collective-permute-start(bf16[2,96,1536]{2,1,0:T(8,128)(2,1)S(1)} %bitcast.67), channel_id=1, source_target_pairs={{0,4},{12,8},{1,5},{13,9},{2,6},{14,10},{3,7},{15,11},{16,20},{28,... | collective-permute-start | bytes 1769480 | tf_op jit(solution)/shard_map/ppermute | solution.py:293
  69.5 20.5 %collective-permute-start.18 = (bf16[2,48,2048]{2,1,0:T(8,128)(2,1)S(1)}, bf16[2,48,2048]{2,1,0:T(8,128)(2,1)S(1)}, u32[]{:S(2)}, u32[]{:S(2)}) collective-permute-start(bf16[2,48,2048]{2,1,0:T(8,128)(2,1)S(1)} %pad_maximum_fusion.3), channel_id=1, source_target_pairs={{0,2},{1,3},{2,0},{3,1},{4,6},{5,7},{6,4},{7,5},{8,10},{9,11},{10,... | collective-permute-start | bytes 1179656 | tf_op jit(solution)/shard_map/ppermute | solution.py:273
  70.1 21.1 %collective-permute-start.27 = (bf16[2,96,2048]{2,1,0:T(8,128)(2,1)S(1)}, bf16[2,96,2048]{2,1,0:T(8,128)(2,1)S(1)}, u32[]{:S(2)}, u32[]{:S(2)}) collective-permute-start(bf16[2,96,2048]{2,1,0:T(8,128)(2,1)S(1)} %maximum_select_fusion.6), channel_id=1, source_target_pairs={{0,1},{1,0},{2,3},{3,2},{4,5},{5,4},{6,7},{7,6},{8,9},{9,8},{10,11... | collective-permute-start | bytes 2359304 | tf_op jit(solution)/shard_map/ppermute | solution.py:281
  73.3 54.3 %collective-permute-start.30 = (bf16[96,1536]{1,0:T(8,128)(2,1)S(1)}, bf16[96,1536]{1,0:T(8,128)(2,1)S(1)}, u32[]{:S(2)}, u32[]{:S(2)}) collective-permute-start(bf16[96,1536]{1,0:T(8,128)(2,1)S(1)} %slice.204), channel_id=1, source_target_pairs={{0,4},{4,0},{8,12},{12,8},{1,5},{5,1},{9,13},{13,9},{2,6},{6,2},{1... | collective-permute-start | bytes 884744 | tf_op jit(solution)/shard_map/ppermute | solution.py:294
  85.5 18.4 %collective-permute-start.26 = (bf16[2,96,1536]{2,1,0:T(8,128)(2,1)S(1)}, bf16[2,96,1536]{2,1,0:T(8,128)(2,1)S(1)}, u32[]{:S(2)}, u32[]{:S(2)}) collective-permute-start(bf16[2,96,1536]{2,1,0:T(8,128)(2,1)S(1)} %bitcast.71), channel_id=1, source_target_pairs={{0,4},{12,8},{1,5},{13,9},{2,6},{14,10},{3,7},{15,11},{16,20},{28,... | collective-permute-start | bytes 1769480 | tf_op jit(solution)/shard_map/ppermute | solution.py:293
  90.1 19.9 %collective-permute-start.25 = (bf16[96,1536]{1,0:T(8,128)(2,1)S(1)}, bf16[96,1536]{1,0:T(8,128)(2,1)S(1)}, u32[]{:S(2)}, u32[]{:S(2)}) collective-permute-start(bf16[96,1536]{1,0:T(8,128)(2,1)S(1)} %get-tuple-element.163), channel_id=1, source_target_pairs={{4,8},{8,4},{5,9},{9,5},{6,10},{10,6},{7,11},{11,7},{20,24},{24,20... | collective-permute-start | bytes 884744 | tf_op jit(solution)/shard_map/ppermute | solution.py:303
  91.2 28.3 %collective-permute-start.22 = (bf16[2,96,2048]{2,1,0:T(8,128)(2,1)S(1)}, bf16[2,96,2048]{2,1,0:T(8,128)(2,1)S(1)}, u32[]{:S(2)}, u32[]{:S(2)}) collective-permute-start(bf16[2,96,2048]{2,1,0:T(8,128)(2,1)S(1)} %maximum_select_fusion.7), channel_id=1, source_target_pairs={{0,1},{1,0},{2,3},{3,2},{4,5},{5,4},{6,7},{7,6},{8,9},{9,8},{10,11... | collective-permute-start | bytes 2359304 | tf_op jit(solution)/shard_map/ppermute | solution.py:281
  103.9 12.7 %collective-permute-start.24 = (bf16[96,1536]{1,0:T(8,128)(2,1)S(1)}, bf16[96,1536]{1,0:T(8,128)(2,1)S(1)}, u32[]{:S(2)}, u32[]{:S(2)}) collective-permute-start(bf16[96,1536]{1,0:T(8,128)(2,1)S(1)} %get-tuple-element.164), channel_id=1, source_target_pairs={{4,12},{8,0},{5,13},{9,1},{6,14},{10,2},{7,15},{11,3},{20,28},{24,... | collective-permute-start | bytes 884744 | tf_op jit(solution)/shard_map/ppermute | solution.py:302
  105.4 22.0 %collective-permute-start.33 = (bf16[2,96,1536]{2,1,0:T(8,128)(2,1)S(1)}, bf16[2,96,1536]{2,1,0:T(8,128)(2,1)S(1)}, u32[]{:S(2)}, u32[]{:S(2)}) collective-permute-start(bf16[2,96,1536]{2,1,0:T(8,128)(2,1)S(1)} %bitcast.65), channel_id=1, source_target_pairs={{0,4},{12,8},{1,5},{13,9},{2,6},{14,10},{3,7},{15,11},{16,20},{28,... | collective-permute-start | bytes 1769480 | tf_op jit(solution)/shard_map/ppermute | solution.py:293
  110.0 19.6 %collective-permute-start.32 = (bf16[96,1536]{1,0:T(8,128)(2,1)S(1)}, bf16[96,1536]{1,0:T(8,128)(2,1)S(1)}, u32[]{:S(2)}, u32[]{:S(2)}) collective-permute-start(bf16[96,1536]{1,0:T(8,128)(2,1)S(1)} %get-tuple-element.161), channel_id=1, source_target_pairs={{4,8},{8,4},{5,9},{9,5},{6,10},{10,6},{7,11},{11,7},{20,24},{24,20... | collective-permute-start | bytes 884744 | tf_op jit(solution)/shard_map/ppermute | solution.py:303
  116.6 13.1 %collective-permute-start.31 = (bf16[96,1536]{1,0:T(8,128)(2,1)S(1)}, bf16[96,1536]{1,0:T(8,128)(2,1)S(1)}, u32[]{:S(2)}, u32[]{:S(2)}) collective-permute-start(bf16[96,1536]{1,0:T(8,128)(2,1)S(1)} %get-tuple-element.162), channel_id=1, source_target_pairs={{4,12},{8,0},{5,13},{9,1},{6,14},{10,2},{7,15},{11,3},{20,28},{24,... | collective-permute-start | bytes 884744 | tf_op jit(solution)/shard_map/ppermute | solution.py:302
  122.6 18.4 %collective-permute-start.29 = (bf16[2,96,1536]{2,1,0:T(8,128)(2,1)S(1)}, bf16[2,96,1536]{2,1,0:T(8,128)(2,1)S(1)}, u32[]{:S(2)}, u32[]{:S(2)}) collective-permute-start(bf16[2,96,1536]{2,1,0:T(8,128)(2,1)S(1)} %bitcast.69), channel_id=1, source_target_pairs={{0,4},{12,8},{1,5},{13,9},{2,6},{14,10},{3,7},{15,11},{16,20},{28,... | collective-permute-start | bytes 1769480 | tf_op jit(solution)/shard_map/ppermute | solution.py:293
  127.3 19.3 %collective-permute-start.36 = (bf16[96,1536]{1,0:T(8,128)(2,1)S(1)}, bf16[96,1536]{1,0:T(8,128)(2,1)S(1)}, u32[]{:S(2)}, u32[]{:S(2)}) collective-permute-start(bf16[96,1536]{1,0:T(8,128)(2,1)S(1)} %slice.209), channel_id=1, source_target_pairs={{0,4},{4,0},{8,12},{12,8},{1,5},{5,1},{9,13},{13,9},{2,6},{6,2},{1... | collective-permute-start | bytes 884744 | tf_op jit(solution)/shard_map/ppermute | solution.py:294
  127.6 22.4 %collective-permute-start.28 = (bf16[96,1536]{1,0:T(8,128)(2,1)S(1)}, bf16[96,1536]{1,0:T(8,128)(2,1)S(1)}, u32[]{:S(2)}, u32[]{:S(2)}) collective-permute-start(bf16[96,1536]{1,0:T(8,128)(2,1)S(1)} %slice.211), channel_id=1, source_target_pairs={{0,4},{4,0},{8,12},{12,8},{1,5},{5,1},{9,13},{13,9},{2,6},{6,2},{1... | collective-permute-start | bytes 884744 | tf_op jit(solution)/shard_map/ppermute | solution.py:294
  129.7 18.4 %collective-permute-start.38 = (bf16[96,1536]{1,0:T(8,128)(2,1)S(1)}, bf16[96,1536]{1,0:T(8,128)(2,1)S(1)}, u32[]{:S(2)}, u32[]{:S(2)}) collective-permute-start(bf16[96,1536]{1,0:T(8,128)(2,1)S(1)} %get-tuple-element.157), channel_id=1, source_target_pairs={{4,8},{8,4},{5,9},{9,5},{6,10},{10,6},{7,11},{11,7},{20,24},{24,20... | collective-permute-start | bytes 884744 | tf_op jit(solution)/shard_map/ppermute | solution.py:303
  130.4 17.7 %collective-permute-start.37 = (bf16[96,1536]{1,0:T(8,128)(2,1)S(1)}, bf16[96,1536]{1,0:T(8,128)(2,1)S(1)}, u32[]{:S(2)}, u32[]{:S(2)}) collective-permute-start(bf16[96,1536]{1,0:T(8,128)(2,1)S(1)} %get-tuple-element.158), channel_id=1, source_target_pairs={{4,12},{8,0},{5,13},{9,1},{6,14},{10,2},{7,15},{11,3},{20,28},{24,... | collective-permute-start | bytes 884744 | tf_op jit(solution)/shard_map/ppermute | solution.py:302
  141.2 8.8 %collective-permute-start.35 = (bf16[96,1536]{1,0:T(8,128)(2,1)S(1)}, bf16[96,1536]{1,0:T(8,128)(2,1)S(1)}, u32[]{:S(2)}, u32[]{:S(2)}) collective-permute-start(bf16[96,1536]{1,0:T(8,128)(2,1)S(1)} %get-tuple-element.159), channel_id=1, source_target_pairs={{4,8},{8,4},{5,9},{9,5},{6,10},{10,6},{7,11},{11,7},{20,24},{24,20... | collective-permute-start | bytes 884744 | tf_op jit(solution)/shard_map/ppermute | solution.py:303
  146.7 9.5 %collective-permute-start.34 = (bf16[96,1536]{1,0:T(8,128)(2,1)S(1)}, bf16[96,1536]{1,0:T(8,128)(2,1)S(1)}, u32[]{:S(2)}, u32[]{:S(2)}) collective-permute-start(bf16[96,1536]{1,0:T(8,128)(2,1)S(1)} %get-tuple-element.160), channel_id=1, source_target_pairs={{4,12},{8,0},{5,13},{9,1},{6,14},{10,2},{7,15},{11,3},{20,28},{24,... | collective-permute-start | bytes 884744 | tf_op jit(solution)/shard_map/ppermute | solution.py:302

commit v4 on v3

--- a/solution.py
+++ b/solution.py
@@ -12,35 +12,47 @@
 HEAD_DIM = 128
 ORDER = ((3, 2, 1, 0), (3, 2, 0, 1), (0, 1, 3, 2), (0, 1, 2, 3))
 SIZES = (48, 48, 48, 48)
-PIECES = ((0, 0, 96), (1, 0, 96), (2, 0, 96), (3, 0, 96))
+JOINT = (0, 1, 2, 3)
 TURNS = (
     "a0",
-    "a1",
     "n",
     "s0",
+    "z0",
+    "a1",
     "a2",
     "s1",
+    "z1",
     "x0",
+    "s2",
+    "a3",
+    "z2",
+    "x1",
+    "s3",
+    "c0",
+    "z3",
+    "x2",
     "w",
-    "a3",
-    "s2",
-    "x1",
-    "c0",
-    "s3",
-    "x2",
     "c1",
     "m0",
+    "k0",
     "x3",
     "c2",
     "m1",
+    "e0",
+    "k1",
     "f0",
     "c3",
     "m2",
+    "e1",
+    "k2",
     "f1",
     "d0",
     "m3",
+    "k3",
+    "e2",
     "f2",
     "d1",
+    "e3",
     "f3",
     "d2",
     "d3",
@@ -244,69 +256,93 @@
         return arrays
 
     state = [{} for _ in SIZES]
-    sums = [{} for _ in PIECES]
     before = ()
 
     def across(n):
         start, size = starts[n], SIZES[n]
-        piece = hidden_states[start + size : start + 2 * size]
         if n:
-            (piece,) = in_turn(piece)
-            done[0] = piece
+            piece = normed[start + size : start + 2 * size]
+        else:
+            piece = hidden_states[size : 2 * size]
         state[n]["a"] = lax.ppermute(piece, "tensor", swap_x)
 
-    def send(n):
-        start, size = starts[n], SIZES[n]
-        mid = start + size
-        stay, other = in_turn(hidden_states[start:mid], state[n]["a"])
-        stay = (stay.astype(jnp.float32) * scale[start:mid] * gain).astype(jnp.bfloat16)
-        other = other.astype(jnp.float32) * scale[mid : mid + size] * crossed_gain
-        other = other.astype(jnp.bfloat16)
+    def first_send():
+        size = SIZES[0]
+        stay, other = in_turn(hidden_states[:size], state[0]["a"])
         far = jnp.where(here_far, stay, other)
         near = jnp.where(here_far, other, stay)
         done[0] = (far, near)
-        state[n]["z"] = lax.ppermute(far, both, toward(True)), lax.ppermute(near, both, toward(False))
-
-    def cross(n):
-        mine = jnp.stack(in_turn(*state[n]["z"]))
+        received = in_turn(partner[:tokens], *squares)
+        scale = lax.rsqrt((local_sq + sum(received)) / D + 1e-05)[:, None]
+
+        def scaled(piece, stays):
+            row = jnp.where(stays, scale[:size], scale[size : 2 * size])
+            col = jnp.where(stays, gain, crossed_gain)
+            return (piece.astype(jnp.float32) * row * col).astype(jnp.bfloat16)
+
+        state[0]["s"] = scaled(far, here_far), scaled(near, jnp.logical_not(here_far))
+        done[0] = state[0]["s"]
+        return (hidden_states.astype(jnp.float32) * scale * gain).astype(jnp.bfloat16)
+
+    def send(n):
+        start, size = starts[n], SIZES[n]
+        if n:
+            stay, other = in_turn(normed[start : start + size], state[n]["a"])
+            far = jnp.where(here_far, stay, other)
+            near = jnp.where(here_far, other, stay)
+            state[n]["s"] = done[0] = (far, near)
+        state[n]["z", 0] = lax.ppermute(state[n]["s"][0], both, toward(True))
+
+    def send_near(n):
+        (near,) = in_turn(state[n]["s"][1])
+        state[n]["z", 1] = lax.ppermute(near, both, toward(False))
+
+    def cross(n, part):
+        if n in JOINT:
+            mine = jnp.stack(in_turn(state[n]["z", 0], state[n]["z", 1]))
+            theirs = lax.ppermute(mine, "tensor", swap_x)
+            for half in (0, 1):
+                state[n]["x", half] = mine[half], theirs[half]
+        else:
+            (mine,) = in_turn(state[n]["z", part])
+            state[n]["x", part] = mine, lax.ppermute(mine, "tensor", swap_x)
         done[0] = mine
-        state[n]["x"] = mine, lax.ppermute(mine, "tensor", swap_x)
-
-    def share(n):
-        mine, theirs = in_turn(*state[n]["x"])
-        mine = jnp.where(
-            here_far, jnp.concatenate((theirs, mine), 1), jnp.concatenate((mine, theirs), 1)
-        )
+
+    def both_stages(mine, theirs):
+        return jnp.where(even_core, jnp.concatenate((mine, theirs)), jnp.concatenate((theirs, mine)))
+
+    def share(n, part):
+        mine, theirs = in_turn(*state[n]["x", part])
+        mine = jnp.where(here_far, jnp.concatenate((theirs, mine)), jnp.concatenate((mine, theirs)))
         done[0] = mine
-        state[n]["c"] = mine, lax.ppermute(mine, "tensor", swap_core)
+        state[n]["c", part] = mine, lax.ppermute(mine, "tensor", swap_core)
 
     def multiply(n):
-        batch, begin, end = PIECES[n]
-        mine, theirs = in_turn(*(array[:, begin:end] for array in state[batch]["c"]))
-        rows = jnp.where(even_core, jnp.stack((mine, theirs), 1), jnp.stack((theirs, mine), 1))
-        rows = rows.reshape(4 * (end - begin), -1)
+        rows = both_stages(*in_turn(*state[n]["c", 0]))
+        outer = jnp.dot(rows, weight, preferred_element_type=jnp.float32).astype(jnp.bfloat16)
+        done[0] = outer
+        state[n]["p"] = outer, lax.ppermute(outer, "fsdp", outer_in)
+
+    def multiply_near(n):
+        rows = both_stages(*in_turn(*state[n]["c", 1]))
         part = jnp.dot(rows, weight, preferred_element_type=jnp.float32)
-        part = part.reshape(4, end - begin, -1)
-        outer = part[:2].astype(jnp.bfloat16)
-        inner = part[2].astype(jnp.bfloat16)
-        done[0] = (outer, inner)
-        passed = lax.ppermute(outer, "fsdp", outer_in)
-        near_sum = lax.ppermute(inner, "fsdp", [(0, 1), (1, 0), (2, 3), (3, 2)])
-        sums[n]["p"] = part[3], outer, passed, near_sum
+        size = 2 * SIZES[n]
+        inner, state[n]["own"] = part[:size].astype(jnp.bfloat16), part[size:]
+        done[0] = inner
+        state[n]["e"] = lax.ppermute(inner, "fsdp", [(0, 1), (1, 0), (2, 3), (3, 2)])
 
     def forward(n):
-        own, outer, passed, near_sum = sums[n]["p"]
-        passed, outer = in_turn(passed, outer)
+        outer, passed = in_turn(*state[n]["p"])
         passed = passed + outer
         done[0] = passed
-        far_sum = lax.ppermute(passed[0], "fsdp", [(1, 3), (2, 0)])
-        mid_sum = lax.ppermute(passed[1], "fsdp", [(1, 2), (2, 1)])
-        sums[n]["f"] = own, near_sum, far_sum, mid_sum
+        half = 2 * SIZES[n]
+        far_sum = lax.ppermute(passed[:half], "fsdp", [(1, 3), (2, 0)])
+        mid_sum = lax.ppermute(passed[half:], "fsdp", [(1, 2), (2, 1)])
+        state[n]["f"] = far_sum, mid_sum
 
     def finish(n):
-        batch, begin, _ = PIECES[n]
-        added = in_turn(*sums[n]["f"])
-        out, kv = attend_piece(starts[batch] + begin, added, tables, before, tokens, q_cols)
+        added = in_turn(state[n]["own"], state[n]["e"], *state[n]["f"])
+        out, kv = attend_piece(starts[n], added, tables, before, tokens, q_cols)
         done[0] = kv
         return kv, out
 
@@ -318,11 +354,21 @@
         seg[:, None],
         seg[None, :],
     )
-    steps = {"a": across, "s": send, "x": cross, "c": share, "m": multiply, "f": forward}
+    steps = {
+        "a": across,
+        "s": send,
+        "z": send_near,
+        "x": lambda n: cross(n, 0),
+        "y": lambda n: cross(n, 1),
+        "c": lambda n: share(n, 0),
+        "k": lambda n: share(n, 1),
+        "m": multiply,
+        "e": multiply_near,
+        "f": forward,
+    }
     for turn in TURNS:
         if turn == "n":
-            *received, state[0]["a"] = in_turn(partner[:tokens], *squares, state[0]["a"])
-            done[0] = scale = lax.rsqrt((local_sq + sum(received)) / D + 1e-05)[:, None]
+            normed = first_send()
         elif turn == "w":
             w_query, w_keyval = in_turn(w_query, w_keyval)
             weight = jnp.concatenate((w_query, w_keyval.reshape(w_keyval.shape[0], -1)), axis=1)

time: 160 us -> 138 us (0.86)
  waiting for transfers between devices: 58.4 us -> 46.1 us
  starting transfers between devices: 66.3 us -> 62.1 us
  local copies, waits for them, and re-layouts: 5.85 us -> 2.12 us
  other arithmetic: 9.14 us -> 5.7 us
    ppermute x32 -> x36, waiting for transfers between devices: 51 us -> 43 us  [the longest x4 16.7 us: multiply_near(): lax.ppermute(inner, 'fsdp', [(0, 1), (1, 0), (2, 3), (3, 2)])]
    ppermute x4, waiting for transfers between devices: 7.46 us -> 0.01 us  [across(): state[n]['a'] = lax.ppermute(piece, 'tensor', swap_x)]
    ppermute x32 -> x36, starting transfers between devices: 59.1 us -> 54.4 us  [the longest x4 15.1 us: multiply(): state[n]['p'] = (outer, lax.ppermute(outer, 'fsdp', outer_in))]
    ppermute x1, waiting for transfers between devices: 0.01 us -> 3.1 us  [partial_sums(): partner = lax.ppermute(jnp.concatenate((local_sq, gain)), 'tensor', swap_x)]
    select_n x4 -> x3, other arithmetic: 2.6 us -> 0.09 us  [send(): near = jnp.where(here_far, other, stay)]
    unnamed x12, local copies, waits for them, and re-layouts: 3.41 us -> 0.99 us
    ppermute x1, starting transfers between devices: 0.07 us -> 2.06 us  [partial_sums(): partner = lax.ppermute(jnp.concatenate((local_sq, gain)), 'tensor', swap_x)]
    dot_general x4 -> x8, matrix products: 10.5 us -> 11.2 us  [the longest x4 5.61 us: multiply(): jnp.dot(rows, weight, preferred_element_type=jnp.float32)]
  transfers between devices with their start and end apart: 39 -> 43, of which waited for: 9 -> 14; matrix products, arithmetic and copies ran while one was open for 13% -> 12% of each run, Pallas kernels for 3% -> 4%
where the time goes in v4:
time: 138 us; the launch traced here: 136 us
  starting transfers between devices  62.1 us (45%)
  waiting for transfers between devices  46.1 us (33%)
  matrix products  11.2 us (8%)
  Pallas kernels  7.84 us (6%)
  other arithmetic  5.7 us (4%)
  local copies, waits for them, and re-layouts  2.12 us (2%)
    ppermute x4, waiting for transfers between devices, multiply_near(): lax.ppermute(inner, 'fsdp', [(0, 1), (1, 0), (2, 3), (3, 2)])  16.7 us
    ppermute x4, starting transfers between devices, multiply(): state[n]['p'] = (outer, lax.ppermute(outer, 'fsdp', outer_in))  15.1 us
    ppermute x4, waiting for transfers between devices, send_near(): state[n]['z', 1] = lax.ppermute(near, both, toward(False))  11.1 us
    ppermute x4, waiting for transfers between devices, multiply(): state[n]['p'] = (outer, lax.ppermute(outer, 'fsdp', outer_in))  9.68 us
    ppermute x4, starting transfers between devices, send_near(): state[n]['z', 1] = lax.ppermute(near, both, toward(False))  8.77 us
    ppermute x4, starting transfers between devices, multiply_near(): lax.ppermute(inner, 'fsdp', [(0, 1), (1, 0), (2, 3), (3, 2)])  8.03 us
    pallas_call x4, Pallas kernels, attend_piece(): pl.pallas_call(functools.partial(attend_kernel, start), in_specs=[here] *...  7.84 us
    ppermute x4, starting transfers between devices, cross(): theirs = lax.ppermute(mine, 'tensor', swap_x)  7.52 us
  transfers between devices with their start and end apart: 43, of which 14 were waited for; matrix products, arithmetic and copies ran while one was open for 12% of the time, Pallas kernels for 4%

profile of v4, /device:TPU:0, one launch (start us, length us, event | category | flops | bytes accessed | tf_op | source)
XLA Modules:
  0.0 136.0 jit_solution(9607191055924318399)
XLA Ops:
  0.0 1.9 %fusion = f32[384]{0:T(512)S(1)} fusion(bf16[384,2048]{1,0:T(8,128)(2,1)} %param.5), kind=kLoop, calls=%fused_computation.2 | loop fusion | flops 2358912 | bytes 1574400 | tf_op jit(solution)/shard_map/reduce_sum | solution.py:241
  1.9 0.5 collective-permute-start.1
  2.4 2.6 %collective-permute-start.2 = (f32[384]{0:T(512)S(1)}, f32[384]{0:T(512)S(1)}, u32[]{:S(2)}, u32[]{:S(2)}) collective-permute-start(f32[384]{0:T(512)S(1)} %fusion), channel_id=1, source_target_pairs={{0,3},{1,2},{2,1},{3,0},{4,7},{5,6},{6,5},{7,4},{8,11},{9,10},{10,... | collective-permute-start | bytes 4616 | tf_op jit(solution)/shard_map/ppermute | solution.py:244
  5.2 2.1 %collective-permute-start = (f32[2432]{0:T(1024)S(1)}, f32[2432]{0:T(1024)S(1)}, u32[]{:S(2)}, u32[]{:S(2)}) collective-permute-start(f32[2432]{0:T(1024)S(1)} %pad_maximum_fusion.6), channel_id=1, source_target_pairs={{0,2},{1,3},{2,0},{3,1},{4,6},{5,7},{6,4},{7,5},{8,10},{9,11},{10,... | collective-permute-start | bytes 29192 | tf_op jit(solution)/shard_map/ppermute | solution.py:246
  8.1 0.8 fusion.55
  9.2 3.1 %collective-permute-done = f32[2432]{0:T(1024)S(1)} collective-permute-done((f32[2432]{0:T(1024)S(1)}, f32[2432]{0:T(1024)S(1)}, u32[]{:S(2)}, u32[]{:S(2)}) %collective-permute-start) | collective-permute-done | bytes 9760 | tf_op jit(solution)/shard_map/ppermute | solution.py:246
  12.4 0.4 fusion.2
  13.0 0.4 collective-permute-start.5
  13.5 2.8 %collective-permute-start.9 = (bf16[48,2048]{1,0:T(8,128)(2,1)S(1)}, bf16[48,2048]{1,0:T(8,128)(2,1)S(1)}, u32[]{:S(2)}, u32[]{:S(2)}) collective-permute-start(bf16[48,2048]{1,0:T(8,128)(2,1)S(1)} %multiply_convert_fusion.1), channel_id=1, source_target_pairs={{0,8},{1,12},{2,10},{3,14},{4,9},{5,13},{6,11},{7,15},{8,1},{9,5},... | collective-permute-start | bytes 589832 | tf_op jit(solution)/shard_map/ppermute | solution.py:294
  16.5 3.0 %collective-permute-start.10 = (bf16[48,2048]{1,0:T(8,128)(2,1)S(1)}, bf16[48,2048]{1,0:T(8,128)(2,1)S(1)}, u32[]{:S(2)}, u32[]{:S(2)}) collective-permute-start(bf16[48,2048]{1,0:T(8,128)(2,1)S(1)} %multiply_convert_fusion), channel_id=1, source_target_pairs={{0,1},{1,4},{2,3},{3,6},{4,0},{5,5},{6,2},{7,7},{8,9},{9,12},{10,1... | collective-permute-start | bytes 589832 | tf_op jit(solution)/shard_map/ppermute | solution.py:298
  19.5 1.5 %collective-permute-start.8 = (bf16[48,2048]{1,0:T(8,128)(2,1)S(1)}, bf16[48,2048]{1,0:T(8,128)(2,1)S(1)}, u32[]{:S(2)}, u32[]{:S(2)}) collective-permute-start(bf16[48,2048]{1,0:T(8,128)(2,1)S(1)} %get-tuple-element.182), channel_id=1, source_target_pairs={{0,2},{1,3},{2,0},{3,1},{4,6},{5,7},{6,4},{7,5},{8,10},{9,11},{10,... | collective-permute-start | bytes 589832 | tf_op jit(solution)/shard_map/ppermute | solution.py:267
  21.1 0.6 collective-permute-start.4
  21.7 4.5 %collective-permute-done.10 = bf16[48,2048]{1,0:T(8,128)(2,1)S(1)} collective-permute-done((bf16[48,2048]{1,0:T(8,128)(2,1)S(1)}, bf16[48,2048]{1,0:T(8,128)(2,1)S(1)}, u32[]{:S(2)}, u32[]{:S(2)}) %collective-permute-start.10) | collective-permute-done | bytes 196640 | tf_op jit(solution)/shard_map/ppermute | solution.py:298
  26.2 1.9 %collective-permute-start.7 = (bf16[48,2048]{1,0:T(8,128)(2,1)S(1)}, bf16[48,2048]{1,0:T(8,128)(2,1)S(1)}, u32[]{:S(2)}, u32[]{:S(2)}) collective-permute-start(bf16[48,2048]{1,0:T(8,128)(2,1)S(1)} %get-tuple-element.100), channel_id=1, source_target_pairs={{0,1},{1,4},{2,3},{3,6},{4,0},{5,5},{6,2},{7,7},{8,9},{9,12},{10,1... | collective-permute-start | bytes 589832 | tf_op jit(solution)/shard_map/ppermute | solution.py:298
  28.2 1.6 %collective-permute-start.12 = (bf16[2,48,2048]{2,1,0:T(8,128)(2,1)S(1)}, bf16[2,48,2048]{2,1,0:T(8,128)(2,1)S(1)}, u32[]{:S(2)}, u32[]{:S(2)}) collective-permute-start(bf16[2,48,2048]{2,1,0:T(8,128)(2,1)S(1)} %pad_maximum_fusion), channel_id=1, source_target_pairs={{0,2},{1,3},{2,0},{3,1},{4,6},{5,7},{6,4},{7,5},{8,10},{9,11},{10,... | collective-permute-start | bytes 1179656 | tf_op jit(solution)/shard_map/ppermute | solution.py:303
  29.8 1.8 %collective-permute-start.16 = (bf16[48,2048]{1,0:T(8,128)(2,1)S(1)}, bf16[48,2048]{1,0:T(8,128)(2,1)S(1)}, u32[]{:S(2)}, u32[]{:S(2)}) collective-permute-start(bf16[48,2048]{1,0:T(8,128)(2,1)S(1)} %get-tuple-element.208), channel_id=1, source_target_pairs={{0,8},{1,12},{2,10},{3,14},{4,9},{5,13},{6,11},{7,15},{8,1},{9,5},... | collective-permute-start | bytes 589832 | tf_op jit(solution)/shard_map/ppermute | solution.py:294
  31.7 3.6 %collective-permute-done.7 = bf16[48,2048]{1,0:T(8,128)(2,1)S(1)} collective-permute-done((bf16[48,2048]{1,0:T(8,128)(2,1)S(1)}, bf16[48,2048]{1,0:T(8,128)(2,1)S(1)}, u32[]{:S(2)}, u32[]{:S(2)}) %collective-permute-start.7) | collective-permute-done | bytes 196640 | tf_op jit(solution)/shard_map/ppermute | solution.py:298
  35.3 1.9 %collective-permute-start.17 = (bf16[48,2048]{1,0:T(8,128)(2,1)S(1)}, bf16[48,2048]{1,0:T(8,128)(2,1)S(1)}, u32[]{:S(2)}, u32[]{:S(2)}) collective-permute-start(bf16[48,2048]{1,0:T(8,128)(2,1)S(1)} %get-tuple-element.113), channel_id=1, source_target_pairs={{0,1},{1,4},{2,3},{3,6},{4,0},{5,5},{6,2},{7,7},{8,9},{9,12},{10,1... | collective-permute-start | bytes 589832 | tf_op jit(solution)/shard_map/ppermute | solution.py:298
  37.3 2.1 %collective-permute-start.15 = (bf16[2,48,2048]{2,1,0:T(8,128)(2,1)S(1)}, bf16[2,48,2048]{2,1,0:T(8,128)(2,1)S(1)}, u32[]{:S(2)}, u32[]{:S(2)}) collective-permute-start(bf16[2,48,2048]{2,1,0:T(8,128)(2,1)S(1)} %pad_maximum_fusion.1), channel_id=1, source_target_pairs={{0,2},{1,3},{2,0},{3,1},{4,6},{5,7},{6,4},{7,5},{8,10},{9,11},{10,... | collective-permute-start | bytes 1179656 | tf_op jit(solution)/shard_map/ppermute | solution.py:303
  39.5 0.6 collective-permute-start.11
  40.2 0.5 collective-permute-start.14
  40.7 3.0 %collective-permute-done.17 = bf16[48,2048]{1,0:T(8,128)(2,1)S(1)} collective-permute-done((bf16[48,2048]{1,0:T(8,128)(2,1)S(1)}, bf16[48,2048]{1,0:T(8,128)(2,1)S(1)}, u32[]{:S(2)}, u32[]{:S(2)}) %collective-permute-start.17) | collective-permute-done | bytes 196640 | tf_op jit(solution)/shard_map/ppermute | solution.py:298
  43.8 2.6 %collective-permute-start.22 = (bf16[2,48,2048]{2,1,0:T(8,128)(2,1)S(1)}, bf16[2,48,2048]{2,1,0:T(8,128)(2,1)S(1)}, u32[]{:S(2)}, u32[]{:S(2)}) collective-permute-start(bf16[2,48,2048]{2,1,0:T(8,128)(2,1)S(1)} %pad_maximum_fusion.2), channel_id=1, source_target_pairs={{0,2},{1,3},{2,0},{3,1},{4,6},{5,7},{6,4},{7,5},{8,10},{9,11},{10,... | collective-permute-start | bytes 1179656 | tf_op jit(solution)/shard_map/ppermute | solution.py:303
  46.4 0.4 constant_dynamic-update-slice_fusion.1
  46.9 0.5 copy.13
  47.4 1.9 %collective-permute-start.13 = (bf16[48,2048]{1,0:T(8,128)(2,1)S(1)}, bf16[48,2048]{1,0:T(8,128)(2,1)S(1)}, u32[]{:S(2)}, u32[]{:S(2)}) collective-permute-start(bf16[48,2048]{1,0:T(8,128)(2,1)S(1)} %get-tuple-element.112), channel_id=1, source_target_pairs={{0,1},{1,4},{2,3},{3,6},{4,0},{5,5},{6,2},{7,7},{8,9},{9,12},{10,1... | collective-permute-start | bytes 589832 | tf_op jit(solution)/shard_map/ppermute | solution.py:298
  49.6 0.4 collective-permute-start.21
  50.0 1.4 %convolution_convert_fusion.3 = bf16[192,1536]{1,0:T(8,128)(2,1)S(1)} fusion(bf16[2048,1536]{1,0:T(8,128)(2,1)S(1)} %constant_dynamic-update-slice_fusion, bf16[96,2048]{1,0:T(8,128)(2,1)S(1)} %collective-permute-done.14, bf16[96,2048]{1,0:T(8,128)(2,1)S(1)} %maximum_select_fusion.16, pred[]{:T(512)S(6)} %eq.5), kind=kOutput, calls=%fused_computation.8 | convolution fusion | flops 1211793408 | bytes 7667713 | tf_op jit(solution)/shard_map/dot_general | solution.py:322
  51.4 3.7 %collective-permute-start.19 = (bf16[192,1536]{1,0:T(8,128)(2,1)S(1)}, bf16[192,1536]{1,0:T(8,128)(2,1)S(1)}, u32[]{:S(2)}, u32[]{:S(2)}) collective-permute-start(bf16[192,1536]{1,0:T(8,128)(2,1)S(1)} %convolution_convert_fusion.3), channel_id=1, source_target_pairs={{0,4},{12,8},{1,5},{13,9},{2,6},{14,10},{3,7},{15,11},{16,20},{28,... | collective-permute-start | bytes 1769480 | tf_op jit(solution)/shard_map/ppermute | solution.py:324
  55.5 1.1 collective-permute-start.18
  56.6 0.9 collective-permute-done.22
  57.8 1.4 %convolution_convert_fusion.2 = bf16[192,1536]{1,0:T(8,128)(2,1)S(1)} fusion(bf16[2048,1536]{1,0:T(8,128)(2,1)S(1)} %constant_dynamic-update-slice_fusion, bf16[96,2048]{1,0:T(8,128)(2,1)S(1)} %collective-permute-done.21, bf16[96,2048]{1,0:T(8,128)(2,1)S(1)} %maximum_select_fusion.17, pred[]{:T(512)S(6)} %eq.5), kind=kOutput, calls=%fused_computation.7 | convolution fusion | flops 1211793408 | bytes 7667713 | tf_op jit(solution)/shard_map/dot_general | solution.py:322
  59.2 1.4 %collective-permute-start.27 = (bf16[192,1536]{1,0:T(8,128)(2,1)S(1)}, bf16[192,1536]{1,0:T(8,128)(2,1)S(1)}, u32[]{:S(2)}, u32[]{:S(2)}) collective-permute-start(bf16[192,1536]{1,0:T(8,128)(2,1)S(1)} %convolution_convert_fusion.2), channel_id=1, source_target_pairs={{0,4},{12,8},{1,5},{13,9},{2,6},{14,10},{3,7},{15,11},{16,20},{28,... | collective-permute-start | bytes 1769480 | tf_op jit(solution)/shard_map/ppermute | solution.py:324
  60.7 1.4 %fusion.13 = f32[192,1536]{1,0:T(8,128)S(1)} fusion(bf16[2048,1536]{1,0:T(8,128)(2,1)S(1)} %constant_dynamic-update-slice_fusion, bf16[96,2048]{1,0:T(8,128)(2,1)S(1)} %collective-permute-done.20, bf16[96,2048]{1,0:T(8,128)(2,1)S(1)} %maximum_select_fusion.18, pred[]{:T(512)S(6)} %eq.5), kind=kOutput, calls=%fused_computation.22 | convolution fusion | flops 1211498496 | bytes 8257537 | tf_op jit(solution)/shard_map/dot_general | solution.py:328
  62.3 4.5 %collective-permute-done.18 = bf16[2,48,2048]{2,1,0:T(8,128)(2,1)S(1)} collective-permute-done((bf16[2,48,2048]{2,1,0:T(8,128)(2,1)S(1)}, bf16[2,48,2048]{2,1,0:T(8,128)(2,1)S(1)}, u32[]{:S(2)}, u32[]{:S(2)}) %collective-permute-start.18) | collective-permute-done | bytes 393248 | tf_op jit(solution)/shard_map/ppermute | solution.py:303
  66.9 1.7 %collective-permute-done.19 = bf16[192,1536]{1,0:T(8,128)(2,1)S(1)} collective-permute-done((bf16[192,1536]{1,0:T(8,128)(2,1)S(1)}, bf16[192,1536]{1,0:T(8,128)(2,1)S(1)}, u32[]{:S(2)}, u32[]{:S(2)}) %collective-permute-start.19) | collective-permute-done | bytes 589856 | tf_op jit(solution)/shard_map/ppermute | solution.py:324
  69.0 1.3 collective-permute-start.25
  70.3 1.4 %convolution_convert_fusion.1 = bf16[192,1536]{1,0:T(8,128)(2,1)S(1)} fusion(bf16[2048,1536]{1,0:T(8,128)(2,1)S(1)} %constant_dynamic-update-slice_fusion, bf16[96,2048]{1,0:T(8,128)(2,1)S(1)} %collective-permute-done.29, bf16[96,2048]{1,0:T(8,128)(2,1)S(1)} %maximum_select_fusion.19, pred[]{:T(512)S(6)} %eq.5), kind=kOutput, calls=%fused_computation.6 | convolution fusion | flops 1211793408 | bytes 7667713 | tf_op jit(solution)/shard_map/dot_general | solution.py:322
  71.7 5.4 %collective-permute-start.34 = (bf16[192,1536]{1,0:T(8,128)(2,1)S(1)}, bf16[192,1536]{1,0:T(8,128)(2,1)S(1)}, u32[]{:S(2)}, u32[]{:S(2)}) collective-permute-start(bf16[192,1536]{1,0:T(8,128)(2,1)S(1)} %convolution_convert_fusion.1), channel_id=1, source_target_pairs={{0,4},{12,8},{1,5},{13,9},{2,6},{14,10},{3,7},{15,11},{16,20},{28,... | collective-permute-start | bytes 1769480 | tf_op jit(solution)/shard_map/ppermute | solution.py:324
  77.1 1.4 %fusion.24 = f32[192,1536]{1,0:T(8,128)S(1)} fusion(bf16[2048,1536]{1,0:T(8,128)(2,1)S(1)} %constant_dynamic-update-slice_fusion, bf16[96,2048]{1,0:T(8,128)(2,1)S(1)} %collective-permute-done.28, bf16[96,2048]{1,0:T(8,128)(2,1)S(1)} %maximum_select_fusion.20, pred[]{:T(512)S(6)} %eq.5), kind=kOutput, calls=%fused_computation.35 | convolution fusion | flops 1211498496 | bytes 8257537 | tf_op jit(solution)/shard_map/dot_general | solution.py:328
  78.7 2.6 %collective-permute-done.27 = bf16[192,1536]{1,0:T(8,128)(2,1)S(1)} collective-permute-done((bf16[192,1536]{1,0:T(8,128)(2,1)S(1)}, bf16[192,1536]{1,0:T(8,128)(2,1)S(1)}, u32[]{:S(2)}, u32[]{:S(2)}) %collective-permute-start.27) | collective-permute-done | bytes 589856 | tf_op jit(solution)/shard_map/ppermute | solution.py:324
  81.3 0.7 collective-permute-start.26
  82.2 5.4 %collective-permute-done.24.refs_1_ = bf16[96,1536]{1,0:T(8,128)(2,1)S(1)} collective-permute-done((bf16[96,1536]{1,0:T(8,128)(2,1)S(1)}, bf16[96,1536]{1,0:T(8,128)(2,1)S(1)}, u32[]{:S(2)}, u32[]{:S(2)}) %collective-permute-start.24) | collective-permute-done | bytes 294944 | tf_op jit(solution)/shard_map/ppermute | solution.py:332
  87.6 2.5 %collective-permute-start.31 = (bf16[96,1536]{1,0:T(8,128)(2,1)S(1)}, bf16[96,1536]{1,0:T(8,128)(2,1)S(1)}, u32[]{:S(2)}, u32[]{:S(2)}) collective-permute-start(bf16[96,1536]{1,0:T(8,128)(2,1)S(1)} %slice.226), channel_id=1, source_target_pairs={{0,4},{4,0},{8,12},{12,8},{1,5},{5,1},{9,13},{13,9},{2,6},{6,2},{1... | collective-permute-start | bytes 884744 | tf_op jit(solution)/shard_map/ppermute | solution.py:332
  90.1 1.3 collective-permute-start.32
  91.4 1.6 %shard_map.55 = (bf16[384,1024]{1,0:T(8,128)(2,1)}, bf16[2,384,256]{2,1,0:T(8,128)(2,1)S(1)}) custom-call(f32[96,1536]{1,0:T(8,128)S(1)} %slice.187.refs_0_, bf16[96,1536]{1,0:T(8,128)(2,1)S(1)} %collective-permute-done.24.refs_1_, bf16[96,1536]{1,0:T(8,128)(2,1)S(1)} %collective-permute-done.25.refs_2_, ...), custom_call_target="tpu_custom_call" | custom-call | tf_op jit(solution)/shard_map/pallas_call | solution.py:208
  93.0 0.7 collective-permute-start.33
  93.7 1.4 %convolution_convert_fusion = bf16[192,1536]{1,0:T(8,128)(2,1)S(1)} fusion(bf16[2048,1536]{1,0:T(8,128)(2,1)S(1)} %constant_dynamic-update-slice_fusion, bf16[96,2048]{1,0:T(8,128)(2,1)S(1)} %collective-permute-done.23, bf16[96,2048]{1,0:T(8,128)(2,1)S(1)} %maximum_select_fusion.21, pred[]{:T(512)S(6)} %eq.5), kind=kOutput, calls=%fused_computation.5 | convolution fusion | flops 1211793408 | bytes 7667713 | tf_op jit(solution)/shard_map/dot_general | solution.py:322
  95.5 1.4 %fusion.35 = f32[192,1536]{1,0:T(8,128)S(1)} fusion(bf16[2048,1536]{1,0:T(8,128)(2,1)S(1)} %constant_dynamic-update-slice_fusion, bf16[96,2048]{1,0:T(8,128)(2,1)S(1)} %collective-permute-done.35, bf16[96,2048]{1,0:T(8,128)(2,1)S(1)} %maximum_select_fusion.22, pred[]{:T(512)S(6)} %eq.5), kind=kOutput, calls=%fused_computation.48 | convolution fusion | flops 1211498496 | bytes 8257537 | tf_op jit(solution)/shard_map/dot_general | solution.py:328
  97.0 3.3 %collective-permute-done.34 = bf16[192,1536]{1,0:T(8,128)(2,1)S(1)} collective-permute-done((bf16[192,1536]{1,0:T(8,128)(2,1)S(1)}, bf16[192,1536]{1,0:T(8,128)(2,1)S(1)}, u32[]{:S(2)}, u32[]{:S(2)}) %collective-permute-start.34) | collective-permute-done | bytes 589856 | tf_op jit(solution)/shard_map/ppermute | solution.py:324
  100.2 4.6 %collective-permute-start.37 = (bf16[192,1536]{1,0:T(8,128)(2,1)S(1)}, bf16[192,1536]{1,0:T(8,128)(2,1)S(1)}, u32[]{:S(2)}, u32[]{:S(2)}) collective-permute-start(bf16[192,1536]{1,0:T(8,128)(2,1)S(1)} %convolution_convert_fusion), channel_id=1, source_target_pairs={{0,4},{12,8},{1,5},{13,9},{2,6},{14,10},{3,7},{15,11},{16,20},{28,... | collective-permute-start | bytes 1769480 | tf_op jit(solution)/shard_map/ppermute | solution.py:324
  105.2 1.4 %collective-permute-done.31.refs_1_ = bf16[96,1536]{1,0:T(8,128)(2,1)S(1)} collective-permute-done((bf16[96,1536]{1,0:T(8,128)(2,1)S(1)}, bf16[96,1536]{1,0:T(8,128)(2,1)S(1)}, u32[]{:S(2)}, u32[]{:S(2)}) %collective-permute-start.31) | collective-permute-done | bytes 294944 | tf_op jit(solution)/shard_map/ppermute | solution.py:332
  106.6 1.3 collective-permute-start.41
  107.9 0.7 collective-permute-start.42
  108.5 1.8 %shard_map.56 = (bf16[384,1024]{1,0:T(8,128)(2,1)}, bf16[2,384,256]{2,1,0:T(8,128)(2,1)S(1)}) custom-call(f32[96,1536]{1,0:T(8,128)S(1)} %slice.192.refs_0_, bf16[96,1536]{1,0:T(8,128)(2,1)S(1)} %collective-permute-done.31.refs_1_, bf16[96,1536]{1,0:T(8,128)(2,1)S(1)} %collective-permute-done.32.refs_2_, ...), custom_call_target="tpu_custom_call", output_to_operand_aliasing={{0}: (9, {})} | custom-call | tf_op jit(solution)/shard_map/pallas_call | solution.py:208
  110.3 1.4 %fusion.41 = f32[192,1536]{1,0:T(8,128)S(1)} fusion(bf16[2048,1536]{1,0:T(8,128)(2,1)S(1)} %constant_dynamic-update-slice_fusion, bf16[96,2048]{1,0:T(8,128)(2,1)S(1)} %collective-permute-done.30, bf16[96,2048]{1,0:T(8,128)(2,1)S(1)} %maximum_select_fusion.23, pred[]{:T(512)S(6)} %eq.5), kind=kOutput, calls=%fused_computation.55 | convolution fusion | flops 1211498496 | bytes 8257537 | tf_op jit(solution)/shard_map/dot_general | solution.py:328
  111.8 5.4 %collective-permute-start.36 = (bf16[96,1536]{1,0:T(8,128)(2,1)S(1)}, bf16[96,1536]{1,0:T(8,128)(2,1)S(1)}, u32[]{:S(2)}, u32[]{:S(2)}) collective-permute-start(bf16[96,1536]{1,0:T(8,128)(2,1)S(1)} %slice.224), channel_id=1, source_target_pairs={{0,4},{4,0},{8,12},{12,8},{1,5},{5,1},{9,13},{13,9},{2,6},{6,2},{1... | collective-permute-start | bytes 884744 | tf_op jit(solution)/shard_map/ppermute | solution.py:332
  117.2 2.0 %collective-permute-done.37 = bf16[192,1536]{1,0:T(8,128)(2,1)S(1)} collective-permute-done((bf16[192,1536]{1,0:T(8,128)(2,1)S(1)}, bf16[192,1536]{1,0:T(8,128)(2,1)S(1)}, u32[]{:S(2)}, u32[]{:S(2)}) %collective-permute-start.37) | collective-permute-done | bytes 589856 | tf_op jit(solution)/shard_map/ppermute | solution.py:324
  119.4 1.3 collective-permute-start.38
  120.8 0.7 collective-permute-start.39
  121.5 4.0 %collective-permute-done.40.refs_1_ = bf16[96,1536]{1,0:T(8,128)(2,1)S(1)} collective-permute-done((bf16[96,1536]{1,0:T(8,128)(2,1)S(1)}, bf16[96,1536]{1,0:T(8,128)(2,1)S(1)}, u32[]{:S(2)}, u32[]{:S(2)}) %collective-permute-start.40) | collective-permute-done | bytes 294944 | tf_op jit(solution)/shard_map/ppermute | solution.py:332
  125.5 1.8 %shard_map.57 = (bf16[384,1024]{1,0:T(8,128)(2,1)}, bf16[2,384,256]{2,1,0:T(8,128)(2,1)S(1)}) custom-call(f32[96,1536]{1,0:T(8,128)S(1)} %slice.200.refs_0_, bf16[96,1536]{1,0:T(8,128)(2,1)S(1)} %collective-permute-done.40.refs_1_, bf16[96,1536]{1,0:T(8,128)(2,1)S(1)} %collective-permute-done.41.refs_2_, ...), custom_call_target="tpu_custom_call", output_to_operand_aliasing={{0}: (9, {})} | custom-call | tf_op jit(solution)/shard_map/pallas_call | solution.py:208
  127.4 5.8 %collective-permute-done.36.refs_1_ = bf16[96,1536]{1,0:T(8,128)(2,1)S(1)} collective-permute-done((bf16[96,1536]{1,0:T(8,128)(2,1)S(1)}, bf16[96,1536]{1,0:T(8,128)(2,1)S(1)}, u32[]{:S(2)}, u32[]{:S(2)}) %collective-permute-start.36) | collective-permute-done | bytes 294944 | tf_op jit(solution)/shard_map/ppermute | solution.py:332
  133.2 2.6 %shard_map.58 = (bf16[384,1024]{1,0:T(8,128)(2,1)}, bf16[2,384,256]{2,1,0:T(8,128)(2,1)}) custom-call(f32[96,1536]{1,0:T(8,128)S(1)} %slice.196.refs_0_, bf16[96,1536]{1,0:T(8,128)(2,1)S(1)} %collective-permute-done.36.refs_1_, bf16[96,1536]{1,0:T(8,128)(2,1)S(1)} %collective-permute-done.38.refs_2_, ...), custom_call_target="tpu_custom_call", output_to_operand_aliasing={{0}: (9, {})} | custom-call | tf_op jit(solution)/shard_map/pallas_call | solution.py:208
  (106 shorter events, 5.0 us)
Async XLA Ops:
  0.0 5.0 %copy-start.1 = (bf16[384,2048]{1,0:T(8,128)(2,1)S(1)}, bf16[384,2048]{1,0:T(8,128)(2,1)}, u32[]{:S(2)}) copy-start(bf16[384,2048]{1,0:T(8,128)(2,1)} %param.5) | copy-start | bytes 4718596
  0.0 5.2 %copy-start.4 = (bf16[2048]{0:T(1024)(128)(2,1)S(1)}, bf16[2048]{0:T(1024)(128)(2,1)}, u32[]{:S(2)}) copy-start(bf16[2048]{0:T(1024)(128)(2,1)} %param.6) | copy-start | bytes 12292
  0.0 7.3 %copy-start = (s32[1,384]{1,0:T(1,128)S(1)}, s32[1,384]{1,0:T(1,128)}, u32[]{:S(2)}) copy-start(s32[1,384]{1,0:T(1,128)} %refs_7_.7) | copy-start | bytes 4612
  1.9 10.4 %collective-permute-start.1 = (f32[384]{0:T(512)S(1)}, f32[384]{0:T(512)S(1)}, u32[]{:S(2)}, u32[]{:S(2)}) collective-permute-start(f32[384]{0:T(512)S(1)} %fusion), channel_id=1, source_target_pairs={{0,1},{1,0},{2,3},{3,2},{4,5},{5,4},{6,7},{7,6},{8,9},{9,8},{10,11... | collective-permute-start | bytes 4616 | tf_op jit(solution)/shard_map/ppermute | solution.py:244
  2.4 9.9 %collective-permute-start.2 = (f32[384]{0:T(512)S(1)}, f32[384]{0:T(512)S(1)}, u32[]{:S(2)}, u32[]{:S(2)}) collective-permute-start(f32[384]{0:T(512)S(1)} %fusion), channel_id=1, source_target_pairs={{0,3},{1,2},{2,1},{3,0},{4,7},{5,6},{6,5},{7,4},{8,11},{9,10},{10,... | collective-permute-start | bytes 4616 | tf_op jit(solution)/shard_map/ppermute | solution.py:244
  5.1 7.2 %collective-permute-start.3 = (bf16[48,2048]{1,0:T(8,128)(2,1)S(1)}, bf16[48,2048]{1,0:T(8,128)(2,1)S(1)}, u32[]{:S(2)}, u32[]{:S(2)}) collective-permute-start(bf16[48,2048]{1,0:T(8,128)(2,1)S(1)} %get-tuple-element.187), channel_id=1, source_target_pairs={{0,2},{1,3},{2,0},{3,1},{4,6},{5,7},{6,4},{7,5},{8,10},{9,11},{10,... | collective-permute-start | bytes 589832 | tf_op jit(solution)/shard_map/ppermute | solution.py:267
  5.2 7.1 %collective-permute-start = (f32[2432]{0:T(1024)S(1)}, f32[2432]{0:T(1024)S(1)}, u32[]{:S(2)}, u32[]{:S(2)}) collective-permute-start(f32[2432]{0:T(1024)S(1)} %pad_maximum_fusion.6), channel_id=1, source_target_pairs={{0,2},{1,3},{2,0},{3,1},{4,6},{5,7},{6,4},{7,5},{8,10},{9,11},{10,... | collective-permute-start | bytes 29192 | tf_op jit(solution)/shard_map/ppermute | solution.py:246
  13.0 8.6 %collective-permute-start.5 = (bf16[48,2048]{1,0:T(8,128)(2,1)S(1)}, bf16[48,2048]{1,0:T(8,128)(2,1)S(1)}, u32[]{:S(2)}, u32[]{:S(2)}) collective-permute-start(bf16[48,2048]{1,0:T(8,128)(2,1)S(1)} %get-tuple-element.184), channel_id=1, source_target_pairs={{0,2},{1,3},{2,0},{3,1},{4,6},{5,7},{6,4},{7,5},{8,10},{9,11},{10,... | collective-permute-start | bytes 589832 | tf_op jit(solution)/shard_map/ppermute | solution.py:267
  13.5 14.6 %collective-permute-start.9 = (bf16[48,2048]{1,0:T(8,128)(2,1)S(1)}, bf16[48,2048]{1,0:T(8,128)(2,1)S(1)}, u32[]{:S(2)}, u32[]{:S(2)}) collective-permute-start(bf16[48,2048]{1,0:T(8,128)(2,1)S(1)} %multiply_convert_fusion.1), channel_id=1, source_target_pairs={{0,8},{1,12},{2,10},{3,14},{4,9},{5,13},{6,11},{7,15},{8,1},{9,5},... | collective-permute-start | bytes 589832 | tf_op jit(solution)/shard_map/ppermute | solution.py:294
  16.5 9.7 %collective-permute-start.10 = (bf16[48,2048]{1,0:T(8,128)(2,1)S(1)}, bf16[48,2048]{1,0:T(8,128)(2,1)S(1)}, u32[]{:S(2)}, u32[]{:S(2)}) collective-permute-start(bf16[48,2048]{1,0:T(8,128)(2,1)S(1)} %multiply_convert_fusion), channel_id=1, source_target_pairs={{0,1},{1,4},{2,3},{3,6},{4,0},{5,5},{6,2},{7,7},{8,9},{9,12},{10,1... | collective-permute-start | bytes 589832 | tf_op jit(solution)/shard_map/ppermute | solution.py:298
  19.5 10.3 %collective-permute-start.8 = (bf16[48,2048]{1,0:T(8,128)(2,1)S(1)}, bf16[48,2048]{1,0:T(8,128)(2,1)S(1)}, u32[]{:S(2)}, u32[]{:S(2)}) collective-permute-start(bf16[48,2048]{1,0:T(8,128)(2,1)S(1)} %get-tuple-element.182), channel_id=1, source_target_pairs={{0,2},{1,3},{2,0},{3,1},{4,6},{5,7},{6,4},{7,5},{8,10},{9,11},{10,... | collective-permute-start | bytes 589832 | tf_op jit(solution)/shard_map/ppermute | solution.py:267
  21.1 18.4 %collective-permute-start.4 = (bf16[48,2048]{1,0:T(8,128)(2,1)S(1)}, bf16[48,2048]{1,0:T(8,128)(2,1)S(1)}, u32[]{:S(2)}, u32[]{:S(2)}) collective-permute-start(bf16[48,2048]{1,0:T(8,128)(2,1)S(1)} %get-tuple-element.181), channel_id=1, source_target_pairs={{0,2},{1,3},{2,0},{3,1},{4,6},{5,7},{6,4},{7,5},{8,10},{9,11},{10,... | collective-permute-start | bytes 589832 | tf_op jit(solution)/shard_map/ppermute | solution.py:267
  21.6 15.6 %collective-permute-start.6 = (bf16[48,2048]{1,0:T(8,128)(2,1)S(1)}, bf16[48,2048]{1,0:T(8,128)(2,1)S(1)}, u32[]{:S(2)}, u32[]{:S(2)}) collective-permute-start(bf16[48,2048]{1,0:T(8,128)(2,1)S(1)} %get-tuple-element.210), channel_id=1, source_target_pairs={{0,8},{1,12},{2,10},{3,14},{4,9},{5,13},{6,11},{7,15},{8,1},{9,5},... | collective-permute-start | bytes 589832 | tf_op jit(solution)/shard_map/ppermute | solution.py:294
  26.2 9.1 %collective-permute-start.7 = (bf16[48,2048]{1,0:T(8,128)(2,1)S(1)}, bf16[48,2048]{1,0:T(8,128)(2,1)S(1)}, u32[]{:S(2)}, u32[]{:S(2)}) collective-permute-start(bf16[48,2048]{1,0:T(8,128)(2,1)S(1)} %get-tuple-element.100), channel_id=1, source_target_pairs={{0,1},{1,4},{2,3},{3,6},{4,0},{5,5},{6,2},{7,7},{8,9},{9,12},{10,1... | collective-permute-start | bytes 589832 | tf_op jit(solution)/shard_map/ppermute | solution.py:298
  28.2 11.9 %collective-permute-start.12 = (bf16[2,48,2048]{2,1,0:T(8,128)(2,1)S(1)}, bf16[2,48,2048]{2,1,0:T(8,128)(2,1)S(1)}, u32[]{:S(2)}, u32[]{:S(2)}) collective-permute-start(bf16[2,48,2048]{2,1,0:T(8,128)(2,1)S(1)} %pad_maximum_fusion), channel_id=1, source_target_pairs={{0,2},{1,3},{2,0},{3,1},{4,6},{5,7},{6,4},{7,5},{8,10},{9,11},{10,... | collective-permute-start | bytes 1179656 | tf_op jit(solution)/shard_map/ppermute | solution.py:303
  29.8 16.6 %copy-start.2 = (bf16[2048,1024]{1,0:T(8,128)(2,1)S(1)}, bf16[2048,1024]{1,0:T(8,128)(2,1)}, u32[]{:S(2)}) copy-start(bf16[2048,1024]{1,0:T(8,128)(2,1)} %param.7) | copy-start | bytes 12582916
  29.8 13.9 %collective-permute-start.16 = (bf16[48,2048]{1,0:T(8,128)(2,1)S(1)}, bf16[48,2048]{1,0:T(8,128)(2,1)S(1)}, u32[]{:S(2)}, u32[]{:S(2)}) collective-permute-start(bf16[48,2048]{1,0:T(8,128)(2,1)S(1)} %get-tuple-element.208), channel_id=1, source_target_pairs={{0,8},{1,12},{2,10},{3,14},{4,9},{5,13},{6,11},{7,15},{8,1},{9,5},... | collective-permute-start | bytes 589832 | tf_op jit(solution)/shard_map/ppermute | solution.py:294
  35.3 8.4 %collective-permute-start.17 = (bf16[48,2048]{1,0:T(8,128)(2,1)S(1)}, bf16[48,2048]{1,0:T(8,128)(2,1)S(1)}, u32[]{:S(2)}, u32[]{:S(2)}) collective-permute-start(bf16[48,2048]{1,0:T(8,128)(2,1)S(1)} %get-tuple-element.113), channel_id=1, source_target_pairs={{0,1},{1,4},{2,3},{3,6},{4,0},{5,5},{6,2},{7,7},{8,9},{9,12},{10,1... | collective-permute-start | bytes 589832 | tf_op jit(solution)/shard_map/ppermute | solution.py:298
  37.3 12.2 %collective-permute-start.15 = (bf16[2,48,2048]{2,1,0:T(8,128)(2,1)S(1)}, bf16[2,48,2048]{2,1,0:T(8,128)(2,1)S(1)}, u32[]{:S(2)}, u32[]{:S(2)}) collective-permute-start(bf16[2,48,2048]{2,1,0:T(8,128)(2,1)S(1)} %pad_maximum_fusion.1), channel_id=1, source_target_pairs={{0,2},{1,3},{2,0},{3,1},{4,6},{5,7},{6,4},{7,5},{8,10},{9,11},{10,... | collective-permute-start | bytes 1179656 | tf_op jit(solution)/shard_map/ppermute | solution.py:303
  39.5 15.7 %collective-permute-start.11 = (bf16[48,2048]{1,0:T(8,128)(2,1)S(1)}, bf16[48,2048]{1,0:T(8,128)(2,1)S(1)}, u32[]{:S(2)}, u32[]{:S(2)}) collective-permute-start(bf16[48,2048]{1,0:T(8,128)(2,1)S(1)} %get-tuple-element.206), channel_id=1, source_target_pairs={{0,8},{1,12},{2,10},{3,14},{4,9},{5,13},{6,11},{7,15},{8,1},{9,5},... | collective-permute-start | bytes 589832 | tf_op jit(solution)/shard_map/ppermute | solution.py:294
  40.2 9.8 %collective-permute-start.14 = (bf16[96,2048]{1,0:T(8,128)(2,1)S(1)}, bf16[96,2048]{1,0:T(8,128)(2,1)S(1)}, u32[]{:S(2)}, u32[]{:S(2)}) collective-permute-start(bf16[96,2048]{1,0:T(8,128)(2,1)S(1)} %maximum_select_fusion.16), channel_id=1, source_target_pairs={{0,1},{1,0},{2,3},{3,2},{4,5},{5,4},{6,7},{7,6},{8,9},{9,8},{10,11... | collective-permute-start | bytes 1179656 | tf_op jit(solution)/shard_map/ppermute | solution.py:318
  43.8 3.1 %copy-start.3 = (bf16[2048,2,256]{2,1,0:T(2,128)(2,1)S(1)}, bf16[2048,2,256]{2,1,0:T(2,128)(2,1)}, u32[]{:S(2)}) copy-start(bf16[2048,2,256]{2,1,0:T(2,128)(2,1)} %param.8) | copy-start | bytes 6291460
  43.8 13.7 %collective-permute-start.22 = (bf16[2,48,2048]{2,1,0:T(8,128)(2,1)S(1)}, bf16[2,48,2048]{2,1,0:T(8,128)(2,1)S(1)}, u32[]{:S(2)}, u32[]{:S(2)}) collective-permute-start(bf16[2,48,2048]{2,1,0:T(8,128)(2,1)S(1)} %pad_maximum_fusion.2), channel_id=1, source_target_pairs={{0,2},{1,3},{2,0},{3,1},{4,6},{5,7},{6,4},{7,5},{8,10},{9,11},{10,... | collective-permute-start | bytes 1179656 | tf_op jit(solution)/shard_map/ppermute | solution.py:303
  47.4 8.0 %collective-permute-start.13 = (bf16[48,2048]{1,0:T(8,128)(2,1)S(1)}, bf16[48,2048]{1,0:T(8,128)(2,1)S(1)}, u32[]{:S(2)}, u32[]{:S(2)}) collective-permute-start(bf16[48,2048]{1,0:T(8,128)(2,1)S(1)} %get-tuple-element.112), channel_id=1, source_target_pairs={{0,1},{1,4},{2,3},{3,6},{4,0},{5,5},{6,2},{7,7},{8,9},{9,12},{10,1... | collective-permute-start | bytes 589832 | tf_op jit(solution)/shard_map/ppermute | solution.py:298
  49.6 8.2 %collective-permute-start.21 = (bf16[96,2048]{1,0:T(8,128)(2,1)S(1)}, bf16[96,2048]{1,0:T(8,128)(2,1)S(1)}, u32[]{:S(2)}, u32[]{:S(2)}) collective-permute-start(bf16[96,2048]{1,0:T(8,128)(2,1)S(1)} %maximum_select_fusion.17), channel_id=1, source_target_pairs={{0,1},{1,0},{2,3},{3,2},{4,5},{5,4},{6,7},{7,6},{8,9},{9,8},{10,11... | collective-permute-start | bytes 1179656 | tf_op jit(solution)/shard_map/ppermute | solution.py:318
  51.4 17.3 %collective-permute-start.19 = (bf16[192,1536]{1,0:T(8,128)(2,1)S(1)}, bf16[192,1536]{1,0:T(8,128)(2,1)S(1)}, u32[]{:S(2)}, u32[]{:S(2)}) collective-permute-start(bf16[192,1536]{1,0:T(8,128)(2,1)S(1)} %convolution_convert_fusion.3), channel_id=1, source_target_pairs={{0,4},{12,8},{1,5},{13,9},{2,6},{14,10},{3,7},{15,11},{16,20},{28,... | collective-permute-start | bytes 1769480 | tf_op jit(solution)/shard_map/ppermute | solution.py:324
  55.2 5.5 %collective-permute-start.20 = (bf16[96,2048]{1,0:T(8,128)(2,1)S(1)}, bf16[96,2048]{1,0:T(8,128)(2,1)S(1)}, u32[]{:S(2)}, u32[]{:S(2)}) collective-permute-start(bf16[96,2048]{1,0:T(8,128)(2,1)S(1)} %maximum_select_fusion.18), channel_id=1, source_target_pairs={{0,1},{1,0},{2,3},{3,2},{4,5},{5,4},{6,7},{7,6},{8,9},{9,8},{10,11... | collective-permute-start | bytes 1179656 | tf_op jit(solution)/shard_map/ppermute | solution.py:318
  55.5 11.4 %collective-permute-start.18 = (bf16[2,48,2048]{2,1,0:T(8,128)(2,1)S(1)}, bf16[2,48,2048]{2,1,0:T(8,128)(2,1)S(1)}, u32[]{:S(2)}, u32[]{:S(2)}) collective-permute-start(bf16[2,48,2048]{2,1,0:T(8,128)(2,1)S(1)} %pad_maximum_fusion.3), channel_id=1, source_target_pairs={{0,2},{1,3},{2,0},{3,1},{4,6},{5,7},{6,4},{7,5},{8,10},{9,11},{10,... | collective-permute-start | bytes 1179656 | tf_op jit(solution)/shard_map/ppermute | solution.py:303
  57.6 11.4 %collective-permute-start.29 = (bf16[96,2048]{1,0:T(8,128)(2,1)S(1)}, bf16[96,2048]{1,0:T(8,128)(2,1)S(1)}, u32[]{:S(2)}, u32[]{:S(2)}) collective-permute-start(bf16[96,2048]{1,0:T(8,128)(2,1)S(1)} %maximum_select_fusion.19), channel_id=1, source_target_pairs={{0,1},{1,0},{2,3},{3,2},{4,5},{5,4},{6,7},{7,6},{8,9},{9,8},{10,11... | collective-permute-start | bytes 1179656 | tf_op jit(solution)/shard_map/ppermute | solution.py:318
  59.2 22.0 %collective-permute-start.27 = (bf16[192,1536]{1,0:T(8,128)(2,1)S(1)}, bf16[192,1536]{1,0:T(8,128)(2,1)S(1)}, u32[]{:S(2)}, u32[]{:S(2)}) collective-permute-start(bf16[192,1536]{1,0:T(8,128)(2,1)S(1)} %convolution_convert_fusion.2), channel_id=1, source_target_pairs={{0,4},{12,8},{1,5},{13,9},{2,6},{14,10},{3,7},{15,11},{16,20},{28,... | collective-permute-start | bytes 1769480 | tf_op jit(solution)/shard_map/ppermute | solution.py:324
  62.2 25.4 %collective-permute-start.24 = (bf16[96,1536]{1,0:T(8,128)(2,1)S(1)}, bf16[96,1536]{1,0:T(8,128)(2,1)S(1)}, u32[]{:S(2)}, u32[]{:S(2)}) collective-permute-start(bf16[96,1536]{1,0:T(8,128)(2,1)S(1)} %slice.227), channel_id=1, source_target_pairs={{0,4},{4,0},{8,12},{12,8},{1,5},{5,1},{9,13},{13,9},{2,6},{6,2},{1... | collective-permute-start | bytes 884744 | tf_op jit(solution)/shard_map/ppermute | solution.py:332
  66.9 4.8 %collective-permute-start.28 = (bf16[96,2048]{1,0:T(8,128)(2,1)S(1)}, bf16[96,2048]{1,0:T(8,128)(2,1)S(1)}, u32[]{:S(2)}, u32[]{:S(2)}) collective-permute-start(bf16[96,2048]{1,0:T(8,128)(2,1)S(1)} %maximum_select_fusion.20), channel_id=1, source_target_pairs={{0,1},{1,0},{2,3},{3,2},{4,5},{5,4},{6,7},{7,6},{8,9},{9,8},{10,11... | collective-permute-start | bytes 1179656 | tf_op jit(solution)/shard_map/ppermute | solution.py:318
  68.9 24.1 %collective-permute-start.23 = (bf16[96,2048]{1,0:T(8,128)(2,1)S(1)}, bf16[96,2048]{1,0:T(8,128)(2,1)S(1)}, u32[]{:S(2)}, u32[]{:S(2)}) collective-permute-start(bf16[96,2048]{1,0:T(8,128)(2,1)S(1)} %maximum_select_fusion.21), channel_id=1, source_target_pairs={{0,1},{1,0},{2,3},{3,2},{4,5},{5,4},{6,7},{7,6},{8,9},{9,8},{10,11... | collective-permute-start | bytes 1179656 | tf_op jit(solution)/shard_map/ppermute | solution.py:318
  69.0 18.6 %collective-permute-start.25 = (bf16[96,1536]{1,0:T(8,128)(2,1)S(1)}, bf16[96,1536]{1,0:T(8,128)(2,1)S(1)}, u32[]{:S(2)}, u32[]{:S(2)}) collective-permute-start(bf16[96,1536]{1,0:T(8,128)(2,1)S(1)} %get-tuple-element.196), channel_id=1, source_target_pairs={{4,12},{8,0},{5,13},{9,1},{6,14},{10,2},{7,15},{11,3},{20,28},{24,... | collective-permute-start | bytes 884744 | tf_op jit(solution)/shard_map/ppermute | solution.py:339
  71.7 28.5 %collective-permute-start.34 = (bf16[192,1536]{1,0:T(8,128)(2,1)S(1)}, bf16[192,1536]{1,0:T(8,128)(2,1)S(1)}, u32[]{:S(2)}, u32[]{:S(2)}) collective-permute-start(bf16[192,1536]{1,0:T(8,128)(2,1)S(1)} %convolution_convert_fusion.1), channel_id=1, source_target_pairs={{0,4},{12,8},{1,5},{13,9},{2,6},{14,10},{3,7},{15,11},{16,20},{28,... | collective-permute-start | bytes 1769480 | tf_op jit(solution)/shard_map/ppermute | solution.py:324
  81.3 8.8 %collective-permute-start.26 = (bf16[96,1536]{1,0:T(8,128)(2,1)S(1)}, bf16[96,1536]{1,0:T(8,128)(2,1)S(1)}, u32[]{:S(2)}, u32[]{:S(2)}) collective-permute-start(bf16[96,1536]{1,0:T(8,128)(2,1)S(1)} %get-tuple-element.195), channel_id=1, source_target_pairs={{4,8},{8,4},{5,9},{9,5},{6,10},{10,6},{7,11},{11,7},{20,24},{24,20... | collective-permute-start | bytes 884744 | tf_op jit(solution)/shard_map/ppermute | solution.py:340
  87.6 7.6 %collective-permute-start.35 = (bf16[96,2048]{1,0:T(8,128)(2,1)S(1)}, bf16[96,2048]{1,0:T(8,128)(2,1)S(1)}, u32[]{:S(2)}, u32[]{:S(2)}) collective-permute-start(bf16[96,2048]{1,0:T(8,128)(2,1)S(1)} %maximum_select_fusion.22), channel_id=1, source_target_pairs={{0,1},{1,0},{2,3},{3,2},{4,5},{5,4},{6,7},{7,6},{8,9},{9,8},{10,11... | collective-permute-start | bytes 1179656 | tf_op jit(solution)/shard_map/ppermute | solution.py:318
  87.6 19.0 %collective-permute-start.31 = (bf16[96,1536]{1,0:T(8,128)(2,1)S(1)}, bf16[96,1536]{1,0:T(8,128)(2,1)S(1)}, u32[]{:S(2)}, u32[]{:S(2)}) collective-permute-start(bf16[96,1536]{1,0:T(8,128)(2,1)S(1)} %slice.226), channel_id=1, source_target_pairs={{0,4},{4,0},{8,12},{12,8},{1,5},{5,1},{9,13},{13,9},{2,6},{6,2},{1... | collective-permute-start | bytes 884744 | tf_op jit(solution)/shard_map/ppermute | solution.py:332
  90.1 15.0 %collective-permute-start.32 = (bf16[96,1536]{1,0:T(8,128)(2,1)S(1)}, bf16[96,1536]{1,0:T(8,128)(2,1)S(1)}, u32[]{:S(2)}, u32[]{:S(2)}) collective-permute-start(bf16[96,1536]{1,0:T(8,128)(2,1)S(1)} %get-tuple-element.194), channel_id=1, source_target_pairs={{4,12},{8,0},{5,13},{9,1},{6,14},{10,2},{7,15},{11,3},{20,28},{24,... | collective-permute-start | bytes 884744 | tf_op jit(solution)/shard_map/ppermute | solution.py:339
  93.0 12.1 %collective-permute-start.33 = (bf16[96,1536]{1,0:T(8,128)(2,1)S(1)}, bf16[96,1536]{1,0:T(8,128)(2,1)S(1)}, u32[]{:S(2)}, u32[]{:S(2)}) collective-permute-start(bf16[96,1536]{1,0:T(8,128)(2,1)S(1)} %get-tuple-element.193), channel_id=1, source_target_pairs={{4,8},{8,4},{5,9},{9,5},{6,10},{10,6},{7,11},{11,7},{20,24},{24,20... | collective-permute-start | bytes 884744 | tf_op jit(solution)/shard_map/ppermute | solution.py:340
  95.2 15.1 %collective-permute-start.30 = (bf16[96,2048]{1,0:T(8,128)(2,1)S(1)}, bf16[96,2048]{1,0:T(8,128)(2,1)S(1)}, u32[]{:S(2)}, u32[]{:S(2)}) collective-permute-start(bf16[96,2048]{1,0:T(8,128)(2,1)S(1)} %maximum_select_fusion.23), channel_id=1, source_target_pairs={{0,1},{1,0},{2,3},{3,2},{4,5},{5,4},{6,7},{7,6},{8,9},{9,8},{10,11... | collective-permute-start | bytes 1179656 | tf_op jit(solution)/shard_map/ppermute | solution.py:318
  100.2 19.0 %collective-permute-start.37 = (bf16[192,1536]{1,0:T(8,128)(2,1)S(1)}, bf16[192,1536]{1,0:T(8,128)(2,1)S(1)}, u32[]{:S(2)}, u32[]{:S(2)}) collective-permute-start(bf16[192,1536]{1,0:T(8,128)(2,1)S(1)} %convolution_convert_fusion), channel_id=1, source_target_pairs={{0,4},{12,8},{1,5},{13,9},{2,6},{14,10},{3,7},{15,11},{16,20},{28,... | collective-permute-start | bytes 1769480 | tf_op jit(solution)/shard_map/ppermute | solution.py:324
  105.1 20.5 %collective-permute-start.40 = (bf16[96,1536]{1,0:T(8,128)(2,1)S(1)}, bf16[96,1536]{1,0:T(8,128)(2,1)S(1)}, u32[]{:S(2)}, u32[]{:S(2)}) collective-permute-start(bf16[96,1536]{1,0:T(8,128)(2,1)S(1)} %slice.225), channel_id=1, source_target_pairs={{0,4},{4,0},{8,12},{12,8},{1,5},{5,1},{9,13},{13,9},{2,6},{6,2},{1... | collective-permute-start | bytes 884744 | tf_op jit(solution)/shard_map/ppermute | solution.py:332
  106.6 14.2 %collective-permute-start.41 = (bf16[96,1536]{1,0:T(8,128)(2,1)S(1)}, bf16[96,1536]{1,0:T(8,128)(2,1)S(1)}, u32[]{:S(2)}, u32[]{:S(2)}) collective-permute-start(bf16[96,1536]{1,0:T(8,128)(2,1)S(1)} %get-tuple-element.190), channel_id=1, source_target_pairs={{4,12},{8,0},{5,13},{9,1},{6,14},{10,2},{7,15},{11,3},{20,28},{24,... | collective-permute-start | bytes 884744 | tf_op jit(solution)/shard_map/ppermute | solution.py:339
  107.9 13.7 %collective-permute-start.42 = (bf16[96,1536]{1,0:T(8,128)(2,1)S(1)}, bf16[96,1536]{1,0:T(8,128)(2,1)S(1)}, u32[]{:S(2)}, u32[]{:S(2)}) collective-permute-start(bf16[96,1536]{1,0:T(8,128)(2,1)S(1)} %get-tuple-element.189), channel_id=1, source_target_pairs={{4,8},{8,4},{5,9},{9,5},{6,10},{10,6},{7,11},{11,7},{20,24},{24,20... | collective-permute-start | bytes 884744 | tf_op jit(solution)/shard_map/ppermute | solution.py:340
  111.8 21.4 %collective-permute-start.36 = (bf16[96,1536]{1,0:T(8,128)(2,1)S(1)}, bf16[96,1536]{1,0:T(8,128)(2,1)S(1)}, u32[]{:S(2)}, u32[]{:S(2)}) collective-permute-start(bf16[96,1536]{1,0:T(8,128)(2,1)S(1)} %slice.224), channel_id=1, source_target_pairs={{0,4},{4,0},{8,12},{12,8},{1,5},{5,1},{9,13},{13,9},{2,6},{6,2},{1... | collective-permute-start | bytes 884744 | tf_op jit(solution)/shard_map/ppermute | solution.py:332
  119.4 13.8 %collective-permute-start.38 = (bf16[96,1536]{1,0:T(8,128)(2,1)S(1)}, bf16[96,1536]{1,0:T(8,128)(2,1)S(1)}, u32[]{:S(2)}, u32[]{:S(2)}) collective-permute-start(bf16[96,1536]{1,0:T(8,128)(2,1)S(1)} %get-tuple-element.192), channel_id=1, source_target_pairs={{4,12},{8,0},{5,13},{9,1},{6,14},{10,2},{7,15},{11,3},{20,28},{24,... | collective-permute-start | bytes 884744 | tf_op jit(solution)/shard_map/ppermute | solution.py:339
  120.8 12.5 %collective-permute-start.39 = (bf16[96,1536]{1,0:T(8,128)(2,1)S(1)}, bf16[96,1536]{1,0:T(8,128)(2,1)S(1)}, u32[]{:S(2)}, u32[]{:S(2)}) collective-permute-start(bf16[96,1536]{1,0:T(8,128)(2,1)S(1)} %get-tuple-element.191), channel_id=1, source_target_pairs={{4,8},{8,4},{5,9},{9,5},{6,10},{10,6},{7,11},{11,7},{20,24},{24,20... | collective-permute-start | bytes 884744 | tf_op jit(solution)/shard_map/ppermute | solution.py:340

commit v5 on v4

--- a/solution.py
+++ b/solution.py
@@ -12,45 +12,40 @@
 HEAD_DIM = 128
 ORDER = ((3, 2, 1, 0), (3, 2, 0, 1), (0, 1, 3, 2), (0, 1, 2, 3))
 SIZES = (48, 48, 48, 48)
-JOINT = (0, 1, 2, 3)
+FAR = ((0,), (1,), (2, 3))
+NEAR = ((0, 1), (2, 3))
 TURNS = (
     "a0",
     "n",
     "s0",
+    "a1",
+    "s1",
     "z0",
-    "a1",
     "a2",
-    "s1",
+    "x0",
+    "x1",
+    "s2",
+    "c0",
+    "w",
     "z1",
-    "x0",
-    "s2",
-    "a3",
-    "z2",
-    "x1",
-    "s3",
-    "c0",
-    "z3",
-    "x2",
-    "w",
+    "y0",
     "c1",
     "m0",
     "k0",
-    "x3",
+    "x2",
+    "m1",
+    "f0",
+    "e0",
     "c2",
-    "m1",
-    "e0",
-    "k1",
-    "f0",
-    "c3",
     "m2",
+    "y1",
     "e1",
-    "k2",
     "f1",
     "d0",
+    "k1",
+    "f2",
     "m3",
-    "k3",
     "e2",
-    "f2",
     "d1",
     "e3",
     "f3",
@@ -256,15 +251,24 @@
         return arrays
 
     state = [{} for _ in SIZES]
+    moved = {}
     before = ()
 
-    def across(n):
-        start, size = starts[n], SIZES[n]
-        if n:
-            piece = normed[start + size : start + 2 * size]
-        else:
-            piece = hidden_states[size : 2 * size]
-        state[n]["a"] = lax.ppermute(piece, "tensor", swap_x)
+    stays = [slice(start, start + size) for start, size in zip(starts, SIZES)]
+    leaves = [slice(start + size, start + 2 * size) for start, size in zip(starts, SIZES)]
+
+    def joined(pieces):
+        return jnp.concatenate(pieces) if len(pieces) > 1 else pieces[0]
+
+    def cut(array, group):
+        ends = [sum(SIZES[m] for m in group[: i + 1]) for i in range(len(group))]
+        return [array[end - SIZES[m] : end] for m, end in zip(group, ends)]
+
+    def across(g):
+        rows = normed if g else hidden_states
+        got = lax.ppermute(joined([rows[leaves[n]] for n in FAR[g]]), "tensor", swap_x)
+        for n, piece in zip(FAR[g], cut(got, FAR[g])):
+            state[n]["a"] = piece
 
     def first_send():
         size = SIZES[0]
@@ -284,38 +288,45 @@
         done[0] = state[0]["s"]
         return (hidden_states.astype(jnp.float32) * scale * gain).astype(jnp.bfloat16)
 
-    def send(n):
-        start, size = starts[n], SIZES[n]
-        if n:
-            stay, other = in_turn(normed[start : start + size], state[n]["a"])
+    def send(g):
+        if g:
+            group = FAR[g]
+            stay, other = in_turn(
+                joined([normed[stays[n]] for n in group]), joined([state[n]["a"] for n in group])
+            )
             far = jnp.where(here_far, stay, other)
             near = jnp.where(here_far, other, stay)
-            state[n]["s"] = done[0] = (far, near)
-        state[n]["z", 0] = lax.ppermute(state[n]["s"][0], both, toward(True))
-
-    def send_near(n):
-        (near,) = in_turn(state[n]["s"][1])
-        state[n]["z", 1] = lax.ppermute(near, both, toward(False))
-
-    def cross(n, part):
-        if n in JOINT:
-            mine = jnp.stack(in_turn(state[n]["z", 0], state[n]["z", 1]))
-            theirs = lax.ppermute(mine, "tensor", swap_x)
-            for half in (0, 1):
-                state[n]["x", half] = mine[half], theirs[half]
+            done[0] = (far, near)
+            for n, one, two in zip(group, cut(far, group), cut(near, group)):
+                state[n]["s"] = one, two
         else:
-            (mine,) = in_turn(state[n]["z", part])
-            state[n]["x", part] = mine, lax.ppermute(mine, "tensor", swap_x)
+            far = state[0]["s"][0]
+        moved[0, g] = lax.ppermute(far, both, toward(True))
+
+    def send_near(g):
+        (near,) = in_turn(joined([state[n]["s"][1] for n in NEAR[g]]))
+        done[0] = near
+        moved[1, g] = lax.ppermute(near, both, toward(False))
+
+    def cross(part, g):
+        (mine,) = in_turn(moved[part, g])
         done[0] = mine
+        moved[part, g] = mine, lax.ppermute(mine, "tensor", swap_x)
 
     def both_stages(mine, theirs):
         return jnp.where(even_core, jnp.concatenate((mine, theirs)), jnp.concatenate((theirs, mine)))
 
-    def share(n, part):
-        mine, theirs = in_turn(*state[n]["x", part])
-        mine = jnp.where(here_far, jnp.concatenate((theirs, mine)), jnp.concatenate((mine, theirs)))
+    def share(part, g):
+        group = (FAR, NEAR)[part][g]
+        mine, theirs = in_turn(*moved[part, g])
+        one, two = jnp.where(here_far, theirs, mine), jnp.where(here_far, mine, theirs)
+        mine = jnp.concatenate([x for pair in zip(cut(one, group), cut(two, group)) for x in pair])
         done[0] = mine
-        state[n]["c", part] = mine, lax.ppermute(mine, "tensor", swap_core)
+        theirs = lax.ppermute(mine, "tensor", swap_core)
+        first = starts[group[0]]
+        for n in group:
+            rows = slice(starts[n] - first, starts[n] - first + 2 * SIZES[n])
+            state[n]["c", part] = mine[rows], theirs[rows]
 
     def multiply(n):
         rows = both_stages(*in_turn(*state[n]["c", 0]))
@@ -358,10 +369,10 @@
         "a": across,
         "s": send,
         "z": send_near,
-        "x": lambda n: cross(n, 0),
-        "y": lambda n: cross(n, 1),
-        "c": lambda n: share(n, 0),
-        "k": lambda n: share(n, 1),
+        "x": functools.partial(cross, 0),
+        "y": functools.partial(cross, 1),
+        "c": functools.partial(share, 0),
+        "k": functools.partial(share, 1),
         "m": multiply,
         "e": multiply_near,
         "f": forward,

time: 138 us -> 131 us (0.949); the launches traced: 136 us -> 131 us
  waiting for transfers between devices: 46.1 us -> 35.7 us
  starting transfers between devices: 62.1 us -> 66.7 us
    ppermute x4, waiting for transfers between devices: 16.7 us -> 7.97 us  [multiply_near(): lax.ppermute(inner, 'fsdp', [(0, 1), (1, 0), (2, 3), (3, 2)])]
    ppermute x4, starting transfers between devices: 8.03 us -> 16.2 us  [multiply_near(): lax.ppermute(inner, 'fsdp', [(0, 1), (1, 0), (2, 3), (3, 2)])]
    ppermute x24 -> x18, waiting for transfers between devices: 16.6 us -> 12.4 us  [the longest x5 8.21 us: cross(): moved[part, g] = (mine, lax.ppermute(mine, 'tensor', swap_x))]
    ppermute x4, waiting for transfers between devices: 0.01 us -> 3.23 us  [forward(): far_sum = lax.ppermute(passed[:half], 'fsdp', [(1, 3), (2, 0)])]
    ppermute x4, starting transfers between devices: 15.1 us -> 12.3 us  [multiply(): state[n]['p'] = (outer, lax.ppermute(outer, 'fsdp', outer_in))]
    ppermute x24 -> x18, starting transfers between devices: 26 us -> 25.1 us  [the longest x3 11.8 us: send(): moved[0, g] = lax.ppermute(far, both, toward(True))]
  transfers between devices with their start and end apart: 43 -> 37, of which waited for: 14 -> 12; matrix products, arithmetic and copies ran while one was open for 12% -> 13% of each run, Pallas kernels for 4% -> 4%
where the time goes in v5:
time: 131 us
  starting transfers between devices  66.7 us (51%)
  waiting for transfers between devices  35.7 us (27%)
  matrix products  11.3 us (9%)
  Pallas kernels  7.85 us (6%)
  other arithmetic  5.64 us (4%)
  local copies, waits for them, and re-layouts  2.35 us (2%)
    ppermute x4, starting transfers between devices, multiply_near(): lax.ppermute(inner, 'fsdp', [(0, 1), (1, 0), (2, 3), (3, 2)])  16.2 us
    ppermute x4, starting transfers between devices, multiply(): state[n]['p'] = (outer, lax.ppermute(outer, 'fsdp', outer_in))  12.3 us
    ppermute x3, starting transfers between devices, send(): moved[0, g] = lax.ppermute(far, both, toward(True))  11.8 us
    ppermute x4, waiting for transfers between devices, multiply(): state[n]['p'] = (outer, lax.ppermute(outer, 'fsdp', outer_in))  9.06 us
    ppermute x5, waiting for transfers between devices, cross(): moved[part, g] = (mine, lax.ppermute(mine, 'tensor', swap_x))  8.21 us
    ppermute x4, waiting for transfers between devices, multiply_near(): lax.ppermute(inner, 'fsdp', [(0, 1), (1, 0), (2, 3), (3, 2)])  7.97 us
    pallas_call x4, Pallas kernels, attend_piece(): pl.pallas_call(functools.partial(attend_kernel, start), in_specs=[here] *...  7.85 us
    ppermute x2, starting transfers between devices, send_near(): moved[1, g] = lax.ppermute(near, both, toward(False))  5.99 us
  transfers between devices with their start and end apart: 37, of which 12 were waited for; matrix products, arithmetic and copies ran while one was open for 13% of the time, Pallas kernels for 4%

profile of v5, /device:TPU:0, one launch (start us, length us, event | category | flops | bytes accessed | tf_op | source)
XLA Modules:
  0.0 130.6 jit_solution(10524772418206964511)
XLA Ops:
  0.0 1.9 %fusion = f32[384]{0:T(512)S(1)} fusion(bf16[384,2048]{1,0:T(8,128)(2,1)} %param.5), kind=kLoop, calls=%fused_computation.2 | loop fusion | flops 2358912 | bytes 1574400 | tf_op jit(solution)/shard_map/reduce_sum | solution.py:236
  1.9 0.5 collective-permute-start.1
  2.4 2.6 %collective-permute-start.2 = (f32[384]{0:T(512)S(1)}, f32[384]{0:T(512)S(1)}, u32[]{:S(2)}, u32[]{:S(2)}) collective-permute-start(f32[384]{0:T(512)S(1)} %fusion), channel_id=1, source_target_pairs={{0,3},{1,2},{2,1},{3,0},{4,7},{5,6},{6,5},{7,4},{8,11},{9,10},{10,... | collective-permute-start | bytes 4616 | tf_op jit(solution)/shard_map/ppermute | solution.py:239
  5.2 2.1 %collective-permute-start = (f32[2432]{0:T(1024)S(1)}, f32[2432]{0:T(1024)S(1)}, u32[]{:S(2)}, u32[]{:S(2)}) collective-permute-start(f32[2432]{0:T(1024)S(1)} %pad_maximum_fusion.16), channel_id=1, source_target_pairs={{0,2},{1,3},{2,0},{3,1},{4,6},{5,7},{6,4},{7,5},{8,10},{9,11},{10,... | collective-permute-start | bytes 29192 | tf_op jit(solution)/shard_map/ppermute | solution.py:241
  7.4 0.3 reduce-window.9
  8.1 0.8 fusion.55
  8.8 0.2 pad_maximum_fusion.14
  9.2 3.1 %collective-permute-done = f32[2432]{0:T(1024)S(1)} collective-permute-done((f32[2432]{0:T(1024)S(1)}, f32[2432]{0:T(1024)S(1)}, u32[]{:S(2)}, u32[]{:S(2)}) %collective-permute-start) | collective-permute-done | bytes 9760 | tf_op jit(solution)/shard_map/ppermute | solution.py:241
  12.4 0.4 fusion.2
  13.0 0.4 collective-permute-start.5
  13.5 2.8 %collective-permute-start.7 = (bf16[48,2048]{1,0:T(8,128)(2,1)S(1)}, bf16[48,2048]{1,0:T(8,128)(2,1)S(1)}, u32[]{:S(2)}, u32[]{:S(2)}) collective-permute-start(bf16[48,2048]{1,0:T(8,128)(2,1)S(1)} %multiply_convert_fusion.1), channel_id=1, source_target_pairs={{0,8},{1,12},{2,10},{3,14},{4,9},{5,13},{6,11},{7,15},{8,1},{9,5},... | collective-permute-start | bytes 589832 | tf_op jit(solution)/shard_map/ppermute | solution.py:304
  16.4 1.5 %collective-permute-start.4 = (bf16[96,2048]{1,0:T(8,128)(2,1)S(1)}, bf16[96,2048]{1,0:T(8,128)(2,1)S(1)}, u32[]{:S(2)}, u32[]{:S(2)}) collective-permute-start(bf16[96,2048]{1,0:T(8,128)(2,1)S(1)} %pad_maximum_fusion.4), channel_id=1, source_target_pairs={{0,2},{1,3},{2,0},{3,1},{4,6},{5,7},{6,4},{7,5},{8,10},{9,11},{10,... | collective-permute-start | bytes 1179656 | tf_op jit(solution)/shard_map/ppermute | solution.py:269
  18.1 1.0 collective-permute-done.5
  19.1 4.5 %collective-permute-start.6 = (bf16[48,2048]{1,0:T(8,128)(2,1)S(1)}, bf16[48,2048]{1,0:T(8,128)(2,1)S(1)}, u32[]{:S(2)}, u32[]{:S(2)}) collective-permute-start(bf16[48,2048]{1,0:T(8,128)(2,1)S(1)} %get-tuple-element.201), channel_id=1, source_target_pairs={{0,8},{1,12},{2,10},{3,14},{4,9},{5,13},{6,11},{7,15},{8,1},{9,5},... | collective-permute-start | bytes 589832 | tf_op jit(solution)/shard_map/ppermute | solution.py:304
  23.6 3.0 %collective-permute-start.11 = (bf16[96,2048]{1,0:T(8,128)(2,1)S(1)}, bf16[96,2048]{1,0:T(8,128)(2,1)S(1)}, u32[]{:S(2)}, u32[]{:S(2)}) collective-permute-start(bf16[96,2048]{1,0:T(8,128)(2,1)S(1)} %pad_maximum_fusion.5), channel_id=1, source_target_pairs={{0,1},{1,4},{2,3},{3,6},{4,0},{5,5},{6,2},{7,7},{8,9},{9,12},{10,1... | collective-permute-start | bytes 1179656 | tf_op jit(solution)/shard_map/ppermute | solution.py:309
  26.7 3.0 %collective-permute-done.6 = bf16[48,2048]{1,0:T(8,128)(2,1)S(1)} collective-permute-done((bf16[48,2048]{1,0:T(8,128)(2,1)S(1)}, bf16[48,2048]{1,0:T(8,128)(2,1)S(1)}, u32[]{:S(2)}, u32[]{:S(2)}) %collective-permute-start.6) | collective-permute-done | bytes 196640 | tf_op jit(solution)/shard_map/ppermute | solution.py:304
  29.8 4.5 %collective-permute-start.10 = (bf16[96,2048]{1,0:T(8,128)(2,1)S(1)}, bf16[96,2048]{1,0:T(8,128)(2,1)S(1)}, u32[]{:S(2)}, u32[]{:S(2)}) collective-permute-start(bf16[96,2048]{1,0:T(8,128)(2,1)S(1)} %get-tuple-element.176), channel_id=1, source_target_pairs={{0,8},{1,12},{2,10},{3,14},{4,9},{5,13},{6,11},{7,15},{8,1},{9,5},... | collective-permute-start | bytes 1179656 | tf_op jit(solution)/shard_map/ppermute | solution.py:304
  34.4 2.7 %collective-permute-start.13 = (bf16[96,2048]{1,0:T(8,128)(2,1)S(1)}, bf16[96,2048]{1,0:T(8,128)(2,1)S(1)}, u32[]{:S(2)}, u32[]{:S(2)}) collective-permute-start(bf16[96,2048]{1,0:T(8,128)(2,1)S(1)} %pad_maximum_fusion.6), channel_id=1, source_target_pairs={{0,1},{1,0},{2,3},{3,2},{4,5},{5,4},{6,7},{7,6},{8,9},{9,8},{10,11... | collective-permute-start | bytes 1179656 | tf_op jit(solution)/shard_map/ppermute | solution.py:325
  37.2 0.4 constant_dynamic-update-slice_fusion.1
  37.6 0.5 copy.13
  38.2 0.1 constant_dynamic-update-slice_fusion
  38.3 3.0 %collective-permute-start.9 = (bf16[96,2048]{1,0:T(8,128)(2,1)S(1)}, bf16[96,2048]{1,0:T(8,128)(2,1)S(1)}, u32[]{:S(2)}, u32[]{:S(2)}) collective-permute-start(bf16[96,2048]{1,0:T(8,128)(2,1)S(1)} %get-tuple-element.96), channel_id=1, source_target_pairs={{0,1},{1,4},{2,3},{3,6},{4,0},{5,5},{6,2},{7,7},{8,9},{9,12},{10,1... | collective-permute-start | bytes 1179656 | tf_op jit(solution)/shard_map/ppermute | solution.py:309
  41.3 0.7 collective-permute-start.12
  42.1 1.4 %convolution_convert_fusion.3 = bf16[192,1536]{1,0:T(8,128)(2,1)S(1)} fusion(bf16[2048,1536]{1,0:T(8,128)(2,1)S(1)} %constant_dynamic-update-slice_fusion, bf16[96,2048]{1,0:T(8,128)(2,1)S(1)} %collective-permute-done.13, bf16[96,2048]{1,0:T(8,128)(2,1)S(1)} %pad_maximum_fusion.6, pred[]{:T(512)S(6)} %eq.5), kind=kOutput, calls=%fused_computation.8 | convolution fusion | flops 1211793408 | bytes 7667713 | tf_op jit(solution)/shard_map/dot_general | solution.py:333
  43.5 2.9 %collective-permute-start.17 = (bf16[192,1536]{1,0:T(8,128)(2,1)S(1)}, bf16[192,1536]{1,0:T(8,128)(2,1)S(1)}, u32[]{:S(2)}, u32[]{:S(2)}) collective-permute-start(bf16[192,1536]{1,0:T(8,128)(2,1)S(1)} %convolution_convert_fusion.3), channel_id=1, source_target_pairs={{0,4},{12,8},{1,5},{13,9},{2,6},{14,10},{3,7},{15,11},{16,20},{28,... | collective-permute-start | bytes 1769480 | tf_op jit(solution)/shard_map/ppermute | solution.py:335
  46.5 5.9 %collective-permute-done.12 = bf16[96,2048]{1,0:T(8,128)(2,1)S(1)} collective-permute-done((bf16[96,2048]{1,0:T(8,128)(2,1)S(1)}, bf16[96,2048]{1,0:T(8,128)(2,1)S(1)}, u32[]{:S(2)}, u32[]{:S(2)}) %collective-permute-start.12) | collective-permute-done | bytes 393248 | tf_op jit(solution)/shard_map/ppermute | solution.py:314
  52.7 0.7 collective-permute-start.15
  53.4 1.4 %convolution_convert_fusion.2 = bf16[192,1536]{1,0:T(8,128)(2,1)S(1)} fusion(bf16[2048,1536]{1,0:T(8,128)(2,1)S(1)} %constant_dynamic-update-slice_fusion, bf16[96,2048]{1,0:T(8,128)(2,1)S(1)} %collective-permute-done.18, bf16[96,2048]{1,0:T(8,128)(2,1)S(1)} %pad_maximum_fusion.7, pred[]{:T(512)S(6)} %eq.5), kind=kOutput, calls=%fused_computation.7 | convolution fusion | flops 1211793408 | bytes 7667713 | tf_op jit(solution)/shard_map/dot_general | solution.py:333
  54.8 2.8 %collective-permute-start.24 = (bf16[192,1536]{1,0:T(8,128)(2,1)S(1)}, bf16[192,1536]{1,0:T(8,128)(2,1)S(1)}, u32[]{:S(2)}, u32[]{:S(2)}) collective-permute-start(bf16[192,1536]{1,0:T(8,128)(2,1)S(1)} %convolution_convert_fusion.2), channel_id=1, source_target_pairs={{0,4},{12,8},{1,5},{13,9},{2,6},{14,10},{3,7},{15,11},{16,20},{28,... | collective-permute-start | bytes 1769480 | tf_op jit(solution)/shard_map/ppermute | solution.py:335
  57.7 2.5 %collective-permute-done.17 = bf16[192,1536]{1,0:T(8,128)(2,1)S(1)} collective-permute-done((bf16[192,1536]{1,0:T(8,128)(2,1)S(1)}, bf16[192,1536]{1,0:T(8,128)(2,1)S(1)}, u32[]{:S(2)}, u32[]{:S(2)}) %collective-permute-start.17) | collective-permute-done | bytes 589856 | tf_op jit(solution)/shard_map/ppermute | solution.py:335
  60.2 0.1 add.40
  60.4 1.4 %fusion.13 = f32[192,1536]{1,0:T(8,128)S(1)} fusion(bf16[2048,1536]{1,0:T(8,128)(2,1)S(1)} %constant_dynamic-update-slice_fusion, bf16[96,2048]{1,0:T(8,128)(2,1)S(1)} %get-tuple-element.110, bf16[96,2048]{1,0:T(8,128)(2,1)S(1)} %pad_maximum_fusion.8, pred[]{:T(512)S(6)} %eq.5), kind=kOutput, calls=%fused_computation.23 | convolution fusion | flops 1211498496 | bytes 8257537 | tf_op jit(solution)/shard_map/dot_general | solution.py:339
  61.9 2.3 %collective-permute-done.15 = bf16[96,2048]{1,0:T(8,128)(2,1)S(1)} collective-permute-done((bf16[96,2048]{1,0:T(8,128)(2,1)S(1)}, bf16[96,2048]{1,0:T(8,128)(2,1)S(1)}, u32[]{:S(2)}, u32[]{:S(2)}) %collective-permute-start.15) | collective-permute-done | bytes 393248 | tf_op jit(solution)/shard_map/ppermute | solution.py:314
  64.5 1.3 collective-permute-start.22
  65.8 0.7 collective-permute-start.23
  66.7 5.3 %collective-permute-start.21 = (bf16[96,1536]{1,0:T(8,128)(2,1)S(1)}, bf16[96,1536]{1,0:T(8,128)(2,1)S(1)}, u32[]{:S(2)}, u32[]{:S(2)}) collective-permute-start(bf16[96,1536]{1,0:T(8,128)(2,1)S(1)} %slice.287), channel_id=1, source_target_pairs={{0,4},{4,0},{8,12},{12,8},{1,5},{5,1},{9,13},{13,9},{2,6},{6,2},{1... | collective-permute-start | bytes 884744 | tf_op jit(solution)/shard_map/ppermute | solution.py:343
  72.1 1.4 %convolution_convert_fusion.1 = bf16[192,1536]{1,0:T(8,128)(2,1)S(1)} fusion(bf16[2048,1536]{1,0:T(8,128)(2,1)S(1)} %constant_dynamic-update-slice_fusion, bf16[96,2048]{1,0:T(8,128)(2,1)S(1)} %get-tuple-element.114, bf16[96,2048]{1,0:T(8,128)(2,1)S(1)} %pad_maximum_fusion.9, pred[]{:T(512)S(6)} %eq.5), kind=kOutput, calls=%fused_computation.6 | convolution fusion | flops 1211793408 | bytes 7667713 | tf_op jit(solution)/shard_map/dot_general | solution.py:333
  73.5 0.8 collective-permute-start.20
  74.4 1.4 %fusion.24 = f32[192,1536]{1,0:T(8,128)S(1)} fusion(bf16[2048,1536]{1,0:T(8,128)(2,1)S(1)} %constant_dynamic-update-slice_fusion, bf16[96,2048]{1,0:T(8,128)(2,1)S(1)} %get-tuple-element.117, bf16[96,2048]{1,0:T(8,128)(2,1)S(1)} %pad_maximum_fusion.10, pred[]{:T(512)S(6)} %eq.5), kind=kOutput, calls=%fused_computation.37 | convolution fusion | flops 1211498496 | bytes 8257537 | tf_op jit(solution)/shard_map/dot_general | solution.py:339
  75.9 2.1 %collective-permute-start.29 = (bf16[192,1536]{1,0:T(8,128)(2,1)S(1)}, bf16[192,1536]{1,0:T(8,128)(2,1)S(1)}, u32[]{:S(2)}, u32[]{:S(2)}) collective-permute-start(bf16[192,1536]{1,0:T(8,128)(2,1)S(1)} %convolution_convert_fusion.1), channel_id=1, source_target_pairs={{0,4},{12,8},{1,5},{13,9},{2,6},{14,10},{3,7},{15,11},{16,20},{28,... | collective-permute-start | bytes 1769480 | tf_op jit(solution)/shard_map/ppermute | solution.py:335
  78.0 0.1 add.41
  78.3 4.8 %collective-permute-done.21.refs_1_ = bf16[96,1536]{1,0:T(8,128)(2,1)S(1)} collective-permute-done((bf16[96,1536]{1,0:T(8,128)(2,1)S(1)}, bf16[96,1536]{1,0:T(8,128)(2,1)S(1)}, u32[]{:S(2)}, u32[]{:S(2)}) %collective-permute-start.21) | collective-permute-done | bytes 294944 | tf_op jit(solution)/shard_map/ppermute | solution.py:343
  83.1 1.3 collective-permute-start.27
  84.4 0.7 collective-permute-start.28
  85.1 1.6 %shard_map.55 = (bf16[384,1024]{1,0:T(8,128)(2,1)}, bf16[2,384,256]{2,1,0:T(8,128)(2,1)S(1)}) custom-call(f32[96,1536]{1,0:T(8,128)S(1)} %slice.248.refs_0_, bf16[96,1536]{1,0:T(8,128)(2,1)S(1)} %collective-permute-done.21.refs_1_, bf16[96,1536]{1,0:T(8,128)(2,1)S(1)} %collective-permute-done.22.refs_2_, ...), custom_call_target="tpu_custom_call" | custom-call | tf_op jit(solution)/shard_map/pallas_call | solution.py:203
  87.1 5.0 %collective-permute-done.29 = bf16[192,1536]{1,0:T(8,128)(2,1)S(1)} collective-permute-done((bf16[192,1536]{1,0:T(8,128)(2,1)S(1)}, bf16[192,1536]{1,0:T(8,128)(2,1)S(1)}, u32[]{:S(2)}, u32[]{:S(2)}) %collective-permute-start.29) | collective-permute-done | bytes 589856 | tf_op jit(solution)/shard_map/ppermute | solution.py:335
  92.2 0.1 add.42
  92.3 1.4 %convolution_convert_fusion = bf16[192,1536]{1,0:T(8,128)(2,1)S(1)} fusion(bf16[2048,1536]{1,0:T(8,128)(2,1)S(1)} %constant_dynamic-update-slice_fusion, bf16[96,2048]{1,0:T(8,128)(2,1)S(1)} %get-tuple-element.130, bf16[96,2048]{1,0:T(8,128)(2,1)S(1)} %pad_maximum_fusion.13, pred[]{:T(512)S(6)} %eq.5), kind=kOutput, calls=%fused_computation.5 | convolution fusion | flops 1211793408 | bytes 7667713 | tf_op jit(solution)/shard_map/dot_general | solution.py:333
  93.7 4.4 %collective-permute-start.31 = (bf16[192,1536]{1,0:T(8,128)(2,1)S(1)}, bf16[192,1536]{1,0:T(8,128)(2,1)S(1)}, u32[]{:S(2)}, u32[]{:S(2)}) collective-permute-start(bf16[192,1536]{1,0:T(8,128)(2,1)S(1)} %convolution_convert_fusion), channel_id=1, source_target_pairs={{0,4},{12,8},{1,5},{13,9},{2,6},{14,10},{3,7},{15,11},{16,20},{28,... | collective-permute-start | bytes 1769480 | tf_op jit(solution)/shard_map/ppermute | solution.py:335
  98.2 1.3 collective-permute-start.35
  99.6 1.4 %fusion.35 = f32[192,1536]{1,0:T(8,128)S(1)} fusion(bf16[2048,1536]{1,0:T(8,128)(2,1)S(1)} %constant_dynamic-update-slice_fusion, bf16[96,2048]{1,0:T(8,128)(2,1)S(1)} %get-tuple-element.132, bf16[96,2048]{1,0:T(8,128)(2,1)S(1)} %pad_maximum_fusion.12, pred[]{:T(512)S(6)} %eq.5), kind=kOutput, calls=%fused_computation.51 | convolution fusion | flops 1211498496 | bytes 8257537 | tf_op jit(solution)/shard_map/dot_general | solution.py:339
  101.0 0.7 collective-permute-start.36
  101.7 5.4 %collective-permute-start.34 = (bf16[96,1536]{1,0:T(8,128)(2,1)S(1)}, bf16[96,1536]{1,0:T(8,128)(2,1)S(1)}, u32[]{:S(2)}, u32[]{:S(2)}) collective-permute-start(bf16[96,1536]{1,0:T(8,128)(2,1)S(1)} %slice.285), channel_id=1, source_target_pairs={{0,4},{4,0},{8,12},{12,8},{1,5},{5,1},{9,13},{13,9},{2,6},{6,2},{1... | collective-permute-start | bytes 884744 | tf_op jit(solution)/shard_map/ppermute | solution.py:343
  107.2 1.8 %shard_map.56 = (bf16[384,1024]{1,0:T(8,128)(2,1)}, bf16[2,384,256]{2,1,0:T(8,128)(2,1)S(1)}) custom-call(f32[96,1536]{1,0:T(8,128)S(1)} %slice.258.refs_0_, bf16[96,1536]{1,0:T(8,128)(2,1)S(1)} %collective-permute-done.26.refs_1_, bf16[96,1536]{1,0:T(8,128)(2,1)S(1)} %collective-permute-done.27.refs_2_, ...), custom_call_target="tpu_custom_call", output_to_operand_aliasing={{0}: (9, {})} | custom-call | tf_op jit(solution)/shard_map/pallas_call | solution.py:203
  108.9 1.4 %fusion.41 = f32[192,1536]{1,0:T(8,128)S(1)} fusion(bf16[2048,1536]{1,0:T(8,128)(2,1)S(1)} %constant_dynamic-update-slice_fusion, bf16[96,2048]{1,0:T(8,128)(2,1)S(1)} %get-tuple-element.140, bf16[96,2048]{1,0:T(8,128)(2,1)S(1)} %pad_maximum_fusion.11, pred[]{:T(512)S(6)} %eq.5), kind=kOutput, calls=%fused_computation.58 | convolution fusion | flops 1211498496 | bytes 8257537 | tf_op jit(solution)/shard_map/dot_general | solution.py:339
  110.4 1.5 %collective-permute-done.31 = bf16[192,1536]{1,0:T(8,128)(2,1)S(1)} collective-permute-done((bf16[192,1536]{1,0:T(8,128)(2,1)S(1)}, bf16[192,1536]{1,0:T(8,128)(2,1)S(1)}, u32[]{:S(2)}, u32[]{:S(2)}) %collective-permute-start.31) | collective-permute-done | bytes 589856 | tf_op jit(solution)/shard_map/ppermute | solution.py:335
  111.9 0.1 add.43
  112.1 1.3 collective-permute-start.32
  113.4 0.7 collective-permute-start.33
  114.1 5.4 %collective-permute-start.30 = (bf16[96,1536]{1,0:T(8,128)(2,1)S(1)}, bf16[96,1536]{1,0:T(8,128)(2,1)S(1)}, u32[]{:S(2)}, u32[]{:S(2)}) collective-permute-start(bf16[96,1536]{1,0:T(8,128)(2,1)S(1)} %slice.284), channel_id=1, source_target_pairs={{0,4},{4,0},{8,12},{12,8},{1,5},{5,1},{9,13},{13,9},{2,6},{6,2},{1... | collective-permute-start | bytes 884744 | tf_op jit(solution)/shard_map/ppermute | solution.py:343
  119.6 1.9 %shard_map.57 = (bf16[384,1024]{1,0:T(8,128)(2,1)}, bf16[2,384,256]{2,1,0:T(8,128)(2,1)S(1)}) custom-call(f32[96,1536]{1,0:T(8,128)S(1)} %slice.268.refs_0_, bf16[96,1536]{1,0:T(8,128)(2,1)S(1)} %collective-permute-done.34.refs_1_, bf16[96,1536]{1,0:T(8,128)(2,1)S(1)} %collective-permute-done.35.refs_2_, ...), custom_call_target="tpu_custom_call", output_to_operand_aliasing={{0}: (9, {})} | custom-call | tf_op jit(solution)/shard_map/pallas_call | solution.py:203
  121.5 3.2 %collective-permute-done.32.refs_2_ = bf16[96,1536]{1,0:T(8,128)(2,1)S(1)} collective-permute-done((bf16[96,1536]{1,0:T(8,128)(2,1)S(1)}, bf16[96,1536]{1,0:T(8,128)(2,1)S(1)}, u32[]{:S(2)}, u32[]{:S(2)}) %collective-permute-start.32) | collective-permute-done | bytes 294944 | tf_op jit(solution)/shard_map/ppermute | solution.py:350
  124.7 3.1 %collective-permute-done.30.refs_1_ = bf16[96,1536]{1,0:T(8,128)(2,1)S(1)} collective-permute-done((bf16[96,1536]{1,0:T(8,128)(2,1)S(1)}, bf16[96,1536]{1,0:T(8,128)(2,1)S(1)}, u32[]{:S(2)}, u32[]{:S(2)}) %collective-permute-start.30) | collective-permute-done | bytes 294944 | tf_op jit(solution)/shard_map/ppermute | solution.py:343
  127.8 2.6 %shard_map.58 = (bf16[384,1024]{1,0:T(8,128)(2,1)}, bf16[2,384,256]{2,1,0:T(8,128)(2,1)}) custom-call(f32[96,1536]{1,0:T(8,128)S(1)} %slice.264.refs_0_, bf16[96,1536]{1,0:T(8,128)(2,1)S(1)} %collective-permute-done.30.refs_1_, bf16[96,1536]{1,0:T(8,128)(2,1)S(1)} %collective-permute-done.32.refs_2_, ...), custom_call_target="tpu_custom_call", output_to_operand_aliasing={{0}: (9, {})} | custom-call | tf_op jit(solution)/shard_map/pallas_call | solution.py:203
  (104 shorter events, 3.4 us)
Async XLA Ops:
  0.0 5.0 %copy-start.1 = (bf16[384,2048]{1,0:T(8,128)(2,1)S(1)}, bf16[384,2048]{1,0:T(8,128)(2,1)}, u32[]{:S(2)}) copy-start(bf16[384,2048]{1,0:T(8,128)(2,1)} %param.5) | copy-start | bytes 4718596
  0.0 5.2 %copy-start.4 = (bf16[2048]{0:T(1024)(128)(2,1)S(1)}, bf16[2048]{0:T(1024)(128)(2,1)}, u32[]{:S(2)}) copy-start(bf16[2048]{0:T(1024)(128)(2,1)} %param.6) | copy-start | bytes 12292
  0.0 7.3 %copy-start = (s32[1,384]{1,0:T(1,128)S(1)}, s32[1,384]{1,0:T(1,128)}, u32[]{:S(2)}) copy-start(s32[1,384]{1,0:T(1,128)} %refs_7_.7) | copy-start | bytes 4612
  1.9 10.4 %collective-permute-start.1 = (f32[384]{0:T(512)S(1)}, f32[384]{0:T(512)S(1)}, u32[]{:S(2)}, u32[]{:S(2)}) collective-permute-start(f32[384]{0:T(512)S(1)} %fusion), channel_id=1, source_target_pairs={{0,1},{1,0},{2,3},{3,2},{4,5},{5,4},{6,7},{7,6},{8,9},{9,8},{10,11... | collective-permute-start | bytes 4616 | tf_op jit(solution)/shard_map/ppermute | solution.py:239
  2.4 9.9 %collective-permute-start.2 = (f32[384]{0:T(512)S(1)}, f32[384]{0:T(512)S(1)}, u32[]{:S(2)}, u32[]{:S(2)}) collective-permute-start(f32[384]{0:T(512)S(1)} %fusion), channel_id=1, source_target_pairs={{0,3},{1,2},{2,1},{3,0},{4,7},{5,6},{6,5},{7,4},{8,11},{9,10},{10,... | collective-permute-start | bytes 4616 | tf_op jit(solution)/shard_map/ppermute | solution.py:239
  5.1 7.2 %collective-permute-start.3 = (bf16[48,2048]{1,0:T(8,128)(2,1)S(1)}, bf16[48,2048]{1,0:T(8,128)(2,1)S(1)}, u32[]{:S(2)}, u32[]{:S(2)}) collective-permute-start(bf16[48,2048]{1,0:T(8,128)(2,1)S(1)} %get-tuple-element.161), channel_id=1, source_target_pairs={{0,2},{1,3},{2,0},{3,1},{4,6},{5,7},{6,4},{7,5},{8,10},{9,11},{10,... | collective-permute-start | bytes 589832 | tf_op jit(solution)/shard_map/ppermute | solution.py:269
  5.2 7.1 %collective-permute-start = (f32[2432]{0:T(1024)S(1)}, f32[2432]{0:T(1024)S(1)}, u32[]{:S(2)}, u32[]{:S(2)}) collective-permute-start(f32[2432]{0:T(1024)S(1)} %pad_maximum_fusion.16), channel_id=1, source_target_pairs={{0,2},{1,3},{2,0},{3,1},{4,6},{5,7},{6,4},{7,5},{8,10},{9,11},{10,... | collective-permute-start | bytes 29192 | tf_op jit(solution)/shard_map/ppermute | solution.py:241
  13.0 6.1 %collective-permute-start.5 = (bf16[48,2048]{1,0:T(8,128)(2,1)S(1)}, bf16[48,2048]{1,0:T(8,128)(2,1)S(1)}, u32[]{:S(2)}, u32[]{:S(2)}) collective-permute-start(bf16[48,2048]{1,0:T(8,128)(2,1)S(1)} %get-tuple-element.156), channel_id=1, source_target_pairs={{0,2},{1,3},{2,0},{3,1},{4,6},{5,7},{6,4},{7,5},{8,10},{9,11},{10,... | collective-permute-start | bytes 589832 | tf_op jit(solution)/shard_map/ppermute | solution.py:269
  13.5 13.1 %collective-permute-start.7 = (bf16[48,2048]{1,0:T(8,128)(2,1)S(1)}, bf16[48,2048]{1,0:T(8,128)(2,1)S(1)}, u32[]{:S(2)}, u32[]{:S(2)}) collective-permute-start(bf16[48,2048]{1,0:T(8,128)(2,1)S(1)} %multiply_convert_fusion.1), channel_id=1, source_target_pairs={{0,8},{1,12},{2,10},{3,14},{4,9},{5,13},{6,11},{7,15},{8,1},{9,5},... | collective-permute-start | bytes 589832 | tf_op jit(solution)/shard_map/ppermute | solution.py:304
  16.4 13.4 %collective-permute-start.4 = (bf16[96,2048]{1,0:T(8,128)(2,1)S(1)}, bf16[96,2048]{1,0:T(8,128)(2,1)S(1)}, u32[]{:S(2)}, u32[]{:S(2)}) collective-permute-start(bf16[96,2048]{1,0:T(8,128)(2,1)S(1)} %pad_maximum_fusion.4), channel_id=1, source_target_pairs={{0,2},{1,3},{2,0},{3,1},{4,6},{5,7},{6,4},{7,5},{8,10},{9,11},{10,... | collective-permute-start | bytes 1179656 | tf_op jit(solution)/shard_map/ppermute | solution.py:269
  19.1 18.1 %copy-start.2 = (bf16[2048,1024]{1,0:T(8,128)(2,1)S(1)}, bf16[2048,1024]{1,0:T(8,128)(2,1)}, u32[]{:S(2)}) copy-start(bf16[2048,1024]{1,0:T(8,128)(2,1)} %param.7) | copy-start | bytes 12582916
  19.1 10.6 %collective-permute-start.6 = (bf16[48,2048]{1,0:T(8,128)(2,1)S(1)}, bf16[48,2048]{1,0:T(8,128)(2,1)S(1)}, u32[]{:S(2)}, u32[]{:S(2)}) collective-permute-start(bf16[48,2048]{1,0:T(8,128)(2,1)S(1)} %get-tuple-element.201), channel_id=1, source_target_pairs={{0,8},{1,12},{2,10},{3,14},{4,9},{5,13},{6,11},{7,15},{8,1},{9,5},... | collective-permute-start | bytes 589832 | tf_op jit(solution)/shard_map/ppermute | solution.py:304
  23.6 17.7 %collective-permute-start.11 = (bf16[96,2048]{1,0:T(8,128)(2,1)S(1)}, bf16[96,2048]{1,0:T(8,128)(2,1)S(1)}, u32[]{:S(2)}, u32[]{:S(2)}) collective-permute-start(bf16[96,2048]{1,0:T(8,128)(2,1)S(1)} %pad_maximum_fusion.5), channel_id=1, source_target_pairs={{0,1},{1,4},{2,3},{3,6},{4,0},{5,5},{6,2},{7,7},{8,9},{9,12},{10,1... | collective-permute-start | bytes 1179656 | tf_op jit(solution)/shard_map/ppermute | solution.py:309
  26.6 7.7 %collective-permute-start.8 = (bf16[48,2048]{1,0:T(8,128)(2,1)S(1)}, bf16[48,2048]{1,0:T(8,128)(2,1)S(1)}, u32[]{:S(2)}, u32[]{:S(2)}) collective-permute-start(bf16[48,2048]{1,0:T(8,128)(2,1)S(1)} %collective-permute-done.7), channel_id=1, source_target_pairs={{0,2},{1,3},{2,0},{3,1},{4,6},{5,7},{6,4},{7,5},{8,10},{9,11},{10,... | collective-permute-start | bytes 589832 | tf_op jit(solution)/shard_map/ppermute | solution.py:314
  29.8 12.2 %collective-permute-start.14 = (bf16[48,2048]{1,0:T(8,128)(2,1)S(1)}, bf16[48,2048]{1,0:T(8,128)(2,1)S(1)}, u32[]{:S(2)}, u32[]{:S(2)}) collective-permute-start(bf16[48,2048]{1,0:T(8,128)(2,1)S(1)} %collective-permute-done.6), channel_id=1, source_target_pairs={{0,2},{1,3},{2,0},{3,1},{4,6},{5,7},{6,4},{7,5},{8,10},{9,11},{10,... | collective-permute-start | bytes 589832 | tf_op jit(solution)/shard_map/ppermute | solution.py:314
  29.8 22.8 %collective-permute-start.10 = (bf16[96,2048]{1,0:T(8,128)(2,1)S(1)}, bf16[96,2048]{1,0:T(8,128)(2,1)S(1)}, u32[]{:S(2)}, u32[]{:S(2)}) collective-permute-start(bf16[96,2048]{1,0:T(8,128)(2,1)S(1)} %get-tuple-element.176), channel_id=1, source_target_pairs={{0,8},{1,12},{2,10},{3,14},{4,9},{5,13},{6,11},{7,15},{8,1},{9,5},... | collective-permute-start | bytes 1179656 | tf_op jit(solution)/shard_map/ppermute | solution.py:304
  34.4 3.2 %copy-start.3 = (bf16[2048,2,256]{2,1,0:T(2,128)(2,1)S(1)}, bf16[2048,2,256]{2,1,0:T(2,128)(2,1)}, u32[]{:S(2)}) copy-start(bf16[2048,2,256]{2,1,0:T(2,128)(2,1)} %param.8) | copy-start | bytes 6291460
  34.4 7.7 %collective-permute-start.13 = (bf16[96,2048]{1,0:T(8,128)(2,1)S(1)}, bf16[96,2048]{1,0:T(8,128)(2,1)S(1)}, u32[]{:S(2)}, u32[]{:S(2)}) collective-permute-start(bf16[96,2048]{1,0:T(8,128)(2,1)S(1)} %pad_maximum_fusion.6), channel_id=1, source_target_pairs={{0,1},{1,0},{2,3},{3,2},{4,5},{5,4},{6,7},{7,6},{8,9},{9,8},{10,11... | collective-permute-start | bytes 1179656 | tf_op jit(solution)/shard_map/ppermute | solution.py:325
  38.3 35.2 %collective-permute-start.9 = (bf16[96,2048]{1,0:T(8,128)(2,1)S(1)}, bf16[96,2048]{1,0:T(8,128)(2,1)S(1)}, u32[]{:S(2)}, u32[]{:S(2)}) collective-permute-start(bf16[96,2048]{1,0:T(8,128)(2,1)S(1)} %get-tuple-element.96), channel_id=1, source_target_pairs={{0,1},{1,4},{2,3},{3,6},{4,0},{5,5},{6,2},{7,7},{8,9},{9,12},{10,1... | collective-permute-start | bytes 1179656 | tf_op jit(solution)/shard_map/ppermute | solution.py:309
  41.3 11.1 %collective-permute-start.12 = (bf16[96,2048]{1,0:T(8,128)(2,1)S(1)}, bf16[96,2048]{1,0:T(8,128)(2,1)S(1)}, u32[]{:S(2)}, u32[]{:S(2)}) collective-permute-start(bf16[96,2048]{1,0:T(8,128)(2,1)S(1)} %collective-permute-done.11), channel_id=1, source_target_pairs={{0,2},{1,3},{2,0},{3,1},{4,6},{5,7},{6,4},{7,5},{8,10},{9,11},{10,... | collective-permute-start | bytes 1179656 | tf_op jit(solution)/shard_map/ppermute | solution.py:314
  42.1 11.3 %collective-permute-start.18 = (bf16[96,2048]{1,0:T(8,128)(2,1)S(1)}, bf16[96,2048]{1,0:T(8,128)(2,1)S(1)}, u32[]{:S(2)}, u32[]{:S(2)}) collective-permute-start(bf16[96,2048]{1,0:T(8,128)(2,1)S(1)} %pad_maximum_fusion.7), channel_id=1, source_target_pairs={{0,1},{1,0},{2,3},{3,2},{4,5},{5,4},{6,7},{7,6},{8,9},{9,8},{10,11... | collective-permute-start | bytes 1179656 | tf_op jit(solution)/shard_map/ppermute | solution.py:325
  43.5 16.7 %collective-permute-start.17 = (bf16[192,1536]{1,0:T(8,128)(2,1)S(1)}, bf16[192,1536]{1,0:T(8,128)(2,1)S(1)}, u32[]{:S(2)}, u32[]{:S(2)}) collective-permute-start(bf16[192,1536]{1,0:T(8,128)(2,1)S(1)} %convolution_convert_fusion.3), channel_id=1, source_target_pairs={{0,4},{12,8},{1,5},{13,9},{2,6},{14,10},{3,7},{15,11},{16,20},{28,... | collective-permute-start | bytes 1769480 | tf_op jit(solution)/shard_map/ppermute | solution.py:335
  52.6 7.8 %collective-permute-start.16 = (bf16[192,2048]{1,0:T(8,128)(2,1)S(1)}, bf16[192,2048]{1,0:T(8,128)(2,1)S(1)}, u32[]{:S(2)}, u32[]{:S(2)}) collective-permute-start(bf16[192,2048]{1,0:T(8,128)(2,1)S(1)} %pad_maximum_fusion), channel_id=1, source_target_pairs={{0,1},{1,0},{2,3},{3,2},{4,5},{5,4},{6,7},{7,6},{8,9},{9,8},{10,11... | collective-permute-start | bytes 2359304 | tf_op jit(solution)/shard_map/ppermute | solution.py:325
  52.7 11.5 %collective-permute-start.15 = (bf16[96,2048]{1,0:T(8,128)(2,1)S(1)}, bf16[96,2048]{1,0:T(8,128)(2,1)S(1)}, u32[]{:S(2)}, u32[]{:S(2)}) collective-permute-start(bf16[96,2048]{1,0:T(8,128)(2,1)S(1)} %collective-permute-done.10), channel_id=1, source_target_pairs={{0,2},{1,3},{2,0},{3,1},{4,6},{5,7},{6,4},{7,5},{8,10},{9,11},{10,... | collective-permute-start | bytes 1179656 | tf_op jit(solution)/shard_map/ppermute | solution.py:314
  54.8 21.1 %collective-permute-start.24 = (bf16[192,1536]{1,0:T(8,128)(2,1)S(1)}, bf16[192,1536]{1,0:T(8,128)(2,1)S(1)}, u32[]{:S(2)}, u32[]{:S(2)}) collective-permute-start(bf16[192,1536]{1,0:T(8,128)(2,1)S(1)} %convolution_convert_fusion.2), channel_id=1, source_target_pairs={{0,4},{12,8},{1,5},{13,9},{2,6},{14,10},{3,7},{15,11},{16,20},{28,... | collective-permute-start | bytes 1769480 | tf_op jit(solution)/shard_map/ppermute | solution.py:335
  64.4 2.4 %collective-permute-start.19 = (bf16[192,2048]{1,0:T(8,128)(2,1)S(1)}, bf16[192,2048]{1,0:T(8,128)(2,1)S(1)}, u32[]{:S(2)}, u32[]{:S(2)}) collective-permute-start(bf16[192,2048]{1,0:T(8,128)(2,1)S(1)} %pad_maximum_fusion.1), channel_id=1, source_target_pairs={{0,1},{1,0},{2,3},{3,2},{4,5},{5,4},{6,7},{7,6},{8,9},{9,8},{10,11... | collective-permute-start | bytes 2359304 | tf_op jit(solution)/shard_map/ppermute | solution.py:325
  64.5 13.7 %collective-permute-start.22 = (bf16[96,1536]{1,0:T(8,128)(2,1)S(1)}, bf16[96,1536]{1,0:T(8,128)(2,1)S(1)}, u32[]{:S(2)}, u32[]{:S(2)}) collective-permute-start(bf16[96,1536]{1,0:T(8,128)(2,1)S(1)} %get-tuple-element.184), channel_id=1, source_target_pairs={{4,12},{8,0},{5,13},{9,1},{6,14},{10,2},{7,15},{11,3},{20,28},{24,... | collective-permute-start | bytes 884744 | tf_op jit(solution)/shard_map/ppermute | solution.py:350
  65.8 12.4 %collective-permute-start.23 = (bf16[96,1536]{1,0:T(8,128)(2,1)S(1)}, bf16[96,1536]{1,0:T(8,128)(2,1)S(1)}, u32[]{:S(2)}, u32[]{:S(2)}) collective-permute-start(bf16[96,1536]{1,0:T(8,128)(2,1)S(1)} %get-tuple-element.183), channel_id=1, source_target_pairs={{4,8},{8,4},{5,9},{9,5},{6,10},{10,6},{7,11},{11,7},{20,24},{24,20... | collective-permute-start | bytes 884744 | tf_op jit(solution)/shard_map/ppermute | solution.py:351
  66.7 16.4 %collective-permute-start.21 = (bf16[96,1536]{1,0:T(8,128)(2,1)S(1)}, bf16[96,1536]{1,0:T(8,128)(2,1)S(1)}, u32[]{:S(2)}, u32[]{:S(2)}) collective-permute-start(bf16[96,1536]{1,0:T(8,128)(2,1)S(1)} %slice.287), channel_id=1, source_target_pairs={{0,4},{4,0},{8,12},{12,8},{1,5},{5,1},{9,13},{13,9},{2,6},{6,2},{1... | collective-permute-start | bytes 884744 | tf_op jit(solution)/shard_map/ppermute | solution.py:343
  73.5 13.2 %collective-permute-start.20 = (bf16[96,2048]{1,0:T(8,128)(2,1)S(1)}, bf16[96,2048]{1,0:T(8,128)(2,1)S(1)}, u32[]{:S(2)}, u32[]{:S(2)}) collective-permute-start(bf16[96,2048]{1,0:T(8,128)(2,1)S(1)} %collective-permute-done.9), channel_id=1, source_target_pairs={{0,2},{1,3},{2,0},{3,1},{4,6},{5,7},{6,4},{7,5},{8,10},{9,11},{10,... | collective-permute-start | bytes 1179656 | tf_op jit(solution)/shard_map/ppermute | solution.py:314
  75.9 16.3 %collective-permute-start.29 = (bf16[192,1536]{1,0:T(8,128)(2,1)S(1)}, bf16[192,1536]{1,0:T(8,128)(2,1)S(1)}, u32[]{:S(2)}, u32[]{:S(2)}) collective-permute-start(bf16[192,1536]{1,0:T(8,128)(2,1)S(1)} %convolution_convert_fusion.1), channel_id=1, source_target_pairs={{0,4},{12,8},{1,5},{13,9},{2,6},{14,10},{3,7},{15,11},{16,20},{28,... | collective-permute-start | bytes 1769480 | tf_op jit(solution)/shard_map/ppermute | solution.py:335
  78.2 29.0 %collective-permute-start.26 = (bf16[96,1536]{1,0:T(8,128)(2,1)S(1)}, bf16[96,1536]{1,0:T(8,128)(2,1)S(1)}, u32[]{:S(2)}, u32[]{:S(2)}) collective-permute-start(bf16[96,1536]{1,0:T(8,128)(2,1)S(1)} %slice.286), channel_id=1, source_target_pairs={{0,4},{4,0},{8,12},{12,8},{1,5},{5,1},{9,13},{13,9},{2,6},{6,2},{1... | collective-permute-start | bytes 884744 | tf_op jit(solution)/shard_map/ppermute | solution.py:343
  83.1 17.9 %collective-permute-start.27 = (bf16[96,1536]{1,0:T(8,128)(2,1)S(1)}, bf16[96,1536]{1,0:T(8,128)(2,1)S(1)}, u32[]{:S(2)}, u32[]{:S(2)}) collective-permute-start(bf16[96,1536]{1,0:T(8,128)(2,1)S(1)} %get-tuple-element.182), channel_id=1, source_target_pairs={{4,12},{8,0},{5,13},{9,1},{6,14},{10,2},{7,15},{11,3},{20,28},{24,... | collective-permute-start | bytes 884744 | tf_op jit(solution)/shard_map/ppermute | solution.py:350
  84.4 17.3 %collective-permute-start.28 = (bf16[96,1536]{1,0:T(8,128)(2,1)S(1)}, bf16[96,1536]{1,0:T(8,128)(2,1)S(1)}, u32[]{:S(2)}, u32[]{:S(2)}) collective-permute-start(bf16[96,1536]{1,0:T(8,128)(2,1)S(1)} %get-tuple-element.181), channel_id=1, source_target_pairs={{4,8},{8,4},{5,9},{9,5},{6,10},{10,6},{7,11},{11,7},{20,24},{24,20... | collective-permute-start | bytes 884744 | tf_op jit(solution)/shard_map/ppermute | solution.py:351
  87.0 11.2 %collective-permute-start.25 = (bf16[192,2048]{1,0:T(8,128)(2,1)S(1)}, bf16[192,2048]{1,0:T(8,128)(2,1)S(1)}, u32[]{:S(2)}, u32[]{:S(2)}) collective-permute-start(bf16[192,2048]{1,0:T(8,128)(2,1)S(1)} %pad_maximum_fusion.2), channel_id=1, source_target_pairs={{0,1},{1,0},{2,3},{3,2},{4,5},{5,4},{6,7},{7,6},{8,9},{9,8},{10,11... | collective-permute-start | bytes 2359304 | tf_op jit(solution)/shard_map/ppermute | solution.py:325
  93.7 18.2 %collective-permute-start.31 = (bf16[192,1536]{1,0:T(8,128)(2,1)S(1)}, bf16[192,1536]{1,0:T(8,128)(2,1)S(1)}, u32[]{:S(2)}, u32[]{:S(2)}) collective-permute-start(bf16[192,1536]{1,0:T(8,128)(2,1)S(1)} %convolution_convert_fusion), channel_id=1, source_target_pairs={{0,4},{12,8},{1,5},{13,9},{2,6},{14,10},{3,7},{15,11},{16,20},{28,... | collective-permute-start | bytes 1769480 | tf_op jit(solution)/shard_map/ppermute | solution.py:335
  98.2 15.9 %collective-permute-start.35 = (bf16[96,1536]{1,0:T(8,128)(2,1)S(1)}, bf16[96,1536]{1,0:T(8,128)(2,1)S(1)}, u32[]{:S(2)}, u32[]{:S(2)}) collective-permute-start(bf16[96,1536]{1,0:T(8,128)(2,1)S(1)} %get-tuple-element.178), channel_id=1, source_target_pairs={{4,12},{8,0},{5,13},{9,1},{6,14},{10,2},{7,15},{11,3},{20,28},{24,... | collective-permute-start | bytes 884744 | tf_op jit(solution)/shard_map/ppermute | solution.py:350
  101.0 18.5 %collective-permute-start.36 = (bf16[96,1536]{1,0:T(8,128)(2,1)S(1)}, bf16[96,1536]{1,0:T(8,128)(2,1)S(1)}, u32[]{:S(2)}, u32[]{:S(2)}) collective-permute-start(bf16[96,1536]{1,0:T(8,128)(2,1)S(1)} %get-tuple-element.177), channel_id=1, source_target_pairs={{4,8},{8,4},{5,9},{9,5},{6,10},{10,6},{7,11},{11,7},{20,24},{24,20... | collective-permute-start | bytes 884744 | tf_op jit(solution)/shard_map/ppermute | solution.py:351
  101.7 17.9 %collective-permute-start.34 = (bf16[96,1536]{1,0:T(8,128)(2,1)S(1)}, bf16[96,1536]{1,0:T(8,128)(2,1)S(1)}, u32[]{:S(2)}, u32[]{:S(2)}) collective-permute-start(bf16[96,1536]{1,0:T(8,128)(2,1)S(1)} %slice.285), channel_id=1, source_target_pairs={{0,4},{4,0},{8,12},{12,8},{1,5},{5,1},{9,13},{13,9},{2,6},{6,2},{1... | collective-permute-start | bytes 884744 | tf_op jit(solution)/shard_map/ppermute | solution.py:343
  112.1 12.6 %collective-permute-start.32 = (bf16[96,1536]{1,0:T(8,128)(2,1)S(1)}, bf16[96,1536]{1,0:T(8,128)(2,1)S(1)}, u32[]{:S(2)}, u32[]{:S(2)}) collective-permute-start(bf16[96,1536]{1,0:T(8,128)(2,1)S(1)} %get-tuple-element.180), channel_id=1, source_target_pairs={{4,12},{8,0},{5,13},{9,1},{6,14},{10,2},{7,15},{11,3},{20,28},{24,... | collective-permute-start | bytes 884744 | tf_op jit(solution)/shard_map/ppermute | solution.py:350
  113.4 11.3 %collective-permute-start.33 = (bf16[96,1536]{1,0:T(8,128)(2,1)S(1)}, bf16[96,1536]{1,0:T(8,128)(2,1)S(1)}, u32[]{:S(2)}, u32[]{:S(2)}) collective-permute-start(bf16[96,1536]{1,0:T(8,128)(2,1)S(1)} %get-tuple-element.179), channel_id=1, source_target_pairs={{4,8},{8,4},{5,9},{9,5},{6,10},{10,6},{7,11},{11,7},{20,24},{24,20... | collective-permute-start | bytes 884744 | tf_op jit(solution)/shard_map/ppermute | solution.py:351
  114.1 13.7 %collective-permute-start.30 = (bf16[96,1536]{1,0:T(8,128)(2,1)S(1)}, bf16[96,1536]{1,0:T(8,128)(2,1)S(1)}, u32[]{:S(2)}, u32[]{:S(2)}) collective-permute-start(bf16[96,1536]{1,0:T(8,128)(2,1)S(1)} %slice.284), channel_id=1, source_target_pairs={{0,4},{4,0},{8,12},{12,8},{1,5},{5,1},{9,13},{13,9},{2,6},{6,2},{1... | collective-permute-start | bytes 884744 | tf_op jit(solution)/shard_map/ppermute | solution.py:343

commit v6 on v5

--- a/solution.py
+++ b/solution.py
@@ -29,8 +29,8 @@
     "w",
     "z1",
     "y0",
+    "m0",
     "c1",
-    "m0",
     "k0",
     "x2",
     "m1",
@@ -46,8 +46,8 @@
     "f2",
     "m3",
     "e2",
+    "e3",
     "d1",
-    "e3",
     "f3",
     "d2",
     "d3",
@@ -181,7 +181,7 @@
             (((1,), (1,)), ((), ())),
             preferred_element_type=jnp.float32,
         )
-        scores = scores * (1.0 / math.sqrt(HEAD_DIM)) + bias
+        scores = jnp.where(bias < 0, bias, scores * (1.0 / math.sqrt(HEAD_DIM)))
         expo = jnp.exp(scores - jnp.max(scores, axis=1, keepdims=True))
         weights = (expo * (1.0 / jnp.sum(expo, axis=1, keepdims=True))).astype(jnp.bfloat16)
         mixed = jnp.dot(weights, kv_ref[1, :seen, cols], preferred_element_type=jnp.float32)

time: 131 us -> 131 us (level)
  no operation moved by 1% of the time
where the time goes in v6:
time: 131 us
  starting transfers between devices  66.5 us (51%)
  waiting for transfers between devices  36 us (27%)
  matrix products  11.3 us (9%)
  Pallas kernels  7.83 us (6%)
  other arithmetic  5.64 us (4%)
  local copies, waits for them, and re-layouts  2.37 us (2%)
    ppermute x4, starting transfers between devices, multiply_near(): lax.ppermute(inner, 'fsdp', [(0, 1), (1, 0), (2, 3), (3, 2)])  16.2 us
    ppermute x4, starting transfers between devices, multiply(): state[n]['p'] = (outer, lax.ppermute(outer, 'fsdp', outer_in))  12.2 us
    ppermute x3, starting transfers between devices, send(): moved[0, g] = lax.ppermute(far, both, toward(True))  11.8 us
    ppermute x4, waiting for transfers between devices, multiply(): state[n]['p'] = (outer, lax.ppermute(outer, 'fsdp', outer_in))  8.99 us
    ppermute x5, waiting for transfers between devices, cross(): moved[part, g] = (mine, lax.ppermute(mine, 'tensor', swap_x))  8.5 us
    ppermute x4, waiting for transfers between devices, multiply_near(): lax.ppermute(inner, 'fsdp', [(0, 1), (1, 0), (2, 3), (3, 2)])  8.2 us
    pallas_call x4, Pallas kernels, attend_piece(): pl.pallas_call(functools.partial(attend_kernel, start), in_specs=[here] *...  7.83 us
    ppermute x2, starting transfers between devices, send_near(): moved[1, g] = lax.ppermute(near, both, toward(False))  5.99 us
  transfers between devices with their start and end apart: 37, of which 12 were waited for; matrix products, arithmetic and copies ran while one was open for 13% of the time, Pallas kernels for 4%

profile of v6, /device:TPU:0, one launch (start us, length us, event | category | flops | bytes accessed | tf_op | source)
XLA Modules:
  0.0 130.6 jit_solution(628099239949063226)
XLA Ops:
  0.0 1.9 %fusion = f32[384]{0:T(512)S(1)} fusion(bf16[384,2048]{1,0:T(8,128)(2,1)} %param.5), kind=kLoop, calls=%fused_computation.2 | loop fusion | flops 2358912 | bytes 1574400 | tf_op jit(solution)/shard_map/reduce_sum | solution.py:236
  1.9 0.5 collective-permute-start.1
  2.4 2.6 %collective-permute-start.2 = (f32[384]{0:T(512)S(1)}, f32[384]{0:T(512)S(1)}, u32[]{:S(2)}, u32[]{:S(2)}) collective-permute-start(f32[384]{0:T(512)S(1)} %fusion), channel_id=1, source_target_pairs={{0,3},{1,2},{2,1},{3,0},{4,7},{5,6},{6,5},{7,4},{8,11},{9,10},{10,... | collective-permute-start | bytes 4616 | tf_op jit(solution)/shard_map/ppermute | solution.py:239
  5.2 2.1 %collective-permute-start = (f32[2432]{0:T(1024)S(1)}, f32[2432]{0:T(1024)S(1)}, u32[]{:S(2)}, u32[]{:S(2)}) collective-permute-start(f32[2432]{0:T(1024)S(1)} %pad_maximum_fusion.16), channel_id=1, source_target_pairs={{0,2},{1,3},{2,0},{3,1},{4,6},{5,7},{6,4},{7,5},{8,10},{9,11},{10,... | collective-permute-start | bytes 29192 | tf_op jit(solution)/shard_map/ppermute | solution.py:241
  7.4 0.3 reduce-window.9
  8.1 0.8 fusion.55
  8.8 0.2 pad_maximum_fusion.14
  9.2 3.1 %collective-permute-done = f32[2432]{0:T(1024)S(1)} collective-permute-done((f32[2432]{0:T(1024)S(1)}, f32[2432]{0:T(1024)S(1)}, u32[]{:S(2)}, u32[]{:S(2)}) %collective-permute-start) | collective-permute-done | bytes 9760 | tf_op jit(solution)/shard_map/ppermute | solution.py:241
  12.4 0.4 fusion.2
  13.0 0.4 collective-permute-start.5
  13.5 2.8 %collective-permute-start.7 = (bf16[48,2048]{1,0:T(8,128)(2,1)S(1)}, bf16[48,2048]{1,0:T(8,128)(2,1)S(1)}, u32[]{:S(2)}, u32[]{:S(2)}) collective-permute-start(bf16[48,2048]{1,0:T(8,128)(2,1)S(1)} %multiply_convert_fusion.1), channel_id=1, source_target_pairs={{0,8},{1,12},{2,10},{3,14},{4,9},{5,13},{6,11},{7,15},{8,1},{9,5},... | collective-permute-start | bytes 589832 | tf_op jit(solution)/shard_map/ppermute | solution.py:304
  16.4 1.5 %collective-permute-start.4 = (bf16[96,2048]{1,0:T(8,128)(2,1)S(1)}, bf16[96,2048]{1,0:T(8,128)(2,1)S(1)}, u32[]{:S(2)}, u32[]{:S(2)}) collective-permute-start(bf16[96,2048]{1,0:T(8,128)(2,1)S(1)} %pad_maximum_fusion.4), channel_id=1, source_target_pairs={{0,2},{1,3},{2,0},{3,1},{4,6},{5,7},{6,4},{7,5},{8,10},{9,11},{10,... | collective-permute-start | bytes 1179656 | tf_op jit(solution)/shard_map/ppermute | solution.py:269
  18.1 1.0 collective-permute-done.5
  19.1 4.5 %collective-permute-start.6 = (bf16[48,2048]{1,0:T(8,128)(2,1)S(1)}, bf16[48,2048]{1,0:T(8,128)(2,1)S(1)}, u32[]{:S(2)}, u32[]{:S(2)}) collective-permute-start(bf16[48,2048]{1,0:T(8,128)(2,1)S(1)} %get-tuple-element.201), channel_id=1, source_target_pairs={{0,8},{1,12},{2,10},{3,14},{4,9},{5,13},{6,11},{7,15},{8,1},{9,5},... | collective-permute-start | bytes 589832 | tf_op jit(solution)/shard_map/ppermute | solution.py:304
  23.6 3.0 %collective-permute-start.11 = (bf16[96,2048]{1,0:T(8,128)(2,1)S(1)}, bf16[96,2048]{1,0:T(8,128)(2,1)S(1)}, u32[]{:S(2)}, u32[]{:S(2)}) collective-permute-start(bf16[96,2048]{1,0:T(8,128)(2,1)S(1)} %pad_maximum_fusion.5), channel_id=1, source_target_pairs={{0,1},{1,4},{2,3},{3,6},{4,0},{5,5},{6,2},{7,7},{8,9},{9,12},{10,1... | collective-permute-start | bytes 1179656 | tf_op jit(solution)/shard_map/ppermute | solution.py:309
  26.7 3.0 %collective-permute-done.6 = bf16[48,2048]{1,0:T(8,128)(2,1)S(1)} collective-permute-done((bf16[48,2048]{1,0:T(8,128)(2,1)S(1)}, bf16[48,2048]{1,0:T(8,128)(2,1)S(1)}, u32[]{:S(2)}, u32[]{:S(2)}) %collective-permute-start.6) | collective-permute-done | bytes 196640 | tf_op jit(solution)/shard_map/ppermute | solution.py:304
  29.8 4.5 %collective-permute-start.10 = (bf16[96,2048]{1,0:T(8,128)(2,1)S(1)}, bf16[96,2048]{1,0:T(8,128)(2,1)S(1)}, u32[]{:S(2)}, u32[]{:S(2)}) collective-permute-start(bf16[96,2048]{1,0:T(8,128)(2,1)S(1)} %get-tuple-element.176), channel_id=1, source_target_pairs={{0,8},{1,12},{2,10},{3,14},{4,9},{5,13},{6,11},{7,15},{8,1},{9,5},... | collective-permute-start | bytes 1179656 | tf_op jit(solution)/shard_map/ppermute | solution.py:304
  34.4 2.7 %collective-permute-start.14 = (bf16[96,2048]{1,0:T(8,128)(2,1)S(1)}, bf16[96,2048]{1,0:T(8,128)(2,1)S(1)}, u32[]{:S(2)}, u32[]{:S(2)}) collective-permute-start(bf16[96,2048]{1,0:T(8,128)(2,1)S(1)} %pad_maximum_fusion.6), channel_id=1, source_target_pairs={{0,1},{1,0},{2,3},{3,2},{4,5},{5,4},{6,7},{7,6},{8,9},{9,8},{10,11... | collective-permute-start | bytes 1179656 | tf_op jit(solution)/shard_map/ppermute | solution.py:325
  37.2 0.4 constant_dynamic-update-slice_fusion.1
  37.6 0.5 copy.13
  38.2 0.1 constant_dynamic-update-slice_fusion
  38.3 3.0 %collective-permute-start.9 = (bf16[96,2048]{1,0:T(8,128)(2,1)S(1)}, bf16[96,2048]{1,0:T(8,128)(2,1)S(1)}, u32[]{:S(2)}, u32[]{:S(2)}) collective-permute-start(bf16[96,2048]{1,0:T(8,128)(2,1)S(1)} %get-tuple-element.96), channel_id=1, source_target_pairs={{0,1},{1,4},{2,3},{3,6},{4,0},{5,5},{6,2},{7,7},{8,9},{9,12},{10,1... | collective-permute-start | bytes 1179656 | tf_op jit(solution)/shard_map/ppermute | solution.py:309
  41.3 0.7 collective-permute-start.12
  42.0 1.4 %convolution_convert_fusion.3 = bf16[192,1536]{1,0:T(8,128)(2,1)S(1)} fusion(bf16[2048,1536]{1,0:T(8,128)(2,1)S(1)} %constant_dynamic-update-slice_fusion, bf16[96,2048]{1,0:T(8,128)(2,1)S(1)} %collective-permute-done.14, bf16[96,2048]{1,0:T(8,128)(2,1)S(1)} %pad_maximum_fusion.6, pred[]{:T(512)S(6)} %eq.5), kind=kOutput, calls=%fused_computation.8 | convolution fusion | flops 1211793408 | bytes 7667713 | tf_op jit(solution)/shard_map/dot_general | solution.py:333
  43.4 2.9 %collective-permute-start.17 = (bf16[192,1536]{1,0:T(8,128)(2,1)S(1)}, bf16[192,1536]{1,0:T(8,128)(2,1)S(1)}, u32[]{:S(2)}, u32[]{:S(2)}) collective-permute-start(bf16[192,1536]{1,0:T(8,128)(2,1)S(1)} %convolution_convert_fusion.3), channel_id=1, source_target_pairs={{0,4},{12,8},{1,5},{13,9},{2,6},{14,10},{3,7},{15,11},{16,20},{28,... | collective-permute-start | bytes 1769480 | tf_op jit(solution)/shard_map/ppermute | solution.py:335
  46.5 5.9 %collective-permute-done.12 = bf16[96,2048]{1,0:T(8,128)(2,1)S(1)} collective-permute-done((bf16[96,2048]{1,0:T(8,128)(2,1)S(1)}, bf16[96,2048]{1,0:T(8,128)(2,1)S(1)}, u32[]{:S(2)}, u32[]{:S(2)}) %collective-permute-start.12) | collective-permute-done | bytes 393248 | tf_op jit(solution)/shard_map/ppermute | solution.py:314
  52.8 0.7 collective-permute-start.15
  53.5 1.4 %convolution_convert_fusion.2 = bf16[192,1536]{1,0:T(8,128)(2,1)S(1)} fusion(bf16[2048,1536]{1,0:T(8,128)(2,1)S(1)} %constant_dynamic-update-slice_fusion, bf16[96,2048]{1,0:T(8,128)(2,1)S(1)} %collective-permute-done.18, bf16[96,2048]{1,0:T(8,128)(2,1)S(1)} %pad_maximum_fusion.7, pred[]{:T(512)S(6)} %eq.5), kind=kOutput, calls=%fused_computation.7 | convolution fusion | flops 1211793408 | bytes 7667713 | tf_op jit(solution)/shard_map/dot_general | solution.py:333
  54.9 2.7 %collective-permute-start.24 = (bf16[192,1536]{1,0:T(8,128)(2,1)S(1)}, bf16[192,1536]{1,0:T(8,128)(2,1)S(1)}, u32[]{:S(2)}, u32[]{:S(2)}) collective-permute-start(bf16[192,1536]{1,0:T(8,128)(2,1)S(1)} %convolution_convert_fusion.2), channel_id=1, source_target_pairs={{0,4},{12,8},{1,5},{13,9},{2,6},{14,10},{3,7},{15,11},{16,20},{28,... | collective-permute-start | bytes 1769480 | tf_op jit(solution)/shard_map/ppermute | solution.py:335
  57.6 2.4 %collective-permute-done.17 = bf16[192,1536]{1,0:T(8,128)(2,1)S(1)} collective-permute-done((bf16[192,1536]{1,0:T(8,128)(2,1)S(1)}, bf16[192,1536]{1,0:T(8,128)(2,1)S(1)}, u32[]{:S(2)}, u32[]{:S(2)}) %collective-permute-start.17) | collective-permute-done | bytes 589856 | tf_op jit(solution)/shard_map/ppermute | solution.py:335
  60.1 0.1 add.40
  60.3 1.4 %fusion.13 = f32[192,1536]{1,0:T(8,128)S(1)} fusion(bf16[2048,1536]{1,0:T(8,128)(2,1)S(1)} %constant_dynamic-update-slice_fusion, bf16[96,2048]{1,0:T(8,128)(2,1)S(1)} %get-tuple-element.110, bf16[96,2048]{1,0:T(8,128)(2,1)S(1)} %pad_maximum_fusion.8, pred[]{:T(512)S(6)} %eq.5), kind=kOutput, calls=%fused_computation.23 | convolution fusion | flops 1211498496 | bytes 8257537 | tf_op jit(solution)/shard_map/dot_general | solution.py:339
  61.7 2.6 %collective-permute-done.15 = bf16[96,2048]{1,0:T(8,128)(2,1)S(1)} collective-permute-done((bf16[96,2048]{1,0:T(8,128)(2,1)S(1)}, bf16[96,2048]{1,0:T(8,128)(2,1)S(1)}, u32[]{:S(2)}, u32[]{:S(2)}) %collective-permute-start.15) | collective-permute-done | bytes 393248 | tf_op jit(solution)/shard_map/ppermute | solution.py:314
  64.7 1.3 collective-permute-start.22
  66.0 0.7 collective-permute-start.23
  66.9 5.3 %collective-permute-start.21 = (bf16[96,1536]{1,0:T(8,128)(2,1)S(1)}, bf16[96,1536]{1,0:T(8,128)(2,1)S(1)}, u32[]{:S(2)}, u32[]{:S(2)}) collective-permute-start(bf16[96,1536]{1,0:T(8,128)(2,1)S(1)} %slice.287), channel_id=1, source_target_pairs={{0,4},{4,0},{8,12},{12,8},{1,5},{5,1},{9,13},{13,9},{2,6},{6,2},{1... | collective-permute-start | bytes 884744 | tf_op jit(solution)/shard_map/ppermute | solution.py:343
  72.2 1.4 %convolution_convert_fusion.1 = bf16[192,1536]{1,0:T(8,128)(2,1)S(1)} fusion(bf16[2048,1536]{1,0:T(8,128)(2,1)S(1)} %constant_dynamic-update-slice_fusion, bf16[96,2048]{1,0:T(8,128)(2,1)S(1)} %get-tuple-element.114, bf16[96,2048]{1,0:T(8,128)(2,1)S(1)} %pad_maximum_fusion.9, pred[]{:T(512)S(6)} %eq.5), kind=kOutput, calls=%fused_computation.6 | convolution fusion | flops 1211793408 | bytes 7667713 | tf_op jit(solution)/shard_map/dot_general | solution.py:333
  73.7 0.7 collective-permute-start.20
  74.4 1.4 %fusion.24 = f32[192,1536]{1,0:T(8,128)S(1)} fusion(bf16[2048,1536]{1,0:T(8,128)(2,1)S(1)} %constant_dynamic-update-slice_fusion, bf16[96,2048]{1,0:T(8,128)(2,1)S(1)} %get-tuple-element.117, bf16[96,2048]{1,0:T(8,128)(2,1)S(1)} %pad_maximum_fusion.10, pred[]{:T(512)S(6)} %eq.5), kind=kOutput, calls=%fused_computation.37 | convolution fusion | flops 1211498496 | bytes 8257537 | tf_op jit(solution)/shard_map/dot_general | solution.py:339
  75.9 2.1 %collective-permute-start.26 = (bf16[192,1536]{1,0:T(8,128)(2,1)S(1)}, bf16[192,1536]{1,0:T(8,128)(2,1)S(1)}, u32[]{:S(2)}, u32[]{:S(2)}) collective-permute-start(bf16[192,1536]{1,0:T(8,128)(2,1)S(1)} %convolution_convert_fusion.1), channel_id=1, source_target_pairs={{0,4},{12,8},{1,5},{13,9},{2,6},{14,10},{3,7},{15,11},{16,20},{28,... | collective-permute-start | bytes 1769480 | tf_op jit(solution)/shard_map/ppermute | solution.py:335
  78.0 0.1 add.41
  78.3 5.0 %collective-permute-done.21.refs_1_ = bf16[96,1536]{1,0:T(8,128)(2,1)S(1)} collective-permute-done((bf16[96,1536]{1,0:T(8,128)(2,1)S(1)}, bf16[96,1536]{1,0:T(8,128)(2,1)S(1)}, u32[]{:S(2)}, u32[]{:S(2)}) %collective-permute-start.21) | collective-permute-done | bytes 294944 | tf_op jit(solution)/shard_map/ppermute | solution.py:343
  83.3 1.3 collective-permute-start.30
  84.6 0.7 collective-permute-start.31
  85.3 1.6 %shard_map.55 = (bf16[384,1024]{1,0:T(8,128)(2,1)}, bf16[2,384,256]{2,1,0:T(8,128)(2,1)S(1)}) custom-call(f32[96,1536]{1,0:T(8,128)S(1)} %slice.248.refs_0_, bf16[96,1536]{1,0:T(8,128)(2,1)S(1)} %collective-permute-done.21.refs_1_, bf16[96,1536]{1,0:T(8,128)(2,1)S(1)} %collective-permute-done.22.refs_2_, ...), custom_call_target="tpu_custom_call" | custom-call | tf_op jit(solution)/shard_map/pallas_call | solution.py:203
  87.3 5.0 %collective-permute-done.26 = bf16[192,1536]{1,0:T(8,128)(2,1)S(1)} collective-permute-done((bf16[192,1536]{1,0:T(8,128)(2,1)S(1)}, bf16[192,1536]{1,0:T(8,128)(2,1)S(1)}, u32[]{:S(2)}, u32[]{:S(2)}) %collective-permute-start.26) | collective-permute-done | bytes 589856 | tf_op jit(solution)/shard_map/ppermute | solution.py:335
  92.3 0.1 add.42
  92.4 1.4 %convolution_convert_fusion = bf16[192,1536]{1,0:T(8,128)(2,1)S(1)} fusion(bf16[2048,1536]{1,0:T(8,128)(2,1)S(1)} %constant_dynamic-update-slice_fusion, bf16[96,2048]{1,0:T(8,128)(2,1)S(1)} %get-tuple-element.130, bf16[96,2048]{1,0:T(8,128)(2,1)S(1)} %pad_maximum_fusion.13, pred[]{:T(512)S(6)} %eq.5), kind=kOutput, calls=%fused_computation.5 | convolution fusion | flops 1211793408 | bytes 7667713 | tf_op jit(solution)/shard_map/dot_general | solution.py:333
  93.9 4.4 %collective-permute-start.28 = (bf16[192,1536]{1,0:T(8,128)(2,1)S(1)}, bf16[192,1536]{1,0:T(8,128)(2,1)S(1)}, u32[]{:S(2)}, u32[]{:S(2)}) collective-permute-start(bf16[192,1536]{1,0:T(8,128)(2,1)S(1)} %convolution_convert_fusion), channel_id=1, source_target_pairs={{0,4},{12,8},{1,5},{13,9},{2,6},{14,10},{3,7},{15,11},{16,20},{28,... | collective-permute-start | bytes 1769480 | tf_op jit(solution)/shard_map/ppermute | solution.py:335
  98.4 1.3 collective-permute-start.35
  99.7 1.4 %fusion.35 = f32[192,1536]{1,0:T(8,128)S(1)} fusion(bf16[2048,1536]{1,0:T(8,128)(2,1)S(1)} %constant_dynamic-update-slice_fusion, bf16[96,2048]{1,0:T(8,128)(2,1)S(1)} %get-tuple-element.132, bf16[96,2048]{1,0:T(8,128)(2,1)S(1)} %pad_maximum_fusion.12, pred[]{:T(512)S(6)} %eq.5), kind=kOutput, calls=%fused_computation.51 | convolution fusion | flops 1211498496 | bytes 8257537 | tf_op jit(solution)/shard_map/dot_general | solution.py:339
  101.2 1.4 %fusion.41 = f32[192,1536]{1,0:T(8,128)S(1)} fusion(bf16[2048,1536]{1,0:T(8,128)(2,1)S(1)} %constant_dynamic-update-slice_fusion, bf16[96,2048]{1,0:T(8,128)(2,1)S(1)} %get-tuple-element.134, bf16[96,2048]{1,0:T(8,128)(2,1)S(1)} %pad_maximum_fusion.11, pred[]{:T(512)S(6)} %eq.5), kind=kOutput, calls=%fused_computation.58 | convolution fusion | flops 1211498496 | bytes 8257537 | tf_op jit(solution)/shard_map/dot_general | solution.py:339
  102.6 0.7 collective-permute-start.36
  103.3 5.4 %collective-permute-start.34 = (bf16[96,1536]{1,0:T(8,128)(2,1)S(1)}, bf16[96,1536]{1,0:T(8,128)(2,1)S(1)}, u32[]{:S(2)}, u32[]{:S(2)}) collective-permute-start(bf16[96,1536]{1,0:T(8,128)(2,1)S(1)} %slice.285), channel_id=1, source_target_pairs={{0,4},{4,0},{8,12},{12,8},{1,5},{5,1},{9,13},{13,9},{2,6},{6,2},{1... | collective-permute-start | bytes 884744 | tf_op jit(solution)/shard_map/ppermute | solution.py:343
  108.8 1.7 %shard_map.56 = (bf16[384,1024]{1,0:T(8,128)(2,1)}, bf16[2,384,256]{2,1,0:T(8,128)(2,1)S(1)}) custom-call(f32[96,1536]{1,0:T(8,128)S(1)} %slice.263.refs_0_, bf16[96,1536]{1,0:T(8,128)(2,1)S(1)} %collective-permute-done.29.refs_1_, bf16[96,1536]{1,0:T(8,128)(2,1)S(1)} %collective-permute-done.30.refs_2_, ...), custom_call_target="tpu_custom_call", output_to_operand_aliasing={{0}: (9, {})} | custom-call | tf_op jit(solution)/shard_map/pallas_call | solution.py:203
  110.5 1.5 %collective-permute-done.28 = bf16[192,1536]{1,0:T(8,128)(2,1)S(1)} collective-permute-done((bf16[192,1536]{1,0:T(8,128)(2,1)S(1)}, bf16[192,1536]{1,0:T(8,128)(2,1)S(1)}, u32[]{:S(2)}, u32[]{:S(2)}) %collective-permute-start.28) | collective-permute-done | bytes 589856 | tf_op jit(solution)/shard_map/ppermute | solution.py:335
  112.0 0.1 add.43
  112.2 1.3 collective-permute-start.32
  113.5 0.7 collective-permute-start.33
  114.2 5.4 %collective-permute-start.27 = (bf16[96,1536]{1,0:T(8,128)(2,1)S(1)}, bf16[96,1536]{1,0:T(8,128)(2,1)S(1)}, u32[]{:S(2)}, u32[]{:S(2)}) collective-permute-start(bf16[96,1536]{1,0:T(8,128)(2,1)S(1)} %slice.284), channel_id=1, source_target_pairs={{0,4},{4,0},{8,12},{12,8},{1,5},{5,1},{9,13},{13,9},{2,6},{6,2},{1... | collective-permute-start | bytes 884744 | tf_op jit(solution)/shard_map/ppermute | solution.py:343
  119.7 1.8 %shard_map.57 = (bf16[384,1024]{1,0:T(8,128)(2,1)}, bf16[2,384,256]{2,1,0:T(8,128)(2,1)S(1)}) custom-call(f32[96,1536]{1,0:T(8,128)S(1)} %slice.268.refs_0_, bf16[96,1536]{1,0:T(8,128)(2,1)S(1)} %collective-permute-done.34.refs_1_, bf16[96,1536]{1,0:T(8,128)(2,1)S(1)} %collective-permute-done.35.refs_2_, ...), custom_call_target="tpu_custom_call", output_to_operand_aliasing={{0}: (9, {})} | custom-call | tf_op jit(solution)/shard_map/pallas_call | solution.py:203
  121.6 3.0 %collective-permute-done.32.refs_2_ = bf16[96,1536]{1,0:T(8,128)(2,1)S(1)} collective-permute-done((bf16[96,1536]{1,0:T(8,128)(2,1)S(1)}, bf16[96,1536]{1,0:T(8,128)(2,1)S(1)}, u32[]{:S(2)}, u32[]{:S(2)}) %collective-permute-start.32) | collective-permute-done | bytes 294944 | tf_op jit(solution)/shard_map/ppermute | solution.py:350
  124.6 3.2 %collective-permute-done.27.refs_1_ = bf16[96,1536]{1,0:T(8,128)(2,1)S(1)} collective-permute-done((bf16[96,1536]{1,0:T(8,128)(2,1)S(1)}, bf16[96,1536]{1,0:T(8,128)(2,1)S(1)}, u32[]{:S(2)}, u32[]{:S(2)}) %collective-permute-start.27) | collective-permute-done | bytes 294944 | tf_op jit(solution)/shard_map/ppermute | solution.py:343
  127.8 2.6 %shard_map.58 = (bf16[384,1024]{1,0:T(8,128)(2,1)}, bf16[2,384,256]{2,1,0:T(8,128)(2,1)}) custom-call(f32[96,1536]{1,0:T(8,128)S(1)} %slice.261.refs_0_, bf16[96,1536]{1,0:T(8,128)(2,1)S(1)} %collective-permute-done.27.refs_1_, bf16[96,1536]{1,0:T(8,128)(2,1)S(1)} %collective-permute-done.32.refs_2_, ...), custom_call_target="tpu_custom_call", output_to_operand_aliasing={{0}: (9, {})} | custom-call | tf_op jit(solution)/shard_map/pallas_call | solution.py:203
  (104 shorter events, 3.4 us)
Async XLA Ops:
  0.0 5.0 %copy-start.1 = (bf16[384,2048]{1,0:T(8,128)(2,1)S(1)}, bf16[384,2048]{1,0:T(8,128)(2,1)}, u32[]{:S(2)}) copy-start(bf16[384,2048]{1,0:T(8,128)(2,1)} %param.5) | copy-start | bytes 4718596
  0.0 5.2 %copy-start.4 = (bf16[2048]{0:T(1024)(128)(2,1)S(1)}, bf16[2048]{0:T(1024)(128)(2,1)}, u32[]{:S(2)}) copy-start(bf16[2048]{0:T(1024)(128)(2,1)} %param.6) | copy-start | bytes 12292
  0.0 7.3 %copy-start = (s32[1,384]{1,0:T(1,128)S(1)}, s32[1,384]{1,0:T(1,128)}, u32[]{:S(2)}) copy-start(s32[1,384]{1,0:T(1,128)} %refs_7_.7) | copy-start | bytes 4612
  1.9 10.4 %collective-permute-start.1 = (f32[384]{0:T(512)S(1)}, f32[384]{0:T(512)S(1)}, u32[]{:S(2)}, u32[]{:S(2)}) collective-permute-start(f32[384]{0:T(512)S(1)} %fusion), channel_id=1, source_target_pairs={{0,1},{1,0},{2,3},{3,2},{4,5},{5,4},{6,7},{7,6},{8,9},{9,8},{10,11... | collective-permute-start | bytes 4616 | tf_op jit(solution)/shard_map/ppermute | solution.py:239
  2.4 9.9 %collective-permute-start.2 = (f32[384]{0:T(512)S(1)}, f32[384]{0:T(512)S(1)}, u32[]{:S(2)}, u32[]{:S(2)}) collective-permute-start(f32[384]{0:T(512)S(1)} %fusion), channel_id=1, source_target_pairs={{0,3},{1,2},{2,1},{3,0},{4,7},{5,6},{6,5},{7,4},{8,11},{9,10},{10,... | collective-permute-start | bytes 4616 | tf_op jit(solution)/shard_map/ppermute | solution.py:239
  5.1 7.2 %collective-permute-start.3 = (bf16[48,2048]{1,0:T(8,128)(2,1)S(1)}, bf16[48,2048]{1,0:T(8,128)(2,1)S(1)}, u32[]{:S(2)}, u32[]{:S(2)}) collective-permute-start(bf16[48,2048]{1,0:T(8,128)(2,1)S(1)} %get-tuple-element.161), channel_id=1, source_target_pairs={{0,2},{1,3},{2,0},{3,1},{4,6},{5,7},{6,4},{7,5},{8,10},{9,11},{10,... | collective-permute-start | bytes 589832 | tf_op jit(solution)/shard_map/ppermute | solution.py:269
  5.2 7.1 %collective-permute-start = (f32[2432]{0:T(1024)S(1)}, f32[2432]{0:T(1024)S(1)}, u32[]{:S(2)}, u32[]{:S(2)}) collective-permute-start(f32[2432]{0:T(1024)S(1)} %pad_maximum_fusion.16), channel_id=1, source_target_pairs={{0,2},{1,3},{2,0},{3,1},{4,6},{5,7},{6,4},{7,5},{8,10},{9,11},{10,... | collective-permute-start | bytes 29192 | tf_op jit(solution)/shard_map/ppermute | solution.py:241
  13.0 6.1 %collective-permute-start.5 = (bf16[48,2048]{1,0:T(8,128)(2,1)S(1)}, bf16[48,2048]{1,0:T(8,128)(2,1)S(1)}, u32[]{:S(2)}, u32[]{:S(2)}) collective-permute-start(bf16[48,2048]{1,0:T(8,128)(2,1)S(1)} %get-tuple-element.156), channel_id=1, source_target_pairs={{0,2},{1,3},{2,0},{3,1},{4,6},{5,7},{6,4},{7,5},{8,10},{9,11},{10,... | collective-permute-start | bytes 589832 | tf_op jit(solution)/shard_map/ppermute | solution.py:269
  13.5 13.1 %collective-permute-start.7 = (bf16[48,2048]{1,0:T(8,128)(2,1)S(1)}, bf16[48,2048]{1,0:T(8,128)(2,1)S(1)}, u32[]{:S(2)}, u32[]{:S(2)}) collective-permute-start(bf16[48,2048]{1,0:T(8,128)(2,1)S(1)} %multiply_convert_fusion.1), channel_id=1, source_target_pairs={{0,8},{1,12},{2,10},{3,14},{4,9},{5,13},{6,11},{7,15},{8,1},{9,5},... | collective-permute-start | bytes 589832 | tf_op jit(solution)/shard_map/ppermute | solution.py:304
  16.4 13.4 %collective-permute-start.4 = (bf16[96,2048]{1,0:T(8,128)(2,1)S(1)}, bf16[96,2048]{1,0:T(8,128)(2,1)S(1)}, u32[]{:S(2)}, u32[]{:S(2)}) collective-permute-start(bf16[96,2048]{1,0:T(8,128)(2,1)S(1)} %pad_maximum_fusion.4), channel_id=1, source_target_pairs={{0,2},{1,3},{2,0},{3,1},{4,6},{5,7},{6,4},{7,5},{8,10},{9,11},{10,... | collective-permute-start | bytes 1179656 | tf_op jit(solution)/shard_map/ppermute | solution.py:269
  19.1 18.1 %copy-start.2 = (bf16[2048,1024]{1,0:T(8,128)(2,1)S(1)}, bf16[2048,1024]{1,0:T(8,128)(2,1)}, u32[]{:S(2)}) copy-start(bf16[2048,1024]{1,0:T(8,128)(2,1)} %param.7) | copy-start | bytes 12582916
  19.1 10.6 %collective-permute-start.6 = (bf16[48,2048]{1,0:T(8,128)(2,1)S(1)}, bf16[48,2048]{1,0:T(8,128)(2,1)S(1)}, u32[]{:S(2)}, u32[]{:S(2)}) collective-permute-start(bf16[48,2048]{1,0:T(8,128)(2,1)S(1)} %get-tuple-element.201), channel_id=1, source_target_pairs={{0,8},{1,12},{2,10},{3,14},{4,9},{5,13},{6,11},{7,15},{8,1},{9,5},... | collective-permute-start | bytes 589832 | tf_op jit(solution)/shard_map/ppermute | solution.py:304
  23.6 17.7 %collective-permute-start.11 = (bf16[96,2048]{1,0:T(8,128)(2,1)S(1)}, bf16[96,2048]{1,0:T(8,128)(2,1)S(1)}, u32[]{:S(2)}, u32[]{:S(2)}) collective-permute-start(bf16[96,2048]{1,0:T(8,128)(2,1)S(1)} %pad_maximum_fusion.5), channel_id=1, source_target_pairs={{0,1},{1,4},{2,3},{3,6},{4,0},{5,5},{6,2},{7,7},{8,9},{9,12},{10,1... | collective-permute-start | bytes 1179656 | tf_op jit(solution)/shard_map/ppermute | solution.py:309
  26.6 7.7 %collective-permute-start.8 = (bf16[48,2048]{1,0:T(8,128)(2,1)S(1)}, bf16[48,2048]{1,0:T(8,128)(2,1)S(1)}, u32[]{:S(2)}, u32[]{:S(2)}) collective-permute-start(bf16[48,2048]{1,0:T(8,128)(2,1)S(1)} %collective-permute-done.7), channel_id=1, source_target_pairs={{0,2},{1,3},{2,0},{3,1},{4,6},{5,7},{6,4},{7,5},{8,10},{9,11},{10,... | collective-permute-start | bytes 589832 | tf_op jit(solution)/shard_map/ppermute | solution.py:314
  29.8 16.6 %collective-permute-start.13 = (bf16[48,2048]{1,0:T(8,128)(2,1)S(1)}, bf16[48,2048]{1,0:T(8,128)(2,1)S(1)}, u32[]{:S(2)}, u32[]{:S(2)}) collective-permute-start(bf16[48,2048]{1,0:T(8,128)(2,1)S(1)} %collective-permute-done.6), channel_id=1, source_target_pairs={{0,2},{1,3},{2,0},{3,1},{4,6},{5,7},{6,4},{7,5},{8,10},{9,11},{10,... | collective-permute-start | bytes 589832 | tf_op jit(solution)/shard_map/ppermute | solution.py:314
  29.8 22.9 %collective-permute-start.10 = (bf16[96,2048]{1,0:T(8,128)(2,1)S(1)}, bf16[96,2048]{1,0:T(8,128)(2,1)S(1)}, u32[]{:S(2)}, u32[]{:S(2)}) collective-permute-start(bf16[96,2048]{1,0:T(8,128)(2,1)S(1)} %get-tuple-element.176), channel_id=1, source_target_pairs={{0,8},{1,12},{2,10},{3,14},{4,9},{5,13},{6,11},{7,15},{8,1},{9,5},... | collective-permute-start | bytes 1179656 | tf_op jit(solution)/shard_map/ppermute | solution.py:304
  34.4 3.2 %copy-start.3 = (bf16[2048,2,256]{2,1,0:T(2,128)(2,1)S(1)}, bf16[2048,2,256]{2,1,0:T(2,128)(2,1)}, u32[]{:S(2)}) copy-start(bf16[2048,2,256]{2,1,0:T(2,128)(2,1)} %param.8) | copy-start | bytes 6291460
  34.4 7.6 %collective-permute-start.14 = (bf16[96,2048]{1,0:T(8,128)(2,1)S(1)}, bf16[96,2048]{1,0:T(8,128)(2,1)S(1)}, u32[]{:S(2)}, u32[]{:S(2)}) collective-permute-start(bf16[96,2048]{1,0:T(8,128)(2,1)S(1)} %pad_maximum_fusion.6), channel_id=1, source_target_pairs={{0,1},{1,0},{2,3},{3,2},{4,5},{5,4},{6,7},{7,6},{8,9},{9,8},{10,11... | collective-permute-start | bytes 1179656 | tf_op jit(solution)/shard_map/ppermute | solution.py:325
  38.3 35.3 %collective-permute-start.9 = (bf16[96,2048]{1,0:T(8,128)(2,1)S(1)}, bf16[96,2048]{1,0:T(8,128)(2,1)S(1)}, u32[]{:S(2)}, u32[]{:S(2)}) collective-permute-start(bf16[96,2048]{1,0:T(8,128)(2,1)S(1)} %get-tuple-element.96), channel_id=1, source_target_pairs={{0,1},{1,4},{2,3},{3,6},{4,0},{5,5},{6,2},{7,7},{8,9},{9,12},{10,1... | collective-permute-start | bytes 1179656 | tf_op jit(solution)/shard_map/ppermute | solution.py:309
  41.3 11.1 %collective-permute-start.12 = (bf16[96,2048]{1,0:T(8,128)(2,1)S(1)}, bf16[96,2048]{1,0:T(8,128)(2,1)S(1)}, u32[]{:S(2)}, u32[]{:S(2)}) collective-permute-start(bf16[96,2048]{1,0:T(8,128)(2,1)S(1)} %collective-permute-done.11), channel_id=1, source_target_pairs={{0,2},{1,3},{2,0},{3,1},{4,6},{5,7},{6,4},{7,5},{8,10},{9,11},{10,... | collective-permute-start | bytes 1179656 | tf_op jit(solution)/shard_map/ppermute | solution.py:314
  43.4 16.7 %collective-permute-start.17 = (bf16[192,1536]{1,0:T(8,128)(2,1)S(1)}, bf16[192,1536]{1,0:T(8,128)(2,1)S(1)}, u32[]{:S(2)}, u32[]{:S(2)}) collective-permute-start(bf16[192,1536]{1,0:T(8,128)(2,1)S(1)} %convolution_convert_fusion.3), channel_id=1, source_target_pairs={{0,4},{12,8},{1,5},{13,9},{2,6},{14,10},{3,7},{15,11},{16,20},{28,... | collective-permute-start | bytes 1769480 | tf_op jit(solution)/shard_map/ppermute | solution.py:335
  46.4 7.1 %collective-permute-start.18 = (bf16[96,2048]{1,0:T(8,128)(2,1)S(1)}, bf16[96,2048]{1,0:T(8,128)(2,1)S(1)}, u32[]{:S(2)}, u32[]{:S(2)}) collective-permute-start(bf16[96,2048]{1,0:T(8,128)(2,1)S(1)} %pad_maximum_fusion.7), channel_id=1, source_target_pairs={{0,1},{1,0},{2,3},{3,2},{4,5},{5,4},{6,7},{7,6},{8,9},{9,8},{10,11... | collective-permute-start | bytes 1179656 | tf_op jit(solution)/shard_map/ppermute | solution.py:325
  52.6 7.6 %collective-permute-start.16 = (bf16[192,2048]{1,0:T(8,128)(2,1)S(1)}, bf16[192,2048]{1,0:T(8,128)(2,1)S(1)}, u32[]{:S(2)}, u32[]{:S(2)}) collective-permute-start(bf16[192,2048]{1,0:T(8,128)(2,1)S(1)} %pad_maximum_fusion), channel_id=1, source_target_pairs={{0,1},{1,0},{2,3},{3,2},{4,5},{5,4},{6,7},{7,6},{8,9},{9,8},{10,11... | collective-permute-start | bytes 2359304 | tf_op jit(solution)/shard_map/ppermute | solution.py:325
  52.8 11.6 %collective-permute-start.15 = (bf16[96,2048]{1,0:T(8,128)(2,1)S(1)}, bf16[96,2048]{1,0:T(8,128)(2,1)S(1)}, u32[]{:S(2)}, u32[]{:S(2)}) collective-permute-start(bf16[96,2048]{1,0:T(8,128)(2,1)S(1)} %collective-permute-done.10), channel_id=1, source_target_pairs={{0,2},{1,3},{2,0},{3,1},{4,6},{5,7},{6,4},{7,5},{8,10},{9,11},{10,... | collective-permute-start | bytes 1179656 | tf_op jit(solution)/shard_map/ppermute | solution.py:314
  54.9 21.0 %collective-permute-start.24 = (bf16[192,1536]{1,0:T(8,128)(2,1)S(1)}, bf16[192,1536]{1,0:T(8,128)(2,1)S(1)}, u32[]{:S(2)}, u32[]{:S(2)}) collective-permute-start(bf16[192,1536]{1,0:T(8,128)(2,1)S(1)} %convolution_convert_fusion.2), channel_id=1, source_target_pairs={{0,4},{12,8},{1,5},{13,9},{2,6},{14,10},{3,7},{15,11},{16,20},{28,... | collective-permute-start | bytes 1769480 | tf_op jit(solution)/shard_map/ppermute | solution.py:335
  64.5 2.4 %collective-permute-start.19 = (bf16[192,2048]{1,0:T(8,128)(2,1)S(1)}, bf16[192,2048]{1,0:T(8,128)(2,1)S(1)}, u32[]{:S(2)}, u32[]{:S(2)}) collective-permute-start(bf16[192,2048]{1,0:T(8,128)(2,1)S(1)} %pad_maximum_fusion.1), channel_id=1, source_target_pairs={{0,1},{1,0},{2,3},{3,2},{4,5},{5,4},{6,7},{7,6},{8,9},{9,8},{10,11... | collective-permute-start | bytes 2359304 | tf_op jit(solution)/shard_map/ppermute | solution.py:325
  64.7 13.5 %collective-permute-start.22 = (bf16[96,1536]{1,0:T(8,128)(2,1)S(1)}, bf16[96,1536]{1,0:T(8,128)(2,1)S(1)}, u32[]{:S(2)}, u32[]{:S(2)}) collective-permute-start(bf16[96,1536]{1,0:T(8,128)(2,1)S(1)} %get-tuple-element.184), channel_id=1, source_target_pairs={{4,12},{8,0},{5,13},{9,1},{6,14},{10,2},{7,15},{11,3},{20,28},{24,... | collective-permute-start | bytes 884744 | tf_op jit(solution)/shard_map/ppermute | solution.py:350
  66.0 12.3 %collective-permute-start.23 = (bf16[96,1536]{1,0:T(8,128)(2,1)S(1)}, bf16[96,1536]{1,0:T(8,128)(2,1)S(1)}, u32[]{:S(2)}, u32[]{:S(2)}) collective-permute-start(bf16[96,1536]{1,0:T(8,128)(2,1)S(1)} %get-tuple-element.183), channel_id=1, source_target_pairs={{4,8},{8,4},{5,9},{9,5},{6,10},{10,6},{7,11},{11,7},{20,24},{24,20... | collective-permute-start | bytes 884744 | tf_op jit(solution)/shard_map/ppermute | solution.py:351
  66.9 16.4 %collective-permute-start.21 = (bf16[96,1536]{1,0:T(8,128)(2,1)S(1)}, bf16[96,1536]{1,0:T(8,128)(2,1)S(1)}, u32[]{:S(2)}, u32[]{:S(2)}) collective-permute-start(bf16[96,1536]{1,0:T(8,128)(2,1)S(1)} %slice.287), channel_id=1, source_target_pairs={{0,4},{4,0},{8,12},{12,8},{1,5},{5,1},{9,13},{13,9},{2,6},{6,2},{1... | collective-permute-start | bytes 884744 | tf_op jit(solution)/shard_map/ppermute | solution.py:343
  73.7 13.2 %collective-permute-start.20 = (bf16[96,2048]{1,0:T(8,128)(2,1)S(1)}, bf16[96,2048]{1,0:T(8,128)(2,1)S(1)}, u32[]{:S(2)}, u32[]{:S(2)}) collective-permute-start(bf16[96,2048]{1,0:T(8,128)(2,1)S(1)} %collective-permute-done.9), channel_id=1, source_target_pairs={{0,2},{1,3},{2,0},{3,1},{4,6},{5,7},{6,4},{7,5},{8,10},{9,11},{10,... | collective-permute-start | bytes 1179656 | tf_op jit(solution)/shard_map/ppermute | solution.py:314
  75.9 16.4 %collective-permute-start.26 = (bf16[192,1536]{1,0:T(8,128)(2,1)S(1)}, bf16[192,1536]{1,0:T(8,128)(2,1)S(1)}, u32[]{:S(2)}, u32[]{:S(2)}) collective-permute-start(bf16[192,1536]{1,0:T(8,128)(2,1)S(1)} %convolution_convert_fusion.1), channel_id=1, source_target_pairs={{0,4},{12,8},{1,5},{13,9},{2,6},{14,10},{3,7},{15,11},{16,20},{28,... | collective-permute-start | bytes 1769480 | tf_op jit(solution)/shard_map/ppermute | solution.py:335
  78.2 30.6 %collective-permute-start.29 = (bf16[96,1536]{1,0:T(8,128)(2,1)S(1)}, bf16[96,1536]{1,0:T(8,128)(2,1)S(1)}, u32[]{:S(2)}, u32[]{:S(2)}) collective-permute-start(bf16[96,1536]{1,0:T(8,128)(2,1)S(1)} %slice.286), channel_id=1, source_target_pairs={{0,4},{4,0},{8,12},{12,8},{1,5},{5,1},{9,13},{13,9},{2,6},{6,2},{1... | collective-permute-start | bytes 884744 | tf_op jit(solution)/shard_map/ppermute | solution.py:343
  83.3 19.4 %collective-permute-start.30 = (bf16[96,1536]{1,0:T(8,128)(2,1)S(1)}, bf16[96,1536]{1,0:T(8,128)(2,1)S(1)}, u32[]{:S(2)}, u32[]{:S(2)}) collective-permute-start(bf16[96,1536]{1,0:T(8,128)(2,1)S(1)} %get-tuple-element.182), channel_id=1, source_target_pairs={{4,12},{8,0},{5,13},{9,1},{6,14},{10,2},{7,15},{11,3},{20,28},{24,... | collective-permute-start | bytes 884744 | tf_op jit(solution)/shard_map/ppermute | solution.py:350
  84.6 18.8 %collective-permute-start.31 = (bf16[96,1536]{1,0:T(8,128)(2,1)S(1)}, bf16[96,1536]{1,0:T(8,128)(2,1)S(1)}, u32[]{:S(2)}, u32[]{:S(2)}) collective-permute-start(bf16[96,1536]{1,0:T(8,128)(2,1)S(1)} %get-tuple-element.181), channel_id=1, source_target_pairs={{4,8},{8,4},{5,9},{9,5},{6,10},{10,6},{7,11},{11,7},{20,24},{24,20... | collective-permute-start | bytes 884744 | tf_op jit(solution)/shard_map/ppermute | solution.py:351
  87.1 11.2 %collective-permute-start.25 = (bf16[192,2048]{1,0:T(8,128)(2,1)S(1)}, bf16[192,2048]{1,0:T(8,128)(2,1)S(1)}, u32[]{:S(2)}, u32[]{:S(2)}) collective-permute-start(bf16[192,2048]{1,0:T(8,128)(2,1)S(1)} %pad_maximum_fusion.2), channel_id=1, source_target_pairs={{0,1},{1,0},{2,3},{3,2},{4,5},{5,4},{6,7},{7,6},{8,9},{9,8},{10,11... | collective-permute-start | bytes 2359304 | tf_op jit(solution)/shard_map/ppermute | solution.py:325
  93.9 18.2 %collective-permute-start.28 = (bf16[192,1536]{1,0:T(8,128)(2,1)S(1)}, bf16[192,1536]{1,0:T(8,128)(2,1)S(1)}, u32[]{:S(2)}, u32[]{:S(2)}) collective-permute-start(bf16[192,1536]{1,0:T(8,128)(2,1)S(1)} %convolution_convert_fusion), channel_id=1, source_target_pairs={{0,4},{12,8},{1,5},{13,9},{2,6},{14,10},{3,7},{15,11},{16,20},{28,... | collective-permute-start | bytes 1769480 | tf_op jit(solution)/shard_map/ppermute | solution.py:335
  98.4 15.9 %collective-permute-start.35 = (bf16[96,1536]{1,0:T(8,128)(2,1)S(1)}, bf16[96,1536]{1,0:T(8,128)(2,1)S(1)}, u32[]{:S(2)}, u32[]{:S(2)}) collective-permute-start(bf16[96,1536]{1,0:T(8,128)(2,1)S(1)} %get-tuple-element.178), channel_id=1, source_target_pairs={{4,12},{8,0},{5,13},{9,1},{6,14},{10,2},{7,15},{11,3},{20,28},{24,... | collective-permute-start | bytes 884744 | tf_op jit(solution)/shard_map/ppermute | solution.py:350
  102.6 17.1 %collective-permute-start.36 = (bf16[96,1536]{1,0:T(8,128)(2,1)S(1)}, bf16[96,1536]{1,0:T(8,128)(2,1)S(1)}, u32[]{:S(2)}, u32[]{:S(2)}) collective-permute-start(bf16[96,1536]{1,0:T(8,128)(2,1)S(1)} %get-tuple-element.177), channel_id=1, source_target_pairs={{4,8},{8,4},{5,9},{9,5},{6,10},{10,6},{7,11},{11,7},{20,24},{24,20... | collective-permute-start | bytes 884744 | tf_op jit(solution)/shard_map/ppermute | solution.py:351
  103.3 16.4 %collective-permute-start.34 = (bf16[96,1536]{1,0:T(8,128)(2,1)S(1)}, bf16[96,1536]{1,0:T(8,128)(2,1)S(1)}, u32[]{:S(2)}, u32[]{:S(2)}) collective-permute-start(bf16[96,1536]{1,0:T(8,128)(2,1)S(1)} %slice.285), channel_id=1, source_target_pairs={{0,4},{4,0},{8,12},{12,8},{1,5},{5,1},{9,13},{13,9},{2,6},{6,2},{1... | collective-permute-start | bytes 884744 | tf_op jit(solution)/shard_map/ppermute | solution.py:343
  112.2 12.4 %collective-permute-start.32 = (bf16[96,1536]{1,0:T(8,128)(2,1)S(1)}, bf16[96,1536]{1,0:T(8,128)(2,1)S(1)}, u32[]{:S(2)}, u32[]{:S(2)}) collective-permute-start(bf16[96,1536]{1,0:T(8,128)(2,1)S(1)} %get-tuple-element.180), channel_id=1, source_target_pairs={{4,12},{8,0},{5,13},{9,1},{6,14},{10,2},{7,15},{11,3},{20,28},{24,... | collective-permute-start | bytes 884744 | tf_op jit(solution)/shard_map/ppermute | solution.py:350
  113.5 11.1 %collective-permute-start.33 = (bf16[96,1536]{1,0:T(8,128)(2,1)S(1)}, bf16[96,1536]{1,0:T(8,128)(2,1)S(1)}, u32[]{:S(2)}, u32[]{:S(2)}) collective-permute-start(bf16[96,1536]{1,0:T(8,128)(2,1)S(1)} %get-tuple-element.179), channel_id=1, source_target_pairs={{4,8},{8,4},{5,9},{9,5},{6,10},{10,6},{7,11},{11,7},{20,24},{24,20... | collective-permute-start | bytes 884744 | tf_op jit(solution)/shard_map/ppermute | solution.py:351
  114.2 13.6 %collective-permute-start.27 = (bf16[96,1536]{1,0:T(8,128)(2,1)S(1)}, bf16[96,1536]{1,0:T(8,128)(2,1)S(1)}, u32[]{:S(2)}, u32[]{:S(2)}) collective-permute-start(bf16[96,1536]{1,0:T(8,128)(2,1)S(1)} %slice.284), channel_id=1, source_target_pairs={{0,4},{4,0},{8,12},{12,8},{1,5},{5,1},{9,13},{13,9},{2,6},{6,2},{1... | collective-permute-start | bytes 884744 | tf_op jit(solution)/shard_map/ppermute | solution.py:343

commit v7 on v6

--- a/solution.py
+++ b/solution.py
@@ -11,17 +11,17 @@
 D = 8192
 HEAD_DIM = 128
 ORDER = ((3, 2, 1, 0), (3, 2, 0, 1), (0, 1, 3, 2), (0, 1, 2, 3))
-SIZES = (48, 48, 48, 48)
+SIZES = (48, 64, 48, 32)
 FAR = ((0,), (1,), (2, 3))
 NEAR = ((0, 1), (2, 3))
 TURNS = (
     "a0",
     "n",
     "s0",
+    "a2",
     "a1",
     "s1",
     "z0",
-    "a2",
     "x0",
     "x1",
     "s2",

time: 131 us -> 131 us (level)
  waiting for transfers between devices: 36 us -> 31.9 us
  starting transfers between devices: 66.5 us -> 69.1 us
    ppermute x4, waiting for transfers between devices: 8.2 us -> 3.68 us  [multiply_near(): lax.ppermute(inner, 'fsdp', [(0, 1), (1, 0), (2, 3), (3, 2)])]
    ppermute x4, starting transfers between devices: 12.2 us -> 15.1 us  [multiply(): state[n]['p'] = (outer, lax.ppermute(outer, 'fsdp', outer_in))]
    ppermute x5, starting transfers between devices: 2.18 us -> 5 us  [cross(): moved[part, g] = (mine, lax.ppermute(mine, 'tensor', swap_x))]
    ppermute x4, waiting for transfers between devices: 3.03 us -> 0.97 us  [forward(): far_sum = lax.ppermute(passed[:half], 'fsdp', [(1, 3), (2, 0)])]
    ppermute x3, waiting for transfers between devices: 1 us -> 2.68 us  [across(): lax.ppermute(joined([rows[leaves[n]] for n in FAR[g]]), 'tensor', swap_x)]
    ppermute x3, starting transfers between devices: 11.8 us -> 10.4 us  [send(): moved[0, g] = lax.ppermute(far, both, toward(True))]
    ppermute x5, starting transfers between devices: 3.03 us -> 1.7 us  [share(): theirs = lax.ppermute(mine, 'tensor', swap_core)]
  transfers between devices with their start and end apart: 37 -> 37, of which waited for: 12 -> 11; matrix products, arithmetic and copies ran while one was open for 13% -> 13% of each run, Pallas kernels for 4% -> 4%
where the time goes in v7:
time: 131 us
  starting transfers between devices  69.1 us (53%)
  waiting for transfers between devices  31.9 us (24%)
  matrix products  11.3 us (9%)
  Pallas kernels  8.21 us (6%)
  other arithmetic  5.65 us (4%)
  local copies, waits for them, and re-layouts  3.28 us (3%)
    ppermute x4, starting transfers between devices, multiply_near(): lax.ppermute(inner, 'fsdp', [(0, 1), (1, 0), (2, 3), (3, 2)])  16.3 us
    ppermute x4, starting transfers between devices, multiply(): state[n]['p'] = (outer, lax.ppermute(outer, 'fsdp', outer_in))  15.1 us
    ppermute x3, starting transfers between devices, send(): moved[0, g] = lax.ppermute(far, both, toward(True))  10.4 us
    ppermute x4, waiting for transfers between devices, multiply(): state[n]['p'] = (outer, lax.ppermute(outer, 'fsdp', outer_in))  9.67 us
    pallas_call x4, Pallas kernels, attend_piece(): pl.pallas_call(functools.partial(attend_kernel, start), in_specs=[here] *...  8.21 us
    ppermute x5, waiting for transfers between devices, cross(): moved[part, g] = (mine, lax.ppermute(mine, 'tensor', swap_x))  7.64 us
    dot_general x4, matrix products, multiply_near(): part = jnp.dot(rows, weight, preferred_element_type=jnp.float32)  5.65 us
    dot_general x4, matrix products, multiply(): jnp.dot(rows, weight, preferred_element_type=jnp.float32)  5.61 us
  transfers between devices with their start and end apart: 37, of which 11 were waited for; matrix products, arithmetic and copies ran while one was open for 13% of the time, Pallas kernels for 4%

profile of v7, /device:TPU:0, one launch (start us, length us, event | category | flops | bytes accessed | tf_op | source)
XLA Modules:
  0.0 130.6 jit_solution(12372788628745565107)
XLA Ops:
  0.0 1.9 %fusion = f32[384]{0:T(512)S(1)} fusion(bf16[384,2048]{1,0:T(8,128)(2,1)} %param.5), kind=kLoop, calls=%fused_computation.2 | loop fusion | flops 2358912 | bytes 1574400 | tf_op jit(solution)/shard_map/reduce_sum | solution.py:236
  1.9 0.5 collective-permute-start.1
  2.4 2.6 %collective-permute-start.2 = (f32[384]{0:T(512)S(1)}, f32[384]{0:T(512)S(1)}, u32[]{:S(2)}, u32[]{:S(2)}) collective-permute-start(f32[384]{0:T(512)S(1)} %fusion), channel_id=1, source_target_pairs={{0,3},{1,2},{2,1},{3,0},{4,7},{5,6},{6,5},{7,4},{8,11},{9,10},{10,... | collective-permute-start | bytes 4616 | tf_op jit(solution)/shard_map/ppermute | solution.py:239
  5.2 2.1 %collective-permute-start = (f32[2432]{0:T(1024)S(1)}, f32[2432]{0:T(1024)S(1)}, u32[]{:S(2)}, u32[]{:S(2)}) collective-permute-start(f32[2432]{0:T(1024)S(1)} %pad_maximum_fusion.16), channel_id=1, source_target_pairs={{0,2},{1,3},{2,0},{3,1},{4,6},{5,7},{6,4},{7,5},{8,10},{9,11},{10,... | collective-permute-start | bytes 29192 | tf_op jit(solution)/shard_map/ppermute | solution.py:241
  7.4 0.3 reduce-window.9
  8.1 0.8 fusion.55
  8.8 0.2 pad_maximum_fusion.14
  9.2 3.1 %collective-permute-done = f32[2432]{0:T(1024)S(1)} collective-permute-done((f32[2432]{0:T(1024)S(1)}, f32[2432]{0:T(1024)S(1)}, u32[]{:S(2)}, u32[]{:S(2)}) %collective-permute-start) | collective-permute-done | bytes 9760 | tf_op jit(solution)/shard_map/ppermute | solution.py:241
  12.4 0.4 fusion.2
  13.0 0.4 collective-permute-start.5
  13.5 2.8 %collective-permute-start.7 = (bf16[48,2048]{1,0:T(8,128)(2,1)S(1)}, bf16[48,2048]{1,0:T(8,128)(2,1)S(1)}, u32[]{:S(2)}, u32[]{:S(2)}) collective-permute-start(bf16[48,2048]{1,0:T(8,128)(2,1)S(1)} %multiply_convert_fusion.1), channel_id=1, source_target_pairs={{0,8},{1,12},{2,10},{3,14},{4,9},{5,13},{6,11},{7,15},{8,1},{9,5},... | collective-permute-start | bytes 589832 | tf_op jit(solution)/shard_map/ppermute | solution.py:304
  16.4 1.5 %collective-permute-start.4 = (bf16[80,2048]{1,0:T(8,128)(2,1)S(1)}, bf16[80,2048]{1,0:T(8,128)(2,1)S(1)}, u32[]{:S(2)}, u32[]{:S(2)}) collective-permute-start(bf16[80,2048]{1,0:T(8,128)(2,1)S(1)} %pad_maximum_fusion.11), channel_id=1, source_target_pairs={{0,2},{1,3},{2,0},{3,1},{4,6},{5,7},{6,4},{7,5},{8,10},{9,11},{10,... | collective-permute-start | bytes 983048 | tf_op jit(solution)/shard_map/ppermute | solution.py:269
  18.1 2.7 %collective-permute-done.5 = bf16[64,2048]{1,0:T(8,128)(2,1)S(1)} collective-permute-done((bf16[64,2048]{1,0:T(8,128)(2,1)S(1)}, bf16[64,2048]{1,0:T(8,128)(2,1)S(1)}, u32[]{:S(2)}, u32[]{:S(2)}) %collective-permute-start.5) | collective-permute-done | bytes 262176 | tf_op jit(solution)/shard_map/ppermute | solution.py:269
  20.8 4.2 %collective-permute-start.6 = (bf16[64,2048]{1,0:T(8,128)(2,1)S(1)}, bf16[64,2048]{1,0:T(8,128)(2,1)S(1)}, u32[]{:S(2)}, u32[]{:S(2)}) collective-permute-start(bf16[64,2048]{1,0:T(8,128)(2,1)S(1)} %get-tuple-element.179), channel_id=1, source_target_pairs={{0,8},{1,12},{2,10},{3,14},{4,9},{5,13},{6,11},{7,15},{8,1},{9,5},... | collective-permute-start | bytes 786440 | tf_op jit(solution)/shard_map/ppermute | solution.py:304
  25.1 3.3 %collective-permute-start.11 = (bf16[112,2048]{1,0:T(8,128)(2,1)S(1)}, bf16[112,2048]{1,0:T(8,128)(2,1)S(1)}, u32[]{:S(2)}, u32[]{:S(2)}) collective-permute-start(bf16[112,2048]{1,0:T(8,128)(2,1)S(1)} %pad_maximum_fusion.5), channel_id=1, source_target_pairs={{0,1},{1,4},{2,3},{3,6},{4,0},{5,5},{6,2},{7,7},{8,9},{9,12},{10,1... | collective-permute-start | bytes 1376264 | tf_op jit(solution)/shard_map/ppermute | solution.py:309
  28.4 0.6 collective-permute-start.8
  29.0 4.1 %collective-permute-done.6 = bf16[64,2048]{1,0:T(8,128)(2,1)S(1)} collective-permute-done((bf16[64,2048]{1,0:T(8,128)(2,1)S(1)}, bf16[64,2048]{1,0:T(8,128)(2,1)S(1)}, u32[]{:S(2)}, u32[]{:S(2)}) %collective-permute-start.6) | collective-permute-done | bytes 262176 | tf_op jit(solution)/shard_map/ppermute | solution.py:304
  33.1 0.6 collective-permute-start.13
  33.7 3.4 %collective-permute-start.10 = (bf16[80,2048]{1,0:T(8,128)(2,1)S(1)}, bf16[80,2048]{1,0:T(8,128)(2,1)S(1)}, u32[]{:S(2)}, u32[]{:S(2)}) collective-permute-start(bf16[80,2048]{1,0:T(8,128)(2,1)S(1)} %get-tuple-element.172), channel_id=1, source_target_pairs={{0,8},{1,12},{2,10},{3,14},{4,9},{5,13},{6,11},{7,15},{8,1},{9,5},... | collective-permute-start | bytes 983048 | tf_op jit(solution)/shard_map/ppermute | solution.py:304
  37.2 0.1 collective-permute-start.14
  37.4 0.4 constant_dynamic-update-slice_fusion.1
  37.8 1.0 copy-done.3
  38.8 0.5 copy.13
  39.5 2.0 %collective-permute-start.9 = (bf16[80,2048]{1,0:T(8,128)(2,1)S(1)}, bf16[80,2048]{1,0:T(8,128)(2,1)S(1)}, u32[]{:S(2)}, u32[]{:S(2)}) collective-permute-start(bf16[80,2048]{1,0:T(8,128)(2,1)S(1)} %get-tuple-element.96), channel_id=1, source_target_pairs={{0,1},{1,4},{2,3},{3,6},{4,0},{5,5},{6,2},{7,7},{8,9},{9,12},{10,1... | collective-permute-start | bytes 983048 | tf_op jit(solution)/shard_map/ppermute | solution.py:309
  41.5 1.3 collective-permute-start.12
  42.8 1.4 %convolution_convert_fusion.2 = bf16[192,1536]{1,0:T(8,128)(2,1)S(1)} fusion(bf16[2048,1536]{1,0:T(8,128)(2,1)S(1)} %constant_dynamic-update-slice_fusion, bf16[96,2048]{1,0:T(8,128)(2,1)S(1)} %collective-permute-done.14, bf16[96,2048]{1,0:T(8,128)(2,1)S(1)} %pad_maximum_fusion.6, pred[]{:T(512)S(6)} %eq.5), kind=kOutput, calls=%fused_computation.7 | convolution fusion | flops 1211793408 | bytes 7667713 | tf_op jit(solution)/shard_map/dot_general | solution.py:333
  44.2 3.8 %collective-permute-start.17 = (bf16[192,1536]{1,0:T(8,128)(2,1)S(1)}, bf16[192,1536]{1,0:T(8,128)(2,1)S(1)}, u32[]{:S(2)}, u32[]{:S(2)}) collective-permute-start(bf16[192,1536]{1,0:T(8,128)(2,1)S(1)} %convolution_convert_fusion.2), channel_id=1, source_target_pairs={{0,4},{12,8},{1,5},{13,9},{2,6},{14,10},{3,7},{15,11},{16,20},{28,... | collective-permute-start | bytes 1769480 | tf_op jit(solution)/shard_map/ppermute | solution.py:335
  48.2 5.3 %collective-permute-done.12 = bf16[112,2048]{1,0:T(8,128)(2,1)S(1)} collective-permute-done((bf16[112,2048]{1,0:T(8,128)(2,1)S(1)}, bf16[112,2048]{1,0:T(8,128)(2,1)S(1)}, u32[]{:S(2)}, u32[]{:S(2)}) %collective-permute-start.12) | collective-permute-done | bytes 458784 | tf_op jit(solution)/shard_map/ppermute | solution.py:314
  53.7 1.3 %collective-permute-start.16 = (bf16[224,2048]{1,0:T(8,128)(2,1)S(1)}, bf16[224,2048]{1,0:T(8,128)(2,1)S(1)}, u32[]{:S(2)}, u32[]{:S(2)}) collective-permute-start(bf16[224,2048]{1,0:T(8,128)(2,1)S(1)} %pad_maximum_fusion), channel_id=1, source_target_pairs={{0,1},{1,0},{2,3},{3,2},{4,5},{5,4},{6,7},{7,6},{8,9},{9,8},{10,11... | collective-permute-start | bytes 2752520 | tf_op jit(solution)/shard_map/ppermute | solution.py:325
  55.1 1.3 collective-permute-start.15
  56.4 1.8 %convolution_convert_fusion = bf16[256,1536]{1,0:T(8,128)(2,1)S(1)} fusion(bf16[2048,1536]{1,0:T(8,128)(2,1)S(1)} %constant_dynamic-update-slice_fusion, bf16[128,2048]{1,0:T(8,128)(2,1)S(1)} %collective-permute-done.18, bf16[128,2048]{1,0:T(8,128)(2,1)S(1)} %pad_maximum_fusion.3, pred[]{:T(512)S(6)} %eq.5), kind=kOutput, calls=%fused_computation.5 | convolution fusion | flops 1615724544 | bytes 8126465 | tf_op jit(solution)/shard_map/dot_general | solution.py:333
  58.2 2.4 %collective-permute-start.24 = (bf16[256,1536]{1,0:T(8,128)(2,1)S(1)}, bf16[256,1536]{1,0:T(8,128)(2,1)S(1)}, u32[]{:S(2)}, u32[]{:S(2)}) collective-permute-start(bf16[256,1536]{1,0:T(8,128)(2,1)S(1)} %convolution_convert_fusion), channel_id=1, source_target_pairs={{0,4},{12,8},{1,5},{13,9},{2,6},{14,10},{3,7},{15,11},{16,20},{28,... | collective-permute-start | bytes 2359304 | tf_op jit(solution)/shard_map/ppermute | solution.py:335
  60.8 0.1 add.40
  61.0 1.4 %fusion.21 = f32[192,1536]{1,0:T(8,128)S(1)} fusion(bf16[2048,1536]{1,0:T(8,128)(2,1)S(1)} %constant_dynamic-update-slice_fusion, bf16[96,2048]{1,0:T(8,128)(2,1)S(1)} %slice.241, bf16[96,2048]{1,0:T(8,128)(2,1)S(1)} %pad_maximum_fusion.7, pred[]{:T(512)S(6)} %eq.5), kind=kOutput, calls=%fused_computation.33 | convolution fusion | flops 1211498496 | bytes 8257537 | tf_op jit(solution)/shard_map/dot_general | solution.py:339
  62.5 2.3 %collective-permute-done.15 = bf16[80,2048]{1,0:T(8,128)(2,1)S(1)} collective-permute-done((bf16[80,2048]{1,0:T(8,128)(2,1)S(1)}, bf16[80,2048]{1,0:T(8,128)(2,1)S(1)}, u32[]{:S(2)}, u32[]{:S(2)}) %collective-permute-start.15) | collective-permute-done | bytes 327712 | tf_op jit(solution)/shard_map/ppermute | solution.py:314
  65.2 1.3 collective-permute-start.22
  66.5 0.9 collective-permute-start.23
  67.5 5.4 %collective-permute-start.21 = (bf16[96,1536]{1,0:T(8,128)(2,1)S(1)}, bf16[96,1536]{1,0:T(8,128)(2,1)S(1)}, u32[]{:S(2)}, u32[]{:S(2)}) collective-permute-start(bf16[96,1536]{1,0:T(8,128)(2,1)S(1)} %slice.286), channel_id=1, source_target_pairs={{0,4},{4,0},{8,12},{12,8},{1,5},{5,1},{9,13},{13,9},{2,6},{6,2},{1... | collective-permute-start | bytes 884744 | tf_op jit(solution)/shard_map/ppermute | solution.py:343
  72.9 1.4 %convolution_convert_fusion.1 = bf16[192,1536]{1,0:T(8,128)(2,1)S(1)} fusion(bf16[2048,1536]{1,0:T(8,128)(2,1)S(1)} %constant_dynamic-update-slice_fusion, bf16[96,2048]{1,0:T(8,128)(2,1)S(1)} %slice.247, bf16[96,2048]{1,0:T(8,128)(2,1)S(1)} %pad_maximum_fusion.8, pred[]{:T(512)S(6)} %eq.5), kind=kOutput, calls=%fused_computation.6 | convolution fusion | flops 1211793408 | bytes 7667713 | tf_op jit(solution)/shard_map/dot_general | solution.py:333
  74.3 1.3 collective-permute-start.20
  75.6 1.8 %fusion.8 = f32[256,1536]{1,0:T(8,128)S(1)} fusion(bf16[2048,1536]{1,0:T(8,128)(2,1)S(1)} %constant_dynamic-update-slice_fusion, bf16[128,2048]{1,0:T(8,128)(2,1)S(1)} %slice-done, bf16[128,2048]{1,0:T(8,128)(2,1)S(1)} %pad_maximum_fusion.4, pred[]{:T(512)S(6)} %eq.5), kind=kOutput, calls=%fused_computation.16 | convolution fusion | flops 1615331328 | bytes 8912897 | tf_op jit(solution)/shard_map/dot_general | solution.py:339
  77.5 1.0 collective-permute-done.24
  78.5 4.4 %collective-permute-start.26 = (bf16[192,1536]{1,0:T(8,128)(2,1)S(1)}, bf16[192,1536]{1,0:T(8,128)(2,1)S(1)}, u32[]{:S(2)}, u32[]{:S(2)}) collective-permute-start(bf16[192,1536]{1,0:T(8,128)(2,1)S(1)} %convolution_convert_fusion.1), channel_id=1, source_target_pairs={{0,4},{12,8},{1,5},{13,9},{2,6},{14,10},{3,7},{15,11},{16,20},{28,... | collective-permute-start | bytes 1769480 | tf_op jit(solution)/shard_map/ppermute | solution.py:335
  82.9 0.2 add.41
  83.2 1.6 %collective-permute-done.21.refs_1_ = bf16[96,1536]{1,0:T(8,128)(2,1)S(1)} collective-permute-done((bf16[96,1536]{1,0:T(8,128)(2,1)S(1)}, bf16[96,1536]{1,0:T(8,128)(2,1)S(1)}, u32[]{:S(2)}, u32[]{:S(2)}) %collective-permute-start.21) | collective-permute-done | bytes 294944 | tf_op jit(solution)/shard_map/ppermute | solution.py:343
  84.9 1.3 collective-permute-start.30
  86.2 0.7 collective-permute-start.31
  86.9 1.6 %shard_map.55 = (bf16[384,1024]{1,0:T(8,128)(2,1)}, bf16[2,384,256]{2,1,0:T(8,128)(2,1)S(1)}) custom-call(f32[96,1536]{1,0:T(8,128)S(1)} %slice.248.refs_0_, bf16[96,1536]{1,0:T(8,128)(2,1)S(1)} %collective-permute-done.21.refs_1_, bf16[96,1536]{1,0:T(8,128)(2,1)S(1)} %collective-permute-done.22.refs_2_, ...), custom_call_target="tpu_custom_call" | custom-call | tf_op jit(solution)/shard_map/pallas_call | solution.py:203
  88.9 8.6 %collective-permute-done.26 = bf16[192,1536]{1,0:T(8,128)(2,1)S(1)} collective-permute-done((bf16[192,1536]{1,0:T(8,128)(2,1)S(1)}, bf16[192,1536]{1,0:T(8,128)(2,1)S(1)}, u32[]{:S(2)}, u32[]{:S(2)}) %collective-permute-start.26) | collective-permute-done | bytes 589856 | tf_op jit(solution)/shard_map/ppermute | solution.py:335
  97.6 1.0 convolution_convert_fusion.3
  98.6 4.4 %collective-permute-start.28 = (bf16[128,1536]{1,0:T(8,128)(2,1)S(1)}, bf16[128,1536]{1,0:T(8,128)(2,1)S(1)}, u32[]{:S(2)}, u32[]{:S(2)}) collective-permute-start(bf16[128,1536]{1,0:T(8,128)(2,1)S(1)} %convolution_convert_fusion.3), channel_id=1, source_target_pairs={{0,4},{12,8},{1,5},{13,9},{2,6},{14,10},{3,7},{15,11},{16,20},{28,... | collective-permute-start | bytes 1179656 | tf_op jit(solution)/shard_map/ppermute | solution.py:335
  103.1 1.3 collective-permute-start.35
  104.5 1.4 %fusion.32 = f32[192,1536]{1,0:T(8,128)S(1)} fusion(bf16[2048,1536]{1,0:T(8,128)(2,1)S(1)} %constant_dynamic-update-slice_fusion, bf16[96,2048]{1,0:T(8,128)(2,1)S(1)} %slice.258, bf16[96,2048]{1,0:T(8,128)(2,1)S(1)} %pad_maximum_fusion.9, pred[]{:T(512)S(6)} %eq.5), kind=kOutput, calls=%fused_computation.46 | convolution fusion | flops 1211498496 | bytes 8257537 | tf_op jit(solution)/shard_map/dot_general | solution.py:339
  106.0 1.0 fusion.47
  107.0 0.7 collective-permute-start.36
  107.7 5.4 %collective-permute-start.34 = (bf16[96,1536]{1,0:T(8,128)(2,1)S(1)}, bf16[96,1536]{1,0:T(8,128)(2,1)S(1)}, u32[]{:S(2)}, u32[]{:S(2)}) collective-permute-start(bf16[96,1536]{1,0:T(8,128)(2,1)S(1)} %slice.285), channel_id=1, source_target_pairs={{0,4},{4,0},{8,12},{12,8},{1,5},{5,1},{9,13},{13,9},{2,6},{6,2},{1... | collective-permute-start | bytes 884744 | tf_op jit(solution)/shard_map/ppermute | solution.py:343
  113.1 2.3 %shard_map.56 = (bf16[384,1024]{1,0:T(8,128)(2,1)}, bf16[2,384,256]{2,1,0:T(8,128)(2,1)S(1)}) custom-call(f32[128,1536]{1,0:T(8,128)S(1)} %slice.263.refs_0_, bf16[128,1536]{1,0:T(8,128)(2,1)S(1)} %collective-permute-done.29.refs_1_, bf16[128,1536]{1,0:T(8,128)(2,1)S(1)} %collective-permute-done.30.refs_2_, ...), custom_call_target="tpu_custom_call", output_to_operand_aliasing={{0}: (9, {})} | custom-call | tf_op jit(solution)/shard_map/pallas_call | solution.py:203
  115.6 1.3 collective-permute-start.32
  116.9 0.7 collective-permute-start.33
  117.6 5.4 %collective-permute-start.27 = (bf16[64,1536]{1,0:T(8,128)(2,1)S(1)}, bf16[64,1536]{1,0:T(8,128)(2,1)S(1)}, u32[]{:S(2)}, u32[]{:S(2)}) collective-permute-start(bf16[64,1536]{1,0:T(8,128)(2,1)S(1)} %slice.287), channel_id=1, source_target_pairs={{0,4},{4,0},{8,12},{12,8},{1,5},{5,1},{9,13},{13,9},{2,6},{6,2},{1... | collective-permute-start | bytes 589832 | tf_op jit(solution)/shard_map/ppermute | solution.py:343
  123.1 1.9 %shard_map.57 = (bf16[384,1024]{1,0:T(8,128)(2,1)}, bf16[2,384,256]{2,1,0:T(8,128)(2,1)S(1)}) custom-call(f32[96,1536]{1,0:T(8,128)S(1)} %slice.268.refs_0_, bf16[96,1536]{1,0:T(8,128)(2,1)S(1)} %collective-permute-done.34.refs_1_, bf16[96,1536]{1,0:T(8,128)(2,1)S(1)} %collective-permute-done.35.refs_2_, ...), custom_call_target="tpu_custom_call", output_to_operand_aliasing={{0}: (9, {})} | custom-call | tf_op jit(solution)/shard_map/pallas_call | solution.py:203
  124.9 1.0 collective-permute-done.32.refs_2_
  125.9 2.1 %collective-permute-done.27.refs_1_ = bf16[64,1536]{1,0:T(8,128)(2,1)S(1)} collective-permute-done((bf16[64,1536]{1,0:T(8,128)(2,1)S(1)}, bf16[64,1536]{1,0:T(8,128)(2,1)S(1)}, u32[]{:S(2)}, u32[]{:S(2)}) %collective-permute-start.27) | collective-permute-done | bytes 196640 | tf_op jit(solution)/shard_map/ppermute | solution.py:343
  128.0 2.5 %shard_map.58 = (bf16[384,1024]{1,0:T(8,128)(2,1)}, bf16[2,384,256]{2,1,0:T(8,128)(2,1)}) custom-call(f32[64,1536]{1,0:T(8,128)S(1)} %slice.261.refs_0_, bf16[64,1536]{1,0:T(8,128)(2,1)S(1)} %collective-permute-done.27.refs_1_, bf16[64,1536]{1,0:T(8,128)(2,1)S(1)} %collective-permute-done.32.refs_2_, ...), custom_call_target="tpu_custom_call", output_to_operand_aliasing={{0}: (9, {})} | custom-call | tf_op jit(solution)/shard_map/pallas_call | solution.py:203
  (122 shorter events, 3.6 us)
Async XLA Ops:
  0.0 5.0 %copy-start.1 = (bf16[384,2048]{1,0:T(8,128)(2,1)S(1)}, bf16[384,2048]{1,0:T(8,128)(2,1)}, u32[]{:S(2)}) copy-start(bf16[384,2048]{1,0:T(8,128)(2,1)} %param.5) | copy-start | bytes 4718596
  0.0 5.2 %copy-start.6 = (bf16[2048]{0:T(1024)(128)(2,1)S(1)}, bf16[2048]{0:T(1024)(128)(2,1)}, u32[]{:S(2)}) copy-start(bf16[2048]{0:T(1024)(128)(2,1)} %param.6) | copy-start | bytes 12292
  0.0 7.3 %copy-start = (s32[1,384]{1,0:T(1,128)S(1)}, s32[1,384]{1,0:T(1,128)}, u32[]{:S(2)}) copy-start(s32[1,384]{1,0:T(1,128)} %refs_7_.7) | copy-start | bytes 4612
  1.9 10.4 %collective-permute-start.1 = (f32[384]{0:T(512)S(1)}, f32[384]{0:T(512)S(1)}, u32[]{:S(2)}, u32[]{:S(2)}) collective-permute-start(f32[384]{0:T(512)S(1)} %fusion), channel_id=1, source_target_pairs={{0,1},{1,0},{2,3},{3,2},{4,5},{5,4},{6,7},{7,6},{8,9},{9,8},{10,11... | collective-permute-start | bytes 4616 | tf_op jit(solution)/shard_map/ppermute | solution.py:239
  2.4 9.9 %collective-permute-start.2 = (f32[384]{0:T(512)S(1)}, f32[384]{0:T(512)S(1)}, u32[]{:S(2)}, u32[]{:S(2)}) collective-permute-start(f32[384]{0:T(512)S(1)} %fusion), channel_id=1, source_target_pairs={{0,3},{1,2},{2,1},{3,0},{4,7},{5,6},{6,5},{7,4},{8,11},{9,10},{10,... | collective-permute-start | bytes 4616 | tf_op jit(solution)/shard_map/ppermute | solution.py:239
  5.1 7.2 %collective-permute-start.3 = (bf16[48,2048]{1,0:T(8,128)(2,1)S(1)}, bf16[48,2048]{1,0:T(8,128)(2,1)S(1)}, u32[]{:S(2)}, u32[]{:S(2)}) collective-permute-start(bf16[48,2048]{1,0:T(8,128)(2,1)S(1)} %get-tuple-element.161), channel_id=1, source_target_pairs={{0,2},{1,3},{2,0},{3,1},{4,6},{5,7},{6,4},{7,5},{8,10},{9,11},{10,... | collective-permute-start | bytes 589832 | tf_op jit(solution)/shard_map/ppermute | solution.py:269
  5.2 7.1 %collective-permute-start = (f32[2432]{0:T(1024)S(1)}, f32[2432]{0:T(1024)S(1)}, u32[]{:S(2)}, u32[]{:S(2)}) collective-permute-start(f32[2432]{0:T(1024)S(1)} %pad_maximum_fusion.16), channel_id=1, source_target_pairs={{0,2},{1,3},{2,0},{3,1},{4,6},{5,7},{6,4},{7,5},{8,10},{9,11},{10,... | collective-permute-start | bytes 29192 | tf_op jit(solution)/shard_map/ppermute | solution.py:241
  13.0 7.7 %collective-permute-start.5 = (bf16[64,2048]{1,0:T(8,128)(2,1)S(1)}, bf16[64,2048]{1,0:T(8,128)(2,1)S(1)}, u32[]{:S(2)}, u32[]{:S(2)}) collective-permute-start(bf16[64,2048]{1,0:T(8,128)(2,1)S(1)} %get-tuple-element.159), channel_id=1, source_target_pairs={{0,2},{1,3},{2,0},{3,1},{4,6},{5,7},{6,4},{7,5},{8,10},{9,11},{10,... | collective-permute-start | bytes 786440 | tf_op jit(solution)/shard_map/ppermute | solution.py:269
  13.5 14.8 %collective-permute-start.7 = (bf16[48,2048]{1,0:T(8,128)(2,1)S(1)}, bf16[48,2048]{1,0:T(8,128)(2,1)S(1)}, u32[]{:S(2)}, u32[]{:S(2)}) collective-permute-start(bf16[48,2048]{1,0:T(8,128)(2,1)S(1)} %multiply_convert_fusion.1), channel_id=1, source_target_pairs={{0,8},{1,12},{2,10},{3,14},{4,9},{5,13},{6,11},{7,15},{8,1},{9,5},... | collective-permute-start | bytes 589832 | tf_op jit(solution)/shard_map/ppermute | solution.py:304
  16.4 17.3 %collective-permute-start.4 = (bf16[80,2048]{1,0:T(8,128)(2,1)S(1)}, bf16[80,2048]{1,0:T(8,128)(2,1)S(1)}, u32[]{:S(2)}, u32[]{:S(2)}) collective-permute-start(bf16[80,2048]{1,0:T(8,128)(2,1)S(1)} %pad_maximum_fusion.11), channel_id=1, source_target_pairs={{0,2},{1,3},{2,0},{3,1},{4,6},{5,7},{6,4},{7,5},{8,10},{9,11},{10,... | collective-permute-start | bytes 983048 | tf_op jit(solution)/shard_map/ppermute | solution.py:269
  20.8 12.3 %collective-permute-start.6 = (bf16[64,2048]{1,0:T(8,128)(2,1)S(1)}, bf16[64,2048]{1,0:T(8,128)(2,1)S(1)}, u32[]{:S(2)}, u32[]{:S(2)}) collective-permute-start(bf16[64,2048]{1,0:T(8,128)(2,1)S(1)} %get-tuple-element.179), channel_id=1, source_target_pairs={{0,8},{1,12},{2,10},{3,14},{4,9},{5,13},{6,11},{7,15},{8,1},{9,5},... | collective-permute-start | bytes 786440 | tf_op jit(solution)/shard_map/ppermute | solution.py:304
  25.0 12.4 %copy-start.2 = (bf16[2048,1024]{1,0:T(8,128)(2,1)S(1)}, bf16[2048,1024]{1,0:T(8,128)(2,1)}, u32[]{:S(2)}) copy-start(bf16[2048,1024]{1,0:T(8,128)(2,1)} %param.7) | copy-start | bytes 12582916
  25.1 16.4 %collective-permute-start.11 = (bf16[112,2048]{1,0:T(8,128)(2,1)S(1)}, bf16[112,2048]{1,0:T(8,128)(2,1)S(1)}, u32[]{:S(2)}, u32[]{:S(2)}) collective-permute-start(bf16[112,2048]{1,0:T(8,128)(2,1)S(1)} %pad_maximum_fusion.5), channel_id=1, source_target_pairs={{0,1},{1,4},{2,3},{3,6},{4,0},{5,5},{6,2},{7,7},{8,9},{9,12},{10,1... | collective-permute-start | bytes 1376264 | tf_op jit(solution)/shard_map/ppermute | solution.py:309
  28.4 8.7 %collective-permute-start.8 = (bf16[48,2048]{1,0:T(8,128)(2,1)S(1)}, bf16[48,2048]{1,0:T(8,128)(2,1)S(1)}, u32[]{:S(2)}, u32[]{:S(2)}) collective-permute-start(bf16[48,2048]{1,0:T(8,128)(2,1)S(1)} %collective-permute-done.7), channel_id=1, source_target_pairs={{0,2},{1,3},{2,0},{3,1},{4,6},{5,7},{6,4},{7,5},{8,10},{9,11},{10,... | collective-permute-start | bytes 589832 | tf_op jit(solution)/shard_map/ppermute | solution.py:314
  33.1 14.9 %collective-permute-start.13 = (bf16[64,2048]{1,0:T(8,128)(2,1)S(1)}, bf16[64,2048]{1,0:T(8,128)(2,1)S(1)}, u32[]{:S(2)}, u32[]{:S(2)}) collective-permute-start(bf16[64,2048]{1,0:T(8,128)(2,1)S(1)} %collective-permute-done.6), channel_id=1, source_target_pairs={{0,2},{1,3},{2,0},{3,1},{4,6},{5,7},{6,4},{7,5},{8,10},{9,11},{10,... | collective-permute-start | bytes 786440 | tf_op jit(solution)/shard_map/ppermute | solution.py:314
  33.7 21.4 %collective-permute-start.10 = (bf16[80,2048]{1,0:T(8,128)(2,1)S(1)}, bf16[80,2048]{1,0:T(8,128)(2,1)S(1)}, u32[]{:S(2)}, u32[]{:S(2)}) collective-permute-start(bf16[80,2048]{1,0:T(8,128)(2,1)S(1)} %get-tuple-element.172), channel_id=1, source_target_pairs={{0,8},{1,12},{2,10},{3,14},{4,9},{5,13},{6,11},{7,15},{8,1},{9,5},... | collective-permute-start | bytes 983048 | tf_op jit(solution)/shard_map/ppermute | solution.py:304
  37.2 1.6 %copy-start.3 = (bf16[2048,2,256]{2,1,0:T(2,128)(2,1)S(1)}, bf16[2048,2,256]{2,1,0:T(2,128)(2,1)}, u32[]{:S(2)}) copy-start(bf16[2048,2,256]{2,1,0:T(2,128)(2,1)} %param.8) | copy-start | bytes 6291460
  37.2 5.6 %collective-permute-start.14 = (bf16[96,2048]{1,0:T(8,128)(2,1)S(1)}, bf16[96,2048]{1,0:T(8,128)(2,1)S(1)}, u32[]{:S(2)}, u32[]{:S(2)}) collective-permute-start(bf16[96,2048]{1,0:T(8,128)(2,1)S(1)} %pad_maximum_fusion.6), channel_id=1, source_target_pairs={{0,1},{1,0},{2,3},{3,2},{4,5},{5,4},{6,7},{7,6},{8,9},{9,8},{10,11... | collective-permute-start | bytes 1179656 | tf_op jit(solution)/shard_map/ppermute | solution.py:325
  39.5 34.9 %collective-permute-start.9 = (bf16[80,2048]{1,0:T(8,128)(2,1)S(1)}, bf16[80,2048]{1,0:T(8,128)(2,1)S(1)}, u32[]{:S(2)}, u32[]{:S(2)}) collective-permute-start(bf16[80,2048]{1,0:T(8,128)(2,1)S(1)} %get-tuple-element.96), channel_id=1, source_target_pairs={{0,1},{1,4},{2,3},{3,6},{4,0},{5,5},{6,2},{7,7},{8,9},{9,12},{10,1... | collective-permute-start | bytes 983048 | tf_op jit(solution)/shard_map/ppermute | solution.py:309
  41.5 12.0 %collective-permute-start.12 = (bf16[112,2048]{1,0:T(8,128)(2,1)S(1)}, bf16[112,2048]{1,0:T(8,128)(2,1)S(1)}, u32[]{:S(2)}, u32[]{:S(2)}) collective-permute-start(bf16[112,2048]{1,0:T(8,128)(2,1)S(1)} %collective-permute-done.11), channel_id=1, source_target_pairs={{0,2},{1,3},{2,0},{3,1},{4,6},{5,7},{6,4},{7,5},{8,10},{9,11},{10,... | collective-permute-start | bytes 1376264 | tf_op jit(solution)/shard_map/ppermute | solution.py:314
  44.2 16.6 %collective-permute-start.17 = (bf16[192,1536]{1,0:T(8,128)(2,1)S(1)}, bf16[192,1536]{1,0:T(8,128)(2,1)S(1)}, u32[]{:S(2)}, u32[]{:S(2)}) collective-permute-start(bf16[192,1536]{1,0:T(8,128)(2,1)S(1)} %convolution_convert_fusion.2), channel_id=1, source_target_pairs={{0,4},{12,8},{1,5},{13,9},{2,6},{14,10},{3,7},{15,11},{16,20},{28,... | collective-permute-start | bytes 1769480 | tf_op jit(solution)/shard_map/ppermute | solution.py:335
  48.1 8.3 %collective-permute-start.18 = (bf16[128,2048]{1,0:T(8,128)(2,1)S(1)}, bf16[128,2048]{1,0:T(8,128)(2,1)S(1)}, u32[]{:S(2)}, u32[]{:S(2)}) collective-permute-start(bf16[128,2048]{1,0:T(8,128)(2,1)S(1)} %pad_maximum_fusion.3), channel_id=1, source_target_pairs={{0,1},{1,0},{2,3},{3,2},{4,5},{5,4},{6,7},{7,6},{8,9},{9,8},{10,11... | collective-permute-start | bytes 1572872 | tf_op jit(solution)/shard_map/ppermute | solution.py:325
  53.7 7.2 %collective-permute-start.16 = (bf16[224,2048]{1,0:T(8,128)(2,1)S(1)}, bf16[224,2048]{1,0:T(8,128)(2,1)S(1)}, u32[]{:S(2)}, u32[]{:S(2)}) collective-permute-start(bf16[224,2048]{1,0:T(8,128)(2,1)S(1)} %pad_maximum_fusion), channel_id=1, source_target_pairs={{0,1},{1,0},{2,3},{3,2},{4,5},{5,4},{6,7},{7,6},{8,9},{9,8},{10,11... | collective-permute-start | bytes 2752520 | tf_op jit(solution)/shard_map/ppermute | solution.py:325
  55.1 9.7 %collective-permute-start.15 = (bf16[80,2048]{1,0:T(8,128)(2,1)S(1)}, bf16[80,2048]{1,0:T(8,128)(2,1)S(1)}, u32[]{:S(2)}, u32[]{:S(2)}) collective-permute-start(bf16[80,2048]{1,0:T(8,128)(2,1)S(1)} %collective-permute-done.10), channel_id=1, source_target_pairs={{0,2},{1,3},{2,0},{3,1},{4,6},{5,7},{6,4},{7,5},{8,10},{9,11},{10,... | collective-permute-start | bytes 983048 | tf_op jit(solution)/shard_map/ppermute | solution.py:314
  58.2 20.3 %collective-permute-start.24 = (bf16[256,1536]{1,0:T(8,128)(2,1)S(1)}, bf16[256,1536]{1,0:T(8,128)(2,1)S(1)}, u32[]{:S(2)}, u32[]{:S(2)}) collective-permute-start(bf16[256,1536]{1,0:T(8,128)(2,1)S(1)} %convolution_convert_fusion), channel_id=1, source_target_pairs={{0,4},{12,8},{1,5},{13,9},{2,6},{14,10},{3,7},{15,11},{16,20},{28,... | collective-permute-start | bytes 2359304 | tf_op jit(solution)/shard_map/ppermute | solution.py:335
  60.9 6.4 %copy-start.4 = (bf16[224,2048]{1,0:T(8,128)(2,1)}, bf16[224,2048]{1,0:T(8,128)(2,1)S(1)}, u32[]{:S(2)}) copy-start(bf16[224,2048]{1,0:T(8,128)(2,1)S(1)} %collective-permute-done.16) | copy-start | bytes 2752516
  65.0 2.4 %collective-permute-start.19 = (bf16[160,2048]{1,0:T(8,128)(2,1)S(1)}, bf16[160,2048]{1,0:T(8,128)(2,1)S(1)}, u32[]{:S(2)}, u32[]{:S(2)}) collective-permute-start(bf16[160,2048]{1,0:T(8,128)(2,1)S(1)} %pad_maximum_fusion.1), channel_id=1, source_target_pairs={{0,1},{1,0},{2,3},{3,2},{4,5},{5,4},{6,7},{7,6},{8,9},{9,8},{10,11... | collective-permute-start | bytes 1966088 | tf_op jit(solution)/shard_map/ppermute | solution.py:325
  65.2 18.0 %collective-permute-start.22 = (bf16[96,1536]{1,0:T(8,128)(2,1)S(1)}, bf16[96,1536]{1,0:T(8,128)(2,1)S(1)}, u32[]{:S(2)}, u32[]{:S(2)}) collective-permute-start(bf16[96,1536]{1,0:T(8,128)(2,1)S(1)} %get-tuple-element.176), channel_id=1, source_target_pairs={{4,12},{8,0},{5,13},{9,1},{6,14},{10,2},{7,15},{11,3},{20,28},{24,... | collective-permute-start | bytes 884744 | tf_op jit(solution)/shard_map/ppermute | solution.py:350
  66.5 16.8 %collective-permute-start.23 = (bf16[96,1536]{1,0:T(8,128)(2,1)S(1)}, bf16[96,1536]{1,0:T(8,128)(2,1)S(1)}, u32[]{:S(2)}, u32[]{:S(2)}) collective-permute-start(bf16[96,1536]{1,0:T(8,128)(2,1)S(1)} %get-tuple-element.175), channel_id=1, source_target_pairs={{4,8},{8,4},{5,9},{9,5},{6,10},{10,6},{7,11},{11,7},{20,24},{24,20... | collective-permute-start | bytes 884744 | tf_op jit(solution)/shard_map/ppermute | solution.py:351
  67.5 21.1 %copy-start.5 = (bf16[160,2048]{1,0:T(8,128)(2,1)}, bf16[160,2048]{1,0:T(8,128)(2,1)S(1)}, u32[]{:S(2)}) copy-start(bf16[160,2048]{1,0:T(8,128)(2,1)S(1)} %collective-permute-done.19) | copy-start | bytes 1966084
  67.5 17.4 %collective-permute-start.21 = (bf16[96,1536]{1,0:T(8,128)(2,1)S(1)}, bf16[96,1536]{1,0:T(8,128)(2,1)S(1)}, u32[]{:S(2)}, u32[]{:S(2)}) collective-permute-start(bf16[96,1536]{1,0:T(8,128)(2,1)S(1)} %slice.286), channel_id=1, source_target_pairs={{0,4},{4,0},{8,12},{12,8},{1,5},{5,1},{9,13},{13,9},{2,6},{6,2},{1... | collective-permute-start | bytes 884744 | tf_op jit(solution)/shard_map/ppermute | solution.py:343
  72.9 2.7 %slice-start = ((bf16[224,2048]{1,0:T(8,128)(2,1)}), bf16[128,2048]{1,0:T(8,128)(2,1)S(1)}, s32[]{:S(2)}) async-start(bf16[224,2048]{1,0:T(8,128)(2,1)} %copy-done.4), calls=%async_computation | async-start | bytes 1048576 | tf_op jit(solution)/shard_map/slice | solution.py:329
  74.3 14.2 %collective-permute-start.20 = (bf16[80,2048]{1,0:T(8,128)(2,1)S(1)}, bf16[80,2048]{1,0:T(8,128)(2,1)S(1)}, u32[]{:S(2)}, u32[]{:S(2)}) collective-permute-start(bf16[80,2048]{1,0:T(8,128)(2,1)S(1)} %collective-permute-done.9), channel_id=1, source_target_pairs={{0,2},{1,3},{2,0},{3,1},{4,6},{5,7},{6,4},{7,5},{8,10},{9,11},{10,... | collective-permute-start | bytes 983048 | tf_op jit(solution)/shard_map/ppermute | solution.py:314
  78.5 19.0 %collective-permute-start.26 = (bf16[192,1536]{1,0:T(8,128)(2,1)S(1)}, bf16[192,1536]{1,0:T(8,128)(2,1)S(1)}, u32[]{:S(2)}, u32[]{:S(2)}) collective-permute-start(bf16[192,1536]{1,0:T(8,128)(2,1)S(1)} %convolution_convert_fusion.1), channel_id=1, source_target_pairs={{0,4},{12,8},{1,5},{13,9},{2,6},{14,10},{3,7},{15,11},{16,20},{28,... | collective-permute-start | bytes 1769480 | tf_op jit(solution)/shard_map/ppermute | solution.py:335
  83.2 30.0 %collective-permute-start.29 = (bf16[128,1536]{1,0:T(8,128)(2,1)S(1)}, bf16[128,1536]{1,0:T(8,128)(2,1)S(1)}, u32[]{:S(2)}, u32[]{:S(2)}) collective-permute-start(bf16[128,1536]{1,0:T(8,128)(2,1)S(1)} %slice.284), channel_id=1, source_target_pairs={{0,4},{4,0},{8,12},{12,8},{1,5},{5,1},{9,13},{13,9},{2,6},{6,2},{1... | collective-permute-start | bytes 1179656 | tf_op jit(solution)/shard_map/ppermute | solution.py:343
  84.9 22.1 %collective-permute-start.30 = (bf16[128,1536]{1,0:T(8,128)(2,1)S(1)}, bf16[128,1536]{1,0:T(8,128)(2,1)S(1)}, u32[]{:S(2)}, u32[]{:S(2)}) collective-permute-start(bf16[128,1536]{1,0:T(8,128)(2,1)S(1)} %get-tuple-element.166), channel_id=1, source_target_pairs={{4,12},{8,0},{5,13},{9,1},{6,14},{10,2},{7,15},{11,3},{20,28},{24,... | collective-permute-start | bytes 1179656 | tf_op jit(solution)/shard_map/ppermute | solution.py:350
  86.2 21.5 %collective-permute-start.31 = (bf16[128,1536]{1,0:T(8,128)(2,1)S(1)}, bf16[128,1536]{1,0:T(8,128)(2,1)S(1)}, u32[]{:S(2)}, u32[]{:S(2)}) collective-permute-start(bf16[128,1536]{1,0:T(8,128)(2,1)S(1)} %get-tuple-element.165), channel_id=1, source_target_pairs={{4,8},{8,4},{5,9},{9,5},{6,10},{10,6},{7,11},{11,7},{20,24},{24,20... | collective-permute-start | bytes 1179656 | tf_op jit(solution)/shard_map/ppermute | solution.py:351
  88.7 8.9 %slice-start.1 = ((bf16[160,2048]{1,0:T(8,128)(2,1)}), bf16[64,2048]{1,0:T(8,128)(2,1)S(1)}, s32[]{:S(2)}) async-start(bf16[160,2048]{1,0:T(8,128)(2,1)} %copy-done.5), calls=%async_computation.1 | async-start | bytes 524288 | tf_op jit(solution)/shard_map/slice | solution.py:329
  88.8 14.4 %collective-permute-start.25 = (bf16[160,2048]{1,0:T(8,128)(2,1)S(1)}, bf16[160,2048]{1,0:T(8,128)(2,1)S(1)}, u32[]{:S(2)}, u32[]{:S(2)}) collective-permute-start(bf16[160,2048]{1,0:T(8,128)(2,1)S(1)} %pad_maximum_fusion.2), channel_id=1, source_target_pairs={{0,1},{1,0},{2,3},{3,2},{4,5},{5,4},{6,7},{7,6},{8,9},{9,8},{10,11... | collective-permute-start | bytes 1966088 | tf_op jit(solution)/shard_map/ppermute | solution.py:325
  98.6 16.8 %collective-permute-start.28 = (bf16[128,1536]{1,0:T(8,128)(2,1)S(1)}, bf16[128,1536]{1,0:T(8,128)(2,1)S(1)}, u32[]{:S(2)}, u32[]{:S(2)}) collective-permute-start(bf16[128,1536]{1,0:T(8,128)(2,1)S(1)} %convolution_convert_fusion.3), channel_id=1, source_target_pairs={{0,4},{12,8},{1,5},{13,9},{2,6},{14,10},{3,7},{15,11},{16,20},{28,... | collective-permute-start | bytes 1179656 | tf_op jit(solution)/shard_map/ppermute | solution.py:335
  103.1 14.4 %collective-permute-start.35 = (bf16[96,1536]{1,0:T(8,128)(2,1)S(1)}, bf16[96,1536]{1,0:T(8,128)(2,1)S(1)}, u32[]{:S(2)}, u32[]{:S(2)}) collective-permute-start(bf16[96,1536]{1,0:T(8,128)(2,1)S(1)} %get-tuple-element.174), channel_id=1, source_target_pairs={{4,12},{8,0},{5,13},{9,1},{6,14},{10,2},{7,15},{11,3},{20,28},{24,... | collective-permute-start | bytes 884744 | tf_op jit(solution)/shard_map/ppermute | solution.py:350
  107.0 16.0 %collective-permute-start.36 = (bf16[96,1536]{1,0:T(8,128)(2,1)S(1)}, bf16[96,1536]{1,0:T(8,128)(2,1)S(1)}, u32[]{:S(2)}, u32[]{:S(2)}) collective-permute-start(bf16[96,1536]{1,0:T(8,128)(2,1)S(1)} %get-tuple-element.173), channel_id=1, source_target_pairs={{4,8},{8,4},{5,9},{9,5},{6,10},{10,6},{7,11},{11,7},{20,24},{24,20... | collective-permute-start | bytes 884744 | tf_op jit(solution)/shard_map/ppermute | solution.py:351
  107.7 15.3 %collective-permute-start.34 = (bf16[96,1536]{1,0:T(8,128)(2,1)S(1)}, bf16[96,1536]{1,0:T(8,128)(2,1)S(1)}, u32[]{:S(2)}, u32[]{:S(2)}) collective-permute-start(bf16[96,1536]{1,0:T(8,128)(2,1)S(1)} %slice.285), channel_id=1, source_target_pairs={{0,4},{4,0},{8,12},{12,8},{1,5},{5,1},{9,13},{13,9},{2,6},{6,2},{1... | collective-permute-start | bytes 884744 | tf_op jit(solution)/shard_map/ppermute | solution.py:343
  115.6 10.3 %collective-permute-start.32 = (bf16[64,1536]{1,0:T(8,128)(2,1)S(1)}, bf16[64,1536]{1,0:T(8,128)(2,1)S(1)}, u32[]{:S(2)}, u32[]{:S(2)}) collective-permute-start(bf16[64,1536]{1,0:T(8,128)(2,1)S(1)} %get-tuple-element.182), channel_id=1, source_target_pairs={{4,12},{8,0},{5,13},{9,1},{6,14},{10,2},{7,15},{11,3},{20,28},{24,... | collective-permute-start | bytes 589832 | tf_op jit(solution)/shard_map/ppermute | solution.py:350
  116.9 9.0 %collective-permute-start.33 = (bf16[64,1536]{1,0:T(8,128)(2,1)S(1)}, bf16[64,1536]{1,0:T(8,128)(2,1)S(1)}, u32[]{:S(2)}, u32[]{:S(2)}) collective-permute-start(bf16[64,1536]{1,0:T(8,128)(2,1)S(1)} %get-tuple-element.181), channel_id=1, source_target_pairs={{4,8},{8,4},{5,9},{9,5},{6,10},{10,6},{7,11},{11,7},{20,24},{24,20... | collective-permute-start | bytes 589832 | tf_op jit(solution)/shard_map/ppermute | solution.py:351
  117.6 10.4 %collective-permute-start.27 = (bf16[64,1536]{1,0:T(8,128)(2,1)S(1)}, bf16[64,1536]{1,0:T(8,128)(2,1)S(1)}, u32[]{:S(2)}, u32[]{:S(2)}) collective-permute-start(bf16[64,1536]{1,0:T(8,128)(2,1)S(1)} %slice.287), channel_id=1, source_target_pairs={{0,4},{4,0},{8,12},{12,8},{1,5},{5,1},{9,13},{13,9},{2,6},{6,2},{1... | collective-permute-start | bytes 589832 | tf_op jit(solution)/shard_map/ppermute | solution.py:343
